TPU v7x, 32 devices: a whole 2x2x4 slice. The times are simulated.
32 devices in a mesh: dp: 4 (over z), expert: 8 (over y, x, core).
Axes of the slice: x: 2, y: 2, z: 4, core: 2. Of those that a mesh axis runs over, the one named last changes fastest.
Arguments:
- tokens: bfloat16 [4096, 2048], P(('dp', 'expert')), may hold values from -6 to 6
- cotangent: bfloat16 [4096, 2048], P(('dp', 'expert')), may hold values from -6 to 6
- lengths: int32 [4], P('dp'), may hold values from 897 to 1024, as said below
- routes: int32 [4096, 6], P(('dp', 'expert')), may hold values from 0 to 15, all different within a row
- place_order: int32 [32, 768], P(('dp', 'expert')), may hold values from 0 to 767, each once within a row
- attn_gain: bfloat16 [2048], P(('dp', 'expert')), may hold values from 0.099609375 to 1.8984375
- w_query: bfloat16 [2048, 3072], P(('dp', 'expert')), may hold values from -0.125 to 0.125
- w_latent: bfloat16 [2048, 576], P(('dp', 'expert')), may hold values from -0.125 to 0.125
- latent_gain: bfloat16 [512], P(('dp', 'expert')), may hold values from 0.099609375 to 1.8984375
- w_expand: bfloat16 [512, 4096], P(('dp', 'expert')), may hold values from -0.25 to 0.25
- w_out: bfloat16 [2048, 2048], P(('dp', 'expert')), may hold values from -1 to 1
- ffn_gain: bfloat16 [2048], P(('dp', 'expert')), may hold values from 0.099609375 to 1.8984375
- w_router: bfloat16 [2048, 16], P(('dp', 'expert')), may hold values from -0.0625 to 0.0625
- shared_gate: bfloat16 [2048, 2816], P(('dp', 'expert')), may hold values from -0.125 to 0.125
- shared_up: bfloat16 [2048, 2816], P(('dp', 'expert')), may hold values from -0.125 to 0.125
- shared_down: bfloat16 [2048, 2816], P(('dp', 'expert')), may hold values from -0.109375 to 0.109375
- expert_gate: bfloat16 [16, 2048, 1408], P('expert', 'dp'), may hold values from -0.125 to 0.125
- expert_up: bfloat16 [16, 2048, 1408], P('expert', 'dp'), may hold values from -0.125 to 0.125
- expert_down: bfloat16 [16, 2048, 1408], P('expert', 'dp'), may hold values from -1.25 to 1.25
Outputs:
- out_tokens: bfloat16 [4096, 2048], P(('dp', 'expert'))
- grad_tokens: float32 [4096, 2048], P(('dp', 'expert'))
- grad_attn_gain: float32 [2048], P(('dp', 'expert'))
- grad_w_query: float32 [2048, 3072], P(('dp', 'expert'))
- grad_w_latent: float32 [2048, 576], P(('dp', 'expert'))
- grad_latent_gain: float32 [512], P(('dp', 'expert'))
- grad_w_expand: float32 [512, 4096], P(('dp', 'expert'))
- grad_w_out: float32 [2048, 2048], P(('dp', 'expert'))
- grad_ffn_gain: float32 [2048], P(('dp', 'expert'))
- grad_w_router: float32 [2048, 16], P(('dp', 'expert'))
- grad_shared_gate: float32 [2048, 2816], P(('dp', 'expert'))
- grad_shared_up: float32 [2048, 2816], P(('dp', 'expert'))
- grad_shared_down: float32 [2048, 2816], P(('dp', 'expert'))
- grad_expert_gate: float32 [16, 2048, 1408], P('expert', 'dp')
- grad_expert_up: float32 [16, 2048, 1408], P('expert', 'dp')
- grad_expert_down: float32 [16, 2048, 1408], P('expert', 'dp')
Inputs may be any that keep to these rules, and one draw needn't show every extreme that they name: `lengths`: each group's length reaches the group's last device, and some group has the full 1024. `routes`: each row names 6 different experts. `place_order`: each device's row is a permutation.
All inputs are finite; a program needn't handle non-finite values.
Results may differ from a plain program's by a relative error of at most 0.02.
Values may be sent and summed in bfloat16 or wider, within the bound.
A program may use at most 448 MiB of HBM per device.

v0:
```python
import jax
import jax.numpy as jnp
from jax import lax
from jax.sharding import PartitionSpec as P

H = 16
DH = 128
DR = 64
DV = 128
KVR = 512


norm_eps = 1e-06
masked_score = -1e30
exact_mode = lax.Precision.HIGHEST


def rms_norm(values, scale_gain):
    return (
        values
        * lax.rsqrt(jnp.mean(values * values, axis=-1, keepdims=True) + norm_eps)
        * scale_gain
    )


def rotate(values, cos_table, sine_table):
    half_dim = values.shape[-1] // 2
    first_half = values[..., :half_dim]
    second_half = values[..., half_dim:]
    return jnp.concatenate(
        [
            first_half * cos_table - second_half * sine_table,
            second_half * cos_table + first_half * sine_table,
        ],
        axis=-1,
    )


def rope_tables(positions):
    half_dim = DR // 2
    inv_freq = 10000.0 ** (-(jnp.arange(half_dim).astype(jnp.float32) * 2.0) / DR)
    angles = positions.astype(jnp.float32)[:, None] * inv_freq[None, :]
    return (jnp.cos(angles), jnp.sin(angles))


def swiglu(gate_in, up_in):
    return jax.nn.silu(gate_in) * up_in


def contract_rows(left_side, right_side):
    return lax.dot_general(
        left_side, right_side, (((0,), (0,)), ((), ())), preferred_element_type=jnp.float32
    )


def contract_cols(left_side, right_side):
    return lax.dot_general(
        left_side, right_side, (((1,), (1,)), ((), ())), preferred_element_type=jnp.float32
    )


def exact_rows(left_side, right_side):
    return lax.dot_general(
        left_side,
        right_side,
        (((0,), (0,)), ((), ())),
        precision=exact_mode,
        preferred_element_type=jnp.float32,
    )


def exact_cols(left_side, right_side):
    return lax.dot_general(
        left_side,
        right_side,
        (((1,), (1,)), ((), ())),
        precision=exact_mode,
        preferred_element_type=jnp.float32,
    )


def slot_places(route_rows, pair_order, capacity):
    pair_expert = route_rows.reshape(-1)
    earlier = pair_order[None, :] < pair_order[:, None]
    same_expert = pair_expert[None, :] == pair_expert[:, None]
    places = jnp.sum((earlier & same_expert).astype(jnp.int32), axis=1)
    slot_index = jnp.where(places < capacity, pair_expert * capacity + places, -1)
    return slot_index.reshape(route_rows.shape)


def shards(
    tokens,
    cotangent,
    lengths,
    routes,
    place_order,
    attn_gain,
    w_query,
    w_latent,
    latent_gain,
    w_expand,
    w_out,
    ffn_gain,
    w_router,
    shared_gate,
    shared_up,
    shared_down,
    expert_gate,
    expert_up,
    expert_down,
):
    local_rows = tokens.shape[0]
    group_size = lax.axis_size("expert")
    group_place = lax.axis_index("expert")
    expert_count = w_router.shape[1]
    top_k = routes.shape[1]
    capacity = (local_rows * top_k * 5 + 4 * expert_count - 1) // (4 * expert_count)
    slots_all = expert_count * capacity
    local_experts = expert_count // group_size
    seq_len = local_rows * group_size
    seq_length = lengths[0]
    model_dim = tokens.shape[1]
    gain_attn, query_full, latent_full, gain_latent, expand_full, out_full = (
        lax.all_gather(attn_gain, ("dp", "expert"), axis=0, tiled=True),
        lax.all_gather(w_query, ("dp", "expert"), axis=0, tiled=True),
        lax.all_gather(w_latent, ("dp", "expert"), axis=0, tiled=True),
        lax.all_gather(latent_gain, ("dp", "expert"), axis=0, tiled=True),
        lax.all_gather(w_expand, ("dp", "expert"), axis=0, tiled=True),
        lax.all_gather(w_out, ("dp", "expert"), axis=0, tiled=True),
    )
    gain_ffn, router_full, sgate_full, sup_full, sdown_full = (
        lax.all_gather(ffn_gain, ("dp", "expert"), axis=0, tiled=True),
        lax.all_gather(w_router, ("dp", "expert"), axis=0, tiled=True),
        lax.all_gather(shared_gate, ("dp", "expert"), axis=0, tiled=True),
        lax.all_gather(shared_up, ("dp", "expert"), axis=0, tiled=True),
        lax.all_gather(shared_down, ("dp", "expert"), axis=0, tiled=True),
    )
    expert_gate_complete, expert_up_complete, expert_down_complete = (
        lax.all_gather(expert_gate, "dp", axis=1, tiled=True),
        lax.all_gather(expert_up, "dp", axis=1, tiled=True),
        lax.all_gather(expert_down, "dp", axis=1, tiled=True),
    )
    tokens_f = tokens.astype(jnp.float32)
    positions = group_place * local_rows + jnp.arange(local_rows)
    cos_table, sine_table = rope_tables(positions)
    gain_one = gain_attn.astype(jnp.float32)
    normed_one, norm_one_back = jax.vjp(rms_norm, tokens_f, gain_one)
    hidden_one = normed_one.astype(jnp.bfloat16)
    query_raw = jnp.dot(hidden_one, query_full, preferred_element_type=jnp.float32).reshape(
        local_rows, H, DH + DR
    )

    def make_queries(query_in):
        return jnp.concatenate(
            [
                query_in[..., :DH],
                rotate(query_in[..., DH:], cos_table[:, None, :], sine_table[:, None, :]),
            ],
            axis=-1,
        )

    query_rot, query_back = jax.vjp(make_queries, query_raw)
    queries = query_rot.astype(jnp.bfloat16)
    latent_raw = jnp.dot(hidden_one, latent_full, preferred_element_type=jnp.float32)

    def make_latent(latent_in, gain_in):
        return (
            rms_norm(latent_in[:, :KVR], gain_in),
            rotate(latent_in[:, KVR:], cos_table, sine_table),
        )

    (latent_normed, rope_key), latent_back = jax.vjp(
        make_latent, latent_raw, gain_latent.astype(jnp.float32)
    )
    latent_low = latent_normed.astype(jnp.bfloat16)
    rope_low = rope_key.astype(jnp.bfloat16)
    expanded = jnp.dot(latent_low, expand_full, preferred_element_type=jnp.float32).astype(
        jnp.bfloat16
    )
    key_rows, rope_rows = (
        lax.all_gather(expanded, "expert", axis=0, tiled=True),
        lax.all_gather(rope_low, "expert", axis=0, tiled=True),
    )
    key_view = key_rows.reshape(seq_len, H, DH + DV)
    key_nope = key_view[..., :DH]
    value_rows = key_view[..., DH:]
    score_scale = (DH + DR) ** (-0.5)
    key_pos = jnp.arange(seq_len)
    allowed = (key_pos[None, :] <= positions[:, None]) & (key_pos[None, :] < seq_length)

    def score_block():
        raw_scores = jnp.einsum(
            "qhd,khd->hqk", queries[..., :DH], key_nope, preferred_element_type=jnp.float32
        ) + jnp.einsum(
            "qhr,kr->hqk", queries[..., DH:], rope_rows, preferred_element_type=jnp.float32
        )
        return jnp.where(allowed[None], raw_scores * score_scale, masked_score)

    scores = score_block()
    top_score = jnp.max(scores, axis=-1, keepdims=True)
    exp_scores = jnp.exp(scores - top_score)
    row_total = jnp.sum(exp_scores, axis=-1, keepdims=True)
    log_total = top_score + jnp.log(row_total)
    probs_low = (exp_scores / row_total).astype(jnp.bfloat16)
    attended = (
        jnp.einsum("hqk,khv->qhv", probs_low, value_rows, preferred_element_type=jnp.float32)
        .astype(jnp.bfloat16)
        .reshape(local_rows, H * DV)
    )
    residual = tokens_f + jnp.dot(attended, out_full, preferred_element_type=jnp.float32)
    normed_two, norm_two_back = jax.vjp(rms_norm, residual, gain_ffn.astype(jnp.float32))
    hidden_two = normed_two.astype(jnp.bfloat16)
    logits = jnp.dot(hidden_two, router_full, preferred_element_type=jnp.float32)
    top_logit = jnp.max(logits, axis=-1, keepdims=True)
    exp_logits = jnp.exp(logits - top_logit)
    router_probs = exp_logits / jnp.sum(exp_logits, axis=-1, keepdims=True)
    chosen = (routes[..., None] == jnp.arange(expert_count)[None, None, :]).astype(jnp.float32)
    gate_values = jnp.sum(router_probs[:, None, :] * chosen, axis=-1)
    shared_a = jnp.dot(hidden_two, sgate_full, preferred_element_type=jnp.float32)
    shared_b = jnp.dot(hidden_two, sup_full, preferred_element_type=jnp.float32)
    shared_hidden = swiglu(shared_a, shared_b).astype(jnp.bfloat16)
    shared_out = contract_cols(shared_hidden, sdown_full)
    slot_index = slot_places(routes, place_order[0], capacity)
    pair_hot = (slot_index[..., None] == jnp.arange(slots_all)[None, None, :]).astype(jnp.bfloat16)
    dispatch = jnp.sum(pair_hot, axis=1)
    send_block = contract_rows(dispatch, hidden_two).astype(jnp.bfloat16)
    incoming = lax.all_to_all(
        send_block.reshape(group_size, local_experts * capacity, model_dim),
        "expert",
        split_axis=0,
        concat_axis=0,
        tiled=True,
    )
    expert_input_rows = (
        incoming.reshape(group_size, local_experts, capacity, model_dim)
        .transpose(1, 0, 2, 3)
        .reshape(local_experts, group_size * capacity, model_dim)
    )
    expert_a = jnp.einsum(
        "yug,ygp->yup", expert_input_rows, expert_gate_complete, preferred_element_type=jnp.float32
    )
    expert_second_operand = jnp.einsum(
        "yug,ygp->yup", expert_input_rows, expert_up_complete, preferred_element_type=jnp.float32
    )
    expert_hidden = swiglu(expert_a, expert_second_operand).astype(jnp.bfloat16)
    expert_rows = jnp.einsum(
        "zan,zin->zai", expert_hidden, expert_down_complete, preferred_element_type=jnp.float32
    ).astype(jnp.bfloat16)
    going_back = (
        expert_rows.reshape(local_experts, group_size, capacity, model_dim)
        .transpose(1, 0, 2, 3)
        .reshape(group_size, local_experts * capacity, model_dim)
    )
    returned = lax.all_to_all(
        going_back, "expert", split_axis=0, concat_axis=0, tiled=True
    ).reshape(slots_all, model_dim)
    pair_rows = jnp.einsum("rke,ed->rkd", pair_hot, returned, preferred_element_type=jnp.float32)
    routed = jnp.sum(gate_values[..., None] * pair_rows, axis=1)
    out_tokens = (residual + shared_out + routed).astype(jnp.bfloat16)
    (
        query_again,
        latent_again,
        expand_again,
        out_again,
        router_again,
        sgate_again,
        sup_again,
        sdown_again,
    ) = (
        lax.all_gather(w_query, ("dp", "expert"), axis=0, tiled=True),
        lax.all_gather(w_latent, ("dp", "expert"), axis=0, tiled=True),
        lax.all_gather(w_expand, ("dp", "expert"), axis=0, tiled=True),
        lax.all_gather(w_out, ("dp", "expert"), axis=0, tiled=True),
        lax.all_gather(w_router, ("dp", "expert"), axis=0, tiled=True),
        lax.all_gather(shared_gate, ("dp", "expert"), axis=0, tiled=True),
        lax.all_gather(shared_up, ("dp", "expert"), axis=0, tiled=True),
        lax.all_gather(shared_down, ("dp", "expert"), axis=0, tiled=True),
    )
    expert_gate_recomputed, expert_up_recomputed, expert_down_recomputed = (
        lax.all_gather(expert_gate, "dp", axis=1, tiled=True),
        lax.all_gather(expert_up, "dp", axis=1, tiled=True),
        lax.all_gather(expert_down, "dp", axis=1, tiled=True),
    )
    grad_out_f = cotangent.astype(jnp.float32)
    grad_gates = jnp.sum(grad_out_f[:, None, :] * pair_rows, axis=-1)
    pair_grad = (gate_values[..., None] * grad_out_f[:, None, :]).astype(jnp.bfloat16)
    slot_grad = jnp.einsum(
        "rke,rkd->ed", pair_hot, pair_grad, preferred_element_type=jnp.float32
    ).astype(jnp.bfloat16)
    grad_incoming = lax.all_to_all(
        slot_grad.reshape(group_size, local_experts * capacity, model_dim),
        "expert",
        split_axis=0,
        concat_axis=0,
        tiled=True,
    )
    grad_rows = (
        grad_incoming.reshape(group_size, local_experts, capacity, model_dim)
        .transpose(1, 0, 2, 3)
        .reshape(local_experts, group_size * capacity, model_dim)
    )
    grad_hidden_e = jnp.einsum(
        "yug,ygp->yup", grad_rows, expert_down_recomputed, preferred_element_type=jnp.float32
    )
    grad_edown = jnp.einsum(
        "erd,erf->edf", grad_rows, expert_hidden, preferred_element_type=jnp.float32
    )
    _, expert_swiglu_back = jax.vjp(swiglu, expert_a, expert_second_operand)
    grad_ea, grad_eb = expert_swiglu_back(grad_hidden_e)
    grad_ea_low = grad_ea.astype(jnp.bfloat16)
    gradient_expert_second_reduced = grad_eb.astype(jnp.bfloat16)
    grad_egate = jnp.einsum(
        "erd,erf->edf", expert_input_rows, grad_ea_low, preferred_element_type=jnp.float32
    )
    gradient_expert_up = jnp.einsum(
        "erd,erf->edf",
        expert_input_rows,
        gradient_expert_second_reduced,
        preferred_element_type=jnp.float32,
    )
    grad_expert_in = (
        jnp.einsum(
            "zan,zin->zai", grad_ea_low, expert_gate_recomputed, preferred_element_type=jnp.float32
        )
        + jnp.einsum(
            "zan,zin->zai",
            gradient_expert_second_reduced,
            expert_up_recomputed,
            preferred_element_type=jnp.float32,
        )
    ).astype(jnp.bfloat16)
    going_grads = (
        grad_expert_in.reshape(local_experts, group_size, capacity, model_dim)
        .transpose(1, 0, 2, 3)
        .reshape(group_size, local_experts * capacity, model_dim)
    )
    grad_slots = lax.all_to_all(
        going_grads, "expert", split_axis=0, concat_axis=0, tiled=True
    ).reshape(slots_all, model_dim)
    grad_hidden_two = jnp.dot(dispatch, grad_slots, preferred_element_type=jnp.float32)
    summed_expert_gate, summed_expert_up, summed_expert_down = (
        lax.psum_scatter(
            grad_egate.astype(jnp.bfloat16), "dp", scatter_dimension=1, tiled=True
        ).astype(jnp.float32),
        lax.psum_scatter(
            gradient_expert_up.astype(jnp.bfloat16), "dp", scatter_dimension=1, tiled=True
        ).astype(jnp.float32),
        lax.psum_scatter(
            grad_edown.astype(jnp.bfloat16), "dp", scatter_dimension=1, tiled=True
        ).astype(jnp.float32),
    )
    grad_probs = jnp.sum(grad_gates[..., None] * chosen, axis=1)
    grad_logits = (
        router_probs * (grad_probs - jnp.sum(grad_probs * router_probs, axis=-1, keepdims=True))
    ).astype(jnp.bfloat16)
    grad_router = contract_rows(hidden_two, grad_logits)
    grad_hidden_two = grad_hidden_two + contract_cols(grad_logits, router_again)
    grad_shared_hidden = jnp.dot(cotangent, sdown_again, preferred_element_type=jnp.float32)
    grad_sdown = contract_rows(cotangent, shared_hidden)
    _, shared_swiglu_back = jax.vjp(swiglu, shared_a, shared_b)
    grad_sa, grad_sb = shared_swiglu_back(grad_shared_hidden)
    grad_sa_low = grad_sa.astype(jnp.bfloat16)
    grad_sb_low = grad_sb.astype(jnp.bfloat16)
    grad_sgate = contract_rows(hidden_two, grad_sa_low)
    grad_sup = contract_rows(hidden_two, grad_sb_low)
    grad_hidden_two = (
        grad_hidden_two
        + contract_cols(grad_sa_low, sgate_again)
        + contract_cols(grad_sb_low, sup_again)
    )
    grad_resid_norm, grad_gain_two = norm_two_back(grad_hidden_two)
    grad_residual = grad_out_f + grad_resid_norm
    grad_attn_low = grad_residual.astype(jnp.bfloat16)
    grad_wout = contract_rows(attended, grad_attn_low)
    grad_attended = (
        contract_cols(grad_attn_low, out_again).astype(jnp.bfloat16).reshape(local_rows, H, DV)
    )
    attn_probs = jnp.exp(score_block() - log_total)
    grad_attn_probs = jnp.einsum(
        "qhv,khv->hqk", grad_attended, value_rows, preferred_element_type=jnp.float32
    )
    grad_scores = attn_probs * (
        grad_attn_probs - jnp.sum(grad_attn_probs * attn_probs, axis=-1, keepdims=True)
    )
    grad_raw = jnp.where(allowed[None], grad_scores * score_scale, 0.0).astype(jnp.bfloat16)
    grad_queries = jnp.concatenate(
        [
            jnp.einsum("hqk,khd->qhd", grad_raw, key_nope, preferred_element_type=jnp.float32),
            jnp.einsum("hqk,kr->qhr", grad_raw, rope_rows, preferred_element_type=jnp.float32),
        ],
        axis=-1,
    )
    grad_key_nope = jnp.einsum(
        "hqk,qhd->khd", grad_raw, queries[..., :DH], preferred_element_type=jnp.float32
    )
    grad_rope = jnp.einsum(
        "hqk,qhr->kr", grad_raw, queries[..., DH:], preferred_element_type=jnp.float32
    )
    grad_value = jnp.einsum(
        "hqk,qhv->khv", probs_low, grad_attended, preferred_element_type=jnp.float32
    )
    grad_expanded = jnp.concatenate([grad_key_nope, grad_value], axis=-1).reshape(
        seq_len, H * (DH + DV)
    )
    expand_exact = expand_again.astype(jnp.float32)
    grad_key_own, grad_rope_own = (
        lax.psum_scatter(
            grad_expanded.astype(jnp.bfloat16), "expert", scatter_dimension=0, tiled=True
        ).astype(jnp.float32),
        lax.psum_scatter(
            grad_rope.astype(jnp.bfloat16), "expert", scatter_dimension=0, tiled=True
        ).astype(jnp.float32),
    )
    grad_wexpand = exact_rows(latent_low.astype(jnp.float32), grad_key_own)
    grad_latent_normed = exact_cols(grad_key_own, expand_exact)
    grad_latent_raw, grad_gain_latent = latent_back((grad_latent_normed, grad_rope_own))
    grad_latent_low = grad_latent_raw.astype(jnp.bfloat16)
    grad_wlatent = contract_rows(hidden_one, grad_latent_low)
    (grad_query_raw,) = query_back(grad_queries)
    grad_query_low = grad_query_raw.reshape(local_rows, H * (DH + DR)).astype(jnp.bfloat16)
    grad_wquery = contract_rows(hidden_one, grad_query_low)
    grad_hidden_one = contract_cols(grad_query_low, query_again) + contract_cols(
        grad_latent_low, latent_again
    )
    grad_tokens_norm, grad_gain_one = norm_one_back(grad_hidden_one)
    grad_tokens = grad_residual + grad_tokens_norm
    sum_gain_one, sum_wquery, sum_wlatent, sum_gain_latent, sum_wexpand, sum_wout = (
        lax.psum_scatter(grad_gain_one, ("dp", "expert"), scatter_dimension=0, tiled=True),
        lax.psum_scatter(grad_wquery, ("dp", "expert"), scatter_dimension=0, tiled=True),
        lax.psum_scatter(grad_wlatent, ("dp", "expert"), scatter_dimension=0, tiled=True),
        lax.psum_scatter(grad_gain_latent, ("dp", "expert"), scatter_dimension=0, tiled=True),
        lax.psum_scatter(grad_wexpand, ("dp", "expert"), scatter_dimension=0, tiled=True),
        lax.psum_scatter(grad_wout, ("dp", "expert"), scatter_dimension=0, tiled=True),
    )
    sum_gain_two, sum_router, sum_sgate, sum_sup, sum_sdown = (
        lax.psum_scatter(grad_gain_two, ("dp", "expert"), scatter_dimension=0, tiled=True),
        lax.psum_scatter(grad_router, ("dp", "expert"), scatter_dimension=0, tiled=True),
        lax.psum_scatter(grad_sgate, ("dp", "expert"), scatter_dimension=0, tiled=True),
        lax.psum_scatter(grad_sup, ("dp", "expert"), scatter_dimension=0, tiled=True),
        lax.psum_scatter(grad_sdown, ("dp", "expert"), scatter_dimension=0, tiled=True),
    )
    return (
        out_tokens,
        grad_tokens,
        sum_gain_one,
        sum_wquery,
        sum_wlatent,
        sum_gain_latent,
        sum_wexpand,
        sum_wout,
        sum_gain_two,
        sum_router,
        sum_sgate,
        sum_sup,
        sum_sdown,
        summed_expert_gate,
        summed_expert_up,
        summed_expert_down,
    )


def solution(mesh):
    in_specs = (
        P(("dp", "expert"), None),
        P(("dp", "expert"), None),
        P("dp"),
        P(("dp", "expert"), None),
        P(("dp", "expert"), None),
        P(("dp", "expert")),
        P(("dp", "expert"), None),
        P(("dp", "expert"), None),
        P(("dp", "expert")),
        P(("dp", "expert"), None),
        P(("dp", "expert"), None),
        P(("dp", "expert")),
        P(("dp", "expert"), None),
        P(("dp", "expert"), None),
        P(("dp", "expert"), None),
        P(("dp", "expert"), None),
        P("expert", "dp", None),
        P("expert", "dp", None),
        P("expert", "dp", None),
    )
    out_specs = (
        P(("dp", "expert"), None),
        P(("dp", "expert"), None),
        P(("dp", "expert")),
        P(("dp", "expert"), None),
        P(("dp", "expert"), None),
        P(("dp", "expert")),
        P(("dp", "expert"), None),
        P(("dp", "expert"), None),
        P(("dp", "expert")),
        P(("dp", "expert"), None),
        P(("dp", "expert"), None),
        P(("dp", "expert"), None),
        P(("dp", "expert"), None),
        P("expert", "dp", None),
        P("expert", "dp", None),
        P("expert", "dp", None),
    )
    return jax.shard_map(shards, mesh=mesh, in_specs=in_specs, out_specs=out_specs, check_vma=False)
```

profile of v0, /device:TPU:11, one launch (start us, length us, event | category | flops | bytes accessed | tf_op | source)
XLA Modules:
  0.0 3766.7 jit_solution(18400609085675641571)
XLA Ops:
  11.3 39.8 %all-reduce.15 = (bf16[2048]{0:T(1024)(128)(2,1)S(1)}, bf16[512]{0:T(512)(128)(2,1)S(1)}, bf16[2048]{0:T(1024)(128)(2,1)S(1)}) all-reduce(bf16[2048]{0:T(1024)(128)(2,1)S(1)} %dynamic-update-slice, bf16[512]{0:T(512)(128)(2,1)S(1)} %dynamic-update-slice.1, ...), channel_id=1, replica_groups=mesh['dp'=4,'expert'=8] {'dp','expert'}, use_global_device_ids=true, to_apply=%add.8 | all-reduce | flops 4608 | bytes 18432
  52.3 16.8 all-gather.13.cloned.1.call-done
  72.4 61.6 %all-gather.15.cloned.1.call-done = bf16[512,4096]{1,0:T(8,128)(2,1)} async-done(((bf16[16,4096]{1,0:T(8,128)(2,1)}), bf16[512,4096]{1,0:T(8,128)(2,1)}) %all-gather.15.cloned.1.call-update) | async-done | bytes 4194320 | tf_op jit(solution)/shard_map/all_gather | solution.py:128
  146.0 9.1 all_gather.65
  155.1 36.8 all-gather.17.cloned.1.call-done
  191.9 9.8 copy.245
  215.0 75.0 %all-gather.19.cloned.1.call-done = bf16[2048,3072]{1,0:T(8,128)(2,1)} async-done(((bf16[64,3072]{1,0:T(8,128)(2,1)}), bf16[2048,3072]{1,0:T(8,128)(2,1)}) %all-gather.19.cloned.1.call-update) | async-done | bytes 12582928 | tf_op jit(solution)/shard_map/all_gather | solution.py:125
  306.7 14.4 divide_convert_fusion
  324.3 44.8 %all-gather.21.cloned.1.call-done = bf16[2048,2048]{1,0:T(8,128)(2,1)} async-done(((bf16[64,2048]{1,0:T(8,128)(2,1)}), bf16[2048,2048]{1,0:T(8,128)(2,1)}) %all-gather.21.cloned.1.call-update) | async-done | bytes 8388624 | tf_op jit(solution)/shard_map/all_gather | solution.py:129
  383.1 83.6 %all-gather = bf16[32,64,16]{1,2,0:T(8,128)(2,1)S(1)} all-gather(bf16[1,64,16]{1,2,0:T(8,128)(2,1)S(1)} %bitcast.156), channel_id=1, replica_groups=mesh['dp'=4,'expert'=8] {'dp','expert'}, dimensions={0}, use_global_device_ids=true | all-gather | bytes 67584 | tf_op jit(solution)/shard_map/all_gather | solution.py:133
  496.0 27.0 all-to-all-done.2
  533.4 140.8 %all-gather.31.cloned.1.call-done = bf16[2,2048,1408]{2,1,0:T(8,128)(2,1)} async-done(((bf16[2,512,1408]{2,1,0:T(8,128)(2,1)}), bf16[2,2048,1408]{2,1,0:T(8,128)(2,1)}) %all-gather.31.cloned.1.call-update) | async-done | bytes 11534352 | tf_op jit(solution)/shard_map/all_gather | solution.py:140
  674.2 14.7 fusion.27
  688.9 186.1 %all-gather.29.cloned.1.call-done = bf16[2,2048,1408]{2,1,0:T(8,128)(2,1)} async-done(((bf16[2,512,1408]{2,1,0:T(8,128)(2,1)}), bf16[2,2048,1408]{2,1,0:T(8,128)(2,1)}) %all-gather.29.cloned.1.call-update) | async-done | bytes 11534352 | tf_op jit(solution)/shard_map/all_gather | solution.py:139
  875.1 14.7 fusion.29
  889.8 186.1 %all-gather.33.cloned.1.call-done = bf16[2,2048,1408]{2,1,0:T(8,128)(2,1)} async-done(((bf16[2,512,1408]{2,1,0:T(8,128)(2,1)}), bf16[2,2048,1408]{2,1,0:T(8,128)(2,1)}) %all-gather.33.cloned.1.call-update) | async-done | bytes 11534352 | tf_op jit(solution)/shard_map/all_gather | solution.py:141
  1075.9 18.4 multiply_convert_fusion.1
  1095.8 12.6 convolution_convert_fusion.4
  1126.1 82.5 %all-gather.25.cloned.1.call-done = bf16[2048,2816]{1,0:T(8,128)(2,1)} async-done(((bf16[64,2816]{1,0:T(8,128)(2,1)}), bf16[2048,2816]{1,0:T(8,128)(2,1)}) %all-gather.25.cloned.1.call-update) | async-done | bytes 11534352 | tf_op jit(solution)/shard_map/all_gather | solution.py:135
  1215.8 9.3 fusion.114
  1225.1 11.6 add_convert_fusion
  1254.4 77.5 %all-gather.23.cloned.1.call-done = bf16[2048,2816]{1,0:T(8,128)(2,1)} async-done(((bf16[64,2816]{1,0:T(8,128)(2,1)}), bf16[2048,2816]{1,0:T(8,128)(2,1)}) %all-gather.23.cloned.1.call-update) | async-done | bytes 11534352 | tf_op jit(solution)/shard_map/all_gather | solution.py:134
  1379.5 21.8 fusion.47
  1401.3 23.9 convert_bitcast_fusion.1
  1439.7 11.3 copy.236
  1452.5 12.8 convolution_convert_fusion
  1465.3 13.7 convolution_convert_fusion.2
  1479.1 13.6 convolution_convert_fusion.1
  1494.0 45.9 %reduce-scatter.42.cloned.1.call-done = bf16[128,4096]{1,0:T(8,128)(2,1)} async-done(((bf16[1024,4096]{1,0:T(8,128)(2,1)}), bf16[128,4096]{1,0:T(8,128)(2,1)}) %reduce-scatter.42.cloned.1.call-update) | async-done | bytes 1048592
  1563.1 22.2 convolution_bitcast_fusion.1
  1587.3 26.8 fusion.42
  1615.6 10.4 fusion.104
  1626.2 10.6 fusion.121
  1636.9 10.5 fusion.122
  1648.4 10.4 convolution_bitcast_fusion
  1658.8 23.3 copy.240
  1682.1 10.8 fusion.120
  1707.2 45.0 %all-reduce.14 = (f32[2048]{0:T(1024)S(1)}, f32[512]{0:T(512)S(1)}, f32[2048]{0:T(1024)S(1)}) all-reduce(f32[2048]{0:T(1024)S(1)} %get-tuple-element.116, f32[512]{0:T(512)S(1)} %get-tuple-element.118, f32[2048]{0:T(1024)S(1)} %copy-done.43), channel_id=4, replica_groups=mesh['dp'=4,'expert'=8] {'dp','expert'}, use_global_device_ids=true, to_apply=%region_21.22.clone | all-reduce | flops 4608 | bytes 36864
  1756.5 115.6 %reduce-scatter.38.cloned.1.call-done = bf16[2,512,1408]{2,1,0:T(8,128)(2,1)} async-done(((bf16[2,2048,1408]{2,1,0:T(8,128)(2,1)}), bf16[2,512,1408]{2,1,0:T(8,128)(2,1)}) %reduce-scatter.38.cloned.1.call-update) | async-done | bytes 2883600 | tf_op jit(solution)/shard_map/reduce_scatter | solution.py:348
  1876.8 193.6 %reduce-scatter.34.cloned.1.call-done = bf16[2,512,1408]{2,1,0:T(8,128)(2,1)} async-done(((bf16[2,2048,1408]{2,1,0:T(8,128)(2,1)}), bf16[2,512,1408]{2,1,0:T(8,128)(2,1)}) %reduce-scatter.34.cloned.1.call-update) | async-done | bytes 2883600 | tf_op jit(solution)/shard_map/reduce_scatter | solution.py:342
  2075.1 193.6 %reduce-scatter.36.cloned.1.call-done = bf16[2,512,1408]{2,1,0:T(8,128)(2,1)} async-done(((bf16[2,2048,1408]{2,1,0:T(8,128)(2,1)}), bf16[2,512,1408]{2,1,0:T(8,128)(2,1)}) %reduce-scatter.36.cloned.1.call-update) | async-done | bytes 2883600 | tf_op jit(solution)/shard_map/reduce_scatter | solution.py:345
  2273.4 112.6 %reduce-scatter.24.cloned.1.call-done = f32[64,576]{1,0:T(8,128)} async-done(((f32[2048,576]{1,0:T(8,128)}), f32[64,576]{1,0:T(8,128)}) %reduce-scatter.24.cloned.1.call-update) | async-done | bytes 147472 | tf_op jit(solution)/shard_map/reduce_scatter | solution.py:430
  2385.9 149.3 %reduce-scatter.26.cloned.1.call-done = f32[16,4096]{1,0:T(8,128)} async-done(((f32[512,4096]{1,0:T(8,128)}), f32[16,4096]{1,0:T(8,128)}) %reduce-scatter.26.cloned.1.call-update) | async-done | bytes 262160 | tf_op jit(solution)/shard_map/reduce_scatter | solution.py:432
  2535.2 211.3 %reduce-scatter.28.cloned.1.call-done = f32[64,2048]{1,0:T(8,128)} async-done(((f32[2048,2048]{1,0:T(8,128)}), f32[64,2048]{1,0:T(8,128)}) %reduce-scatter.28.cloned.1.call-update) | async-done | bytes 524304 | tf_op jit(solution)/shard_map/reduce_scatter | solution.py:433
  2746.5 253.5 %reduce-scatter.22.cloned.1.call-done = f32[64,3072]{1,0:T(8,128)} async-done(((f32[2048,3072]{1,0:T(8,128)}), f32[64,3072]{1,0:T(8,128)}) %reduce-scatter.22.cloned.1.call-update) | async-done | bytes 786448 | tf_op jit(solution)/shard_map/reduce_scatter | solution.py:429
  3000.0 251.1 %reduce-scatter.30.cloned.1.call-done = f32[64,2816]{1,0:T(8,128)} async-done(((f32[2048,2816]{1,0:T(8,128)}), f32[64,2816]{1,0:T(8,128)}) %reduce-scatter.30.cloned.1.call-update) | async-done | bytes 720912 | tf_op jit(solution)/shard_map/reduce_scatter | solution.py:438
  3251.1 254.3 %reduce-scatter.32.cloned.1.call-done = f32[64,2816]{1,0:T(8,128)} async-done(((f32[2048,2816]{1,0:T(8,128)}), f32[64,2816]{1,0:T(8,128)}) %reduce-scatter.32.cloned.1.call-update) | async-done | bytes 720912 | tf_op jit(solution)/shard_map/reduce_scatter | solution.py:439
  3505.4 254.2 %reduce-scatter.46.cloned.1.call-done = f32[64,2816]{1,0:T(8,128)} async-done(((f32[2048,2816]{1,0:T(8,128)}), f32[64,2816]{1,0:T(8,128)}) %reduce-scatter.46.cloned.1.call-update) | async-done | bytes 720912
  (298 shorter events, 275.4 us)
Async XLA Ops:
  7.2 62.0 %all-gather.13.cloned.1.call-start = ((), (), s32[]{:S(2)}) async-start(), calls=%async_computation.17 | async-start | bytes 2703360 | tf_op jit(solution)/shard_map/all_gather | solution.py:126
  7.9 126.1 %all-gather.15.cloned.1.call-start = ((), (), s32[]{:S(2)}) async-start(), calls=%async_computation.18 | async-start | bytes 4325376 | tf_op jit(solution)/shard_map/all_gather | solution.py:128
  8.7 183.2 %all-gather.17.cloned.1.call-start = ((), (), s32[]{:S(2)}) async-start(), calls=%async_computation.19 | async-start | bytes 9437184 | tf_op jit(solution)/shard_map/all_gather | solution.py:181
  51.1 238.9 %copy-start.32 = (f32[2048]{0:T(1024)}, f32[2048]{0:T(1024)S(1)}, u32[]{:S(2)}) copy-start(f32[2048]{0:T(1024)S(1)} %convert_element_type.150) | copy-start | bytes 24580
  51.1 88.7 %copy-start.40 = (f32[512]{0:T(512)}, f32[512]{0:T(512)S(1)}, u32[]{:S(2)}) copy-start(f32[512]{0:T(512)S(1)} %convert_element_type.152) | copy-start | bytes 6148
  52.3 237.7 %copy-start.44 = (f32[128]{0:T(128)}, f32[128]{0:T(128)S(1)}, u32[]{:S(2)}) copy-start(f32[128]{0:T(128)S(1)} %fusion.92) | copy-start | bytes 1540
  72.2 73.6 %copy-start.13 = (f32[128,576]{0,1:T(8,128)}, f32[128,576]{0,1:T(8,128)S(1)}, u32[]{:S(2)}) copy-start(f32[128,576]{0,1:T(8,128)S(1)} %fusion.108) | copy-start | bytes 884740
  72.3 68.9 %copy-start.60 = (f32[128]{0:T(128)}, f32[128]{0:T(128)S(1)}, u32[]{:S(2)}) copy-start(f32[128]{0:T(128)S(1)} %multiply_reduce_fusion.8) | copy-start | bytes 1540
  72.3 68.9 %copy-start.46 = (f32[128]{0:T(128)}, f32[128]{0:T(128)S(1)}, u32[]{:S(2)}) copy-start(f32[128]{0:T(128)S(1)} %fusion.93) | copy-start | bytes 1540
  138.0 152.0 %all-gather.19.cloned.1.call-start = ((), (), s32[]{:S(2)}) async-start(), calls=%async_computation.20 | async-start | bytes 12976128 | tf_op jit(solution)/shard_map/all_gather | solution.py:125
  138.6 230.5 %all-gather.21.cloned.1.call-start = ((), (), s32[]{:S(2)}) async-start(), calls=%async_computation.21 | async-start | bytes 8650752 | tf_op jit(solution)/shard_map/all_gather | solution.py:129
  139.2 339.0 %all-gather.27.cloned.1.call-start = ((), (), s32[]{:S(2)}) async-start(), calls=%async_computation.24 | async-start | bytes 11894784 | tf_op jit(solution)/shard_map/all_gather | solution.py:136
  139.8 534.4 %all-gather.31.cloned.1.call-start = ((), (), s32[]{:S(2)}) async-start(), calls=%async_computation.26 | async-start | bytes 14417920 | tf_op jit(solution)/shard_map/all_gather | solution.py:140
  140.5 734.5 %all-gather.29.cloned.1.call-start = ((), (), s32[]{:S(2)}) async-start(), calls=%async_computation.25 | async-start | bytes 14417920 | tf_op jit(solution)/shard_map/all_gather | solution.py:139
  141.3 934.6 %all-gather.33.cloned.1.call-start = ((), (), s32[]{:S(2)}) async-start(), calls=%async_computation.27 | async-start | bytes 14417920 | tf_op jit(solution)/shard_map/all_gather | solution.py:141
  142.0 1066.6 %all-gather.25.cloned.1.call-start = ((), (), s32[]{:S(2)}) async-start(), calls=%async_computation.23 | async-start | bytes 11894784 | tf_op jit(solution)/shard_map/all_gather | solution.py:135
  142.6 1189.3 %all-gather.23.cloned.1.call-start = ((), (), s32[]{:S(2)}) async-start(), calls=%async_computation.22 | async-start | bytes 11894784 | tf_op jit(solution)/shard_map/all_gather | solution.py:134
  143.4 58.3 %copy-start.52 = (f32[32]{0:T(128)}, f32[32]{0:T(128)S(1)}, u32[]{:S(2)}) copy-start(f32[32]{0:T(128)S(1)} %multiply_power_fusion) | copy-start | bytes 388
  143.4 58.3 %copy-start.54 = (f32[128]{0:T(128)}, f32[128]{0:T(128)S(1)}, u32[]{:S(2)}) copy-start(f32[128]{0:T(128)S(1)} %fusion.101) | copy-start | bytes 1540
  144.2 229.7 %copy-start.38 = (f32[2048]{0:T(1024)}, f32[2048]{0:T(1024)S(1)}, u32[]{:S(2)}) copy-start(f32[2048]{0:T(1024)S(1)} %convert_element_type.160) | copy-start | bytes 24580
  145.8 153.7 %copy-start.28 = (pred[128,1024]{1,0:T(8,128)(4,1)}, pred[128,1024]{1,0:T(8,128)(4,1)S(1)}, u32[]{:S(2)}) copy-start(pred[128,1024]{1,0:T(8,128)(4,1)S(1)} %fusion.62) | copy-start | bytes 393220
  146.0 152.1 %copy-start.34 = (f32[128,32]{0,1:T(8,128)}, f32[128,32]{0,1:T(8,128)S(1)}, u32[]{:S(2)}) copy-start(f32[128,32]{0,1:T(8,128)S(1)} %get-tuple-element.142) | copy-start | bytes 49156
  146.0 152.1 %copy-start.36 = (f32[128,32]{0,1:T(8,128)}, f32[128,32]{0,1:T(8,128)S(1)}, u32[]{:S(2)}) copy-start(f32[128,32]{0,1:T(8,128)S(1)} %get-tuple-element.143) | copy-start | bytes 49156
  155.1 143.1 %copy-start.30 = (bf16[1024,64]{0,1:T(8,128)(2,1)}, bf16[1024,64]{0,1:T(8,128)(2,1)S(1)}, u32[]{:S(2)}) copy-start(bf16[1024,64]{0,1:T(8,128)(2,1)S(1)} %all_gather.65) | copy-start | bytes 393220
  208.2 81.8 %copy-start.3 = (bf16[128,2048]{1,0:T(8,128)(2,1)S(1)}, bf16[128,2048]{1,0:T(8,128)(2,1)}, u32[]{:S(2)}) copy-start(bf16[128,2048]{1,0:T(8,128)(2,1)} %param.19) | copy-start | bytes 1572868
  378.1 88.9 %copy-start.9 = (bf16[128,2048]{1,0:T(8,128)(2,1)S(1)}, bf16[128,2048]{1,0:T(8,128)(2,1)}, u32[]{:S(2)}) copy-start(bf16[128,2048]{1,0:T(8,128)(2,1)} %param.20) | copy-start | bytes 1572868
  378.1 94.2 %all-to-all-start = ((bf16[8,120,2048]{2,1,0:T(8,128)(2,1)}), bf16[8,120,2048]{2,1,0:T(8,128)(2,1)}, u32[]{:S(2)}, u32[]{:S(2)}) async-start(bf16[8,120,2048]{2,1,0:T(8,128)(2,1)} %bitcast.132), calls=%async_computation | async-start | bytes 7864320 | tf_op jit(solution)/shard_map/all_to_all | solution.py:227
  472.3 50.7 %all-to-all-start.2 = ((bf16[8,120,2048]{2,1,0:T(8,128)(2,1)}), bf16[8,120,2048]{2,1,0:T(8,128)(2,1)}, u32[]{:S(2)}, u32[]{:S(2)}) async-start(bf16[8,120,2048]{2,1,0:T(8,128)(2,1)} %bitcast.155), calls=%async_computation.2 | async-start | bytes 7864320 | tf_op jit(solution)/shard_map/all_to_all | solution.py:290
  1120.8 128.6 %all-to-all-start.1 = ((bf16[8,120,2048]{2,1,0:T(8,128)(2,1)}), bf16[8,120,2048]{2,1,0:T(8,128)(2,1)}, u32[]{:S(2)}, u32[]{:S(2)}) async-start(bf16[8,120,2048]{2,1,0:T(8,128)(2,1)} %copy.211), calls=%async_computation.1 | async-start | bytes 7864320 | tf_op jit(solution)/shard_map/all_to_all | solution.py:254
  1249.4 112.2 %all-to-all-start.3 = ((bf16[8,120,2048]{2,1,0:T(8,128)(2,1)}), bf16[8,120,2048]{2,1,0:T(8,128)(2,1)}, u32[]{:S(2)}, u32[]{:S(2)}) async-start(bf16[8,120,2048]{2,1,0:T(8,128)(2,1)} %copy.217), calls=%async_computation.3 | async-start | bytes 7864320 | tf_op jit(solution)/shard_map/all_to_all | solution.py:337
  1253.9 239.0 %reduce-scatter.40.cloned.1.call-start = ((), (), s32[]{:S(2)}) async-start(), calls=%async_computation.37 | async-start | bytes 294912
  1431.5 108.4 %reduce-scatter.42.cloned.1.call-start = ((), (), s32[]{:S(2)}) async-start(), calls=%async_computation.38 | async-start | bytes 9437184
  1451.0 251.0 %reduce-scatter.44.cloned.1.call-start = ((), (), s32[]{:S(2)}) async-start(), calls=%async_computation.39 | async-start | bytes 1081344
  1452.4 419.7 %reduce-scatter.38.cloned.1.call-start = ((), (), s32[]{:S(2)}) async-start(), calls=%async_computation.36 | async-start | bytes 14417920 | tf_op jit(solution)/shard_map/reduce_scatter | solution.py:348
  1465.3 605.1 %reduce-scatter.34.cloned.1.call-start = ((), (), s32[]{:S(2)}) async-start(), calls=%async_computation.34 | async-start | bytes 14417920 | tf_op jit(solution)/shard_map/reduce_scatter | solution.py:342
  1479.0 789.6 %reduce-scatter.36.cloned.1.call-start = ((), (), s32[]{:S(2)}) async-start(), calls=%async_computation.35 | async-start | bytes 14417920 | tf_op jit(solution)/shard_map/reduce_scatter | solution.py:345
  1492.8 51.0 %copy-start.61 = (f32[128]{0:T(128)S(1)}, f32[128]{0:T(128)}, u32[]{:S(2)}) copy-start(f32[128]{0:T(128)} %copy-done.60) | copy-start | bytes 1540
  1492.8 51.2 %copy-start.4 = (bf16[128,2048]{1,0:T(8,128)(2,1)S(1)}, bf16[128,2048]{1,0:T(8,128)(2,1)}, u32[]{:S(2)}) copy-start(bf16[128,2048]{1,0:T(8,128)(2,1)} %param.19) | copy-start | bytes 1572868
  1492.8 51.2 %copy-start.33 = (f32[2048]{0:T(1024)S(1)}, f32[2048]{0:T(1024)}, u32[]{:S(2)}) copy-start(f32[2048]{0:T(1024)} %copy-done.32) | copy-start | bytes 24580
  1492.8 51.2 %copy-start.45 = (f32[128]{0:T(128)S(1)}, f32[128]{0:T(128)}, u32[]{:S(2)}) copy-start(f32[128]{0:T(128)} %copy-done.44) | copy-start | bytes 1540
  1492.8 893.1 %reduce-scatter.24.cloned.1.call-start = ((), (), s32[]{:S(2)}) async-start(), calls=%async_computation.29 | async-start | bytes 5406720 | tf_op jit(solution)/shard_map/reduce_scatter | solution.py:430
  1547.3 987.9 %reduce-scatter.26.cloned.1.call-start = ((), (), s32[]{:S(2)}) async-start(), calls=%async_computation.30 | async-start | bytes 8650752 | tf_op jit(solution)/shard_map/reduce_scatter | solution.py:432
  1553.1 1193.4 %reduce-scatter.28.cloned.1.call-start = ((), (), s32[]{:S(2)}) async-start(), calls=%async_computation.31 | async-start | bytes 17301504 | tf_op jit(solution)/shard_map/reduce_scatter | solution.py:433
  1562.2 1437.8 %reduce-scatter.22.cloned.1.call-start = ((), (), s32[]{:S(2)}) async-start(), calls=%async_computation.28 | async-start | bytes 25952256 | tf_op jit(solution)/shard_map/reduce_scatter | solution.py:429
  1626.0 1625.2 %reduce-scatter.30.cloned.1.call-start = ((), (), s32[]{:S(2)}) async-start(), calls=%async_computation.32 | async-start | bytes 23789568 | tf_op jit(solution)/shard_map/reduce_scatter | solution.py:438
  1636.8 1868.6 %reduce-scatter.32.cloned.1.call-start = ((), (), s32[]{:S(2)}) async-start(), calls=%async_computation.33 | async-start | bytes 23789568 | tf_op jit(solution)/shard_map/reduce_scatter | solution.py:439
  1647.4 2112.2 %reduce-scatter.46.cloned.1.call-start = ((), (), s32[]{:S(2)}) async-start(), calls=%async_computation.40 | async-start | bytes 23789568
  1693.0 61.0 %copy-start.59 = (f32[128]{0:T(128)S(1)}, f32[128]{0:T(128)}, u32[]{:S(2)}) copy-start(f32[128]{0:T(128)} %copy-done.58) | copy-start | bytes 1540
  (46 other events, 531.7 us)
Sparse Core Ops, SparseCore 0:
  10.8 58.2 all-gather.12
  72.0 61.9 all-gather.14
  138.1 53.7 all-gather.16
  194.6 95.3 all-gather.18
  292.7 76.3 all-gather.20
  371.8 101.5 all-gather.26
  474.9 199.2 all-gather.30
  675.8 199.2 all-gather.28
  876.6 199.2 all-gather.32
  1078.6 129.9 all-gather.24
  1211.5 120.3 all-gather.22
  1431.7 32.7 reduce-scatter.39
  1468.3 71.6 reduce-scatter.41
  1542.6 105.9 reduce-scatter.43
  1650.9 221.0 reduce-scatter.37
  1874.4 195.9 reduce-scatter.33
  2072.7 195.9 reduce-scatter.35
  2271.5 114.4 reduce-scatter.23
  2388.9 146.2 reduce-scatter.25
  2538.0 208.4 reduce-scatter.27
  2754.7 245.2 reduce-scatter.21
  3002.9 248.1 reduce-scatter.29
  3254.0 251.3 reduce-scatter.31
  3508.2 251.3 reduce-scatter.45
where the time goes:
time: 3780 us; the launch traced here: 3770 us
  waiting for transfers between devices  2980 us (79%)
  matrix products  406 us (11%)
  blocking collectives  178 us (5%)
  local copies, waits for them, and re-layouts  120 us (3%)
  other arithmetic  48.1 us (1%)
    unnamed x28, waiting for transfers between devices  307 us
    reduce_scatter x1, waiting for transfers between devices, shards(): lax.psum_scatter(grad_sup, ('dp', 'expert'), scatter_dimension=0, tiled=T...  254 us
    reduce_scatter x1, waiting for transfers between devices, shards(): lax.psum_scatter(grad_wquery, ('dp', 'expert'), scatter_dimension=0, tile...  253 us
    reduce_scatter x1, waiting for transfers between devices, shards(): lax.psum_scatter(grad_sgate, ('dp', 'expert'), scatter_dimension=0, tiled...  251 us
    reduce_scatter x1, waiting for transfers between devices, shards(): lax.psum_scatter(grad_wout, ('dp', 'expert'), scatter_dimension=0, tiled=...  211 us
    reduce_scatter x1, waiting for transfers between devices, shards(): lax.psum_scatter(gradient_expert_up.astype(jnp.bfloat16), 'dp', scatter_d...  194 us
    reduce_scatter x1, waiting for transfers between devices, shards(): lax.psum_scatter(grad_egate.astype(jnp.bfloat16), 'dp', scatter_dimension...  194 us
    all_gather x1, waiting for transfers between devices, shards(): lax.all_gather(expert_down, 'dp', axis=1, tiled=True)  186 us
  transfers between devices with their start and end apart: 28, of which 22 were waited for; matrix products, arithmetic and copies ran while one was open for 13% of the time, Pallas kernels for 0%

commit v1 on v0

v1 whole, which is shorter than its diff:
```python
import jax
import jax.numpy as jnp
from jax import lax
from jax.experimental import pallas as pl
from jax.experimental.pallas import tpu as pltpu
from jax.sharding import PartitionSpec as P

H = 16
DH = 128
DR = 64
DV = 128
KVR = 512

norm_eps = 1e-06
masked_score = -1e30
MESH = pl.DeviceIdType.MESH
ANY = pl.BlockSpec(memory_space=pl.ANY)
VMEM = pl.BlockSpec(memory_space=pltpu.VMEM)
BF = jnp.bfloat16
F32 = jnp.float32


def rms_norm(values, scale_gain):
    return (
        values
        * lax.rsqrt(jnp.mean(values * values, axis=-1, keepdims=True) + norm_eps)
        * scale_gain
    )


def rotate(values, cos_table, sine_table):
    half_dim = values.shape[-1] // 2
    first_half = values[..., :half_dim]
    second_half = values[..., half_dim:]
    return jnp.concatenate(
        [
            first_half * cos_table - second_half * sine_table,
            second_half * cos_table + first_half * sine_table,
        ],
        axis=-1,
    )


def rope_tables(positions):
    half_dim = DR // 2
    inv_freq = 10000.0 ** (-(jnp.arange(half_dim).astype(F32) * 2.0) / DR)
    angles = positions.astype(F32)[:, None] * inv_freq[None, :]
    return (jnp.cos(angles), jnp.sin(angles))


def swiglu(gate_in, up_in):
    return jax.nn.silu(gate_in) * up_in


def mm(left, right):
    return jnp.dot(left, right, preferred_element_type=F32)


def mm_rows(left, right):
    return lax.dot_general(left, right, (((0,), (0,)), ((), ())), preferred_element_type=F32)


def mm_cols(left, right):
    return lax.dot_general(left, right, (((1,), (1,)), ((), ())), preferred_element_type=F32)


def slot_places(route_rows, pair_order, capacity):
    pair_expert = route_rows.reshape(-1)
    earlier = pair_order[None, :] < pair_order[:, None]
    same_expert = pair_expert[None, :] == pair_expert[:, None]
    places = jnp.sum((earlier & same_expert).astype(jnp.int32), axis=1)
    slot_index = jnp.where(places < capacity, pair_expert * capacity + places, -1)
    return slot_index.reshape(route_rows.shape)


def params(collective_id):
    return pltpu.CompilerParams(
        collective_id=collective_id, has_side_effects=True, vmem_limit_bytes=48 << 20
    )


def remote(src, dst, send_sem, recv_sem, device):
    return pltpu.make_async_remote_copy(
        src_ref=src,
        dst_ref=dst,
        send_sem=send_sem,
        recv_sem=recv_sem,
        device_id=device,
        device_id_type=MESH,
    )


def greet(devices):
    barrier = pltpu.get_barrier_semaphore()
    for device in devices:
        pl.semaphore_signal(barrier, inc=1, device_id=device, device_id_type=MESH)
    pl.semaphore_wait(barrier, len(devices))


def places(n_dp, n_ex):
    z = lax.axis_index("dp")
    e = lax.axis_index("expert")
    chips = n_ex // 2
    c, k = e // 2, lax.rem(e, 2)
    sibling = (z, e + 1 - 2 * k)
    same_core = [(z, lax.rem(c + i, chips) * 2 + k) for i in range(1, chips)]
    column = [(lax.rem(z + i, n_dp), e) for i in range(1, n_dp)]
    return z, e, c, k, sibling, same_core, column


def plane_gather(block, n_dp, n_ex, collective_id):
    chips = n_ex // 2

    def kernel(x_ref, o_ref, send, recv, sib_send, sib_recv, local):
        z, e, c, k, sibling, same_core, _ = places(n_dp, n_ex)
        greet(same_core + [sibling])
        far = []
        for i in range(1, chips):
            copy = remote(x_ref, o_ref.at[e], send.at[i], recv.at[i], same_core[i - 1])
            copy.start()
            far.append(copy)
        near = [remote(x_ref, o_ref.at[e], sib_send.at[0], sib_recv.at[0], sibling)]
        near[0].start()
        own = pltpu.make_async_copy(x_ref, o_ref.at[e], local)
        own.start()
        for i in range(1, chips):
            source = lax.rem(c + chips - i, chips) * 2 + k
            far[i - 1].wait_recv()
            copy = remote(
                o_ref.at[source], o_ref.at[source], sib_send.at[i], sib_recv.at[i], sibling
            )
            copy.start()
            near.append(copy)
        own.wait()
        for copy in far:
            copy.wait_send()
        for copy in near:
            copy.wait()

    return pl.pallas_call(
        kernel,
        out_shape=jax.ShapeDtypeStruct((n_ex,) + block.shape, block.dtype),
        in_specs=[ANY],
        out_specs=ANY,
        scratch_shapes=[pltpu.SemaphoreType.DMA((chips,))] * 4 + [pltpu.SemaphoreType.DMA],
        compiler_params=params(collective_id),
    )(block)


def plane_sum(blocks, n_dp, n_ex, collective_id):
    chips = n_ex // 2
    rows, cols = blocks.shape[1:]

    def kernel(x_ref, o_ref, from_sib, out_buf, from_far, send, recv, sib_send, sib_recv):
        z, e, c, k, sibling, same_core, _ = places(n_dp, n_ex)
        greet(same_core + [sibling])
        near = []
        for i in list(range(1, chips)) + [0]:
            chip = lax.rem(c + i, chips)
            copy = remote(
                x_ref.at[chip * 2 + 1 - k],
                from_sib.at[chip],
                sib_send.at[i],
                sib_recv.at[i],
                sibling,
            )
            copy.start()
            near.append(copy)
        far = []
        for i in range(1, chips):
            chip = lax.rem(c + i, chips)
            near[i - 1].wait_recv()
            out_buf[i] = (
                x_ref[chip * 2 + k].astype(F32) + from_sib[chip].astype(F32)
            ).astype(BF)
            copy = remote(out_buf.at[i], from_far.at[i], send.at[i], recv.at[i], same_core[i - 1])
            copy.start()
            far.append(copy)
        near[chips - 1].wait_recv()
        o_ref[...] = x_ref[e].astype(F32) + from_sib[c].astype(F32)
        for i in range(1, chips):
            far[i - 1].wait_recv()
            o_ref[...] += from_far[i].astype(F32)
        for copy in near:
            copy.wait_send()
        for copy in far:
            copy.wait_send()

    return pl.pallas_call(
        kernel,
        out_shape=jax.ShapeDtypeStruct((rows, cols), F32),
        in_specs=[VMEM],
        out_specs=VMEM,
        scratch_shapes=[pltpu.VMEM((chips, rows, cols), BF)] * 3
        + [pltpu.SemaphoreType.DMA((chips,))] * 4,
        compiler_params=params(collective_id),
    )(blocks)


def column_gather(block, n_dp, n_ex, collective_id):
    def kernel(x_ref, o_ref, send, recv, local):
        z, e, c, k, sibling, same_core, column = places(n_dp, n_ex)
        greet(column)
        copies = []
        for i in range(1, n_dp):
            copy = remote(x_ref, o_ref.at[z], send.at[i], recv.at[i], column[i - 1])
            copy.start()
            copies.append(copy)
        own = pltpu.make_async_copy(x_ref, o_ref.at[z], local)
        own.start()
        own.wait()
        for copy in copies:
            copy.wait()

    return pl.pallas_call(
        kernel,
        out_shape=jax.ShapeDtypeStruct((n_dp,) + block.shape, block.dtype),
        in_specs=[ANY],
        out_specs=ANY,
        scratch_shapes=[pltpu.SemaphoreType.DMA((n_dp,))] * 2 + [pltpu.SemaphoreType.DMA],
        compiler_params=params(collective_id),
    )(block)


def first_exchange(tok, heads_w, pack, n_dp, n_ex, collective_id):
    chips = n_ex // 2

    def kernel(
        tok_ref, wa_ref, pk_ref, tok_out, wa_out, pk_out,
        t_send, t_recv, ts_send, ts_recv, a_send, a_recv, az_send, az_recv,
        p_send, p_recv, pf_send, pf_recv, ps_send, ps_recv, local,
    ):
        z, e, c, k, sibling, same_core, column = places(n_dp, n_ex)
        plane = [(z, lax.rem(e + i, n_ex)) for i in range(1, n_ex)]
        greet(plane + column)
        wa_far, pk_col, tok_far = [], [], []
        for i in range(1, n_ex):
            copy = remote(
                wa_ref.at[lax.rem(e + i, n_ex)], wa_out.at[z, e],
                a_send.at[i], a_recv.at[i], plane[i - 1],
            )
            copy.start()
            wa_far.append(copy)
        for i in range(1, n_dp):
            copy = remote(pk_ref, pk_out.at[z, e], p_send.at[i], p_recv.at[i], column[i - 1])
            copy.start()
            pk_col.append(copy)
        for i in range(1, chips):
            copy = remote(tok_ref, tok_out.at[e], t_send.at[i], t_recv.at[i], same_core[i - 1])
            copy.start()
            tok_far.append(copy)
        near = [remote(tok_ref, tok_out.at[e], ts_send.at[0], ts_recv.at[0], sibling)]
        near[0].start()
        own = [
            pltpu.make_async_copy(wa_ref.at[e], wa_out.at[z, e], local.at[0]),
            pltpu.make_async_copy(pk_ref, pk_out.at[z, e], local.at[1]),
            pltpu.make_async_copy(tok_ref, tok_out.at[e], local.at[2]),
        ]
        for copy in own:
            copy.start()
        for copy in own:
            copy.wait()
        for copy in wa_far:
            copy.wait_recv()
        wa_col = []
        for i in range(1, n_dp):
            copy = remote(
                wa_out.at[z], wa_out.at[z], az_send.at[i], az_recv.at[i], column[i - 1]
            )
            copy.start()
            wa_col.append(copy)
        for copy in pk_col:
            copy.wait_recv()
        pk_far = []
        for i in range(1, chips):
            copy = remote(
                pk_out.at[:, e], pk_out.at[:, e], pf_send.at[i], pf_recv.at[i], same_core[i - 1]
            )
            copy.start()
            pk_far.append(copy)
        copy = remote(pk_out.at[:, e], pk_out.at[:, e], ps_send.at[0], ps_recv.at[0], sibling)
        copy.start()
        near.append(copy)
        for i in range(1, chips):
            source = lax.rem(c + chips - i, chips) * 2 + k
            tok_far[i - 1].wait_recv()
            copy = remote(
                tok_out.at[source], tok_out.at[source], ts_send.at[i], ts_recv.at[i], sibling
            )
            copy.start()
            near.append(copy)
            pk_far[i - 1].wait_recv()
            copy = remote(
                pk_out.at[:, source], pk_out.at[:, source], ps_send.at[i], ps_recv.at[i], sibling
            )
            copy.start()
            near.append(copy)
        for copy in near + wa_col:
            copy.wait()
        for copy in wa_far + pk_col + tok_far + pk_far:
            copy.wait_send()

    dma = pltpu.SemaphoreType.DMA
    return pl.pallas_call(
        kernel,
        out_shape=[
            jax.ShapeDtypeStruct((n_ex,) + tok.shape, tok.dtype),
            jax.ShapeDtypeStruct((n_dp,) + heads_w.shape, heads_w.dtype),
            jax.ShapeDtypeStruct((n_dp, n_ex) + pack.shape, pack.dtype),
        ],
        in_specs=[ANY] * 3,
        out_specs=[ANY] * 3,
        scratch_shapes=[dma((chips,))] * 4
        + [dma((n_ex,))] * 2
        + [dma((n_dp,))] * 4
        + [dma((chips,))] * 4
        + [dma((3,))],
        compiler_params=params(collective_id),
    )(tok, heads_w, pack)


def shards(
    tokens,
    cotangent,
    lengths,
    routes,
    place_order,
    attn_gain,
    w_query,
    w_latent,
    latent_gain,
    w_expand,
    w_out,
    ffn_gain,
    w_router,
    shared_gate,
    shared_up,
    shared_down,
    expert_gate,
    expert_up,
    expert_down,
):
    rows, width = tokens.shape
    n_dp = lax.axis_size("dp")
    n_ex = lax.axis_size("expert")
    chips = n_ex // 2
    z = lax.axis_index("dp")
    e = lax.axis_index("expert")
    chip, core = e // 2, lax.rem(e, 2)
    n_experts = w_router.shape[1]
    top_k = routes.shape[1]
    capacity = (rows * top_k * 5 + 4 * n_experts - 1) // (4 * n_experts)
    cap = (capacity + 15) // 16 * 16
    seq = rows * n_ex
    r = w_query.shape[0]
    rl = w_expand.shape[0]
    hp = H // n_ex
    parts = DV // r
    heads = [
        (d * n_ex + (j // parts) * parts) * r // DV
        for j in range(n_ex)
        for d in range(j % parts * hp, j % parts * hp + hp)
    ]
    heads_back = [heads.index(h) for h in range(H)]
    per_chip = n_experts // chips
    splits = n_dp // per_chip
    my_local = z // splits
    same_core_groups = [[2 * i + s for i in range(chips)] for s in range(2)]
    pair_groups = [[2 * i, 2 * i + 1] for i in range(chips)]
    sib_perm = [(i, i ^ 1) for i in range(n_ex)]
    part_groups = [[i * parts + m for m in range(parts)] for i in range(n_ex // parts)]
    ff_e = expert_gate.shape[2]
    ff_part = ff_e // splits
    half = expert_gate.shape[1] // 2
    ff_s = shared_gate.shape[1] // n_dp
    lat = KVR + DR
    head_cols = hp * (DH + DR)
    kv_cols = hp * (DH + DV)

    wq_send = jnp.take(w_query.reshape(r, H, DH + DR), jnp.array(heads), axis=1)
    wq_send = wq_send.reshape(r, n_ex, head_cols).transpose(1, 0, 2)
    we_send = jnp.take(w_expand.reshape(rl, H, DH + DV), jnp.array(heads), axis=1)
    we_send = we_send.reshape(rl, n_ex, kv_cols).transpose(1, 0, 2)
    we_send = we_send.reshape(n_ex, r, rl * kv_cols // r)
    wa_send = jnp.concatenate([wq_send, we_send], axis=-1)
    pack_cols = (lat + n_experts + 3 + 127) // 128 * 128
    pack = jnp.concatenate(
        [
            w_latent,
            w_router,
            attn_gain[:, None],
            ffn_gain[:, None],
            jnp.pad(latent_gain, (0, r - rl))[:, None],
            jnp.zeros((r, pack_cols - lat - n_experts - 3), BF),
        ],
        axis=1,
    )
    tok_all, wa_all, pk_all = first_exchange(tokens, wa_send, pack, n_dp, n_ex, 1)
    wq = wa_all[..., :head_cols].reshape(width, head_cols)
    wexp = wa_all[..., head_cols:].reshape(KVR, kv_cols)
    pk_flat = pk_all.reshape(width, pack_cols)
    w_lat = pk_flat[:, :lat]
    router = pk_flat[:, lat : lat + n_experts]
    gain_one = pk_flat[:, lat + n_experts].astype(F32)
    gain_two = pk_flat[:, lat + n_experts + 1].astype(F32)
    gain_lat = (
        pk_all[..., lat + n_experts + 2].reshape(n_dp * n_ex, r)[:, :rl].reshape(KVR).astype(F32)
    )

    def expert_half(weight, after):
        two = weight.reshape(-1, 2, half, ff_e).transpose(1, 0, 2, 3)
        two = lax.all_to_all(two, "expert", 0, 0, axis_index_groups=pair_groups, tiled=True)
        out = two.reshape(per_chip, half, splits, ff_part).transpose(0, 2, 1, 3)
        out = out.reshape(n_dp, half, ff_part)
        out, _ = lax.optimization_barrier((out, after))
        own = lax.all_to_all(out, "dp", 0, 0, tiled=True).reshape(width // 2, ff_part)
        return own, lax.ppermute(own, "expert", sib_perm)

    gate_w = expert_half(expert_gate, pk_all)
    up_w = expert_half(expert_up, gate_w[0])
    down_w = expert_half(expert_down, up_w[0])
    wo_send, _ = lax.optimization_barrier((w_out, pk_all))
    wo_col = lax.all_gather(wo_send, "dp", axis=0, tiled=False)
    wo_rows = lax.all_to_all(
        wo_col.reshape(parts, hp, r, width),
        "expert",
        0,
        0,
        axis_index_groups=part_groups,
        tiled=True,
    )
    wo_rows = wo_rows.transpose(1, 0, 2, 3).reshape(hp * DV, width)
    shared_send = jnp.stack(
        [w.reshape(r, n_dp, ff_s).transpose(1, 0, 2) for w in (shared_gate, shared_up, shared_down)],
        axis=1,
    )
    shared_send, _ = lax.optimization_barrier((shared_send, pk_all))
    shared_col = lax.all_to_all(shared_send, "dp", 0, 0, tiled=True)
    sgate, sup, sdown = (
        lax.all_gather(shared_col[:, i], "expert", axis=1, tiled=True).reshape(width, ff_s)
        for i in range(3)
    )

    slot_own = slot_places(routes, place_order[0], capacity)
    slot_col = lax.all_gather(slot_own, "dp", axis=0, tiled=False)
    slots_all = n_experts * capacity
    slot_ids = jnp.where(
        slot_col >= 0, slot_col + (jnp.arange(n_dp) * slots_all)[:, None, None], -1
    ).reshape(n_dp * rows, top_k)
    place = jnp.arange(cap)
    wanted = (
        (jnp.arange(chips) * per_chip + my_local)[:, None, None] * capacity
        + (jnp.arange(n_dp) * slots_all)[None, :, None]
        + place[None, None, :]
    )
    wanted = jnp.where(place[None, None, :] < capacity, wanted, -2).reshape(-1)
    n_slots = wanted.shape[0]
    hot = sum(
        (wanted[:, None] == slot_ids[None, :, j]).astype(BF) for j in range(top_k)
    )
    hot_t = sum(
        (slot_ids[:, j][:, None] == wanted[None, :]).astype(BF) for j in range(top_k)
    )
    cot_send, _ = lax.optimization_barrier((cotangent, pk_all))
    cot_col = lax.all_gather(cot_send, "dp", axis=0, tiled=True)

    def halves(values):
        cut = values.reshape(values.shape[0], n_dp, 2, half)
        first = cut[:, :, 0].reshape(values.shape[0], width // 2)
        second = cut[:, :, 1].reshape(values.shape[0], width // 2)
        return jnp.where(core == 0, first, second), jnp.where(core == 0, second, first)

    def whole(own, other):
        first = jnp.where(core == 0, own, other).reshape(own.shape[0], n_dp, 1, half)
        second = jnp.where(core == 0, other, own).reshape(own.shape[0], n_dp, 1, half)
        return jnp.concatenate([first, second], axis=2).reshape(own.shape[0], width)

    def between(values):
        return lax.all_to_all(
            values.reshape(chips, n_slots // chips, -1),
            "expert",
            0,
            0,
            axis_index_groups=same_core_groups,
            tiled=True,
        ).reshape(n_slots, -1)

    cot_halves = halves(cot_col)
    grad_in = [between(mm(hot, part).astype(BF)) for part in cot_halves]

    tok_plane = tok_all.reshape(seq, width)
    hidden_one = rms_norm(tok_plane.astype(F32), gain_one).astype(BF)
    positions = jnp.arange(seq)
    cos_table, sine_table = rope_tables(positions)
    query_raw = mm(hidden_one, wq).reshape(seq, hp, DH + DR)

    def make_queries(query_in):
        return jnp.concatenate(
            [
                query_in[..., :DH],
                rotate(query_in[..., DH:], cos_table[:, None, :], sine_table[:, None, :]),
            ],
            axis=-1,
        )

    query_rot, query_back = jax.vjp(make_queries, query_raw)
    queries = query_rot.astype(BF)
    latent_raw = mm(hidden_one, w_lat)
    latent_low = rms_norm(latent_raw[:, :KVR], gain_lat).astype(BF)
    rope_low = rotate(latent_raw[:, KVR:], cos_table, sine_table).astype(BF)
    expanded = mm(latent_low, wexp).astype(BF).reshape(seq, hp, DH + DV)
    score_scale = (DH + DR) ** (-0.5)
    allowed = (positions[None, :] <= positions[:, None]) & (positions[None, :] < lengths[0])
    attn_probs, probs_low, keys, attended = [], [], [], []
    for h in range(hp):
        key = jnp.concatenate([expanded[:, h, :DH], rope_low], axis=1)
        scores = jnp.where(allowed, mm_cols(queries[:, h], key) * score_scale, masked_score)
        top = jnp.max(scores, axis=-1, keepdims=True)
        exp_scores = jnp.exp(scores - top)
        probs = exp_scores / jnp.sum(exp_scores, axis=-1, keepdims=True)
        low = probs.astype(BF)
        attn_probs.append(probs)
        probs_low.append(low)
        keys.append(key)
        attended.append(mm(low, expanded[:, h, DH:]).astype(BF))
    attended = jnp.concatenate(attended, axis=1)
    out_part = mm(attended, wo_rows).astype(BF)
    tokens_f = tokens.astype(F32)
    residual = tokens_f + plane_sum(out_part.reshape(n_ex, rows, width), n_dp, n_ex, 2)
    normed_two, norm_two_back = jax.vjp(rms_norm, residual, gain_two)
    hidden_two = normed_two.astype(BF)
    x_col = column_gather(hidden_two, n_dp, n_ex, 3).reshape(n_dp * rows, width)

    x_halves = halves(x_col)
    x_in = [between(mm(hot, part).astype(BF)) for part in x_halves]
    router_halves = [part.T for part in halves(router.T)]

    def probs_of(logits):
        top = jnp.max(logits, axis=-1, keepdims=True)
        exp_logits = jnp.exp(logits - top)
        return exp_logits / jnp.sum(exp_logits, axis=-1, keepdims=True)

    shared_a = mm(x_col, sgate)
    shared_b = mm(x_col, sup)
    shared_hidden, shared_back = jax.vjp(swiglu, shared_a, shared_b)
    shared_hidden = shared_hidden.astype(BF)
    shared_out = mm_cols(shared_hidden, sdown)
    grad_sa, grad_sb = (v.astype(BF) for v in shared_back(mm(cot_col, sdown)))
    shared_grads = [
        mm_rows(x_col, grad_sa).astype(BF),
        mm_rows(x_col, grad_sb).astype(BF),
        mm_rows(cot_col, shared_hidden).astype(BF),
    ]
    shared_dx = mm_cols(grad_sa, sgate) + mm_cols(grad_sb, sup)

    expert_id = chip * per_chip + my_local
    slot_probs = probs_of(mm(x_in[0], router_halves[0]) + mm(x_in[1], router_halves[1]))
    slot_gate = jnp.sum(
        jnp.where(jnp.arange(n_experts)[None, :] == expert_id, slot_probs, 0.0),
        axis=1,
        keepdims=True,
    )
    expert_a = mm(x_in[0], gate_w[0]) + mm(x_in[1], gate_w[1])
    expert_b = mm(x_in[0], up_w[0]) + mm(x_in[1], up_w[1])
    expert_hidden, expert_back = jax.vjp(swiglu, expert_a, expert_b)
    expert_hidden = expert_hidden.astype(BF)
    rows_back = [between(mm_cols(expert_hidden, w).astype(BF)) for w in down_w]
    slot_grad = [(slot_gate * part.astype(F32)).astype(BF) for part in grad_in]
    grad_hidden = mm(slot_grad[0], down_w[0]) + mm(slot_grad[1], down_w[1])
    grad_ea, grad_eb = (v.astype(BF) for v in expert_back(grad_hidden))
    dx_back = [
        between((mm_cols(grad_ea, gw) + mm_cols(grad_eb, uw)).astype(BF))
        for gw, uw in zip(gate_w, up_w)
    ]

    def expert_sum(left, right):
        own, other = (mm_rows(a, b) for a, b in zip(left, right))
        got = lax.ppermute(other.astype(BF), "expert", sib_perm)
        total = (own + got.astype(F32)).astype(BF).reshape(n_dp, half, ff_part)
        back = lax.all_to_all(total, "dp", 0, 0, tiled=True)
        back = back.reshape(per_chip, splits, half, ff_part).transpose(0, 2, 1, 3)
        back = back.reshape(2, per_chip // 2, half, ff_e)
        back = lax.all_to_all(back, "expert", 0, 0, axis_index_groups=pair_groups, tiled=True)
        return back.transpose(1, 0, 2, 3).reshape(-1, 2 * half, ff_e).astype(F32)

    sum_egate = expert_sum(x_in, (grad_ea, grad_ea))
    sum_eup = expert_sum(x_in, (grad_eb, grad_eb))
    sum_edown = expert_sum(slot_grad, (expert_hidden, expert_hidden))

    col_probs = probs_of(mm(x_col, router))
    mine = jnp.arange(n_experts)[None, :] % per_chip == my_local
    col_gates = jnp.sum(
        jnp.where(mine, col_probs, 0.0).reshape(n_dp * rows, chips, per_chip), axis=-1
    )
    gate_hot = hot_t * jnp.repeat(col_gates, n_slots // chips, axis=1).astype(BF)
    routed = whole(*(mm(gate_hot, part) for part in rows_back))
    out_col = (routed + shared_out).astype(BF).reshape(n_dp, rows, width)
    dots = sum(mm_cols(a, b) for a, b in zip(cot_halves, rows_back)) * hot_t.astype(F32)
    dots = jnp.sum(dots.reshape(n_dp * rows, chips, n_slots // chips), axis=-1)
    grad_probs_col = jnp.where(mine, jnp.repeat(dots, per_chip, axis=1), 0.0)
    dx_col = whole(*(mm(hot_t, part) for part in dx_back)) + shared_dx
    dx_send = jnp.concatenate(
        [dx_col, grad_probs_col, jnp.zeros((n_dp * rows, 128 - n_experts), F32)], axis=1
    ).astype(BF)
    dx_got = lax.all_to_all(dx_send.reshape(n_dp, rows, width + 128), "dp", 0, 0, tiled=True)
    dx_sum = jnp.sum(dx_got.astype(F32), axis=0)
    out_got = lax.all_to_all(out_col, "dp", 0, 0, tiled=True)
    out_tokens = (residual + jnp.sum(out_got.astype(F32), axis=0)).astype(BF)

    router_probs = probs_of(mm(hidden_two, router))
    grad_probs = dx_sum[:, width : width + n_experts]
    grad_logits = (
        router_probs * (grad_probs - jnp.sum(grad_probs * router_probs, axis=-1, keepdims=True))
    ).astype(BF)
    grad_router = mm_rows(hidden_two, grad_logits)
    grad_hidden_two = dx_sum[:, :width] + mm_cols(grad_logits, router)
    grad_resid_norm, grad_gain_two = norm_two_back(grad_hidden_two)
    grad_residual = cotangent.astype(F32) + grad_resid_norm

    grad_attn = plane_gather(grad_residual.astype(BF), n_dp, n_ex, 4).reshape(seq, width)
    grad_attended = mm_cols(grad_attn, wo_rows).astype(BF)
    grad_wout = mm_rows(attended, grad_attn).astype(BF)
    grad_rope = 0.0
    grad_queries, grad_expanded = [], []
    for h in range(hp):
        gat = grad_attended[:, h * DV : (h + 1) * DV]
        probs = attn_probs[h]
        dp = mm_cols(gat, expanded[:, h, DH:])
        grad_scores = probs * (dp - jnp.sum(dp * probs, axis=-1, keepdims=True))
        grad_raw = jnp.where(allowed, grad_scores * score_scale, 0.0).astype(BF)
        grad_queries.append(mm(grad_raw, keys[h]))
        grad_key = mm_rows(grad_raw, queries[:, h])
        grad_rope = grad_rope + grad_key[:, DH:]
        grad_expanded += [grad_key[:, :DH], mm_rows(probs_low[h], gat)]
    grad_expanded = jnp.concatenate(grad_expanded, axis=1).astype(BF)
    (grad_query_raw,) = query_back(jnp.stack(grad_queries, axis=1))
    grad_query_low = grad_query_raw.reshape(seq, head_cols).astype(BF)
    grad_latent_part = jnp.concatenate([mm_cols(grad_expanded, wexp), grad_rope], axis=1)
    grad_part = jnp.concatenate(
        [
            mm_cols(grad_query_low, wq).astype(BF),
            grad_latent_part.astype(BF),
            jnp.zeros((seq, -lat % 128), BF),
        ],
        axis=1,
    )
    grad_sum = plane_sum(grad_part.reshape(n_ex, rows, -1), n_dp, n_ex, 5)
    own_start = e * rows
    latent_own = lax.dynamic_slice_in_dim(latent_raw, own_start, rows, 0)
    cos_own = lax.dynamic_slice_in_dim(cos_table, own_start, rows, 0)
    sine_own = lax.dynamic_slice_in_dim(sine_table, own_start, rows, 0)

    def make_latent(latent_in, gain_in):
        return (
            rms_norm(latent_in[:, :KVR], gain_in),
            rotate(latent_in[:, KVR:], cos_own, sine_own),
        )

    _, latent_back = jax.vjp(make_latent, latent_own, gain_lat)
    grad_latent_raw, grad_gain_lat = latent_back(
        (grad_sum[:, width : width + KVR], grad_sum[:, width + KVR : width + lat])
    )
    grad_latent_low = grad_latent_raw.astype(BF)
    _, norm_one_back = jax.vjp(rms_norm, tokens_f, gain_one)
    grad_hidden_one = grad_sum[:, :width] + mm_cols(grad_latent_low, w_lat)
    grad_tokens_norm, grad_gain_one = norm_one_back(grad_hidden_one)
    grad_tokens = grad_residual + grad_tokens_norm

    def column_sum(values):
        got = lax.all_to_all(values, "dp", 0, 0, tiled=True)
        return jnp.sum(got.astype(F32), axis=0)

    wout_back = lax.all_to_all(
        grad_wout.reshape(hp, parts, r, width).transpose(1, 0, 2, 3),
        "expert",
        0,
        0,
        axis_index_groups=part_groups,
        tiled=True,
    )
    sum_wout = column_sum(wout_back.reshape(n_dp, r, width))
    shared_sums = [
        lax.psum_scatter(
            grad.reshape(n_dp, n_ex, r, ff_s), "expert", scatter_dimension=1, tiled=True
        ).reshape(n_dp, r, ff_s)
        for grad in shared_grads
    ]
    shared_back_col = lax.all_to_all(jnp.stack(shared_sums, axis=1), "dp", 0, 0, tiled=True)
    sum_sgate, sum_sup, sum_sdown = (
        shared_back_col[:, i].transpose(1, 0, 2).reshape(r, n_dp * ff_s).astype(F32)
        for i in range(3)
    )
    grad_wq = mm_rows(hidden_one, grad_query_low).astype(BF).reshape(n_dp, n_ex, r, head_cols)
    grad_we = mm_rows(latent_low, grad_expanded).astype(BF)
    grad_we = grad_we.reshape(n_dp, n_ex, r, rl * kv_cols // r)
    heads_sum = column_sum(jnp.concatenate([grad_wq, grad_we], axis=-1)).astype(BF)
    heads_back_all = lax.all_to_all(heads_sum, "expert", 0, 0, tiled=True).astype(F32)
    sum_wq = heads_back_all[..., :head_cols].transpose(1, 0, 2).reshape(r, H, DH + DR)
    sum_wq = jnp.take(sum_wq, jnp.array(heads_back), axis=1).reshape(r, H * (DH + DR))
    sum_we = heads_back_all[..., head_cols:].reshape(n_ex, rl, kv_cols).transpose(1, 0, 2)
    sum_we = jnp.take(sum_we.reshape(rl, H, DH + DV), jnp.array(heads_back), axis=1)
    sum_we = sum_we.reshape(rl, H * (DH + DV))

    latent_plane = plane_gather(grad_latent_low, n_dp, n_ex, 6).reshape(seq, lat)
    hidden_cut = lax.dynamic_index_in_dim(
        hidden_one.reshape(seq, n_dp, n_ex, r), e, 2, keepdims=False
    )
    grad_wlat = mm_rows(hidden_cut.reshape(seq, n_dp * r), latent_plane).reshape(n_dp, r, lat)
    small = jnp.concatenate(
        [
            grad_router.reshape(n_dp, n_ex, r, n_experts),
            grad_gain_one.reshape(n_dp, n_ex, r, 1),
            grad_gain_two.reshape(n_dp, n_ex, r, 1),
            jnp.pad(grad_gain_lat.reshape(n_dp, n_ex, rl, 1), ((0, 0),) * 2 + ((0, r - rl), (0, 0))),
            jnp.zeros((n_dp, n_ex, r, pack_cols - lat - n_experts - 3), F32),
        ],
        axis=-1,
    ).transpose(1, 0, 2, 3)
    small = jnp.sum(lax.all_to_all(small, "expert", 0, 0, tiled=True), axis=0)
    pack_sum = column_sum(jnp.concatenate([grad_wlat, small], axis=-1).astype(BF))
    return (
        out_tokens,
        grad_tokens,
        pack_sum[:, lat + n_experts],
        sum_wq,
        pack_sum[:, :lat],
        pack_sum[:rl, lat + n_experts + 2],
        sum_we,
        sum_wout,
        pack_sum[:, lat + n_experts + 1],
        pack_sum[:, lat : lat + n_experts],
        sum_sgate,
        sum_sup,
        sum_sdown,
        sum_egate,
        sum_eup,
        sum_edown,
    )


def solution(mesh):
    both = ("dp", "expert")
    in_specs = (
        P(both, None),
        P(both, None),
        P("dp"),
        P(both, None),
        P(both, None),
        P(both),
        P(both, None),
        P(both, None),
        P(both),
        P(both, None),
        P(both, None),
        P(both),
        P(both, None),
        P(both, None),
        P(both, None),
        P(both, None),
        P("expert", "dp", None),
        P("expert", "dp", None),
        P("expert", "dp", None),
    )
    out_specs = (
        P(both, None),
        P(both, None),
        P(both),
        P(both, None),
        P(both, None),
        P(both),
        P(both, None),
        P(both, None),
        P(both),
        P(both, None),
        P(both, None),
        P(both, None),
        P(both, None),
        P("expert", "dp", None),
        P("expert", "dp", None),
        P("expert", "dp", None),
    )
    return jax.shard_map(shards, mesh=mesh, in_specs=in_specs, out_specs=out_specs, check_vma=False)
```

time: 3780 us -> 1580 us (0.42)
  waiting for transfers between devices: 2980 us -> 493 us
  Pallas kernels: 0 us -> 213 us
  matrix products: 406 us -> 264 us
  starting transfers between devices: 22.5 us -> 162 us
  local copies, waits for them, and re-layouts: 120 us -> 257 us
  blocking collectives: 178 us -> 71.9 us
  other arithmetic: 48.1 us -> 89.4 us
    reduce_scatter x9 -> x0, waiting for transfers between devices: 1730 us -> none  [the longest x1 254 us: shards(): lax.psum_scatter(grad_sup, ('dp', 'expert'), scatter_dimension=0, tiled=T...]
    all_gather x11 -> x5, waiting for transfers between devices: 908 us -> 0.05 us  [the longest x1 0.02 us: shards(): wo_col = lax.all_gather(wo_send, 'dp', axis=0, tiled=False)]
    all_to_all x4 -> x24, waiting for transfers between devices: 27 us -> 423 us  [the longest x3 140 us: expert_sum(): back = lax.all_to_all(total, 'dp', 0, 0, tiled=True)]
    unnamed x28 -> x7, waiting for transfers between devices: 307 us -> 59.5 us
    pallas_call x0 -> x6, Pallas kernels: none -> 213 us  [the longest x2 66.7 us: plane_sum(): pl.pallas_call(kernel, out_shape=jax.ShapeDtypeStruct((rows, cols), F32),...]
    dot_general x45 -> x67, matrix products: 405 us -> 264 us  [the longest x29 110 us: mm(): return jnp.dot(left, right, preferred_element_type=F32)]
    all_to_all x4 -> x24, starting transfers between devices: 20.7 us -> 152 us  [the longest x8 44.6 us: between(): lax.all_to_all(values.reshape(chips, n_slots // chips, -1), 'expert', 0,...]
    unnamed x2 -> x0, blocking collectives: 84.8 us -> none
  transfers between devices with their start and end apart: 28 -> 36, of which waited for: 22 -> 22; matrix products, arithmetic and copies ran while one was open for 13% -> 35% of each run, Pallas kernels for 0% -> 10%
where the time goes in v1:
time: 1580 us; the launch traced here: 1570 us
  waiting for transfers between devices  493 us (31%)
  matrix products  264 us (17%)
  local copies, waits for them, and re-layouts  257 us (16%)
  Pallas kernels  213 us (13%)
  starting transfers between devices  162 us (10%)
  other arithmetic  89.4 us (6%)
  blocking collectives  71.9 us (5%)
  between operations  17.3 us (1%)
    all_to_all x3, waiting for transfers between devices, expert_sum(): back = lax.all_to_all(total, 'dp', 0, 0, tiled=True)  140 us
    all_to_all x3, waiting for transfers between devices, expert_half(): lax.all_to_all(out, 'dp', 0, 0, tiled=True).reshape(width // 2, ff_part)  128 us
    all_to_all x8, waiting for transfers between devices, between(): lax.all_to_all(values.reshape(chips, n_slots // chips, -1), 'expert', 0,...  118 us
    dot_general x29, matrix products, mm(): return jnp.dot(left, right, preferred_element_type=F32)  110 us
    dot_general x20, matrix products, mm_cols(): lax.dot_general(left, right, (((1,), (1,)), ((), ())), preferred_element_...  86.6 us
    unnamed x313, local copies, waits for them, and re-layouts  73.4 us
    dot_general x18, matrix products, mm_rows(): lax.dot_general(left, right, (((0,), (0,)), ((), ())), preferred_element_...  67.8 us
    pallas_call x2, Pallas kernels, plane_sum(): pl.pallas_call(kernel, out_shape=jax.ShapeDtypeStruct((rows, cols), F32),...  66.7 us
  transfers between devices with their start and end apart: 36, of which 22 were waited for; matrix products, arithmetic and copies ran while one was open for 35% of the time, Pallas kernels for 10%

profile of v1, /device:TPU:11, one launch (start us, length us, event | category | flops | bytes accessed | tf_op | source)
XLA Modules:
  0.0 1567.3 jit_solution(14861169604094427399)
XLA Ops:
  15.3 57.6 %shard_map.342 = (bf16[8,128,2048]{2,1,0:T(8,128)(2,1)}, bf16[4,8,64,512]{3,2,1,0:T(8,128)(2,1)S(1)}, bf16[4,8,64,640]{3,2,1,0:T(8,128)(2,1)S(1)}) custom-call(bf16[128,2048]{1,0:T(8,128)(2,1)S(1)} %copy-done.2, bf16[8,64,512]{2,1,0:T(8,128)(2,1)S(1)} %copy-done.10, bf16[64,640]{1,0:T(8,128)(2,1)S(1)} %concatenate.57.pk_ref), custom_call_target="tpu_custom_call" | custom-call | tf_op jit(solution)/shard_map/pallas_call | solution.py:304
  121.8 12.1 all-gather.1
  171.7 7.4 all_to_all.155
  186.0 27.9 %shard_map.343 = f32[128,2048]{1,0:T(8,128)S(1)} custom-call(bf16[8,128,2048]{2,1,0:T(8,128)(2,1)S(1)} %bitcast.356), custom_call_target="tpu_custom_call" | custom-call | tf_op jit(solution)/shard_map/pallas_call | solution.py:189
  215.9 48.6 %shard_map.344 = bf16[4,128,2048]{2,1,0:T(8,128)(2,1)S(1)} custom-call(bf16[128,2048]{1,0:T(8,128)(2,1)S(1)} %multiply_convert_fusion.7.x_ref), custom_call_target="tpu_custom_call" | custom-call | tf_op jit(solution)/shard_map/pallas_call | solution.py:215
  268.1 10.3 all_to_all.156
  326.6 16.6 %all-to-all-done.1 = bf16[4,256,1024]{2,1,0:T(8,128)(2,1)} async-done(((bf16[4,256,1024]{2,1,0:T(8,128)(2,1)}), bf16[4,256,1024]{2,1,0:T(8,128)(2,1)}, u32[]{:S(2)}, u32[]{:S(2)}) %all-to-all-start.1) | async-done | bytes 2097184 | tf_op jit(solution)/shard_map/all_to_all | solution.py:479
  348.9 23.2 %all-to-all-done.4 = bf16[4,256,1024]{2,1,0:T(8,128)(2,1)} async-done(((bf16[4,256,1024]{2,1,0:T(8,128)(2,1)}), bf16[4,256,1024]{2,1,0:T(8,128)(2,1)}, u32[]{:S(2)}, u32[]{:S(2)}) %all-to-all-start.4) | async-done | bytes 2097184 | tf_op jit(solution)/shard_map/all_to_all | solution.py:479
  372.0 7.9 all-to-all-start.3
  388.0 51.6 %all-to-all-done.3 = bf16[4,256,1408]{2,1,0:T(8,128)(2,1)} async-done(((bf16[4,256,1408]{2,1,0:T(8,128)(2,1)}), bf16[4,256,1408]{2,1,0:T(8,128)(2,1)}, u32[]{:S(2)}, u32[]{:S(2)}) %all-to-all-start.3) | async-done | bytes 2883616 | tf_op jit(solution)/shard_map/all_to_all | solution.py:416
  446.2 22.3 %all-to-all-done.13 = bf16[4,256,1024]{2,1,0:T(8,128)(2,1)} async-done(((bf16[4,256,1024]{2,1,0:T(8,128)(2,1)}), bf16[4,256,1024]{2,1,0:T(8,128)(2,1)}, u32[]{:S(2)}, u32[]{:S(2)}) %all-to-all-start.13) | async-done | bytes 2097184 | tf_op jit(solution)/shard_map/all_to_all | solution.py:479
  468.4 9.6 all-to-all-start.6
  483.2 54.6 %all-to-all-done.6 = bf16[4,256,1408]{2,1,0:T(8,128)(2,1)} async-done(((bf16[4,256,1408]{2,1,0:T(8,128)(2,1)}), bf16[4,256,1408]{2,1,0:T(8,128)(2,1)}, u32[]{:S(2)}, u32[]{:S(2)}) %all-to-all-start.6) | async-done | bytes 2883616 | tf_op jit(solution)/shard_map/all_to_all | solution.py:416
  545.4 25.4 %all-to-all-done.14 = bf16[4,256,1024]{2,1,0:T(8,128)(2,1)} async-done(((bf16[4,256,1024]{2,1,0:T(8,128)(2,1)}), bf16[4,256,1024]{2,1,0:T(8,128)(2,1)}, u32[]{:S(2)}, u32[]{:S(2)}) %all-to-all-start.14) | async-done | bytes 2097184 | tf_op jit(solution)/shard_map/all_to_all | solution.py:479
  570.8 9.6 all-to-all-start.8
  589.8 8.4 fusion.114
  606.5 7.2 copy.435
  618.0 22.0 %all-to-all-done.8 = bf16[4,256,1408]{2,1,0:T(8,128)(2,1)} async-done(((bf16[4,256,1408]{2,1,0:T(8,128)(2,1)}), bf16[4,256,1408]{2,1,0:T(8,128)(2,1)}, u32[]{:S(2)}, u32[]{:S(2)}) %all-to-all-start.8) | async-done | bytes 2883616 | tf_op jit(solution)/shard_map/all_to_all | solution.py:416
  648.1 7.2 copy.437
  659.6 7.4 copy.439
  697.0 10.7 fusion.4
  707.7 7.3 fusion.121
  739.9 12.1 all-to-all-done.16
  779.2 7.5 convolution_convert_fusion.13
  811.3 9.3 all-to-all-done.9
  861.1 9.7 all-to-all-done.10
  882.3 8.3 add_convert_fusion.3
  895.2 9.6 all-to-all-start.17
  911.1 59.4 %all-reduce.15.cloned.1.call-done = (bf16[4,8,64,704]{3,2,1,0:T(8,128)(2,1)}, bf16[4,8,64,704]{3,2,1,0:T(8,128)(2,1)}, bf16[4,8,64,704]{3,2,1,0:T(8,128)(2,1)}) async-done(((bf16[4,8,64,704]{3,2,1,0:T(8,128)(2,1)}, bf16[4,8,64,704]{3,2,1,0:T(8,128)(2,1)}, bf16[4,8,64,704]{3,2,1,0:T(8,128)(2,1)}), (bf16[4,8,64,704]{3,2,1,0:T(8,128)(2,1)}, bf16[4,8,64,704]{3,2,1,0:T(8,128)(2,1)}, ...) | async-done | bytes 8650768
  1014.5 28.0 %shard_map.345 = bf16[8,128,2048]{2,1,0:T(8,128)(2,1)S(1)} custom-call(bf16[128,2048]{1,0:T(8,128)(2,1)S(1)} %fusion.105.x_ref), custom_call_target="tpu_custom_call" | custom-call | tf_op jit(solution)/shard_map/pallas_call | solution.py:140
  1070.3 8.8 concatenate.67
  1079.1 38.8 %shard_map.346 = f32[128,2688]{1,0:T(8,128)S(1)} custom-call(bf16[8,128,2688]{2,1,0:T(8,128)(2,1)} %bitcast.372), custom_call_target="tpu_custom_call" | custom-call | tf_op jit(solution)/shard_map/pallas_call | solution.py:189
  1159.7 7.5 convolution_convert_fusion.4
  1168.2 7.2 copy.451
  1175.3 9.4 reshape.915
  1184.8 12.1 shard_map.347
  1217.7 11.8 all_to_all.159
  1236.2 8.4 add_convert_fusion.2
  1244.6 12.7 all-to-all-done.23
  1257.3 7.8 all-to-all-start.25
  1284.4 41.4 %all-to-all-done.25 = bf16[4,256,1408]{2,1,0:T(8,128)(2,1)S(1)} async-done(((bf16[4,256,1408]{2,1,0:T(8,128)(2,1)}), bf16[4,256,1408]{2,1,0:T(8,128)(2,1)S(1)}, u32[]{:S(2)}, u32[]{:S(2)}) %all-to-all-start.25) | async-done | bytes 2883616 | tf_op jit(solution)/shard_map/all_to_all | solution.py:580
  1325.8 9.0 all_to_all.160
  1358.4 45.2 %all-to-all-done.27 = bf16[4,256,1408]{2,1,0:T(8,128)(2,1)S(1)} async-done(((bf16[4,256,1408]{2,1,0:T(8,128)(2,1)}), bf16[4,256,1408]{2,1,0:T(8,128)(2,1)S(1)}, u32[]{:S(2)}, u32[]{:S(2)}) %all-to-all-start.27) | async-done | bytes 2883616 | tf_op jit(solution)/shard_map/all_to_all | solution.py:580
  1403.6 7.9 all_to_all.161
  1411.5 7.7 all-to-all-start.29
  1427.9 53.1 %all-to-all-done.29 = bf16[4,256,1408]{2,1,0:T(8,128)(2,1)} async-done(((bf16[4,256,1408]{2,1,0:T(8,128)(2,1)}), bf16[4,256,1408]{2,1,0:T(8,128)(2,1)}, u32[]{:S(2)}, u32[]{:S(2)}) %all-to-all-start.29) | async-done | bytes 2883616 | tf_op jit(solution)/shard_map/all_to_all | solution.py:580
  1481.0 7.7 all-to-all-start.20
  1516.1 16.6 %all-to-all-done.20 = bf16[4,8,64,512]{3,2,1,0:T(8,128)(2,1)} async-done(((bf16[4,8,64,512]{3,2,1,0:T(8,128)(2,1)}), bf16[4,8,64,512]{3,2,1,0:T(8,128)(2,1)}, u32[]{:S(2)}, u32[]{:S(2)}) %all-to-all-start.20) | async-done | bytes 2097184 | tf_op jit(solution)/shard_map/all_to_all | solution.py:670
  (635 shorter events, 638.1 us)
Async XLA Ops:
  7.2 164.5 %all-gather.13.cloned.1.call-start = ((), (), s32[]{:S(2)}) async-start(), calls=%async_computation.32 | async-start | bytes 1310720 | tf_op jit(solution)/shard_map/all_gather | solution.py:423
  77.6 29.2 %copy-start.87 = (f32[2048,1]{0,1:T(1,128)}, f32[2048,1]{0,1:T(1,128)S(1)}, u32[]{:S(2)}) copy-start(f32[2048,1]{0,1:T(1,128)S(1)} %convert_element_type.597) | copy-start | bytes 24580
  111.8 46.8 %copy-start.57 = (f32[1024,32]{0,1:T(8,128)}, f32[1024,32]{0,1:T(8,128)S(1)}, u32[]{:S(2)}) copy-start(f32[1024,32]{0,1:T(8,128)S(1)} %copy.414) | copy-start | bytes 393220
  118.6 96.2 %copy-start.85 = (f32[2048,1]{0,1:T(1,128)}, f32[2048,1]{0,1:T(1,128)S(1)}, u32[]{:S(2)}) copy-start(f32[2048,1]{0,1:T(1,128)S(1)} %copy.508) | copy-start | bytes 24580
  120.8 26.7 %copy-start.38 = (bf16[2,512,1408]{2,1,0:T(8,128)(2,1)S(1)}, bf16[2,512,1408]{2,1,0:T(8,128)(2,1)}, u32[]{:S(2)}) copy-start(bf16[2,512,1408]{2,1,0:T(8,128)(2,1)} %param.41) | copy-start | bytes 8650756
  179.1 89.0 %all-to-all-start.7 = ((bf16[2,2,256,1408]{3,2,1,0:T(8,128)(2,1)}), bf16[2,2,256,1408]{3,2,1,0:T(8,128)(2,1)}, u32[]{:S(2)}, u32[]{:S(2)}) async-start(bf16[2,2,256,1408]{3,2,1,0:T(8,128)(2,1)} %copy.431), calls=%async_computation.7 | async-start | bytes 5767168 | tf_op jit(solution)/shard_map/all_to_all | solution.py:412
  285.3 29.5 %all-to-all-start.11 = ((bf16[4,3,64,704]{3,2,1,0:T(8,128)(2,1)}), bf16[4,3,64,704]{3,2,1,0:T(8,128)(2,1)S(1)}, u32[]{:S(2)}, u32[]{:S(2)}) async-start(bf16[4,3,64,704]{3,2,1,0:T(8,128)(2,1)} %copy.433), calls=%async_computation.11 | async-start | bytes 2359296 | tf_op jit(solution)/shard_map/all_to_all | solution.py:438
  314.9 28.3 %all-to-all-start.1 = ((bf16[4,256,1024]{2,1,0:T(8,128)(2,1)}), bf16[4,256,1024]{2,1,0:T(8,128)(2,1)}, u32[]{:S(2)}, u32[]{:S(2)}) async-start(bf16[4,256,1024]{2,1,0:T(8,128)(2,1)} %bitcast.421), calls=%async_computation.1 | async-start | bytes 4194304 | tf_op jit(solution)/shard_map/all_to_all | solution.py:479
  320.0 61.9 %all-gather.11.cloned.1.call-start = ((), (), s32[]{:S(2)}) async-start(), calls=%async_computation.31 | async-start | bytes 2621440 | tf_op jit(solution)/shard_map/all_gather | solution.py:465
  343.2 28.9 %all-to-all-start.4 = ((bf16[4,256,1024]{2,1,0:T(8,128)(2,1)}), bf16[4,256,1024]{2,1,0:T(8,128)(2,1)}, u32[]{:S(2)}, u32[]{:S(2)}) async-start(bf16[4,256,1024]{2,1,0:T(8,128)(2,1)} %bitcast.424), calls=%async_computation.4 | async-start | bytes 4194304 | tf_op jit(solution)/shard_map/all_to_all | solution.py:479
  372.0 67.5 %all-to-all-start.3 = ((bf16[4,256,1408]{2,1,0:T(8,128)(2,1)}), bf16[4,256,1408]{2,1,0:T(8,128)(2,1)}, u32[]{:S(2)}, u32[]{:S(2)}) async-start(bf16[4,256,1408]{2,1,0:T(8,128)(2,1)} %bitcast.378), calls=%async_computation.3 | async-start | bytes 5767168 | tf_op jit(solution)/shard_map/all_to_all | solution.py:416
  379.9 226.6 %all-gather.15.cloned.1.call-start = ((), (), s32[]{:S(2)}) async-start(), calls=%async_computation.33 | async-start | bytes 3538944 | tf_op jit(solution)/shard_map/all_gather | solution.py:440
  383.7 95.5 %copy-start.61 = (bf16[512,4,1,256]{0,3,1,2:T(8,128)(2,1)}, bf16[512,4,1,256]{0,3,1,2:T(8,128)(2,1)S(1)}, u32[]{:S(2)}) copy-start(bf16[512,4,1,256]{0,3,1,2:T(8,128)(2,1)S(1)} %get-tuple-element.177) | copy-start | bytes 3145732
  439.5 28.9 %all-to-all-start.13 = ((bf16[4,256,1024]{2,1,0:T(8,128)(2,1)}), bf16[4,256,1024]{2,1,0:T(8,128)(2,1)}, u32[]{:S(2)}, u32[]{:S(2)}) async-start(bf16[4,256,1024]{2,1,0:T(8,128)(2,1)} %bitcast.425), calls=%async_computation.13 | async-start | bytes 4194304 | tf_op jit(solution)/shard_map/all_to_all | solution.py:479
  446.2 31.9 %copy-start.54 = (bf16[4,1,64,704]{3,2,1,0:T(8,128)(2,1)S(1)}, bf16[4,1,64,704]{3,2,1,0:T(8,128)(2,1)}, u32[]{:S(2)}) copy-start(bf16[4,1,64,704]{3,2,1,0:T(8,128)(2,1)} %get-tuple-element.191) | copy-start | bytes 1081348
  468.4 69.3 %all-to-all-start.6 = ((bf16[4,256,1408]{2,1,0:T(8,128)(2,1)}), bf16[4,256,1408]{2,1,0:T(8,128)(2,1)}, u32[]{:S(2)}, u32[]{:S(2)}) async-start(bf16[4,256,1408]{2,1,0:T(8,128)(2,1)} %bitcast.377), calls=%async_computation.6 | async-start | bytes 5767168 | tf_op jit(solution)/shard_map/all_to_all | solution.py:416
  478.1 170.0 %all-gather.17.cloned.1.call-start = ((), (), s32[]{:S(2)}) async-start(), calls=%async_computation.34 | async-start | bytes 3538944 | tf_op jit(solution)/shard_map/all_gather | solution.py:440
  483.2 61.1 %copy-start.53 = (bf16[4,1,64,704]{3,2,1,0:T(8,128)(2,1)S(1)}, bf16[4,1,64,704]{3,2,1,0:T(8,128)(2,1)}, u32[]{:S(2)}) copy-start(bf16[4,1,64,704]{3,2,1,0:T(8,128)(2,1)} %get-tuple-element.190) | copy-start | bytes 1081348
  537.8 33.0 %all-to-all-start.14 = ((bf16[4,256,1024]{2,1,0:T(8,128)(2,1)}), bf16[4,256,1024]{2,1,0:T(8,128)(2,1)}, u32[]{:S(2)}, u32[]{:S(2)}) async-start(bf16[4,256,1024]{2,1,0:T(8,128)(2,1)} %bitcast.422), calls=%async_computation.14 | async-start | bytes 4194304 | tf_op jit(solution)/shard_map/all_to_all | solution.py:479
  544.3 115.3 %all-gather.19.cloned.1.call-start = ((), (), s32[]{:S(2)}) async-start(), calls=%async_computation.35 | async-start | bytes 3538944 | tf_op jit(solution)/shard_map/all_gather | solution.py:440
  570.8 69.3 %all-to-all-start.8 = ((bf16[4,256,1408]{2,1,0:T(8,128)(2,1)}), bf16[4,256,1408]{2,1,0:T(8,128)(2,1)}, u32[]{:S(2)}, u32[]{:S(2)}) async-start(bf16[4,256,1408]{2,1,0:T(8,128)(2,1)} %bitcast.54), calls=%async_computation.8 | async-start | bytes 5767168 | tf_op jit(solution)/shard_map/all_to_all | solution.py:416
  587.0 110.0 %collective-permute-start = (bf16[1024,1408]{1,0:T(8,128)(2,1)}, bf16[1024,1408]{1,0:T(8,128)(2,1)}, u32[]{:S(2)}, u32[]{:S(2)}) collective-permute-start(bf16[1024,1408]{1,0:T(8,128)(2,1)} %bitcast.44), channel_id=1, source_target_pairs={{0,1},{1,0},{2,3},{3,2},{4,5},{5,4},{6,7},{7,6},{8,9},{9,8},{10,11... | collective-permute-start | bytes 8650760 | tf_op jit(solution)/shard_map/ppermute | solution.py:417
  589.7 90.5 %collective-permute-start.1 = (bf16[1024,1408]{1,0:T(8,128)(2,1)}, bf16[1024,1408]{1,0:T(8,128)(2,1)}, u32[]{:S(2)}, u32[]{:S(2)}) collective-permute-start(bf16[1024,1408]{1,0:T(8,128)(2,1)} %bitcast.51), channel_id=1, source_target_pairs={{0,1},{1,0},{2,3},{3,2},{4,5},{5,4},{6,7},{7,6},{8,9},{9,8},{10,11... | collective-permute-start | bytes 8650760 | tf_op jit(solution)/shard_map/ppermute | solution.py:417
  640.1 51.6 %collective-permute-start.2 = (bf16[1024,1408]{1,0:T(8,128)(2,1)}, bf16[1024,1408]{1,0:T(8,128)(2,1)}, u32[]{:S(2)}, u32[]{:S(2)}) collective-permute-start(bf16[1024,1408]{1,0:T(8,128)(2,1)} %bitcast.55), channel_id=1, source_target_pairs={{0,1},{1,0},{2,3},{3,2},{4,5},{5,4},{6,7},{7,6},{8,9},{9,8},{10,11... | collective-permute-start | bytes 8650760 | tf_op jit(solution)/shard_map/ppermute | solution.py:417
  721.6 30.4 %all-to-all-start.16 = ((bf16[4,256,1024]{2,1,0:T(8,128)(2,1)}), bf16[4,256,1024]{2,1,0:T(8,128)(2,1)}, u32[]{:S(2)}, u32[]{:S(2)}) async-start(bf16[4,256,1024]{2,1,0:T(8,128)(2,1)} %bitcast.423), calls=%async_computation.16 | async-start | bytes 4194304 | tf_op jit(solution)/shard_map/all_to_all | solution.py:479
  752.0 34.6 %all-to-all-start.15 = ((bf16[4,256,1024]{2,1,0:T(8,128)(2,1)}), bf16[4,256,1024]{2,1,0:T(8,128)(2,1)}, u32[]{:S(2)}, u32[]{:S(2)}) async-start(bf16[4,256,1024]{2,1,0:T(8,128)(2,1)} %bitcast.420), calls=%async_computation.15 | async-start | bytes 4194304 | tf_op jit(solution)/shard_map/all_to_all | solution.py:479
  786.6 34.0 %all-to-all-start.9 = ((bf16[4,256,1024]{2,1,0:T(8,128)(2,1)}), bf16[4,256,1024]{2,1,0:T(8,128)(2,1)}, u32[]{:S(2)}, u32[]{:S(2)}) async-start(bf16[4,256,1024]{2,1,0:T(8,128)(2,1)} %bitcast.418), calls=%async_computation.9 | async-start | bytes 4194304 | tf_op jit(solution)/shard_map/all_to_all | solution.py:479
  791.1 179.4 %all-reduce.15.cloned.1.call-start = ((), (), s32[]{:S(2)}) async-start(), calls=%async_computation.36 | async-start | bytes 18874368
  820.6 50.1 %all-to-all-start.10 = ((bf16[4,256,1024]{2,1,0:T(8,128)(2,1)}), bf16[4,256,1024]{2,1,0:T(8,128)(2,1)}, u32[]{:S(2)}, u32[]{:S(2)}) async-start(bf16[4,256,1024]{2,1,0:T(8,128)(2,1)} %bitcast.419), calls=%async_computation.10 | async-start | bytes 4194304 | tf_op jit(solution)/shard_map/all_to_all | solution.py:479
  895.2 108.8 %all-to-all-start.17 = ((bf16[4,128,2176]{2,1,0:T(8,128)(2,1)}), bf16[4,128,2176]{2,1,0:T(8,128)(2,1)}, u32[]{:S(2)}, u32[]{:S(2)}) async-start(bf16[4,128,2176]{2,1,0:T(8,128)(2,1)} %concatenate.65), calls=%async_computation.17 | async-start | bytes 4456448 | tf_op jit(solution)/shard_map/all_to_all | solution.py:605
  905.9 68.1 %copy-start.32 = (f32[128,512]{1,0:T(8,128)}, f32[128,512]{1,0:T(8,128)S(1)}, u32[]{:S(2)}) copy-start(f32[128,512]{1,0:T(8,128)S(1)} %copy.501) | copy-start | bytes 786436
  1004.0 137.8 %all-to-all-start.24 = ((bf16[4,3,64,704]{3,2,1,0:T(8,128)(2,1)}), bf16[4,3,64,704]{3,2,1,0:T(8,128)(2,1)}, u32[]{:S(2)}, u32[]{:S(2)}) async-start(bf16[4,3,64,704]{3,2,1,0:T(8,128)(2,1)} %pad_maximum_fusion.5), calls=%async_computation.24 | async-start | bytes 2359296 | tf_op jit(solution)/shard_map/all_to_all | solution.py:688
  1014.5 28.1 %copy-start.28 = (bf16[2,2,64,2048]{3,2,1,0:T(8,128)(2,1)S(1)}, bf16[2,2,64,2048]{3,2,1,0:T(8,128)(2,1)}, u32[]{:S(2)}) copy-start(bf16[2,2,64,2048]{3,2,1,0:T(8,128)(2,1)} %copy-done.27) | copy-start | bytes 3145732
  1141.8 12.6 all-to-all-start.18
  1155.1 56.1 %all-to-all-start.12 = ((bf16[4,128,2048]{2,1,0:T(8,128)(2,1)}), bf16[4,128,2048]{2,1,0:T(8,128)(2,1)S(1)}, u32[]{:S(2)}, u32[]{:S(2)}) async-start(bf16[4,128,2048]{2,1,0:T(8,128)(2,1)} %bitcast.417), calls=%async_computation.12 | async-start | bytes 4194304 | tf_op jit(solution)/shard_map/all_to_all | solution.py:607
  1167.1 69.0 %collective-permute-start.3 = (bf16[1024,1408]{1,0:T(8,128)(2,1)}, bf16[1024,1408]{1,0:T(8,128)(2,1)}, u32[]{:S(2)}, u32[]{:S(2)}) collective-permute-start(bf16[1024,1408]{1,0:T(8,128)(2,1)} %convolution_convert_fusion.4), channel_id=1, source_target_pairs={{0,1},{1,0},{2,3},{3,2},{4,5},{5,4},{6,7},{7,6},{8,9},{9,8},{10,11... | collective-permute-start | bytes 8650760 | tf_op jit(solution)/shard_map/ppermute | solution.py:578
  1175.3 21.6 %copy-start.66 = (bf16[1024,128]{0,1:T(8,128)(2,1)S(1)}, bf16[1024,128]{0,1:T(8,128)(2,1)}, u32[]{:S(2)}) copy-start(bf16[1024,128]{0,1:T(8,128)(2,1)} %copy-done.65) | copy-start | bytes 786436
  1175.3 21.6 %copy-start.68 = (bf16[1024,128]{0,1:T(8,128)(2,1)S(1)}, bf16[1024,128]{0,1:T(8,128)(2,1)}, u32[]{:S(2)}) copy-start(bf16[1024,128]{0,1:T(8,128)(2,1)} %copy-done.67) | copy-start | bytes 786436
  1211.3 33.3 %copy-start.22 = (bf16[4,128,2048]{2,1,0:T(8,128)(2,1)}, bf16[4,128,2048]{2,1,0:T(8,128)(2,1)S(1)}, u32[]{:S(2)}) copy-start(bf16[4,128,2048]{2,1,0:T(8,128)(2,1)S(1)} %all-to-all-done.12) | copy-start | bytes 6291460
  1229.5 27.8 %all-to-all-start.23 = ((bf16[4,64,2048]{2,1,0:T(8,128)(2,1)}), bf16[4,64,2048]{2,1,0:T(8,128)(2,1)}, u32[]{:S(2)}, u32[]{:S(2)}) async-start(bf16[4,64,2048]{2,1,0:T(8,128)(2,1)} %bitcast.397), calls=%async_computation.23 | async-start | bytes 2097152 | tf_op jit(solution)/shard_map/all_to_all | solution.py:670
  1257.3 68.5 %all-to-all-start.25 = ((bf16[4,256,1408]{2,1,0:T(8,128)(2,1)}), bf16[4,256,1408]{2,1,0:T(8,128)(2,1)S(1)}, u32[]{:S(2)}, u32[]{:S(2)}) async-start(bf16[4,256,1408]{2,1,0:T(8,128)(2,1)} %bitcast.409), calls=%async_computation.25 | async-start | bytes 5767168 | tf_op jit(solution)/shard_map/all_to_all | solution.py:580
  1271.2 6.7 collective-permute-start.4
  1334.8 68.8 %all-to-all-start.27 = ((bf16[4,256,1408]{2,1,0:T(8,128)(2,1)}), bf16[4,256,1408]{2,1,0:T(8,128)(2,1)S(1)}, u32[]{:S(2)}, u32[]{:S(2)}) async-start(bf16[4,256,1408]{2,1,0:T(8,128)(2,1)} %bitcast.408), calls=%async_computation.27 | async-start | bytes 5767168 | tf_op jit(solution)/shard_map/all_to_all | solution.py:580
  1347.9 5.6 collective-permute-start.5
  1411.5 69.5 %all-to-all-start.29 = ((bf16[4,256,1408]{2,1,0:T(8,128)(2,1)}), bf16[4,256,1408]{2,1,0:T(8,128)(2,1)}, u32[]{:S(2)}, u32[]{:S(2)}) async-start(bf16[4,256,1408]{2,1,0:T(8,128)(2,1)} %bitcast.407), calls=%async_computation.29 | async-start | bytes 5767168 | tf_op jit(solution)/shard_map/all_to_all | solution.py:580
  1481.0 51.7 %all-to-all-start.20 = ((bf16[4,8,64,512]{3,2,1,0:T(8,128)(2,1)}), bf16[4,8,64,512]{3,2,1,0:T(8,128)(2,1)}, u32[]{:S(2)}, u32[]{:S(2)}) async-start(bf16[4,8,64,512]{3,2,1,0:T(8,128)(2,1)} %pad_maximum_fusion.3), calls=%async_computation.20 | async-start | bytes 4194304 | tf_op jit(solution)/shard_map/all_to_all | solution.py:670
  1532.7 9.1 all-to-all-start.30
  1541.8 12.4 all-to-all-start.21
  (131 other events, 680.1 us)
Sparse Core Ops, SparseCore 0:
  74.4 27.0 all-gather.12
  323.0 46.4 all-gather.10
  383.2 34.7 all-gather.14
  481.0 34.7 all-gather.16
  547.3 48.0 all-gather.18
  799.2 171.2 all-reduce.14

commit v2 on v1

--- a/solution.py
+++ b/solution.py
@@ -203,10 +203,10 @@
         greet(column)
         copies = []
         for i in range(1, n_dp):
-            copy = remote(x_ref, o_ref.at[z], send.at[i], recv.at[i], column[i - 1])
+            copy = remote(x_ref, o_ref.at[i], send.at[i], recv.at[i], column[i - 1])
             copy.start()
             copies.append(copy)
-        own = pltpu.make_async_copy(x_ref, o_ref.at[z], local)
+        own = pltpu.make_async_copy(x_ref, o_ref.at[0], local)
         own.start()
         own.wait()
         for copy in copies:
@@ -365,8 +365,6 @@
     per_chip = n_experts // chips
     splits = n_dp // per_chip
     my_local = z // splits
-    same_core_groups = [[2 * i + s for i in range(chips)] for s in range(2)]
-    pair_groups = [[2 * i, 2 * i + 1] for i in range(chips)]
     sib_perm = [(i, i ^ 1) for i in range(n_ex)]
     part_groups = [[i * parts + m for m in range(parts)] for i in range(n_ex // parts)]
     ff_e = expert_gate.shape[2]
@@ -407,18 +405,42 @@
         pk_all[..., lat + n_experts + 2].reshape(n_dp * n_ex, r)[:, :rl].reshape(KVR).astype(F32)
     )
 
-    def expert_half(weight, after):
-        two = weight.reshape(-1, 2, half, ff_e).transpose(1, 0, 2, 3)
-        two = lax.all_to_all(two, "expert", 0, 0, axis_index_groups=pair_groups, tiled=True)
-        out = two.reshape(per_chip, half, splits, ff_part).transpose(0, 2, 1, 3)
-        out = out.reshape(n_dp, half, ff_part)
-        out, _ = lax.optimization_barrier((out, after))
-        own = lax.all_to_all(out, "dp", 0, 0, tiled=True).reshape(width // 2, ff_part)
-        return own, lax.ppermute(own, "expert", sib_perm)
+    def shift(values, step):
+        return lax.ppermute(values, "dp", [(i, (i + step) % n_dp) for i in range(n_dp)])
+
+    def before(step):
+        return lax.rem(z + n_dp - step, n_dp)
+
+    def after(step):
+        return lax.rem(z + step, n_dp)
+
+    def swap(values):
+        return lax.ppermute(values, "expert", sib_perm)
+
+    def pick(values, index, axis=0):
+        return lax.dynamic_index_in_dim(values, index, axis, keepdims=False)
+
+    def expert_half(weight, held):
+        two = weight.reshape(-1, 2, half, ff_e)
+        experts = jnp.concatenate([pick(two, core, 1), swap(pick(two, 1 - core, 1))], axis=0)
+        experts = experts.reshape(per_chip, n_ex // 2, r, splits, ff_part)
+        experts, _ = lax.optimization_barrier((experts, held))
+
+        def block_for(index):
+            expert = lax.rem(index // splits + per_chip - core * (per_chip // 2), per_chip)
+            return pick(pick(experts, expert), lax.rem(index, splits), 2)
+
+        own = jnp.zeros((n_ex // 2, n_dp, r, ff_part), BF)
+        for i in range(n_dp):
+            block = block_for(after(i))
+            block = shift(block, i) if i else block
+            own = lax.dynamic_update_index_in_dim(own, block, before(i), 1)
+        own = own.reshape(width // 2, ff_part)
+        return own, swap(own)
 
     gate_w = expert_half(expert_gate, pk_all)
-    up_w = expert_half(expert_up, gate_w[0])
-    down_w = expert_half(expert_down, up_w[0])
+    up_w = expert_half(expert_up, pk_all)
+    down_w = expert_half(expert_down, pk_all)
     wo_send, _ = lax.optimization_barrier((w_out, pk_all))
     wo_col = lax.all_gather(wo_send, "dp", axis=0, tiled=False)
     wo_rows = lax.all_to_all(
@@ -430,60 +452,73 @@
         tiled=True,
     )
     wo_rows = wo_rows.transpose(1, 0, 2, 3).reshape(hp * DV, width)
-    shared_send = jnp.stack(
-        [w.reshape(r, n_dp, ff_s).transpose(1, 0, 2) for w in (shared_gate, shared_up, shared_down)],
-        axis=1,
-    )
+    shared_send = [
+        w.reshape(r, n_dp, ff_s).transpose(1, 0, 2) for w in (shared_gate, shared_up, shared_down)
+    ]
     shared_send, _ = lax.optimization_barrier((shared_send, pk_all))
-    shared_col = lax.all_to_all(shared_send, "dp", 0, 0, tiled=True)
-    sgate, sup, sdown = (
-        lax.all_gather(shared_col[:, i], "expert", axis=1, tiled=True).reshape(width, ff_s)
-        for i in range(3)
-    )
+
+    def shared_whole(weight):
+        mine = jnp.zeros((n_dp, r, ff_s), BF)
+        for i in range(n_dp):
+            block = pick(weight, after(i))
+            block = shift(block, i) if i else block
+            mine = lax.dynamic_update_index_in_dim(mine, block, before(i), 0)
+        return lax.all_gather(mine, "expert", axis=0, tiled=False).reshape(width, ff_s)
+
+    sgate, sup, sdown = (shared_whole(w) for w in shared_send)
+
+    def to_owner_order(values):
+        cut = values.reshape(values.shape[0], n_dp, n_ex, r)
+        return cut.transpose(0, 2, 1, 3).reshape(values.shape)
+
+    def from_owner_order(values):
+        cut = values.reshape(values.shape[0], n_ex, n_dp, r)
+        return cut.transpose(0, 2, 1, 3).reshape(values.shape)
+
+    def column(values):
+        return jnp.concatenate([values] + [shift(values, i) for i in range(1, n_dp)], axis=0)
 
     slot_own = slot_places(routes, place_order[0], capacity)
-    slot_col = lax.all_gather(slot_own, "dp", axis=0, tiled=False)
     slots_all = n_experts * capacity
+    slot_ids = column(slot_own).reshape(n_dp, rows, top_k)
     slot_ids = jnp.where(
-        slot_col >= 0, slot_col + (jnp.arange(n_dp) * slots_all)[:, None, None], -1
+        slot_ids >= 0, slot_ids + (jnp.arange(n_dp) * slots_all)[:, None, None], -1
     ).reshape(n_dp * rows, top_k)
     place = jnp.arange(cap)
+    far_experts = [(chip ^ m) * per_chip + my_local for m in range(chips)]
     wanted = (
-        (jnp.arange(chips) * per_chip + my_local)[:, None, None] * capacity
+        jnp.stack(far_experts)[:, None, None] * capacity
         + (jnp.arange(n_dp) * slots_all)[None, :, None]
         + place[None, None, :]
     )
     wanted = jnp.where(place[None, None, :] < capacity, wanted, -2).reshape(-1)
     n_slots = wanted.shape[0]
+    per_far = n_slots // chips
     hot = sum(
         (wanted[:, None] == slot_ids[None, :, j]).astype(BF) for j in range(top_k)
     )
     hot_t = sum(
         (slot_ids[:, j][:, None] == wanted[None, :]).astype(BF) for j in range(top_k)
     )
-    cot_send, _ = lax.optimization_barrier((cotangent, pk_all))
-    cot_col = lax.all_gather(cot_send, "dp", axis=0, tiled=True)
+    cot_send, _ = lax.optimization_barrier((to_owner_order(cotangent), pk_all))
+    cot_col = column(cot_send)
 
     def halves(values):
-        cut = values.reshape(values.shape[0], n_dp, 2, half)
-        first = cut[:, :, 0].reshape(values.shape[0], width // 2)
-        second = cut[:, :, 1].reshape(values.shape[0], width // 2)
+        first, second = values[:, : width // 2], values[:, width // 2 :]
         return jnp.where(core == 0, first, second), jnp.where(core == 0, second, first)
 
     def whole(own, other):
-        first = jnp.where(core == 0, own, other).reshape(own.shape[0], n_dp, 1, half)
-        second = jnp.where(core == 0, other, own).reshape(own.shape[0], n_dp, 1, half)
-        return jnp.concatenate([first, second], axis=2).reshape(own.shape[0], width)
+        return jnp.concatenate(
+            [jnp.where(core == 0, own, other), jnp.where(core == 0, other, own)], axis=1
+        )
 
     def between(values):
-        return lax.all_to_all(
-            values.reshape(chips, n_slots // chips, -1),
-            "expert",
-            0,
-            0,
-            axis_index_groups=same_core_groups,
-            tiled=True,
-        ).reshape(n_slots, -1)
+        cut = values.reshape(chips, per_far, -1)
+        got = [cut[0]]
+        for m in range(1, chips):
+            perm = [(i, i ^ (2 * m)) for i in range(n_ex)]
+            got.append(lax.ppermute(cut[m], "expert", perm))
+        return jnp.concatenate(got, axis=0)
 
     cot_halves = halves(cot_col)
     grad_in = [between(mm(hot, part).astype(BF)) for part in cot_halves]
@@ -529,11 +564,12 @@
     residual = tokens_f + plane_sum(out_part.reshape(n_ex, rows, width), n_dp, n_ex, 2)
     normed_two, norm_two_back = jax.vjp(rms_norm, residual, gain_two)
     hidden_two = normed_two.astype(BF)
-    x_col = column_gather(hidden_two, n_dp, n_ex, 3).reshape(n_dp * rows, width)
+    x_col = column_gather(to_owner_order(hidden_two), n_dp, n_ex, 3).reshape(n_dp * rows, width)
 
     x_halves = halves(x_col)
     x_in = [between(mm(hot, part).astype(BF)) for part in x_halves]
-    router_halves = [part.T for part in halves(router.T)]
+    router_owner = to_owner_order(router.T).T
+    router_halves = [part.T for part in halves(router_owner.T)]
 
     def probs_of(logits):
         top = jnp.max(logits, axis=-1, keepdims=True)
@@ -575,37 +611,51 @@
 
     def expert_sum(left, right):
         own, other = (mm_rows(a, b) for a, b in zip(left, right))
-        got = lax.ppermute(other.astype(BF), "expert", sib_perm)
-        total = (own + got.astype(F32)).astype(BF).reshape(n_dp, half, ff_part)
-        back = lax.all_to_all(total, "dp", 0, 0, tiled=True)
-        back = back.reshape(per_chip, splits, half, ff_part).transpose(0, 2, 1, 3)
+        got = swap(other.astype(BF))
+        total = (own + got.astype(F32)).astype(BF).reshape(n_ex // 2, n_dp, r, ff_part)
+        back = jnp.zeros((n_dp, n_ex // 2, r, ff_part), BF)
+        for i in range(n_dp):
+            block = pick(total, before(i), 1)
+            block = shift(block, -i) if i else block
+            back = lax.dynamic_update_index_in_dim(back, block, after(i), 0)
+        back = back.reshape(2, per_chip // 2, splits, half, ff_part).transpose(0, 1, 3, 2, 4)
         back = back.reshape(2, per_chip // 2, half, ff_e)
-        back = lax.all_to_all(back, "expert", 0, 0, axis_index_groups=pair_groups, tiled=True)
-        return back.transpose(1, 0, 2, 3).reshape(-1, 2 * half, ff_e).astype(F32)
+        keep, got = pick(back, core), swap(pick(back, 1 - core))
+        halves_of = [jnp.where(core == 0, keep, got), jnp.where(core == 0, got, keep)]
+        return jnp.concatenate(halves_of, axis=1).astype(F32)
 
     sum_egate = expert_sum(x_in, (grad_ea, grad_ea))
     sum_eup = expert_sum(x_in, (grad_eb, grad_eb))
     sum_edown = expert_sum(slot_grad, (expert_hidden, expert_hidden))
 
-    col_probs = probs_of(mm(x_col, router))
-    mine = jnp.arange(n_experts)[None, :] % per_chip == my_local
-    col_gates = jnp.sum(
-        jnp.where(mine, col_probs, 0.0).reshape(n_dp * rows, chips, per_chip), axis=-1
-    )
-    gate_hot = hot_t * jnp.repeat(col_gates, n_slots // chips, axis=1).astype(BF)
-    routed = whole(*(mm(gate_hot, part) for part in rows_back))
-    out_col = (routed + shared_out).astype(BF).reshape(n_dp, rows, width)
+    col_probs = probs_of(mm(x_col, router_owner))
+    expert_axis = jnp.arange(n_experts)[None, :]
+    gates = [
+        jnp.sum(jnp.where(expert_axis == expert, col_probs, 0.0), axis=1, keepdims=True)
+        for expert in far_experts
+    ]
+    gate_hot = jnp.concatenate(
+        [hot_t[:, m * per_far : (m + 1) * per_far] * gates[m].astype(BF) for m in range(chips)],
+        axis=1,
+    )
+    out_col = (whole(*(mm(gate_hot, part) for part in rows_back)) + shared_out).astype(BF)
     dots = sum(mm_cols(a, b) for a, b in zip(cot_halves, rows_back)) * hot_t.astype(F32)
-    dots = jnp.sum(dots.reshape(n_dp * rows, chips, n_slots // chips), axis=-1)
-    grad_probs_col = jnp.where(mine, jnp.repeat(dots, per_chip, axis=1), 0.0)
+    dots = jnp.sum(dots.reshape(n_dp * rows, chips, per_far), axis=-1)
+    grad_probs_col = sum(
+        jnp.where(expert_axis == far_experts[m], dots[:, m : m + 1], 0.0) for m in range(chips)
+    )
     dx_col = whole(*(mm(hot_t, part) for part in dx_back)) + shared_dx
     dx_send = jnp.concatenate(
         [dx_col, grad_probs_col, jnp.zeros((n_dp * rows, 128 - n_experts), F32)], axis=1
     ).astype(BF)
-    dx_got = lax.all_to_all(dx_send.reshape(n_dp, rows, width + 128), "dp", 0, 0, tiled=True)
-    dx_sum = jnp.sum(dx_got.astype(F32), axis=0)
-    out_got = lax.all_to_all(out_col, "dp", 0, 0, tiled=True)
-    out_tokens = (residual + jnp.sum(out_got.astype(F32), axis=0)).astype(BF)
+
+    def to_owners(values):
+        cut = values.reshape(n_dp, rows, -1)
+        got = [shift(cut[i], -i) for i in range(1, n_dp)]
+        return sum((part.astype(F32) for part in got), cut[0].astype(F32))
+
+    dx_sum = to_owners(dx_send)
+    out_tokens = (residual + from_owner_order(to_owners(out_col))).astype(BF)
 
     router_probs = probs_of(mm(hidden_two, router))
     grad_probs = dx_sum[:, width : width + n_experts]
@@ -613,7 +663,7 @@
         router_probs * (grad_probs - jnp.sum(grad_probs * router_probs, axis=-1, keepdims=True))
     ).astype(BF)
     grad_router = mm_rows(hidden_two, grad_logits)
-    grad_hidden_two = dx_sum[:, :width] + mm_cols(grad_logits, router)
+    grad_hidden_two = from_owner_order(dx_sum[:, :width]) + mm_cols(grad_logits, router)
     grad_resid_norm, grad_gain_two = norm_two_back(grad_hidden_two)
     grad_residual = cotangent.astype(F32) + grad_resid_norm
 
@@ -667,8 +717,10 @@
     grad_tokens = grad_residual + grad_tokens_norm
 
     def column_sum(values):
-        got = lax.all_to_all(values, "dp", 0, 0, tiled=True)
-        return jnp.sum(got.astype(F32), axis=0)
+        total = pick(values, z).astype(F32)
+        for i in range(1, n_dp):
+            total = total + shift(pick(values, before(i)), -i).astype(F32)
+        return total
 
     wout_back = lax.all_to_all(
         grad_wout.reshape(hp, parts, r, width).transpose(1, 0, 2, 3),
@@ -679,17 +731,18 @@
         tiled=True,
     )
     sum_wout = column_sum(wout_back.reshape(n_dp, r, width))
-    shared_sums = [
-        lax.psum_scatter(
-            grad.reshape(n_dp, n_ex, r, ff_s), "expert", scatter_dimension=1, tiled=True
+    def shared_sum(grad):
+        grad = lax.psum_scatter(
+            grad.reshape(n_ex, n_dp, r, ff_s), "expert", scatter_dimension=0, tiled=True
         ).reshape(n_dp, r, ff_s)
-        for grad in shared_grads
-    ]
-    shared_back_col = lax.all_to_all(jnp.stack(shared_sums, axis=1), "dp", 0, 0, tiled=True)
-    sum_sgate, sum_sup, sum_sdown = (
-        shared_back_col[:, i].transpose(1, 0, 2).reshape(r, n_dp * ff_s).astype(F32)
-        for i in range(3)
-    )
+        back = jnp.zeros((n_dp, r, ff_s), BF)
+        for i in range(n_dp):
+            block = pick(grad, before(i))
+            block = shift(block, -i) if i else block
+            back = lax.dynamic_update_index_in_dim(back, block, after(i), 0)
+        return back.transpose(1, 0, 2).reshape(r, n_dp * ff_s).astype(F32)
+
+    sum_sgate, sum_sup, sum_sdown = (shared_sum(grad) for grad in shared_grads)
     grad_wq = mm_rows(hidden_one, grad_query_low).astype(BF).reshape(n_dp, n_ex, r, head_cols)
     grad_we = mm_rows(latent_low, grad_expanded).astype(BF)
     grad_we = grad_we.reshape(n_dp, n_ex, r, rl * kv_cols // r)
@@ -702,10 +755,7 @@
     sum_we = sum_we.reshape(rl, H * (DH + DV))
 
     latent_plane = plane_gather(grad_latent_low, n_dp, n_ex, 6).reshape(seq, lat)
-    hidden_cut = lax.dynamic_index_in_dim(
-        hidden_one.reshape(seq, n_dp, n_ex, r), e, 2, keepdims=False
-    )
-    grad_wlat = mm_rows(hidden_cut.reshape(seq, n_dp * r), latent_plane).reshape(n_dp, r, lat)
+    grad_wlat = pick(mm_rows(hidden_one, latent_plane).reshape(n_dp, n_ex, r, lat), e, 1)
     small = jnp.concatenate(
         [
             grad_router.reshape(n_dp, n_ex, r, n_experts),

time: 1580 us -> 1450 us (0.918)
  waiting for transfers between devices: 493 us -> 364 us
  blocking collectives: 71.9 us -> 13 us
  Pallas kernels: 213 us -> 264 us
  local copies, waits for them, and re-layouts: 257 us -> 307 us
  matrix products: 264 us -> 218 us
    all_to_all x22 -> x0, waiting for transfers between devices: 416 us -> none  [the longest x3 140 us: expert_sum(): back = lax.all_to_all(total, 'dp', 0, 0, tiled=True)]
    ppermute x6 -> x93, waiting for transfers between devices: 9.83 us -> 359 us  [the longest x57 288 us: shift(): lax.ppermute(values, 'dp', [(i, (i + step) % n_dp) for i in range(n_dp)])]
    all_to_all x22 -> x0, starting transfers between devices: 144 us -> none  [the longest x8 44.6 us: between(): lax.all_to_all(values.reshape(chips, n_slots // chips, -1), 'expert', 0,...]
    ppermute x6 -> x93, starting transfers between devices: 9.67 us -> 154 us  [the longest x57 87.3 us: shift(): lax.ppermute(values, 'dp', [(i, (i + step) % n_dp) for i in range(n_dp)])]
    dynamic_update_slice x0 -> x48, local copies, waits for them, and re-layouts: none -> 66.6 us  [the longest x12 49.2 us: shared_sum(): back = lax.dynamic_update_index_in_dim(back, block, after(i), 0)]
    unnamed x7, waiting for transfers between devices: 59.5 us -> 0.11 us
    pallas_call x1, Pallas kernels: 48.6 us -> 98 us  [column_gather(): pl.pallas_call(kernel, out_shape=jax.ShapeDtypeStruct((n_dp,) + block.sha...]
    all_to_all x5 -> x0, blocking collectives: 45.9 us -> none  [the longest x2 17.3 us: expert_half(): lax.all_to_all(two, 'expert', 0, 0, axis_index_groups=pair_groups, tiled=...]
  transfers between devices with their start and end apart: 36 -> 102, of which waited for: 22 -> 37; matrix products, arithmetic and copies ran while one was open for 35% -> 40% of each run, Pallas kernels for 10% -> 14%
where the time goes in v2:
time: 1450 us; the launch traced here: 1440 us
  waiting for transfers between devices  364 us (25%)
  local copies, waits for them, and re-layouts  307 us (21%)
  Pallas kernels  264 us (18%)
  matrix products  218 us (15%)
  starting transfers between devices  165 us (11%)
  other arithmetic  85.1 us (6%)
  between operations  18.8 us (1%)
    ppermute x57, waiting for transfers between devices, shift(): lax.ppermute(values, 'dp', [(i, (i + step) % n_dp) for i in range(n_dp)])  288 us
    dot_general x29, matrix products, mm(): return jnp.dot(left, right, preferred_element_type=F32)  99.4 us
    pallas_call x1, Pallas kernels, column_gather(): pl.pallas_call(kernel, out_shape=jax.ShapeDtypeStruct((n_dp,) + block.sha...  98 us
    ppermute x57, starting transfers between devices, shift(): lax.ppermute(values, 'dp', [(i, (i + step) % n_dp) for i in range(n_dp)])  87.3 us
    ppermute x24, waiting for transfers between devices, between(): got.append(lax.ppermute(cut[m], 'expert', perm))  71 us
    pallas_call x2, Pallas kernels, plane_sum(): pl.pallas_call(kernel, out_shape=jax.ShapeDtypeStruct((rows, cols), F32),...  67.9 us
    dot_general x18, matrix products, mm_rows(): lax.dot_general(left, right, (((0,), (0,)), ((), ())), preferred_element_...  60 us
    dot_general x20, matrix products, mm_cols(): lax.dot_general(left, right, (((1,), (1,)), ((), ())), preferred_element_...  59.1 us
  transfers between devices with their start and end apart: 102, of which 37 were waited for; matrix products, arithmetic and copies ran while one was open for 40% of the time, Pallas kernels for 14%

profile of v2, /device:TPU:11, one launch (start us, length us, event | category | flops | bytes accessed | tf_op | source)
XLA Modules:
  0.0 1435.5 jit_solution(12149250203504806096)
XLA Ops:
  16.5 57.6 %shard_map.342 = (bf16[8,128,2048]{2,1,0:T(8,128)(2,1)}, bf16[4,8,64,512]{3,2,1,0:T(8,128)(2,1)S(1)}, bf16[4,8,64,640]{3,2,1,0:T(8,128)(2,1)S(1)}) custom-call(bf16[128,2048]{1,0:T(8,128)(2,1)S(1)} %copy-done, bf16[8,64,512]{2,1,0:T(8,128)(2,1)S(1)} %copy-done.6, bf16[64,640]{1,0:T(8,128)(2,1)S(1)} %concatenate.124.pk_ref), custom_call_target="tpu_custom_call" | custom-call | tf_op jit(solution)/shard_map/pallas_call | solution.py:304
  112.8 5.4 multiply_convert_fusion
  134.8 5.7 fusion.171
  231.6 6.4 copy.429
  262.4 7.1 collective-permute-start.14
  298.6 7.7 all_to_all.20
  307.8 29.0 %shard_map.343 = f32[128,2048]{1,0:T(8,128)S(1)} custom-call(bf16[8,128,2048]{2,1,0:T(8,128)(2,1)S(1)} %bitcast.451), custom_call_target="tpu_custom_call" | custom-call | tf_op jit(solution)/shard_map/pallas_call | solution.py:189
  341.6 98.0 %shard_map.344 = bf16[4,128,2048]{2,1,0:T(8,128)(2,1)S(1)} custom-call(bf16[128,2048]{1,0:T(8,128)(2,1)S(1)} %copy.408.x_ref), custom_call_target="tpu_custom_call" | custom-call | tf_op jit(solution)/shard_map/pallas_call | solution.py:215
  454.2 10.5 collective-permute-done.17
  466.5 16.2 %collective-permute-start.18 = (bf16[1024,1408]{1,0:T(8,128)(2,1)S(1)}, bf16[1024,1408]{1,0:T(8,128)(2,1)S(1)}, u32[]{:S(2)}, u32[]{:S(2)}) collective-permute-start(bf16[1024,1408]{1,0:T(8,128)(2,1)S(1)} %bitcast.518), channel_id=1, source_target_pairs={{0,1},{1,0},{2,3},{3,2},{4,5},{5,4},{6,7},{7,6},{8,9},{9,8},{10,11... | collective-permute-start | bytes 8650760 | tf_op jit(solution)/shard_map/ppermute | solution.py:418
  492.4 38.2 %collective-permute-done.8 = bf16[4,64,1408]{2,1,0:T(8,128)(2,1)S(1)} collective-permute-done((bf16[4,64,1408]{2,1,0:T(8,128)(2,1)S(1)}, bf16[4,64,1408]{2,1,0:T(8,128)(2,1)S(1)}, u32[]{:S(2)}, u32[]{:S(2)}) %collective-permute-start.8) | collective-permute-done | bytes 720928 | tf_op jit(solution)/shard_map/ppermute | solution.py:409
  535.1 9.3 collective-permute-done.5
  547.6 9.0 collective-permute-done.4
  563.9 6.7 collective-permute-done.50
  571.5 11.9 collective-permute-done.49
  589.8 7.5 convolution_add_fusion.1
  597.3 7.2 fusion.155
  605.1 7.7 convolution_add_fusion
  612.9 16.2 %fusion.4 = (bf16[1024,1408]{1,0:T(8,128)(2,1)}, bf16[1024,1408]{1,0:T(8,128)(2,1)}, bf16[1024,1408]{1,0:T(8,128)(2,1)}) fusion(f32[1024,1408]{1,0:T(8,128)} %convolution_add_fusion, f32[1024,1408]{1,0:T(8,128)} %convolution_add_fusion.1, f32[1024,1408]{1,0:T(8,128)} %fusion.155, bf16[1024,1408]{1,0:T(8,128)(2,1)} %bitcast.57, ...), kind=kOutput, calls=%fused_computation.12 | convolution fusion | flops 2985689088 | bytes 30932992 | tf_op jit(solution)/shard_map/dot_general | solution.py:56
  629.0 6.1 convolution_convert_fusion.12
  642.7 5.6 add_convert_fusion.4
  670.4 6.2 fusion.39
  689.1 7.2 convolution_convert_fusion.3
  732.2 9.0 collective-permute-done.23
  761.1 6.7 collective-permute-done.54
  773.4 6.6 collective-permute-done.53
  780.5 9.7 collective-permute-done.51
  818.5 15.0 %collective-permute-done.39 = bf16[128,2048]{1,0:T(8,128)(2,1)} collective-permute-done((bf16[128,2048]{1,0:T(8,128)(2,1)S(1)}, bf16[128,2048]{1,0:T(8,128)(2,1)}, u32[]{:S(2)}, u32[]{:S(2)}) %collective-permute-start.39) | collective-permute-done | bytes 524320 | tf_op jit(solution)/shard_map/ppermute | solution.py:409
  840.3 12.1 collective-permute-done.58
  873.1 28.3 %shard_map.345 = bf16[8,128,2048]{2,1,0:T(8,128)(2,1)S(1)} custom-call(bf16[128,2048]{1,0:T(8,128)(2,1)S(1)} %fusion.148.x_ref), custom_call_target="tpu_custom_call" | custom-call | tf_op jit(solution)/shard_map/pallas_call | solution.py:140
  932.6 9.0 concatenate.153
  941.6 38.9 %shard_map.346 = f32[128,2688]{1,0:T(8,128)S(1)} custom-call(bf16[8,128,2688]{2,1,0:T(8,128)(2,1)} %bitcast.468), custom_call_target="tpu_custom_call" | custom-call | tf_op jit(solution)/shard_map/pallas_call | solution.py:189
  982.0 12.1 shard_map.347
  1034.6 9.1 collective-permute-done.67
  1046.8 19.8 %collective-permute-done.66 = bf16[64,2048]{1,0:T(8,128)(2,1)S(1)} collective-permute-done((bf16[64,2048]{1,0:T(8,128)(2,1)S(1)}, bf16[64,2048]{1,0:T(8,128)(2,1)S(1)}, u32[]{:S(2)}, u32[]{:S(2)}) %collective-permute-start.66) | collective-permute-done | bytes 262176 | tf_op jit(solution)/shard_map/ppermute | solution.py:409
  1079.7 10.8 collective-permute-done.64
  1096.1 5.9 all-to-all-start.2
  1104.7 5.4 all-to-all-done.2
  1116.2 6.0 add_convert_fusion.2
  1133.6 5.3 add_convert_fusion
  1142.4 27.8 %collective-permute-done.80 = bf16[4,64,1408]{2,1,0:T(8,128)(2,1)S(1)} collective-permute-done((bf16[4,64,1408]{2,1,0:T(8,128)(2,1)S(1)}, bf16[4,64,1408]{2,1,0:T(8,128)(2,1)S(1)}, u32[]{:S(2)}, u32[]{:S(2)}) %collective-permute-start.80) | collective-permute-done | bytes 720928 | tf_op jit(solution)/shard_map/ppermute | solution.py:409
  1170.3 17.5 %collective-permute-start.89 = (bf16[4,64,1408]{2,1,0:T(8,128)(2,1)S(1)}, bf16[4,64,1408]{2,1,0:T(8,128)(2,1)S(1)}, u32[]{:S(2)}, u32[]{:S(2)}) collective-permute-start(bf16[4,64,1408]{2,1,0:T(8,128)(2,1)S(1)} %get-tuple-element.169), channel_id=1, source_target_pairs={{0,24},{8,0},{16,8},{24,16},{1,25},{9,1},{17,9},{25,17},{2,26},{10... | collective-permute-start | bytes 2162696 | tf_op jit(solution)/shard_map/ppermute | solution.py:409
  1187.9 28.7 %collective-permute-done.81 = bf16[4,64,1408]{2,1,0:T(8,128)(2,1)S(1)} collective-permute-done((bf16[4,64,1408]{2,1,0:T(8,128)(2,1)S(1)}, bf16[4,64,1408]{2,1,0:T(8,128)(2,1)S(1)}, u32[]{:S(2)}, u32[]{:S(2)}) %collective-permute-start.81) | collective-permute-done | bytes 720928 | tf_op jit(solution)/shard_map/ppermute | solution.py:409
  1216.7 16.3 %collective-permute-done.84 = bf16[4,64,1408]{2,1,0:T(8,128)(2,1)S(1)} collective-permute-done((bf16[4,64,1408]{2,1,0:T(8,128)(2,1)S(1)}, bf16[4,64,1408]{2,1,0:T(8,128)(2,1)S(1)}, u32[]{:S(2)}, u32[]{:S(2)}) %collective-permute-start.84) | collective-permute-done | bytes 720928 | tf_op jit(solution)/shard_map/ppermute | solution.py:409
  1234.4 28.5 %collective-permute-done.85 = bf16[4,64,1408]{2,1,0:T(8,128)(2,1)S(1)} collective-permute-done((bf16[4,64,1408]{2,1,0:T(8,128)(2,1)S(1)}, bf16[4,64,1408]{2,1,0:T(8,128)(2,1)S(1)}, u32[]{:S(2)}, u32[]{:S(2)}) %collective-permute-start.85) | collective-permute-done | bytes 720928 | tf_op jit(solution)/shard_map/ppermute | solution.py:409
  1263.6 14.8 %collective-permute-done.86 = bf16[4,64,1408]{2,1,0:T(8,128)(2,1)S(1)} collective-permute-done((bf16[4,64,1408]{2,1,0:T(8,128)(2,1)S(1)}, bf16[4,64,1408]{2,1,0:T(8,128)(2,1)S(1)}, u32[]{:S(2)}, u32[]{:S(2)}) %collective-permute-start.86) | collective-permute-done | bytes 720928 | tf_op jit(solution)/shard_map/ppermute | solution.py:409
  1278.5 16.3 %collective-permute-done.89 = bf16[4,64,1408]{2,1,0:T(8,128)(2,1)S(1)} collective-permute-done((bf16[4,64,1408]{2,1,0:T(8,128)(2,1)S(1)}, bf16[4,64,1408]{2,1,0:T(8,128)(2,1)S(1)}, u32[]{:S(2)}, u32[]{:S(2)}) %collective-permute-start.89) | collective-permute-done | bytes 720928 | tf_op jit(solution)/shard_map/ppermute | solution.py:409
  1294.9 14.3 collective-permute-done.91
  (1063 shorter events, 660.4 us)
Async XLA Ops:
  7.2 291.5 %all-gather.12.cloned.1.call-start = ((), (), s32[]{:S(2)}) async-start(), calls=%async_computation.13 | async-start | bytes 1310720 | tf_op jit(solution)/shard_map/all_gather | solution.py:445
  77.8 192.4 %collective-permute-start.44 = (bf16[128,2048]{1,0:T(8,128)(2,1)}, bf16[128,2048]{1,0:T(8,128)(2,1)}, u32[]{:S(2)}, u32[]{:S(2)}) collective-permute-start(bf16[128,2048]{1,0:T(8,128)(2,1)} %copy.419), channel_id=1, source_target_pairs={{0,24},{8,0},{16,8},{24,16},{1,25},{9,1},{17,9},{25,17},{2,26},{10... | collective-permute-start | bytes 1572872 | tf_op jit(solution)/shard_map/ppermute | solution.py:409
  77.8 192.5 %collective-permute-start.43 = (bf16[128,2048]{1,0:T(8,128)(2,1)}, bf16[128,2048]{1,0:T(8,128)(2,1)}, u32[]{:S(2)}, u32[]{:S(2)}) collective-permute-start(bf16[128,2048]{1,0:T(8,128)(2,1)} %copy.419), channel_id=1, source_target_pairs={{0,16},{8,24},{16,0},{24,8},{1,17},{9,25},{17,1},{25,9},{2,18},{10... | collective-permute-start | bytes 1572872 | tf_op jit(solution)/shard_map/ppermute | solution.py:409
  81.5 156.5 %collective-permute-start.2 = (s32[128,6]{1,0:T(8,128)}, s32[128,6]{1,0:T(8,128)}, u32[]{:S(2)}, u32[]{:S(2)}) collective-permute-start(s32[128,6]{1,0:T(8,128)} %add_select_fusion), channel_id=1, source_target_pairs={{0,24},{8,0},{16,8},{24,16},{1,25},{9,1},{17,9},{25,17},{2,26},{10... | collective-permute-start | bytes 9224 | tf_op jit(solution)/shard_map/ppermute | solution.py:409
  82.7 159.3 %collective-permute-start.1 = (s32[128,6]{1,0:T(8,128)}, s32[128,6]{1,0:T(8,128)}, u32[]{:S(2)}, u32[]{:S(2)}) collective-permute-start(s32[128,6]{1,0:T(8,128)} %add_select_fusion), channel_id=1, source_target_pairs={{0,16},{8,24},{16,0},{24,8},{1,17},{9,25},{17,1},{25,9},{2,18},{10... | collective-permute-start | bytes 9224 | tf_op jit(solution)/shard_map/ppermute | solution.py:409
  85.1 575.3 %all-gather.8.cloned.1.call-start = ((), (), s32[]{:S(2)}) async-start(), calls=%async_computation.8 | async-start | bytes 3538944 | tf_op jit(solution)/shard_map/all_gather | solution.py:466
  94.9 47.3 %collective-permute-start.33 = (bf16[64,704]{1,0:T(8,128)(2,1)}, bf16[64,704]{1,0:T(8,128)(2,1)}, u32[]{:S(2)}, u32[]{:S(2)}) collective-permute-start(bf16[64,704]{1,0:T(8,128)(2,1)} %bitcast.445), channel_id=1, source_target_pairs={{0,8},{8,16},{16,24},{24,0},{1,9},{9,17},{17,25},{25,1},{2,10},{10... | collective-permute-start | bytes 270344 | tf_op jit(solution)/shard_map/ppermute | solution.py:409
  154.6 510.6 %all-gather.10.cloned.1.call-start = ((), (), s32[]{:S(2)}) async-start(), calls=%async_computation.9 | async-start | bytes 3538944 | tf_op jit(solution)/shard_map/all_gather | solution.py:466
  199.6 48.4 %collective-permute-start = (s32[128,6]{1,0:T(8,128)}, s32[128,6]{1,0:T(8,128)}, u32[]{:S(2)}, u32[]{:S(2)}) collective-permute-start(s32[128,6]{1,0:T(8,128)} %add_select_fusion), channel_id=1, source_target_pairs={{0,8},{8,16},{16,24},{24,0},{1,9},{9,17},{17,25},{25,1},{2,10},{10... | collective-permute-start | bytes 9224 | tf_op jit(solution)/shard_map/ppermute | solution.py:409
  201.8 468.5 %all-gather.6.cloned.1.call-start = ((), (), s32[]{:S(2)}) async-start(), calls=%async_computation.7 | async-start | bytes 3538944 | tf_op jit(solution)/shard_map/all_gather | solution.py:466
  270.2 1042.4 %reduce-scatter.4.cloned.1.call-start = ((), (), s32[]{:S(2)}) async-start(), calls=%async_computation.10 | async-start | bytes 3538944 | tf_op jit(solution)/shard_map/reduce_scatter | solution.py:735
  282.7 164.5 %collective-permute-start.20 = (bf16[4,64,1408]{2,1,0:T(8,128)(2,1)}, bf16[4,64,1408]{2,1,0:T(8,128)(2,1)}, u32[]{:S(2)}, u32[]{:S(2)}) collective-permute-start(bf16[4,64,1408]{2,1,0:T(8,128)(2,1)} %get-tuple-element.181), channel_id=1, source_target_pairs={{0,8},{8,16},{16,24},{24,0},{1,9},{9,17},{17,25},{25,1},{2,10},{10... | collective-permute-start | bytes 2162696 | tf_op jit(solution)/shard_map/ppermute | solution.py:409
  284.5 182.0 %collective-permute-start.21 = (bf16[4,64,1408]{2,1,0:T(8,128)(2,1)}, bf16[4,64,1408]{2,1,0:T(8,128)(2,1)}, u32[]{:S(2)}, u32[]{:S(2)}) collective-permute-start(bf16[4,64,1408]{2,1,0:T(8,128)(2,1)} %get-tuple-element.180), channel_id=1, source_target_pairs={{0,16},{8,24},{16,0},{24,8},{1,17},{9,25},{17,1},{25,9},{2,18},{10... | collective-permute-start | bytes 2162696 | tf_op jit(solution)/shard_map/ppermute | solution.py:409
  285.7 198.1 %collective-permute-start.22 = (bf16[4,64,1408]{2,1,0:T(8,128)(2,1)}, bf16[4,64,1408]{2,1,0:T(8,128)(2,1)}, u32[]{:S(2)}, u32[]{:S(2)}) collective-permute-start(bf16[4,64,1408]{2,1,0:T(8,128)(2,1)} %get-tuple-element.179), channel_id=1, source_target_pairs={{0,24},{8,0},{16,8},{24,16},{1,25},{9,1},{17,9},{25,17},{2,26},{10... | collective-permute-start | bytes 2162696 | tf_op jit(solution)/shard_map/ppermute | solution.py:409
  288.8 161.4 %collective-permute-start.15 = (bf16[4,64,1408]{2,1,0:T(8,128)(2,1)}, bf16[4,64,1408]{2,1,0:T(8,128)(2,1)}, u32[]{:S(2)}, u32[]{:S(2)}) collective-permute-start(bf16[4,64,1408]{2,1,0:T(8,128)(2,1)} %get-tuple-element.191), channel_id=1, source_target_pairs={{0,8},{8,16},{16,24},{24,0},{1,9},{9,17},{17,25},{25,1},{2,10},{10... | collective-permute-start | bytes 2162696 | tf_op jit(solution)/shard_map/ppermute | solution.py:409
  291.1 160.5 %collective-permute-start.16 = (bf16[4,64,1408]{2,1,0:T(8,128)(2,1)}, bf16[4,64,1408]{2,1,0:T(8,128)(2,1)}, u32[]{:S(2)}, u32[]{:S(2)}) collective-permute-start(bf16[4,64,1408]{2,1,0:T(8,128)(2,1)} %get-tuple-element.190), channel_id=1, source_target_pairs={{0,16},{8,24},{16,0},{24,8},{1,17},{9,25},{17,1},{25,9},{2,18},{10... | collective-permute-start | bytes 2162696 | tf_op jit(solution)/shard_map/ppermute | solution.py:409
  466.5 92.9 %collective-permute-start.18 = (bf16[1024,1408]{1,0:T(8,128)(2,1)S(1)}, bf16[1024,1408]{1,0:T(8,128)(2,1)S(1)}, u32[]{:S(2)}, u32[]{:S(2)}) collective-permute-start(bf16[1024,1408]{1,0:T(8,128)(2,1)S(1)} %bitcast.518), channel_id=1, source_target_pairs={{0,1},{1,0},{2,3},{3,2},{4,5},{5,4},{6,7},{7,6},{8,9},{9,8},{10,11... | collective-permute-start | bytes 8650760 | tf_op jit(solution)/shard_map/ppermute | solution.py:418
  483.9 46.7 %collective-permute-start.8 = (bf16[4,64,1408]{2,1,0:T(8,128)(2,1)S(1)}, bf16[4,64,1408]{2,1,0:T(8,128)(2,1)S(1)}, u32[]{:S(2)}, u32[]{:S(2)}) collective-permute-start(bf16[4,64,1408]{2,1,0:T(8,128)(2,1)S(1)} %copy-done.88), channel_id=1, source_target_pairs={{0,16},{8,24},{16,0},{24,8},{1,17},{9,25},{17,1},{25,9},{2,18},{10... | collective-permute-start | bytes 2162696 | tf_op jit(solution)/shard_map/ppermute | solution.py:409
  485.2 48.3 %collective-permute-start.9 = (bf16[4,64,1408]{2,1,0:T(8,128)(2,1)S(1)}, bf16[4,64,1408]{2,1,0:T(8,128)(2,1)S(1)}, u32[]{:S(2)}, u32[]{:S(2)}) collective-permute-start(bf16[4,64,1408]{2,1,0:T(8,128)(2,1)S(1)} %copy-done.87), channel_id=1, source_target_pairs={{0,24},{8,0},{16,8},{24,16},{1,25},{9,1},{17,9},{25,17},{2,26},{10... | collective-permute-start | bytes 2162696 | tf_op jit(solution)/shard_map/ppermute | solution.py:409
  485.9 46.6 %collective-permute-start.10 = (bf16[256,1024]{1,0:T(8,128)(2,1)S(1)}, bf16[256,1024]{1,0:T(8,128)(2,1)S(1)}, u32[]{:S(2)}, u32[]{:S(2)}) collective-permute-start(bf16[256,1024]{1,0:T(8,128)(2,1)S(1)} %get-tuple-element.240), channel_id=1, source_target_pairs={{0,2},{1,3},{2,0},{3,1},{4,6},{5,7},{6,4},{7,5},{8,10},{9,11},{10,... | collective-permute-start | bytes 1572872 | tf_op jit(solution)/shard_map/ppermute | solution.py:520
  486.6 98.1 %collective-permute-start.26 = (bf16[1024,1408]{1,0:T(8,128)(2,1)S(1)}, bf16[1024,1408]{1,0:T(8,128)(2,1)S(1)}, u32[]{:S(2)}, u32[]{:S(2)}) collective-permute-start(bf16[1024,1408]{1,0:T(8,128)(2,1)S(1)} %bitcast.515), channel_id=1, source_target_pairs={{0,1},{1,0},{2,3},{3,2},{4,5},{5,4},{6,7},{7,6},{8,9},{9,8},{10,11... | collective-permute-start | bytes 8650760 | tf_op jit(solution)/shard_map/ppermute | solution.py:418
  544.4 52.8 %collective-permute-start.13 = (bf16[1024,1408]{1,0:T(8,128)(2,1)}, bf16[1024,1408]{1,0:T(8,128)(2,1)S(1)}, u32[]{:S(2)}, u32[]{:S(2)}) collective-permute-start(bf16[1024,1408]{1,0:T(8,128)(2,1)} %bitcast.57), channel_id=1, source_target_pairs={{0,1},{1,0},{2,3},{3,2},{4,5},{5,4},{6,7},{7,6},{8,9},{9,8},{10,11... | collective-permute-start | bytes 8650760 | tf_op jit(solution)/shard_map/ppermute | solution.py:418
  636.6 79.0 %collective-permute-start.29 = (bf16[256,1024]{1,0:T(8,128)(2,1)}, bf16[256,1024]{1,0:T(8,128)(2,1)}, u32[]{:S(2)}, u32[]{:S(2)}) collective-permute-start(bf16[256,1024]{1,0:T(8,128)(2,1)} %get-tuple-element.230), channel_id=1, source_target_pairs={{0,6},{1,7},{2,4},{3,5},{4,2},{5,3},{6,0},{7,1},{8,14},{9,15},{10,... | collective-permute-start | bytes 1572872 | tf_op jit(solution)/shard_map/ppermute | solution.py:520
  637.5 86.8 %collective-permute-start.28 = (bf16[256,1024]{1,0:T(8,128)(2,1)}, bf16[256,1024]{1,0:T(8,128)(2,1)}, u32[]{:S(2)}, u32[]{:S(2)}) collective-permute-start(bf16[256,1024]{1,0:T(8,128)(2,1)} %get-tuple-element.231), channel_id=1, source_target_pairs={{0,4},{1,5},{2,6},{3,7},{4,0},{5,1},{6,2},{7,3},{8,12},{9,13},{10,... | collective-permute-start | bytes 1572872 | tf_op jit(solution)/shard_map/ppermute | solution.py:520
  638.5 87.4 %collective-permute-start.27 = (bf16[256,1024]{1,0:T(8,128)(2,1)}, bf16[256,1024]{1,0:T(8,128)(2,1)}, u32[]{:S(2)}, u32[]{:S(2)}) collective-permute-start(bf16[256,1024]{1,0:T(8,128)(2,1)} %get-tuple-element.232), channel_id=1, source_target_pairs={{0,2},{1,3},{2,0},{3,1},{4,6},{5,7},{6,4},{7,5},{8,10},{9,11},{10,... | collective-permute-start | bytes 1572872 | tf_op jit(solution)/shard_map/ppermute | solution.py:520
  685.3 632.8 %reduce-scatter.6.cloned.1.call-start = ((), (), s32[]{:S(2)}) async-start(), calls=%async_computation.11 | async-start | bytes 3538944 | tf_op jit(solution)/shard_map/reduce_scatter | solution.py:735
  724.0 601.0 %reduce-scatter.8.cloned.1.call-start = ((), (), s32[]{:S(2)}) async-start(), calls=%async_computation.12 | async-start | bytes 3538944 | tf_op jit(solution)/shard_map/reduce_scatter | solution.py:735
  731.9 48.2 %collective-permute-start.53 = (bf16[256,1024]{1,0:T(8,128)(2,1)}, bf16[256,1024]{1,0:T(8,128)(2,1)}, u32[]{:S(2)}, u32[]{:S(2)}) collective-permute-start(bf16[256,1024]{1,0:T(8,128)(2,1)} %get-tuple-element.207), channel_id=1, source_target_pairs={{0,6},{1,7},{2,4},{3,5},{4,2},{5,3},{6,0},{7,1},{8,14},{9,15},{10,... | collective-permute-start | bytes 1572872 | tf_op jit(solution)/shard_map/ppermute | solution.py:520
  767.9 47.2 %collective-permute-start.40 = (bf16[128,2048]{1,0:T(8,128)(2,1)}, bf16[128,2048]{1,0:T(8,128)(2,1)}, u32[]{:S(2)}, u32[]{:S(2)}) collective-permute-start(bf16[128,2048]{1,0:T(8,128)(2,1)} %get-tuple-element.224), channel_id=1, source_target_pairs={{0,16},{8,24},{16,0},{24,8},{1,17},{9,25},{17,1},{25,9},{2,18},{10... | collective-permute-start | bytes 1572872 | tf_op jit(solution)/shard_map/ppermute | solution.py:409
  780.1 53.5 %collective-permute-start.39 = (bf16[128,2048]{1,0:T(8,128)(2,1)S(1)}, bf16[128,2048]{1,0:T(8,128)(2,1)}, u32[]{:S(2)}, u32[]{:S(2)}) collective-permute-start(bf16[128,2048]{1,0:T(8,128)(2,1)S(1)} %get-tuple-element.222), channel_id=1, source_target_pairs={{0,24},{8,0},{16,8},{24,16},{1,25},{9,1},{17,9},{25,17},{2,26},{10... | collective-permute-start | bytes 1572872 | tf_op jit(solution)/shard_map/ppermute | solution.py:409
  802.0 50.4 %collective-permute-start.58 = (bf16[128,2176]{1,0:T(8,128)(2,1)}, bf16[128,2176]{1,0:T(8,128)(2,1)}, u32[]{:S(2)}, u32[]{:S(2)}) collective-permute-start(bf16[128,2176]{1,0:T(8,128)(2,1)} %get-tuple-element.202), channel_id=1, source_target_pairs={{0,16},{8,24},{16,0},{24,8},{1,17},{9,25},{17,1},{25,9},{2,18},{10... | collective-permute-start | bytes 1671176 | tf_op jit(solution)/shard_map/ppermute | solution.py:409
  804.2 53.2 %collective-permute-start.57 = (bf16[128,2176]{1,0:T(8,128)(2,1)}, bf16[128,2176]{1,0:T(8,128)(2,1)}, u32[]{:S(2)}, u32[]{:S(2)}) collective-permute-start(bf16[128,2176]{1,0:T(8,128)(2,1)} %get-tuple-element.200), channel_id=1, source_target_pairs={{0,24},{8,0},{16,8},{24,16},{1,25},{9,1},{17,9},{25,17},{2,26},{10... | collective-permute-start | bytes 1671176 | tf_op jit(solution)/shard_map/ppermute | solution.py:409
  815.0 301.1 %collective-permute-start.78 = (bf16[1024,1408]{1,0:T(8,128)(2,1)}, bf16[1024,1408]{1,0:T(8,128)(2,1)}, u32[]{:S(2)}, u32[]{:S(2)}) collective-permute-start(bf16[1024,1408]{1,0:T(8,128)(2,1)} %convolution_convert_fusion.4), channel_id=1, source_target_pairs={{0,1},{1,0},{2,3},{3,2},{4,5},{5,4},{6,7},{7,6},{8,9},{9,8},{10,11... | collective-permute-start | bytes 8650760 | tf_op jit(solution)/shard_map/ppermute | solution.py:418
  833.6 291.8 %collective-permute-start.83 = (bf16[1024,1408]{1,0:T(8,128)(2,1)}, bf16[1024,1408]{1,0:T(8,128)(2,1)}, u32[]{:S(2)}, u32[]{:S(2)}) collective-permute-start(bf16[1024,1408]{1,0:T(8,128)(2,1)} %convolution_convert_fusion.3), channel_id=1, source_target_pairs={{0,1},{1,0},{2,3},{3,2},{4,5},{5,4},{6,7},{7,6},{8,9},{9,8},{10,11... | collective-permute-start | bytes 8650760 | tf_op jit(solution)/shard_map/ppermute | solution.py:418
  1015.1 53.4 %all-to-all-start.1 = ((f32[8,1,16384]{2,1,0:T(1,128)}), f32[8,1,16384]{2,1,0:T(1,128)}, u32[]{:S(2)}, u32[]{:S(2)}) async-start(f32[8,1,16384]{2,1,0:T(1,128)} %reshape.923), calls=%async_computation.1 | async-start | bytes 1048576 | tf_op jit(solution)/shard_map/all_to_all | solution.py:769
  1043.7 46.8 %collective-permute-start.64 = (bf16[8,64,512]{2,1,0:T(8,128)(2,1)}, bf16[8,64,512]{2,1,0:T(8,128)(2,1)}, u32[]{:S(2)}, u32[]{:S(2)}) collective-permute-start(bf16[8,64,512]{2,1,0:T(8,128)(2,1)} %get-tuple-element.204), channel_id=1, source_target_pairs={{0,16},{8,24},{16,0},{24,8},{1,17},{9,25},{17,1},{25,9},{2,18},{10... | collective-permute-start | bytes 1572872 | tf_op jit(solution)/shard_map/ppermute | solution.py:409
  1123.6 46.6 %collective-permute-start.80 = (bf16[4,64,1408]{2,1,0:T(8,128)(2,1)S(1)}, bf16[4,64,1408]{2,1,0:T(8,128)(2,1)S(1)}, u32[]{:S(2)}, u32[]{:S(2)}) collective-permute-start(bf16[4,64,1408]{2,1,0:T(8,128)(2,1)S(1)} %get-tuple-element.174), channel_id=1, source_target_pairs={{0,16},{8,24},{16,0},{24,8},{1,17},{9,25},{17,1},{25,9},{2,18},{10... | collective-permute-start | bytes 2162696 | tf_op jit(solution)/shard_map/ppermute | solution.py:409
  1125.4 91.2 %collective-permute-start.81 = (bf16[4,64,1408]{2,1,0:T(8,128)(2,1)S(1)}, bf16[4,64,1408]{2,1,0:T(8,128)(2,1)S(1)}, u32[]{:S(2)}, u32[]{:S(2)}) collective-permute-start(bf16[4,64,1408]{2,1,0:T(8,128)(2,1)S(1)} %get-tuple-element.173), channel_id=1, source_target_pairs={{0,8},{8,16},{16,24},{24,0},{1,9},{9,17},{17,25},{25,1},{2,10},{10... | collective-permute-start | bytes 2162696 | tf_op jit(solution)/shard_map/ppermute | solution.py:409
  1130.8 102.1 %collective-permute-start.84 = (bf16[4,64,1408]{2,1,0:T(8,128)(2,1)S(1)}, bf16[4,64,1408]{2,1,0:T(8,128)(2,1)S(1)}, u32[]{:S(2)}, u32[]{:S(2)}) collective-permute-start(bf16[4,64,1408]{2,1,0:T(8,128)(2,1)S(1)} %get-tuple-element.172), channel_id=1, source_target_pairs={{0,24},{8,0},{16,8},{24,16},{1,25},{9,1},{17,9},{25,17},{2,26},{10... | collective-permute-start | bytes 2162696 | tf_op jit(solution)/shard_map/ppermute | solution.py:409
  1132.7 130.2 %collective-permute-start.85 = (bf16[4,64,1408]{2,1,0:T(8,128)(2,1)S(1)}, bf16[4,64,1408]{2,1,0:T(8,128)(2,1)S(1)}, u32[]{:S(2)}, u32[]{:S(2)}) collective-permute-start(bf16[4,64,1408]{2,1,0:T(8,128)(2,1)S(1)} %get-tuple-element.171), channel_id=1, source_target_pairs={{0,16},{8,24},{16,0},{24,8},{1,17},{9,25},{17,1},{25,9},{2,18},{10... | collective-permute-start | bytes 2162696 | tf_op jit(solution)/shard_map/ppermute | solution.py:409
  1140.2 138.1 %collective-permute-start.86 = (bf16[4,64,1408]{2,1,0:T(8,128)(2,1)S(1)}, bf16[4,64,1408]{2,1,0:T(8,128)(2,1)S(1)}, u32[]{:S(2)}, u32[]{:S(2)}) collective-permute-start(bf16[4,64,1408]{2,1,0:T(8,128)(2,1)S(1)} %get-tuple-element.170), channel_id=1, source_target_pairs={{0,8},{8,16},{16,24},{24,0},{1,9},{9,17},{17,25},{25,1},{2,10},{10... | collective-permute-start | bytes 2162696 | tf_op jit(solution)/shard_map/ppermute | solution.py:409
  1170.3 124.5 %collective-permute-start.89 = (bf16[4,64,1408]{2,1,0:T(8,128)(2,1)S(1)}, bf16[4,64,1408]{2,1,0:T(8,128)(2,1)S(1)}, u32[]{:S(2)}, u32[]{:S(2)}) collective-permute-start(bf16[4,64,1408]{2,1,0:T(8,128)(2,1)S(1)} %get-tuple-element.169), channel_id=1, source_target_pairs={{0,24},{8,0},{16,8},{24,16},{1,25},{9,1},{17,9},{25,17},{2,26},{10... | collective-permute-start | bytes 2162696 | tf_op jit(solution)/shard_map/ppermute | solution.py:409
  1216.6 78.2 %collective-permute-start.90 = (bf16[4,64,1408]{2,1,0:T(8,128)(2,1)S(1)}, bf16[4,64,1408]{2,1,0:T(8,128)(2,1)S(1)}, u32[]{:S(2)}, u32[]{:S(2)}) collective-permute-start(bf16[4,64,1408]{2,1,0:T(8,128)(2,1)S(1)} %get-tuple-element.168), channel_id=1, source_target_pairs={{0,16},{8,24},{16,0},{24,8},{1,17},{9,25},{17,1},{25,9},{2,18},{10... | collective-permute-start | bytes 2162696 | tf_op jit(solution)/shard_map/ppermute | solution.py:409
  1232.9 76.3 %collective-permute-start.91 = (bf16[4,64,1408]{2,1,0:T(8,128)(2,1)S(1)}, bf16[4,64,1408]{2,1,0:T(8,128)(2,1)S(1)}, u32[]{:S(2)}, u32[]{:S(2)}) collective-permute-start(bf16[4,64,1408]{2,1,0:T(8,128)(2,1)S(1)} %get-tuple-element.167), channel_id=1, source_target_pairs={{0,8},{8,16},{16,24},{24,0},{1,9},{9,17},{17,25},{25,1},{2,10},{10... | collective-permute-start | bytes 2162696 | tf_op jit(solution)/shard_map/ppermute | solution.py:409
  1262.9 151.7 %collective-permute-start.82 = (bf16[2,256,1408]{2,1,0:T(8,128)(2,1)}, bf16[2,256,1408]{2,1,0:T(8,128)(2,1)}, u32[]{:S(2)}, u32[]{:S(2)}) collective-permute-start(bf16[2,256,1408]{2,1,0:T(8,128)(2,1)} %dynamic-slice_bitcast_fusion.2), channel_id=1, source_target_pairs={{0,1},{1,0},{2,3},{3,2},{4,5},{5,4},{6,7},{7,6},{8,9},{9,8},{10,11... | collective-permute-start | bytes 4325384 | tf_op jit(solution)/shard_map/ppermute | solution.py:418
  1342.9 76.3 %collective-permute-start.87 = (bf16[2,256,1408]{2,1,0:T(8,128)(2,1)}, bf16[2,256,1408]{2,1,0:T(8,128)(2,1)}, u32[]{:S(2)}, u32[]{:S(2)}) collective-permute-start(bf16[2,256,1408]{2,1,0:T(8,128)(2,1)} %dynamic-slice_bitcast_fusion.1), channel_id=1, source_target_pairs={{0,1},{1,0},{2,3},{3,2},{4,5},{5,4},{6,7},{7,6},{8,9},{9,8},{10,11... | collective-permute-start | bytes 4325384 | tf_op jit(solution)/shard_map/ppermute | solution.py:418
  1347.0 48.0 %collective-permute-start.75 = (bf16[64,704]{1,0:T(8,128)(2,1)}, bf16[64,704]{1,0:T(8,128)(2,1)}, u32[]{:S(2)}, u32[]{:S(2)}) collective-permute-start(bf16[64,704]{1,0:T(8,128)(2,1)} %get-tuple-element.261), channel_id=1, source_target_pairs={{0,24},{8,0},{16,8},{24,16},{1,25},{9,1},{17,9},{25,17},{2,26},{10... | collective-permute-start | bytes 270344 | tf_op jit(solution)/shard_map/ppermute | solution.py:409
  1350.9 46.0 %collective-permute-start.76 = (bf16[64,704]{1,0:T(8,128)(2,1)}, bf16[64,704]{1,0:T(8,128)(2,1)}, u32[]{:S(2)}, u32[]{:S(2)}) collective-permute-start(bf16[64,704]{1,0:T(8,128)(2,1)} %get-tuple-element.260), channel_id=1, source_target_pairs={{0,16},{8,24},{16,0},{24,8},{1,17},{9,25},{17,1},{25,9},{2,18},{10... | collective-permute-start | bytes 270344 | tf_op jit(solution)/shard_map/ppermute | solution.py:409
  (307 other events, 5653.8 us)
Sparse Core Ops, SparseCore 0:
  85.2 47.0 all-gather.11
  154.7 35.6 all-gather.7
  201.9 38.5 all-gather.9
  270.3 32.9 all-gather.5
  685.4 78.1 reduce-scatter.3
  767.2 46.8 reduce-scatter.5
  817.4 48.4 reduce-scatter.7

commit v3 on v2

--- a/solution.py
+++ b/solution.py
@@ -147,54 +147,66 @@
     )(block)
 
 
-def plane_sum(blocks, n_dp, n_ex, collective_id):
+def plane_sum(arrays, n_dp, n_ex, collective_id):
     chips = n_ex // 2
-    rows, cols = blocks.shape[1:]
-
-    def kernel(x_ref, o_ref, from_sib, out_buf, from_far, send, recv, sib_send, sib_recv):
+    count = len(arrays)
+
+    def kernel(*refs):
+        x_refs, o_refs = refs[:count], refs[count : 2 * count]
+        bufs = refs[2 * count : 5 * count]
+        sems = refs[5 * count :]
         z, e, c, k, sibling, same_core, _ = places(n_dp, n_ex)
         greet(same_core + [sibling])
-        near = []
+        near, far = {}, {}
         for i in list(range(1, chips)) + [0]:
             chip = lax.rem(c + i, chips)
-            copy = remote(
-                x_ref.at[chip * 2 + 1 - k],
-                from_sib.at[chip],
-                sib_send.at[i],
-                sib_recv.at[i],
-                sibling,
-            )
-            copy.start()
-            near.append(copy)
-        far = []
+            for j in range(count):
+                near[i, j] = remote(
+                    x_refs[j].at[chip * 2 + 1 - k],
+                    bufs[3 * j].at[chip],
+                    sems[4 * j].at[i],
+                    sems[4 * j + 1].at[i],
+                    sibling,
+                )
+                near[i, j].start()
         for i in range(1, chips):
             chip = lax.rem(c + i, chips)
-            near[i - 1].wait_recv()
-            out_buf[i] = (
-                x_ref[chip * 2 + k].astype(F32) + from_sib[chip].astype(F32)
-            ).astype(BF)
-            copy = remote(out_buf.at[i], from_far.at[i], send.at[i], recv.at[i], same_core[i - 1])
-            copy.start()
-            far.append(copy)
-        near[chips - 1].wait_recv()
-        o_ref[...] = x_ref[e].astype(F32) + from_sib[c].astype(F32)
+            for j in range(count):
+                from_sib, out_buf, from_far = bufs[3 * j : 3 * j + 3]
+                near[i, j].wait_recv()
+                out_buf[i] = (
+                    x_refs[j][chip * 2 + k].astype(F32) + from_sib[chip].astype(F32)
+                ).astype(BF)
+                far[i, j] = remote(
+                    out_buf.at[i],
+                    from_far.at[i],
+                    sems[4 * j + 2].at[i],
+                    sems[4 * j + 3].at[i],
+                    same_core[i - 1],
+                )
+                far[i, j].start()
+        for j in range(count):
+            near[0, j].wait_recv()
+            o_refs[j][...] = x_refs[j][e].astype(F32) + bufs[3 * j][c].astype(F32)
         for i in range(1, chips):
-            far[i - 1].wait_recv()
-            o_ref[...] += from_far[i].astype(F32)
-        for copy in near:
+            for j in range(count):
+                far[i, j].wait_recv()
+                o_refs[j][...] += bufs[3 * j + 2][i].astype(F32)
+        for copy in list(near.values()) + list(far.values()):
             copy.wait_send()
-        for copy in far:
-            copy.wait_send()
-
+
+    scratch = []
+    for array in arrays:
+        scratch += [pltpu.VMEM((chips,) + array.shape[1:], BF)] * 3
+    scratch += [pltpu.SemaphoreType.DMA((chips,))] * (4 * count)
     return pl.pallas_call(
         kernel,
-        out_shape=jax.ShapeDtypeStruct((rows, cols), F32),
-        in_specs=[VMEM],
-        out_specs=VMEM,
-        scratch_shapes=[pltpu.VMEM((chips, rows, cols), BF)] * 3
-        + [pltpu.SemaphoreType.DMA((chips,))] * 4,
+        out_shape=[jax.ShapeDtypeStruct(array.shape[1:], F32) for array in arrays],
+        in_specs=[VMEM] * count,
+        out_specs=[VMEM] * count,
+        scratch_shapes=scratch,
         compiler_params=params(collective_id),
-    )(blocks)
+    )(*arrays)
 
 
 def column_gather(block, n_dp, n_ex, collective_id):
@@ -420,27 +432,39 @@
     def pick(values, index, axis=0):
         return lax.dynamic_index_in_dim(values, index, axis, keepdims=False)
 
-    def expert_half(weight, held):
-        two = weight.reshape(-1, 2, half, ff_e)
-        experts = jnp.concatenate([pick(two, core, 1), swap(pick(two, 1 - core, 1))], axis=0)
-        experts = experts.reshape(per_chip, n_ex // 2, r, splits, ff_part)
-        experts, _ = lax.optimization_barrier((experts, held))
-
-        def block_for(index):
-            expert = lax.rem(index // splits + per_chip - core * (per_chip // 2), per_chip)
-            return pick(pick(experts, expert), lax.rem(index, splits), 2)
-
-        own = jnp.zeros((n_ex // 2, n_dp, r, ff_part), BF)
-        for i in range(n_dp):
-            block = block_for(after(i))
-            block = shift(block, i) if i else block
-            own = lax.dynamic_update_index_in_dim(own, block, before(i), 1)
-        own = own.reshape(width // 2, ff_part)
-        return own, swap(own)
-
-    gate_w = expert_half(expert_gate, pk_all)
-    up_w = expert_half(expert_up, pk_all)
-    down_w = expert_half(expert_down, pk_all)
+    def shared_blocks(index):
+        return jnp.stack([pick(w, index) for w in shared_cut])
+
+    shared_cut = [
+        w.reshape(r, n_dp, ff_s).transpose(1, 0, 2) for w in (shared_gate, shared_up, shared_down)
+    ]
+    shared_cut, _ = lax.optimization_barrier((shared_cut, pk_all))
+    shared_mine = jnp.zeros((3, n_dp, r, ff_s), BF)
+    for i in range(n_dp):
+        block = shared_blocks(after(i))
+        block = shift(block, i) if i else block
+        shared_mine = lax.dynamic_update_index_in_dim(shared_mine, block, before(i), 1)
+    sgate, sup, sdown = (
+        lax.all_gather(shared_mine[i], "expert", axis=0, tiled=False).reshape(width, ff_s)
+        for i in range(3)
+    )
+
+    expert_w = [w.reshape(-1, 2, half, ff_e) for w in (expert_gate, expert_up, expert_down)]
+    kept = jnp.stack([pick(w, core, 1) for w in expert_w])
+    given = jnp.stack([pick(w, 1 - core, 1) for w in expert_w])
+    experts = jnp.concatenate([kept, swap(given)], axis=1)
+    experts = experts.reshape(3, per_chip, n_ex // 2, r, splits, ff_part)
+    experts, _ = lax.optimization_barrier((experts, pk_all))
+    own = jnp.zeros((3, n_ex // 2, n_dp, r, ff_part), BF)
+    for i in range(n_dp):
+        to = after(i)
+        expert = lax.rem(to // splits + per_chip - core * (per_chip // 2), per_chip)
+        block = pick(pick(experts, expert, 1), lax.rem(to, splits), 3)
+        block = shift(block, i) if i else block
+        own = lax.dynamic_update_index_in_dim(own, block, before(i), 2)
+    own = own.reshape(3, width // 2, ff_part)
+    other = swap(own)
+    gate_w, up_w, down_w = ((own[i], other[i]) for i in range(3))
     wo_send, _ = lax.optimization_barrier((w_out, pk_all))
     wo_col = lax.all_gather(wo_send, "dp", axis=0, tiled=False)
     wo_rows = lax.all_to_all(
@@ -452,21 +476,6 @@
         tiled=True,
     )
     wo_rows = wo_rows.transpose(1, 0, 2, 3).reshape(hp * DV, width)
-    shared_send = [
-        w.reshape(r, n_dp, ff_s).transpose(1, 0, 2) for w in (shared_gate, shared_up, shared_down)
-    ]
-    shared_send, _ = lax.optimization_barrier((shared_send, pk_all))
-
-    def shared_whole(weight):
-        mine = jnp.zeros((n_dp, r, ff_s), BF)
-        for i in range(n_dp):
-            block = pick(weight, after(i))
-            block = shift(block, i) if i else block
-            mine = lax.dynamic_update_index_in_dim(mine, block, before(i), 0)
-        return lax.all_gather(mine, "expert", axis=0, tiled=False).reshape(width, ff_s)
-
-    sgate, sup, sdown = (shared_whole(w) for w in shared_send)
-
     def to_owner_order(values):
         cut = values.reshape(values.shape[0], n_dp, n_ex, r)
         return cut.transpose(0, 2, 1, 3).reshape(values.shape)
@@ -503,13 +512,10 @@
     cot_send, _ = lax.optimization_barrier((to_owner_order(cotangent), pk_all))
     cot_col = column(cot_send)
 
-    def halves(values):
+    def turned(values):
         first, second = values[:, : width // 2], values[:, width // 2 :]
-        return jnp.where(core == 0, first, second), jnp.where(core == 0, second, first)
-
-    def whole(own, other):
         return jnp.concatenate(
-            [jnp.where(core == 0, own, other), jnp.where(core == 0, other, own)], axis=1
+            [jnp.where(core == 0, first, second), jnp.where(core == 0, second, first)], axis=1
         )
 
     def between(values):
@@ -520,8 +526,8 @@
             got.append(lax.ppermute(cut[m], "expert", perm))
         return jnp.concatenate(got, axis=0)
 
-    cot_halves = halves(cot_col)
-    grad_in = [between(mm(hot, part).astype(BF)) for part in cot_halves]
+    cot_turned = turned(cot_col)
+    grad_in = between(mm(hot, cot_turned).astype(BF))
 
     tok_plane = tok_all.reshape(seq, width)
     hidden_one = rms_norm(tok_plane.astype(F32), gain_one).astype(BF)
@@ -561,15 +567,14 @@
     attended = jnp.concatenate(attended, axis=1)
     out_part = mm(attended, wo_rows).astype(BF)
     tokens_f = tokens.astype(F32)
-    residual = tokens_f + plane_sum(out_part.reshape(n_ex, rows, width), n_dp, n_ex, 2)
+    residual = tokens_f + plane_sum([out_part.reshape(n_ex, rows, width)], n_dp, n_ex, 2)[0]
     normed_two, norm_two_back = jax.vjp(rms_norm, residual, gain_two)
     hidden_two = normed_two.astype(BF)
     x_col = column_gather(to_owner_order(hidden_two), n_dp, n_ex, 3).reshape(n_dp * rows, width)
 
-    x_halves = halves(x_col)
-    x_in = [between(mm(hot, part).astype(BF)) for part in x_halves]
+    x_in = between(mm(hot, turned(x_col)).astype(BF))
     router_owner = to_owner_order(router.T).T
-    router_halves = [part.T for part in halves(router_owner.T)]
+    router_turned = turned(router_owner.T).T
 
     def probs_of(logits):
         top = jnp.max(logits, axis=-1, keepdims=True)
@@ -590,43 +595,41 @@
     shared_dx = mm_cols(grad_sa, sgate) + mm_cols(grad_sb, sup)
 
     expert_id = chip * per_chip + my_local
-    slot_probs = probs_of(mm(x_in[0], router_halves[0]) + mm(x_in[1], router_halves[1]))
+    slot_probs = probs_of(mm(x_in, router_turned))
     slot_gate = jnp.sum(
         jnp.where(jnp.arange(n_experts)[None, :] == expert_id, slot_probs, 0.0),
         axis=1,
         keepdims=True,
     )
-    expert_a = mm(x_in[0], gate_w[0]) + mm(x_in[1], gate_w[1])
-    expert_b = mm(x_in[0], up_w[0]) + mm(x_in[1], up_w[1])
+    mid = width // 2
+
+    def into(values, weight):
+        return mm(values[:, :mid], weight[0]) + mm(values[:, mid:], weight[1])
+
+    expert_a = into(x_in, gate_w)
+    expert_b = into(x_in, up_w)
     expert_hidden, expert_back = jax.vjp(swiglu, expert_a, expert_b)
     expert_hidden = expert_hidden.astype(BF)
-    rows_back = [between(mm_cols(expert_hidden, w).astype(BF)) for w in down_w]
-    slot_grad = [(slot_gate * part.astype(F32)).astype(BF) for part in grad_in]
-    grad_hidden = mm(slot_grad[0], down_w[0]) + mm(slot_grad[1], down_w[1])
+    rows_back = between(
+        jnp.concatenate([mm_cols(expert_hidden, w).astype(BF) for w in down_w], axis=1)
+    )
+    slot_grad = (slot_gate * grad_in.astype(F32)).astype(BF)
+    grad_hidden = into(slot_grad, down_w)
     grad_ea, grad_eb = (v.astype(BF) for v in expert_back(grad_hidden))
-    dx_back = [
-        between((mm_cols(grad_ea, gw) + mm_cols(grad_eb, uw)).astype(BF))
-        for gw, uw in zip(gate_w, up_w)
-    ]
-
-    def expert_sum(left, right):
-        own, other = (mm_rows(a, b) for a, b in zip(left, right))
-        got = swap(other.astype(BF))
-        total = (own + got.astype(F32)).astype(BF).reshape(n_ex // 2, n_dp, r, ff_part)
-        back = jnp.zeros((n_dp, n_ex // 2, r, ff_part), BF)
-        for i in range(n_dp):
-            block = pick(total, before(i), 1)
-            block = shift(block, -i) if i else block
-            back = lax.dynamic_update_index_in_dim(back, block, after(i), 0)
-        back = back.reshape(2, per_chip // 2, splits, half, ff_part).transpose(0, 1, 3, 2, 4)
-        back = back.reshape(2, per_chip // 2, half, ff_e)
-        keep, got = pick(back, core), swap(pick(back, 1 - core))
-        halves_of = [jnp.where(core == 0, keep, got), jnp.where(core == 0, got, keep)]
-        return jnp.concatenate(halves_of, axis=1).astype(F32)
-
-    sum_egate = expert_sum(x_in, (grad_ea, grad_ea))
-    sum_eup = expert_sum(x_in, (grad_eb, grad_eb))
-    sum_edown = expert_sum(slot_grad, (expert_hidden, expert_hidden))
+    dx_back = between(
+        jnp.concatenate(
+            [
+                (mm_cols(grad_ea, gw) + mm_cols(grad_eb, uw)).astype(BF)
+                for gw, uw in zip(gate_w, up_w)
+            ],
+            axis=1,
+        )
+    )
+    sides = [(x_in, grad_ea), (x_in, grad_eb), (slot_grad, expert_hidden)]
+    kept = jnp.stack([mm_rows(a[:, :mid], b).astype(BF) for a, b in sides])
+    given = jnp.stack([mm_rows(a[:, mid:], b).astype(BF) for a, b in sides])
+    expert_total = (kept.astype(F32) + swap(given).astype(F32)).astype(BF)
+    expert_total = expert_total.reshape(3, n_ex // 2, n_dp, r, ff_part)
 
     col_probs = probs_of(mm(x_col, router_owner))
     expert_axis = jnp.arange(n_experts)[None, :]
@@ -638,13 +641,13 @@
         [hot_t[:, m * per_far : (m + 1) * per_far] * gates[m].astype(BF) for m in range(chips)],
         axis=1,
     )
-    out_col = (whole(*(mm(gate_hot, part) for part in rows_back)) + shared_out).astype(BF)
-    dots = sum(mm_cols(a, b) for a, b in zip(cot_halves, rows_back)) * hot_t.astype(F32)
+    out_col = (turned(mm(gate_hot, rows_back)) + shared_out).astype(BF)
+    dots = mm_cols(cot_turned, rows_back) * hot_t.astype(F32)
     dots = jnp.sum(dots.reshape(n_dp * rows, chips, per_far), axis=-1)
     grad_probs_col = sum(
         jnp.where(expert_axis == far_experts[m], dots[:, m : m + 1], 0.0) for m in range(chips)
     )
-    dx_col = whole(*(mm(hot_t, part) for part in dx_back)) + shared_dx
+    dx_col = turned(mm(hot_t, dx_back)) + shared_dx
     dx_send = jnp.concatenate(
         [dx_col, grad_probs_col, jnp.zeros((n_dp * rows, 128 - n_experts), F32)], axis=1
     ).astype(BF)
@@ -667,7 +670,13 @@
     grad_resid_norm, grad_gain_two = norm_two_back(grad_hidden_two)
     grad_residual = cotangent.astype(F32) + grad_resid_norm
 
-    grad_attn = plane_gather(grad_residual.astype(BF), n_dp, n_ex, 4).reshape(seq, width)
+    grad_attn_low, expert_total = lax.optimization_barrier(
+        (grad_residual.astype(BF), expert_total)
+    )
+    grad_attn = plane_gather(grad_attn_low, n_dp, n_ex, 4).reshape(seq, width)
+    expert_far = [pick(expert_total, z, 2)]
+    for i in range(1, n_dp):
+        expert_far.append(shift(pick(expert_total, before(i), 2), -i))
     grad_attended = mm_cols(grad_attn, wo_rows).astype(BF)
     grad_wout = mm_rows(attended, grad_attn).astype(BF)
     grad_rope = 0.0
@@ -686,15 +695,17 @@
     (grad_query_raw,) = query_back(jnp.stack(grad_queries, axis=1))
     grad_query_low = grad_query_raw.reshape(seq, head_cols).astype(BF)
     grad_latent_part = jnp.concatenate([mm_cols(grad_expanded, wexp), grad_rope], axis=1)
-    grad_part = jnp.concatenate(
-        [
-            mm_cols(grad_query_low, wq).astype(BF),
-            grad_latent_part.astype(BF),
-            jnp.zeros((seq, -lat % 128), BF),
-        ],
-        axis=1,
-    )
-    grad_sum = plane_sum(grad_part.reshape(n_ex, rows, -1), n_dp, n_ex, 5)
+    grad_latent_part = jnp.pad(grad_latent_part, ((0, 0), (0, -lat % 128))).astype(BF)
+    grad_query_part = mm_cols(grad_query_low, wq).astype(BF)
+    (grad_query_part, grad_latent_part), expert_far[: n_dp // 2] = lax.optimization_barrier(
+        ((grad_query_part, grad_latent_part), expert_far[: n_dp // 2])
+    )
+    grad_query_sum, grad_latent_sum = plane_sum(
+        [grad_query_part.reshape(n_ex, rows, width), grad_latent_part.reshape(n_ex, rows, -1)],
+        n_dp,
+        n_ex,
+        5,
+    )
     own_start = e * rows
     latent_own = lax.dynamic_slice_in_dim(latent_raw, own_start, rows, 0)
     cos_own = lax.dynamic_slice_in_dim(cos_table, own_start, rows, 0)
@@ -708,11 +719,11 @@
 
     _, latent_back = jax.vjp(make_latent, latent_own, gain_lat)
     grad_latent_raw, grad_gain_lat = latent_back(
-        (grad_sum[:, width : width + KVR], grad_sum[:, width + KVR : width + lat])
+        (grad_latent_sum[:, :KVR], grad_latent_sum[:, KVR:lat])
     )
     grad_latent_low = grad_latent_raw.astype(BF)
     _, norm_one_back = jax.vjp(rms_norm, tokens_f, gain_one)
-    grad_hidden_one = grad_sum[:, :width] + mm_cols(grad_latent_low, w_lat)
+    grad_hidden_one = grad_query_sum + mm_cols(grad_latent_low, w_lat)
     grad_tokens_norm, grad_gain_one = norm_one_back(grad_hidden_one)
     grad_tokens = grad_residual + grad_tokens_norm
 
@@ -731,18 +742,35 @@
         tiled=True,
     )
     sum_wout = column_sum(wout_back.reshape(n_dp, r, width))
-    def shared_sum(grad):
-        grad = lax.psum_scatter(
-            grad.reshape(n_ex, n_dp, r, ff_s), "expert", scatter_dimension=0, tiled=True
-        ).reshape(n_dp, r, ff_s)
-        back = jnp.zeros((n_dp, r, ff_s), BF)
-        for i in range(n_dp):
-            block = pick(grad, before(i))
-            block = shift(block, -i) if i else block
-            back = lax.dynamic_update_index_in_dim(back, block, after(i), 0)
-        return back.transpose(1, 0, 2).reshape(r, n_dp * ff_s).astype(F32)
-
-    sum_sgate, sum_sup, sum_sdown = (shared_sum(grad) for grad in shared_grads)
+    def in_order(blocks):
+        stacked = jnp.stack(blocks)
+        return [pick(stacked, lax.rem(j + n_dp - z, n_dp)) for j in range(n_dp)]
+
+    shared_sums = jnp.stack(
+        [
+            lax.psum_scatter(
+                grad.reshape(n_ex, n_dp, r, ff_s), "expert", scatter_dimension=0, tiled=True
+            ).reshape(n_dp, r, ff_s)
+            for grad in shared_grads
+        ]
+    )
+    shared_far = [pick(shared_sums, z, 1)]
+    for i in range(1, n_dp):
+        shared_far.append(shift(pick(shared_sums, before(i), 1), -i))
+    shared_far = in_order(shared_far)
+    sum_sgate, sum_sup, sum_sdown = (
+        jnp.concatenate([part[i] for part in shared_far], axis=1).astype(F32) for i in range(3)
+    )
+    expert_all = jnp.stack(in_order(expert_far), axis=1)
+    expert_all = expert_all.reshape(3, 2, per_chip // 2, splits, half, ff_part)
+    expert_all = expert_all.transpose(0, 1, 2, 4, 3, 5).reshape(3, 2, per_chip // 2, half, ff_e)
+    keep, got = pick(expert_all, core, 1), swap(pick(expert_all, 1 - core, 1))
+    sum_egate, sum_eup, sum_edown = (
+        jnp.concatenate(
+            [jnp.where(core == 0, keep[i], got[i]), jnp.where(core == 0, got[i], keep[i])], axis=1
+        ).astype(F32)
+        for i in range(3)
+    )
     grad_wq = mm_rows(hidden_one, grad_query_low).astype(BF).reshape(n_dp, n_ex, r, head_cols)
     grad_we = mm_rows(latent_low, grad_expanded).astype(BF)
     grad_we = grad_we.reshape(n_dp, n_ex, r, rl * kv_cols // r)

time: 1450 us -> 1500 us (1.034)
  waiting for transfers between devices: 364 us -> 628 us
  local copies, waits for them, and re-layouts: 307 us -> 206 us
  starting transfers between devices: 165 us -> 75.1 us
  Pallas kernels: 264 us -> 212 us
  other arithmetic: 85.1 us -> 126 us
    ppermute x57 -> x33, waiting for transfers between devices: 288 us -> 485 us  [shift(): lax.ppermute(values, 'dp', [(i, (i + step) % n_dp) for i in range(n_dp)])]
    ppermute x24 -> x12, waiting for transfers between devices: 71 us -> 134 us  [between(): got.append(lax.ppermute(cut[m], 'expert', perm))]
    ppermute x57 -> x33, starting transfers between devices: 87.3 us -> 30.5 us  [shift(): lax.ppermute(values, 'dp', [(i, (i + step) % n_dp) for i in range(n_dp)])]
    dynamic_update_slice x48 -> x8, local copies, waits for them, and re-layouts: 66.6 us -> 15.8 us  [the longest x4 12.7 us: shards(): own = lax.dynamic_update_index_in_dim(own, block, before(i), 2)]
    pallas_call x1, Pallas kernels: 98 us -> 48.6 us  [column_gather(): pl.pallas_call(kernel, out_shape=jax.ShapeDtypeStruct((n_dp,) + block.sha...]
    ppermute x12 -> x4, starting transfers between devices: 44 us -> 5.04 us  [swap(): return lax.ppermute(values, 'expert', sib_perm)]
    another operation x3 -> x11, other arithmetic: 6.06 us -> 24.4 us
    dot_general x29 -> x24, matrix products: 99.4 us -> 86.4 us  [mm(): return jnp.dot(left, right, preferred_element_type=F32)]
  transfers between devices with their start and end apart: 102 -> 58, of which waited for: 37 -> 21; matrix products, arithmetic and copies ran while one was open for 40% -> 26% of each run, Pallas kernels for 14% -> 9%
where the time goes in v3:
time: 1500 us; the launch traced here: 1490 us
  waiting for transfers between devices  628 us (42%)
  Pallas kernels  212 us (14%)
  matrix products  210 us (14%)
  local copies, waits for them, and re-layouts  206 us (14%)
  other arithmetic  126 us (8%)
  starting transfers between devices  75.1 us (5%)
  between operations  18.1 us (1%)
    ppermute x33, waiting for transfers between devices, shift(): lax.ppermute(values, 'dp', [(i, (i + step) % n_dp) for i in range(n_dp)])  485 us
    ppermute x12, waiting for transfers between devices, between(): got.append(lax.ppermute(cut[m], 'expert', perm))  134 us
    dot_general x24, matrix products, mm(): return jnp.dot(left, right, preferred_element_type=F32)  86.4 us
    dot_general x19, matrix products, mm_cols(): lax.dot_general(left, right, (((1,), (1,)), ((), ())), preferred_element_...  67.5 us
    pallas_call x2, Pallas kernels, plane_sum(): pl.pallas_call(kernel, out_shape=[jax.ShapeDtypeStruct(array.shape[1:], F...  65.7 us
    pallas_call x1, Pallas kernels, first_exchange(): pl.pallas_call(kernel, out_shape=[jax.ShapeDtypeStruct((n_ex,) + tok.shap...  57.6 us
    dot_general x18, matrix products, mm_rows(): lax.dot_general(left, right, (((0,), (0,)), ((), ())), preferred_element_...  56.5 us
    unnamed x354, local copies, waits for them, and re-layouts  48.7 us
  transfers between devices with their start and end apart: 58, of which 21 were waited for; matrix products, arithmetic and copies ran while one was open for 26% of the time, Pallas kernels for 9%

profile of v3, /device:TPU:11, one launch (start us, length us, event | category | flops | bytes accessed | tf_op | source)
XLA Modules:
  0.0 1485.7 jit_solution(14638619597674294686)
XLA Ops:
  15.3 57.6 %shard_map.342 = (bf16[8,128,2048]{2,1,0:T(8,128)(2,1)}, bf16[4,8,64,512]{3,2,1,0:T(8,128)(2,1)S(1)}, bf16[4,8,64,640]{3,2,1,0:T(8,128)(2,1)S(1)}) custom-call(bf16[128,2048]{1,0:T(8,128)(2,1)S(1)} %copy-done, bf16[8,64,512]{2,1,0:T(8,128)(2,1)S(1)} %copy-done.7, bf16[64,640]{1,0:T(8,128)(2,1)S(1)} %concatenate.113.pk_ref), custom_call_target="tpu_custom_call" | custom-call | tf_op jit(solution)/shard_map/pallas_call | solution.py:316
  93.9 20.0 %collective-permute-done.14 = bf16[3,64,704]{2,0,1:T(4,128)(2,1)} collective-permute-done((bf16[3,64,704]{2,0,1:T(4,128)(2,1)}, bf16[3,64,704]{2,0,1:T(4,128)(2,1)}, u32[]{:S(2)}, u32[]{:S(2)}) %collective-permute-start.14) | collective-permute-done | bytes 270368 | tf_op jit(solution)/shard_map/ppermute | solution.py:421
  114.9 18.1 %collective-permute-done.15 = bf16[3,64,704]{2,0,1:T(4,128)(2,1)} collective-permute-done((bf16[3,64,704]{2,0,1:T(4,128)(2,1)}, bf16[3,64,704]{2,0,1:T(4,128)(2,1)}, u32[]{:S(2)}, u32[]{:S(2)}) %collective-permute-start.15) | collective-permute-done | bytes 270368 | tf_op jit(solution)/shard_map/ppermute | solution.py:421
  201.2 11.8 reduce-scatter.4.cloned.1.call-start
  213.1 6.1 fusion.18
  231.6 5.6 all_to_all.20
  238.6 28.5 %shard_map.343 = f32[128,2048]{1,0:T(8,128)S(1)} custom-call(bf16[8,128,2048]{2,1,0:T(8,128)(2,1)S(1)} %bitcast.396), custom_call_target="tpu_custom_call" | custom-call | tf_op jit(solution)/shard_map/pallas_call | solution.py:202
  269.1 48.6 %shard_map.344 = bf16[4,128,2048]{2,1,0:T(8,128)(2,1)S(1)} custom-call(bf16[128,2048]{1,0:T(8,128)(2,1)S(1)} %copy.444.x_ref), custom_call_target="tpu_custom_call" | custom-call | tf_op jit(solution)/shard_map/pallas_call | solution.py:227
  328.4 6.6 multiply_convert_fusion.5
  362.6 6.5 copy.467
  370.0 171.8 %collective-permute-done = s32[128,6]{1,0:T(8,128)S(1)} collective-permute-done((s32[128,6]{1,0:T(8,128)S(1)}, s32[128,6]{1,0:T(8,128)S(1)}, u32[]{:S(2)}, u32[]{:S(2)}) %collective-permute-start) | collective-permute-done | bytes 3104 | tf_op jit(solution)/shard_map/ppermute | solution.py:421
  589.1 4.9 convolution_convert_fusion.2
  605.6 19.8 %collective-permute-done.5 = bf16[256,2048]{1,0:T(8,128)(2,1)} collective-permute-done((bf16[256,2048]{1,0:T(8,128)(2,1)}, bf16[256,2048]{1,0:T(8,128)(2,1)}, u32[]{:S(2)}, u32[]{:S(2)}) %collective-permute-start.5) | collective-permute-done | bytes 1048608 | tf_op jit(solution)/shard_map/ppermute | solution.py:526
  625.6 26.4 %collective-permute-done.4 = bf16[256,2048]{1,0:T(8,128)(2,1)} collective-permute-done((bf16[256,2048]{1,0:T(8,128)(2,1)}, bf16[256,2048]{1,0:T(8,128)(2,1)}, u32[]{:S(2)}, u32[]{:S(2)}) %collective-permute-start.4) | collective-permute-done | bytes 1048608 | tf_op jit(solution)/shard_map/ppermute | solution.py:526
  658.7 15.8 %collective-permute-done.25 = bf16[256,2048]{1,0:T(8,128)(2,1)} collective-permute-done((bf16[256,2048]{1,0:T(8,128)(2,1)}, bf16[256,2048]{1,0:T(8,128)(2,1)}, u32[]{:S(2)}, u32[]{:S(2)}) %collective-permute-start.25) | collective-permute-done | bytes 1048608 | tf_op jit(solution)/shard_map/ppermute | solution.py:526
  674.6 23.8 %collective-permute-done.24 = bf16[256,2048]{1,0:T(8,128)(2,1)S(1)} collective-permute-done((bf16[256,2048]{1,0:T(8,128)(2,1)}, bf16[256,2048]{1,0:T(8,128)(2,1)S(1)}, u32[]{:S(2)}, u32[]{:S(2)}) %collective-permute-start.24) | collective-permute-done | bytes 1048608 | tf_op jit(solution)/shard_map/ppermute | solution.py:526
  698.4 7.9 multiply_convert_fusion
  712.2 6.1 reduce-scatter.8.cloned.1.call-done
  723.1 5.5 fusion.171
  728.6 16.7 %collective-permute-done.44 = bf16[3,64,704]{2,1,0:T(8,128)(2,1)S(1)} collective-permute-done((bf16[3,64,704]{2,1,0:T(8,128)(2,1)S(1)}, bf16[3,64,704]{2,1,0:T(8,128)(2,1)S(1)}, u32[]{:S(2)}, u32[]{:S(2)}) %collective-permute-start.44) | collective-permute-done | bytes 270368 | tf_op jit(solution)/shard_map/ppermute | solution.py:421
  755.6 6.0 fusion.33
  761.7 5.2 convolution_add_fusion
  766.9 5.4 fusion.32
  772.3 5.2 convolution_add_fusion.1
  777.5 7.0 fusion.30
  784.5 11.1 fusion.4
  795.6 7.2 convolution_convert_fusion.15
  813.7 4.8 fusion.23
  818.6 4.8 fusion.22
  830.9 5.7 fusion.43
  840.4 5.3 fusion.31
  845.7 5.5 add_convert_fusion.1
  863.3 23.7 %collective-permute-done.12 = bf16[256,2048]{0,1:T(8,128)(2,1)S(1)} collective-permute-done((bf16[256,2048]{0,1:T(8,128)(2,1)S(1)}, bf16[256,2048]{0,1:T(8,128)(2,1)S(1)}, u32[]{:S(2)}, u32[]{:S(2)}) %collective-permute-start.12) | collective-permute-done | bytes 1048608 | tf_op jit(solution)/shard_map/ppermute | solution.py:526
  910.4 20.9 %collective-permute-done.27 = bf16[256,2048]{0,1:T(8,128)(2,1)} collective-permute-done((bf16[256,2048]{0,1:T(8,128)(2,1)}, bf16[256,2048]{0,1:T(8,128)(2,1)}, u32[]{:S(2)}, u32[]{:S(2)}) %collective-permute-start.27) | collective-permute-done | bytes 1048608 | tf_op jit(solution)/shard_map/ppermute | solution.py:526
  931.3 5.0 fusion.7
  951.3 6.8 fusion.21
  958.1 50.2 %collective-permute-done.17 = bf16[128,2048]{1,0:T(8,128)(2,1)S(1)} collective-permute-done((bf16[128,2048]{1,0:T(8,128)(2,1)S(1)}, bf16[128,2048]{1,0:T(8,128)(2,1)S(1)}, u32[]{:S(2)}, u32[]{:S(2)}) %collective-permute-start.17) | collective-permute-done | bytes 524320 | tf_op jit(solution)/shard_map/ppermute | solution.py:421
  1029.8 6.2 add_convert_fusion
  1036.1 28.0 %shard_map.345 = bf16[8,128,2048]{2,1,0:T(8,128)(2,1)S(1)} custom-call(bf16[128,2048]{1,0:T(8,128)(2,1)S(1)} %fusion.168.x_ref), custom_call_target="tpu_custom_call" | custom-call | tf_op jit(solution)/shard_map/pallas_call | solution.py:140
  1101.6 5.3 all_to_all.21
  1109.6 190.7 %collective-permute-done.39 = bf16[8,64,512]{2,1,0:T(8,128)(2,1)S(1)} collective-permute-done((bf16[8,64,512]{2,1,0:T(8,128)(2,1)S(1)}, bf16[8,64,512]{2,1,0:T(8,128)(2,1)S(1)}, u32[]{:S(2)}, u32[]{:S(2)}) %collective-permute-start.39) | collective-permute-done | bytes 524320 | tf_op jit(solution)/shard_map/ppermute | solution.py:421
  1306.1 5.4 collective-permute-done.38
  1311.5 5.1 collective-permute-done.37
  1317.7 13.4 all-to-all-start.2
  1363.4 37.2 %shard_map.346 = (f32[128,2048]{1,0:T(8,128)S(1)}, f32[128,640]{1,0:T(8,128)S(1)}) custom-call(bf16[8,128,2048]{2,1,0:T(8,128)(2,1)} %bitcast.433, bf16[8,128,640]{2,1,0:T(8,128)(2,1)S(1)} %bitcast.403), custom_call_target="tpu_custom_call" | custom-call | tf_op jit(solution)/shard_map/pallas_call | solution.py:202
  1402.2 12.1 shard_map.347
  1429.4 5.1 all-to-all-start.1
  1434.5 5.6 fusion.187
  (733 shorter events, 465.5 us)
Async XLA Ops:
  7.2 224.4 %all-gather.12.cloned.1.call-start = ((), (), s32[]{:S(2)}) async-start(), calls=%async_computation.13 | async-start | bytes 1310720 | tf_op jit(solution)/shard_map/all_gather | solution.py:469
  74.2 243.5 %all-gather.6.cloned.1.call-start = ((), (), s32[]{:S(2)}) async-start(), calls=%async_computation.7 | async-start | bytes 3538944 | tf_op jit(solution)/shard_map/all_gather | solution.py:448
  86.5 27.4 %collective-permute-start.14 = (bf16[3,64,704]{2,0,1:T(4,128)(2,1)}, bf16[3,64,704]{2,0,1:T(4,128)(2,1)}, u32[]{:S(2)}, u32[]{:S(2)}) collective-permute-start(bf16[3,64,704]{2,0,1:T(4,128)(2,1)} %pad_maximum_fusion.25), channel_id=1, source_target_pairs={{0,8},{8,16},{16,24},{24,0},{1,9},{9,17},{17,25},{25,1},{2,10},{10... | collective-permute-start | bytes 811016 | tf_op jit(solution)/shard_map/ppermute | solution.py:421
  88.0 45.0 %collective-permute-start.15 = (bf16[3,64,704]{2,0,1:T(4,128)(2,1)}, bf16[3,64,704]{2,0,1:T(4,128)(2,1)}, u32[]{:S(2)}, u32[]{:S(2)}) collective-permute-start(bf16[3,64,704]{2,0,1:T(4,128)(2,1)} %pad_maximum_fusion.26), channel_id=1, source_target_pairs={{0,16},{8,24},{16,0},{24,8},{1,17},{9,25},{17,1},{25,9},{2,18},{10... | collective-permute-start | bytes 811016 | tf_op jit(solution)/shard_map/ppermute | solution.py:421
  91.5 43.6 %collective-permute-start.16 = (bf16[3,64,704]{2,0,1:T(4,128)(2,1)}, bf16[3,64,704]{2,0,1:T(4,128)(2,1)}, u32[]{:S(2)}, u32[]{:S(2)}) collective-permute-start(bf16[3,64,704]{2,0,1:T(4,128)(2,1)} %pad_maximum_fusion.27), channel_id=1, source_target_pairs={{0,24},{8,0},{16,8},{24,16},{1,25},{9,1},{17,9},{25,17},{2,26},{10... | collective-permute-start | bytes 811016 | tf_op jit(solution)/shard_map/ppermute | solution.py:421
  137.2 185.3 %all-gather.8.cloned.1.call-start = ((), (), s32[]{:S(2)}) async-start(), calls=%async_computation.8 | async-start | bytes 3538944 | tf_op jit(solution)/shard_map/all_gather | solution.py:448
  143.2 184.0 %collective-permute-start.22 = (bf16[128,2048]{1,0:T(8,128)(2,1)}, bf16[128,2048]{1,0:T(8,128)(2,1)}, u32[]{:S(2)}, u32[]{:S(2)}) collective-permute-start(bf16[128,2048]{1,0:T(8,128)(2,1)} %copy.459), channel_id=1, source_target_pairs={{0,24},{8,0},{16,8},{24,16},{1,25},{9,1},{17,9},{25,17},{2,26},{10... | collective-permute-start | bytes 1572872 | tf_op jit(solution)/shard_map/ppermute | solution.py:421
  143.2 185.2 %collective-permute-start.21 = (bf16[128,2048]{1,0:T(8,128)(2,1)}, bf16[128,2048]{1,0:T(8,128)(2,1)}, u32[]{:S(2)}, u32[]{:S(2)}) collective-permute-start(bf16[128,2048]{1,0:T(8,128)(2,1)} %copy.459), channel_id=1, source_target_pairs={{0,16},{8,24},{16,0},{24,8},{1,17},{9,25},{17,1},{25,9},{2,18},{10... | collective-permute-start | bytes 1572872 | tf_op jit(solution)/shard_map/ppermute | solution.py:421
  145.2 183.1 %collective-permute-start.20 = (bf16[128,2048]{1,0:T(8,128)(2,1)}, bf16[128,2048]{1,0:T(8,128)(2,1)}, u32[]{:S(2)}, u32[]{:S(2)}) collective-permute-start(bf16[128,2048]{1,0:T(8,128)(2,1)} %copy.459), channel_id=1, source_target_pairs={{0,8},{8,16},{16,24},{24,0},{1,9},{9,17},{17,25},{25,1},{2,10},{10... | collective-permute-start | bytes 1572872 | tf_op jit(solution)/shard_map/ppermute | solution.py:421
  156.3 189.2 %collective-permute-start.6 = (bf16[3,2,256,1408]{3,2,0,1:T(8,128)(2,1)}, bf16[3,2,256,1408]{3,2,0,1:T(8,128)(2,1)}, u32[]{:S(2)}, u32[]{:S(2)}) collective-permute-start(bf16[3,2,256,1408]{3,2,0,1:T(8,128)(2,1)} %pad_maximum_fusion.4), channel_id=1, source_target_pairs={{0,1},{1,0},{2,3},{3,2},{4,5},{5,4},{6,7},{7,6},{8,9},{9,8},{10,11... | collective-permute-start | bytes 12976136 | tf_op jit(solution)/shard_map/ppermute | solution.py:430
  158.6 203.7 %collective-permute-start.2 = (s32[128,6]{1,0:T(8,128)S(1)}, s32[128,6]{1,0:T(8,128)}, u32[]{:S(2)}, u32[]{:S(2)}) collective-permute-start(s32[128,6]{1,0:T(8,128)S(1)} %add_select_fusion), channel_id=1, source_target_pairs={{0,24},{8,0},{16,8},{24,16},{1,25},{9,1},{17,9},{25,17},{2,26},{10... | collective-permute-start | bytes 9224 | tf_op jit(solution)/shard_map/ppermute | solution.py:421
  165.1 163.3 %all-gather.10.cloned.1.call-start = ((), (), s32[]{:S(2)}) async-start(), calls=%async_computation.9 | async-start | bytes 3538944 | tf_op jit(solution)/shard_map/all_gather | solution.py:448
  201.2 508.9 %reduce-scatter.4.cloned.1.call-start = ((), (), s32[]{:S(2)}) async-start(), calls=%async_computation.10 | async-start | bytes 3538944 | tf_op jit(solution)/shard_map/reduce_scatter | solution.py:751
  327.2 42.8 %collective-permute-start.1 = (s32[128,6]{1,0:T(8,128)S(1)}, s32[128,6]{1,0:T(8,128)S(1)}, u32[]{:S(2)}, u32[]{:S(2)}) collective-permute-start(s32[128,6]{1,0:T(8,128)S(1)} %add_select_fusion), channel_id=1, source_target_pairs={{0,16},{8,24},{16,0},{24,8},{1,17},{9,25},{17,1},{25,9},{2,18},{10... | collective-permute-start | bytes 9224 | tf_op jit(solution)/shard_map/ppermute | solution.py:421
  343.7 367.5 %reduce-scatter.6.cloned.1.call-start = ((), (), s32[]{:S(2)}) async-start(), calls=%async_computation.11 | async-start | bytes 3538944 | tf_op jit(solution)/shard_map/reduce_scatter | solution.py:751
  355.9 201.6 %collective-permute-start.7 = (bf16[3,4,64,1408]{3,2,1,0:T(8,128)(2,1)}, bf16[3,4,64,1408]{3,2,1,0:T(8,128)(2,1)}, u32[]{:S(2)}, u32[]{:S(2)}) collective-permute-start(bf16[3,4,64,1408]{3,2,1,0:T(8,128)(2,1)} %get-tuple-element.204), channel_id=1, source_target_pairs={{0,8},{8,16},{16,24},{24,0},{1,9},{9,17},{17,25},{25,1},{2,10},{10... | collective-permute-start | bytes 6488072 | tf_op jit(solution)/shard_map/ppermute | solution.py:421
  358.5 202.2 %collective-permute-start.8 = (bf16[3,4,64,1408]{3,2,1,0:T(8,128)(2,1)}, bf16[3,4,64,1408]{3,2,1,0:T(8,128)(2,1)}, u32[]{:S(2)}, u32[]{:S(2)}) collective-permute-start(bf16[3,4,64,1408]{3,2,1,0:T(8,128)(2,1)} %get-tuple-element.203), channel_id=1, source_target_pairs={{0,16},{8,24},{16,0},{24,8},{1,17},{9,25},{17,1},{25,9},{2,18},{10... | collective-permute-start | bytes 6488072 | tf_op jit(solution)/shard_map/ppermute | solution.py:421
  359.9 204.0 %collective-permute-start.9 = (bf16[3,4,64,1408]{3,2,1,0:T(8,128)(2,1)}, bf16[3,4,64,1408]{3,2,1,0:T(8,128)(2,1)}, u32[]{:S(2)}, u32[]{:S(2)}) collective-permute-start(bf16[3,4,64,1408]{3,2,1,0:T(8,128)(2,1)} %get-tuple-element.202), channel_id=1, source_target_pairs={{0,24},{8,0},{16,8},{24,16},{1,25},{9,1},{17,9},{25,17},{2,26},{10... | collective-permute-start | bytes 6488072 | tf_op jit(solution)/shard_map/ppermute | solution.py:421
  362.3 179.5 %collective-permute-start = (s32[128,6]{1,0:T(8,128)S(1)}, s32[128,6]{1,0:T(8,128)S(1)}, u32[]{:S(2)}, u32[]{:S(2)}) collective-permute-start(s32[128,6]{1,0:T(8,128)S(1)} %add_select_fusion), channel_id=1, source_target_pairs={{0,8},{8,16},{16,24},{24,0},{1,9},{9,17},{17,25},{25,1},{2,10},{10... | collective-permute-start | bytes 9224 | tf_op jit(solution)/shard_map/ppermute | solution.py:421
  557.5 160.8 %reduce-scatter.8.cloned.1.call-start = ((), (), s32[]{:S(2)}) async-start(), calls=%async_computation.12 | async-start | bytes 3538944 | tf_op jit(solution)/shard_map/reduce_scatter | solution.py:751
  567.1 188.6 %collective-permute-start.10 = (bf16[3,1024,1408]{2,1,0:T(8,128)(2,1)}, bf16[3,1024,1408]{2,1,0:T(8,128)(2,1)}, u32[]{:S(2)}, u32[]{:S(2)}) collective-permute-start(bf16[3,1024,1408]{2,1,0:T(8,128)(2,1)} %bitcast.64), channel_id=1, source_target_pairs={{0,1},{1,0},{2,3},{3,2},{4,5},{5,4},{6,7},{7,6},{8,9},{9,8},{10,11... | collective-permute-start | bytes 25952264 | tf_op jit(solution)/shard_map/ppermute | solution.py:430
  596.3 29.1 %collective-permute-start.5 = (bf16[256,2048]{1,0:T(8,128)(2,1)}, bf16[256,2048]{1,0:T(8,128)(2,1)}, u32[]{:S(2)}, u32[]{:S(2)}) collective-permute-start(bf16[256,2048]{1,0:T(8,128)(2,1)} %get-tuple-element.222), channel_id=1, source_target_pairs={{0,6},{1,7},{2,4},{3,5},{4,2},{5,3},{6,0},{7,1},{8,14},{9,15},{10,... | collective-permute-start | bytes 3145736 | tf_op jit(solution)/shard_map/ppermute | solution.py:526
  597.5 54.6 %collective-permute-start.4 = (bf16[256,2048]{1,0:T(8,128)(2,1)}, bf16[256,2048]{1,0:T(8,128)(2,1)}, u32[]{:S(2)}, u32[]{:S(2)}) collective-permute-start(bf16[256,2048]{1,0:T(8,128)(2,1)} %get-tuple-element.223), channel_id=1, source_target_pairs={{0,4},{1,5},{2,6},{3,7},{4,0},{5,1},{6,2},{7,3},{8,12},{9,13},{10,... | collective-permute-start | bytes 3145736 | tf_op jit(solution)/shard_map/ppermute | solution.py:526
  597.8 55.2 %collective-permute-start.3 = (bf16[256,2048]{1,0:T(8,128)(2,1)}, bf16[256,2048]{1,0:T(8,128)(2,1)}, u32[]{:S(2)}, u32[]{:S(2)}) collective-permute-start(bf16[256,2048]{1,0:T(8,128)(2,1)} %get-tuple-element.224), channel_id=1, source_target_pairs={{0,2},{1,3},{2,0},{3,1},{4,6},{5,7},{6,4},{7,5},{8,10},{9,11},{10,... | collective-permute-start | bytes 3145736 | tf_op jit(solution)/shard_map/ppermute | solution.py:526
  601.2 73.4 %collective-permute-start.25 = (bf16[256,2048]{1,0:T(8,128)(2,1)}, bf16[256,2048]{1,0:T(8,128)(2,1)}, u32[]{:S(2)}, u32[]{:S(2)}) collective-permute-start(bf16[256,2048]{1,0:T(8,128)(2,1)} %get-tuple-element.212), channel_id=1, source_target_pairs={{0,6},{1,7},{2,4},{3,5},{4,2},{5,3},{6,0},{7,1},{8,14},{9,15},{10,... | collective-permute-start | bytes 3145736 | tf_op jit(solution)/shard_map/ppermute | solution.py:526
  625.4 73.0 %collective-permute-start.24 = (bf16[256,2048]{1,0:T(8,128)(2,1)}, bf16[256,2048]{1,0:T(8,128)(2,1)S(1)}, u32[]{:S(2)}, u32[]{:S(2)}) collective-permute-start(bf16[256,2048]{1,0:T(8,128)(2,1)} %get-tuple-element.213), channel_id=1, source_target_pairs={{0,4},{1,5},{2,6},{3,7},{4,0},{5,1},{6,2},{7,3},{8,12},{9,13},{10,... | collective-permute-start | bytes 3145736 | tf_op jit(solution)/shard_map/ppermute | solution.py:526
  652.1 46.3 %collective-permute-start.23 = (bf16[256,2048]{1,0:T(8,128)(2,1)}, bf16[256,2048]{1,0:T(8,128)(2,1)S(1)}, u32[]{:S(2)}, u32[]{:S(2)}) collective-permute-start(bf16[256,2048]{1,0:T(8,128)(2,1)} %get-tuple-element.214), channel_id=1, source_target_pairs={{0,2},{1,3},{2,0},{3,1},{4,6},{5,7},{6,4},{7,5},{8,10},{9,11},{10,... | collective-permute-start | bytes 3145736 | tf_op jit(solution)/shard_map/ppermute | solution.py:526
  838.9 48.1 %collective-permute-start.12 = (bf16[256,2048]{0,1:T(8,128)(2,1)S(1)}, bf16[256,2048]{0,1:T(8,128)(2,1)S(1)}, u32[]{:S(2)}, u32[]{:S(2)}) collective-permute-start(bf16[256,2048]{0,1:T(8,128)(2,1)S(1)} %get-tuple-element.220), channel_id=1, source_target_pairs={{0,4},{1,5},{2,6},{3,7},{4,0},{5,1},{6,2},{7,3},{8,12},{9,13},{10,... | collective-permute-start | bytes 3145736 | tf_op jit(solution)/shard_map/ppermute | solution.py:526
  839.3 48.5 %collective-permute-start.11 = (bf16[256,2048]{0,1:T(8,128)(2,1)S(1)}, bf16[256,2048]{0,1:T(8,128)(2,1)S(1)}, u32[]{:S(2)}, u32[]{:S(2)}) collective-permute-start(bf16[256,2048]{0,1:T(8,128)(2,1)S(1)} %get-tuple-element.218), channel_id=1, source_target_pairs={{0,2},{1,3},{2,0},{3,1},{4,6},{5,7},{6,4},{7,5},{8,10},{9,11},{10,... | collective-permute-start | bytes 3145736 | tf_op jit(solution)/shard_map/ppermute | solution.py:526
  853.7 55.4 %collective-permute-start.28 = (bf16[256,2048]{0,1:T(8,128)(2,1)}, bf16[256,2048]{0,1:T(8,128)(2,1)}, u32[]{:S(2)}, u32[]{:S(2)}) collective-permute-start(bf16[256,2048]{0,1:T(8,128)(2,1)} %get-tuple-element.209), channel_id=1, source_target_pairs={{0,6},{1,7},{2,4},{3,5},{4,2},{5,3},{6,0},{7,1},{8,14},{9,15},{10,... | collective-permute-start | bytes 3145736 | tf_op jit(solution)/shard_map/ppermute | solution.py:526
  854.9 76.3 %collective-permute-start.27 = (bf16[256,2048]{0,1:T(8,128)(2,1)}, bf16[256,2048]{0,1:T(8,128)(2,1)}, u32[]{:S(2)}, u32[]{:S(2)}) collective-permute-start(bf16[256,2048]{0,1:T(8,128)(2,1)} %get-tuple-element.210), channel_id=1, source_target_pairs={{0,4},{1,5},{2,6},{3,7},{4,0},{5,1},{6,2},{7,3},{8,12},{9,13},{10,... | collective-permute-start | bytes 3145736 | tf_op jit(solution)/shard_map/ppermute | solution.py:526
  863.0 68.3 %collective-permute-start.26 = (bf16[256,2048]{0,1:T(8,128)(2,1)}, bf16[256,2048]{0,1:T(8,128)(2,1)}, u32[]{:S(2)}, u32[]{:S(2)}) collective-permute-start(bf16[256,2048]{0,1:T(8,128)(2,1)} %get-tuple-element.208), channel_id=1, source_target_pairs={{0,2},{1,3},{2,0},{3,1},{4,6},{5,7},{6,4},{7,5},{8,10},{9,11},{10,... | collective-permute-start | bytes 3145736 | tf_op jit(solution)/shard_map/ppermute | solution.py:526
  887.0 141.3 %collective-permute-start.32 = (bf16[3,1024,1408]{2,1,0:T(8,128)(2,1)}, bf16[3,1024,1408]{2,1,0:T(8,128)(2,1)}, u32[]{:S(2)}, u32[]{:S(2)}) collective-permute-start(bf16[3,1024,1408]{2,1,0:T(8,128)(2,1)} %pad_maximum_fusion.1), channel_id=1, source_target_pairs={{0,1},{1,0},{2,3},{3,2},{4,5},{5,4},{6,7},{7,6},{8,9},{9,8},{10,11... | collective-permute-start | bytes 25952264 | tf_op jit(solution)/shard_map/ppermute | solution.py:430
  909.1 38.7 %collective-permute-start.19 = (bf16[128,2048]{1,0:T(8,128)(2,1)}, bf16[128,2048]{1,0:T(8,128)(2,1)S(1)}, u32[]{:S(2)}, u32[]{:S(2)}) collective-permute-start(bf16[128,2048]{1,0:T(8,128)(2,1)} %get-tuple-element.247), channel_id=1, source_target_pairs={{0,8},{8,16},{16,24},{24,0},{1,9},{9,17},{17,25},{25,1},{2,10},{10... | collective-permute-start | bytes 1572872 | tf_op jit(solution)/shard_map/ppermute | solution.py:421
  909.1 40.2 %collective-permute-start.18 = (bf16[128,2048]{1,0:T(8,128)(2,1)}, bf16[128,2048]{1,0:T(8,128)(2,1)}, u32[]{:S(2)}, u32[]{:S(2)}) collective-permute-start(bf16[128,2048]{1,0:T(8,128)(2,1)} %get-tuple-element.248), channel_id=1, source_target_pairs={{0,16},{8,24},{16,0},{24,8},{1,17},{9,25},{17,1},{25,9},{2,18},{10... | collective-permute-start | bytes 1572872 | tf_op jit(solution)/shard_map/ppermute | solution.py:421
  947.7 66.2 %collective-permute-start.31 = (bf16[128,2176]{1,0:T(8,128)(2,1)}, bf16[128,2176]{1,0:T(8,128)(2,1)}, u32[]{:S(2)}, u32[]{:S(2)}) collective-permute-start(bf16[128,2176]{1,0:T(8,128)(2,1)} %get-tuple-element.239), channel_id=1, source_target_pairs={{0,8},{8,16},{16,24},{24,0},{1,9},{9,17},{17,25},{25,1},{2,10},{10... | collective-permute-start | bytes 1671176 | tf_op jit(solution)/shard_map/ppermute | solution.py:421
  947.7 66.2 %collective-permute-start.30 = (bf16[128,2176]{1,0:T(8,128)(2,1)}, bf16[128,2176]{1,0:T(8,128)(2,1)}, u32[]{:S(2)}, u32[]{:S(2)}) collective-permute-start(bf16[128,2176]{1,0:T(8,128)(2,1)} %get-tuple-element.240), channel_id=1, source_target_pairs={{0,16},{8,24},{16,0},{24,8},{1,17},{9,25},{17,1},{25,9},{2,18},{10... | collective-permute-start | bytes 1671176 | tf_op jit(solution)/shard_map/ppermute | solution.py:421
  947.8 66.1 %collective-permute-start.29 = (bf16[128,2176]{1,0:T(8,128)(2,1)}, bf16[128,2176]{1,0:T(8,128)(2,1)}, u32[]{:S(2)}, u32[]{:S(2)}) collective-permute-start(bf16[128,2176]{1,0:T(8,128)(2,1)} %get-tuple-element.238), channel_id=1, source_target_pairs={{0,24},{8,0},{16,8},{24,16},{1,25},{9,1},{17,9},{25,17},{2,26},{10... | collective-permute-start | bytes 1671176 | tf_op jit(solution)/shard_map/ppermute | solution.py:421
  949.3 59.0 %collective-permute-start.17 = (bf16[128,2048]{1,0:T(8,128)(2,1)S(1)}, bf16[128,2048]{1,0:T(8,128)(2,1)S(1)}, u32[]{:S(2)}, u32[]{:S(2)}) collective-permute-start(bf16[128,2048]{1,0:T(8,128)(2,1)S(1)} %get-tuple-element.246), channel_id=1, source_target_pairs={{0,24},{8,0},{16,8},{24,16},{1,25},{9,1},{17,9},{25,17},{2,26},{10... | collective-permute-start | bytes 1572872 | tf_op jit(solution)/shard_map/ppermute | solution.py:421
  1083.6 247.5 %collective-permute-start.33 = (bf16[3,4,64,1408]{3,2,1,0:T(8,128)(2,1)}, bf16[3,4,64,1408]{3,2,1,0:T(8,128)(2,1)}, u32[]{:S(2)}, u32[]{:S(2)}) collective-permute-start(bf16[3,4,64,1408]{3,2,1,0:T(8,128)(2,1)} %get-tuple-element.197), channel_id=1, source_target_pairs={{0,24},{8,0},{16,8},{24,16},{1,25},{9,1},{17,9},{25,17},{2,26},{10... | collective-permute-start | bytes 6488072 | tf_op jit(solution)/shard_map/ppermute | solution.py:421
  1083.6 248.3 %collective-permute-start.47 = (bf16[3,4,64,1408]{3,2,1,0:T(8,128)(2,1)}, bf16[3,4,64,1408]{3,2,1,0:T(8,128)(2,1)}, u32[]{:S(2)}, u32[]{:S(2)}) collective-permute-start(bf16[3,4,64,1408]{3,2,1,0:T(8,128)(2,1)} %get-tuple-element.196), channel_id=1, source_target_pairs={{0,8},{8,16},{16,24},{24,0},{1,9},{9,17},{17,25},{25,1},{2,10},{10... | collective-permute-start | bytes 6488072 | tf_op jit(solution)/shard_map/ppermute | solution.py:421
  1085.0 246.9 %collective-permute-start.46 = (bf16[3,4,64,1408]{3,2,1,0:T(8,128)(2,1)}, bf16[3,4,64,1408]{3,2,1,0:T(8,128)(2,1)}, u32[]{:S(2)}, u32[]{:S(2)}) collective-permute-start(bf16[3,4,64,1408]{3,2,1,0:T(8,128)(2,1)} %get-tuple-element.195), channel_id=1, source_target_pairs={{0,16},{8,24},{16,0},{24,8},{1,17},{9,25},{17,1},{25,9},{2,18},{10... | collective-permute-start | bytes 6488072 | tf_op jit(solution)/shard_map/ppermute | solution.py:421
  1095.1 205.2 %collective-permute-start.39 = (bf16[8,64,512]{2,1,0:T(8,128)(2,1)S(1)}, bf16[8,64,512]{2,1,0:T(8,128)(2,1)S(1)}, u32[]{:S(2)}, u32[]{:S(2)}) collective-permute-start(bf16[8,64,512]{2,1,0:T(8,128)(2,1)S(1)} %get-tuple-element.243), channel_id=1, source_target_pairs={{0,8},{8,16},{16,24},{24,0},{1,9},{9,17},{17,25},{25,1},{2,10},{10... | collective-permute-start | bytes 1572872 | tf_op jit(solution)/shard_map/ppermute | solution.py:421
  1099.7 211.8 %collective-permute-start.38 = (bf16[8,64,512]{2,1,0:T(8,128)(2,1)S(1)}, bf16[8,64,512]{2,1,0:T(8,128)(2,1)S(1)}, u32[]{:S(2)}, u32[]{:S(2)}) collective-permute-start(bf16[8,64,512]{2,1,0:T(8,128)(2,1)S(1)} %get-tuple-element.242), channel_id=1, source_target_pairs={{0,16},{8,24},{16,0},{24,8},{1,17},{9,25},{17,1},{25,9},{2,18},{10... | collective-permute-start | bytes 1572872 | tf_op jit(solution)/shard_map/ppermute | solution.py:421
  1311.5 35.6 %collective-permute-start.42 = (bf16[64,2048]{1,0:T(8,128)(2,1)}, bf16[64,2048]{1,0:T(8,128)(2,1)}, u32[]{:S(2)}, u32[]{:S(2)}) collective-permute-start(bf16[64,2048]{1,0:T(8,128)(2,1)} %get-tuple-element.279), channel_id=1, source_target_pairs={{0,8},{8,16},{16,24},{24,0},{1,9},{9,17},{17,25},{25,1},{2,10},{10... | collective-permute-start | bytes 786440 | tf_op jit(solution)/shard_map/ppermute | solution.py:421
  1316.6 30.5 %collective-permute-start.41 = (bf16[64,2048]{1,0:T(8,128)(2,1)}, bf16[64,2048]{1,0:T(8,128)(2,1)}, u32[]{:S(2)}, u32[]{:S(2)}) collective-permute-start(bf16[64,2048]{1,0:T(8,128)(2,1)} %get-tuple-element.280), channel_id=1, source_target_pairs={{0,16},{8,24},{16,0},{24,8},{1,17},{9,25},{17,1},{25,9},{2,18},{10... | collective-permute-start | bytes 786440 | tf_op jit(solution)/shard_map/ppermute | solution.py:421
  1317.7 31.6 %all-to-all-start.2 = ((bf16[8,64,512]{2,1,0:T(8,128)(2,1)}), bf16[8,64,512]{2,1,0:T(8,128)(2,1)S(1)}, u32[]{:S(2)}, u32[]{:S(2)}) async-start(bf16[8,64,512]{2,1,0:T(8,128)(2,1)} %fusion.96), calls=%async_computation.2 | async-start | bytes 1048576 | tf_op jit(solution)/shard_map/all_to_all | solution.py:778
  1346.5 119.4 %collective-permute-start.48 = (bf16[3,2,256,1408]{3,2,1,0:T(8,128)(2,1)}, bf16[3,2,256,1408]{3,2,1,0:T(8,128)(2,1)}, u32[]{:S(2)}, u32[]{:S(2)}) collective-permute-start(bf16[3,2,256,1408]{3,2,1,0:T(8,128)(2,1)} %dynamic-slice_bitcast_fusion), channel_id=1, source_target_pairs={{0,1},{1,0},{2,3},{3,2},{4,5},{5,4},{6,7},{7,6},{8,9},{9,8},{10,11... | collective-permute-start | bytes 12976136 | tf_op jit(solution)/shard_map/ppermute | solution.py:430
  (179 other events, 3075.1 us)
Sparse Core Ops, SparseCore 0:
  74.4 38.2 all-gather.11
  137.3 33.2 all-gather.5
  172.5 32.3 all-gather.7
  207.2 32.3 all-gather.9
  343.8 47.0 reduce-scatter.3
  557.6 91.7 reduce-scatter.5
  652.8 65.4 reduce-scatter.7

commit v4 on v2

v4 whole, which is shorter than its diff:
```python
import jax
import jax.numpy as jnp
from jax import lax
from jax.experimental import pallas as pl
from jax.experimental.pallas import tpu as pltpu
from jax.sharding import PartitionSpec as P

H = 16
DH = 128
DR = 64
DV = 128
KVR = 512

norm_eps = 1e-06
masked_score = -1e30
MESH = pl.DeviceIdType.MESH
ANY = pl.BlockSpec(memory_space=pl.ANY)
VMEM = pl.BlockSpec(memory_space=pltpu.VMEM)
BF = jnp.bfloat16
F32 = jnp.float32


def rms_norm(values, scale_gain):
    return (
        values
        * lax.rsqrt(jnp.mean(values * values, axis=-1, keepdims=True) + norm_eps)
        * scale_gain
    )


def rotate(values, cos_table, sine_table):
    half_dim = values.shape[-1] // 2
    first_half = values[..., :half_dim]
    second_half = values[..., half_dim:]
    return jnp.concatenate(
        [
            first_half * cos_table - second_half * sine_table,
            second_half * cos_table + first_half * sine_table,
        ],
        axis=-1,
    )


def rope_tables(positions):
    half_dim = DR // 2
    inv_freq = 10000.0 ** (-(jnp.arange(half_dim).astype(F32) * 2.0) / DR)
    angles = positions.astype(F32)[:, None] * inv_freq[None, :]
    return (jnp.cos(angles), jnp.sin(angles))


def swiglu(gate_in, up_in):
    return jax.nn.silu(gate_in) * up_in


def mm(left, right):
    return jnp.dot(left, right, preferred_element_type=F32)


def mm_rows(left, right):
    return lax.dot_general(left, right, (((0,), (0,)), ((), ())), preferred_element_type=F32)


def mm_cols(left, right):
    return lax.dot_general(left, right, (((1,), (1,)), ((), ())), preferred_element_type=F32)


def slot_places(route_rows, pair_order, capacity):
    pair_expert = route_rows.reshape(-1)
    earlier = pair_order[None, :] < pair_order[:, None]
    same_expert = pair_expert[None, :] == pair_expert[:, None]
    places = jnp.sum((earlier & same_expert).astype(jnp.int32), axis=1)
    slot_index = jnp.where(places < capacity, pair_expert * capacity + places, -1)
    return slot_index.reshape(route_rows.shape)


def params(collective_id):
    return pltpu.CompilerParams(
        collective_id=collective_id, has_side_effects=True, vmem_limit_bytes=48 << 20
    )


def remote(src, dst, send_sem, recv_sem, device):
    return pltpu.make_async_remote_copy(
        src_ref=src,
        dst_ref=dst,
        send_sem=send_sem,
        recv_sem=recv_sem,
        device_id=device,
        device_id_type=MESH,
    )


def greet(devices):
    barrier = pltpu.get_barrier_semaphore()
    for device in devices:
        pl.semaphore_signal(barrier, inc=1, device_id=device, device_id_type=MESH)
    pl.semaphore_wait(barrier, len(devices))


def places(n_dp, n_ex):
    z = lax.axis_index("dp")
    e = lax.axis_index("expert")
    chips = n_ex // 2
    c, k = e // 2, lax.rem(e, 2)
    sibling = (z, e + 1 - 2 * k)
    same_core = [(z, lax.rem(c + i, chips) * 2 + k) for i in range(1, chips)]
    column = [(lax.rem(z + i, n_dp), e) for i in range(1, n_dp)]
    return z, e, c, k, sibling, same_core, column


def plane_gather(block, n_dp, n_ex, collective_id):
    chips = n_ex // 2

    def kernel(x_ref, o_ref, send, recv, sib_send, sib_recv, local):
        z, e, c, k, sibling, same_core, _ = places(n_dp, n_ex)
        greet(same_core + [sibling])
        far = []
        for i in range(1, chips):
            copy = remote(x_ref, o_ref.at[e], send.at[i], recv.at[i], same_core[i - 1])
            copy.start()
            far.append(copy)
        near = [remote(x_ref, o_ref.at[e], sib_send.at[0], sib_recv.at[0], sibling)]
        near[0].start()
        own = pltpu.make_async_copy(x_ref, o_ref.at[e], local)
        own.start()
        for i in range(1, chips):
            source = lax.rem(c + chips - i, chips) * 2 + k
            far[i - 1].wait_recv()
            copy = remote(
                o_ref.at[source], o_ref.at[source], sib_send.at[i], sib_recv.at[i], sibling
            )
            copy.start()
            near.append(copy)
        own.wait()
        for copy in far:
            copy.wait_send()
        for copy in near:
            copy.wait()

    return pl.pallas_call(
        kernel,
        out_shape=jax.ShapeDtypeStruct((n_ex,) + block.shape, block.dtype),
        in_specs=[ANY],
        out_specs=ANY,
        scratch_shapes=[pltpu.SemaphoreType.DMA((chips,))] * 4 + [pltpu.SemaphoreType.DMA],
        compiler_params=params(collective_id),
    )(block)


def wait_recv(region, sem, device):
    remote(region, region, sem, sem, device).wait_recv()


def column_sum(array, n_dp, n_ex, inner, collective_id):
    shape = array.shape[1:]

    def kernel(x_ref, o_ref, buf, send, recv):
        z, e, c, k, sibling, same_core, _ = places(n_dp, n_ex)
        group = column_group(z, e, inner)
        greet(group[1:])
        copies = []
        for i in range(1, inner):
            copy = remote(x_ref.at[i], buf.at[i], send.at[i], recv.at[i], group[inner - i])
            copy.start()
            copies.append(copy)
        o_ref[...] = x_ref[0].astype(F32)
        for i in range(1, inner):
            copies[i - 1].wait_recv()
            o_ref[...] += buf[i].astype(F32)
        for copy in copies:
            copy.wait_send()

    return pl.pallas_call(
        kernel,
        out_shape=jax.ShapeDtypeStruct(shape, F32),
        in_specs=[VMEM],
        out_specs=VMEM,
        scratch_shapes=[pltpu.VMEM((inner,) + shape, BF)] + [pltpu.SemaphoreType.DMA((inner,))] * 2,
        compiler_params=params(collective_id),
    )(array)


def column_group(z, e, inner):
    start = z // inner * inner
    return [(start + lax.rem(z - start + i, inner), e) for i in range(inner)]


def first_exchange(tok, heads_w, pack, slot, cot, n_dp, n_ex, inner, collective_id):
    chips = n_ex // 2

    def kernel(
        tok_ref, wa_ref, pk_ref, sl_ref, co_ref, tok_out, wa_out, pk_out, sl_out, co_out,
        t_send, t_recv, ts_send, ts_recv, a_send, a_recv, az_send, az_recv,
        p_send, p_recv, pf_send, pf_recv, ps_send, ps_recv, s_send, s_recv, c_send, c_recv, local,
    ):
        z, e, c, k, sibling, same_core, column = places(n_dp, n_ex)
        plane = [(z, lax.rem(e + i, n_ex)) for i in range(1, n_ex)]
        group = column_group(z, e, inner)
        greet(plane + column)
        wa_far, pk_col, tok_far, near = [], [], [], []
        for i in range(1, n_ex):
            copy = remote(
                wa_ref.at[lax.rem(e + i, n_ex)], wa_out.at[z, e],
                a_send.at[i], a_recv.at[i], plane[i - 1],
            )
            copy.start()
            wa_far.append(copy)
        for i in range(1, n_dp):
            copy = remote(pk_ref, pk_out.at[z, e], p_send.at[i], p_recv.at[i], column[i - 1])
            copy.start()
            pk_col.append(copy)
        for i in range(1, inner):
            copy = remote(sl_ref, sl_out.at[i], s_send.at[i], s_recv.at[i], group[i])
            copy.start()
            near.append(copy)
        for i in range(1, chips):
            copy = remote(tok_ref, tok_out.at[e], t_send.at[i], t_recv.at[i], same_core[i - 1])
            copy.start()
            tok_far.append(copy)
        copy = remote(tok_ref, tok_out.at[e], ts_send.at[0], ts_recv.at[0], sibling)
        copy.start()
        near.append(copy)
        own = [
            pltpu.make_async_copy(wa_ref.at[e], wa_out.at[z, e], local.at[0]),
            pltpu.make_async_copy(pk_ref, pk_out.at[z, e], local.at[1]),
            pltpu.make_async_copy(tok_ref, tok_out.at[e], local.at[2]),
            pltpu.make_async_copy(sl_ref, sl_out.at[0], local.at[3]),
            pltpu.make_async_copy(co_ref, co_out.at[0], local.at[4]),
        ]
        for copy in own:
            copy.start()
        for copy in own:
            copy.wait()
        for copy in wa_far:
            copy.wait_recv()
        wa_col = []
        for i in range(1, n_dp):
            copy = remote(
                wa_out.at[z], wa_out.at[z], az_send.at[i], az_recv.at[i], column[i - 1]
            )
            copy.start()
            wa_col.append(copy)
        for i in range(1, inner):
            copy = remote(co_ref, co_out.at[i], c_send.at[i], c_recv.at[i], group[i])
            copy.start()
            near.append(copy)
        for copy in pk_col:
            copy.wait_recv()
        pk_far = []
        for i in range(1, chips):
            copy = remote(
                pk_out.at[:, e], pk_out.at[:, e], pf_send.at[i], pf_recv.at[i], same_core[i - 1]
            )
            copy.start()
            pk_far.append(copy)
        copy = remote(pk_out.at[:, e], pk_out.at[:, e], ps_send.at[0], ps_recv.at[0], sibling)
        copy.start()
        near.append(copy)
        for i in range(1, chips):
            source = lax.rem(c + chips - i, chips) * 2 + k
            tok_far[i - 1].wait_recv()
            copy = remote(
                tok_out.at[source], tok_out.at[source], ts_send.at[i], ts_recv.at[i], sibling
            )
            copy.start()
            near.append(copy)
            pk_far[i - 1].wait_recv()
            copy = remote(
                pk_out.at[:, source], pk_out.at[:, source], ps_send.at[i], ps_recv.at[i], sibling
            )
            copy.start()
            near.append(copy)
        for copy in near + wa_col:
            copy.wait()
        for copy in wa_far + pk_col + tok_far + pk_far:
            copy.wait_send()

    dma = pltpu.SemaphoreType.DMA
    return pl.pallas_call(
        kernel,
        out_shape=[
            jax.ShapeDtypeStruct((n_ex,) + tok.shape, tok.dtype),
            jax.ShapeDtypeStruct((n_dp,) + heads_w.shape, heads_w.dtype),
            jax.ShapeDtypeStruct((n_dp, n_ex) + pack.shape, pack.dtype),
            jax.ShapeDtypeStruct((inner,) + slot.shape, slot.dtype),
            jax.ShapeDtypeStruct((inner,) + cot.shape, cot.dtype),
        ],
        in_specs=[ANY] * 5,
        out_specs=[ANY] * 5,
        scratch_shapes=[dma((chips,))] * 4
        + [dma((n_ex,))] * 2
        + [dma((n_dp,))] * 4
        + [dma((chips,))] * 4
        + [dma((inner,))] * 4
        + [dma((5,))],
        compiler_params=params(collective_id),
    )(tok, heads_w, pack, slot, cot)


def forward_exchange(parts, tok, gain, slots, experts, shared, n_dp, n_ex, inner, collective_id):
    chips = n_ex // 2
    hh = n_ex // 2
    local_experts = experts[0].shape[0]
    rows, width = tok.shape

    def kernel(x_ref, tok_ref, gain_ref, slot_ref, *refs):
        e_in, s_in = refs[:3], refs[3:6]
        res_ref, xcol_ref, slot_out = refs[6:9]
        w_out, s_out = refs[9:12], refs[12:15]
        from_sib, out_buf, from_far, xbuf = refs[15:19]
        (
            near_s, near_r, far_s, far_r, x_s, x_r, g_s, g_r, we_s, we_r, wf_s, wf_r,
            sh_s, sh_r, sp_s, sp_r, sf_s, sf_r, local,
        ) = refs[19:]
        z, e, c, k, sibling, same_core, column = places(n_dp, n_ex)
        group = column_group(z, e, inner)
        sib_column = [(device[0], sibling[1]) for device in column]
        greet(same_core + [sibling] + column + sib_column)
        my_l = lax.rem(z, inner)

        def expert_sends(m, start):
            for i in list(range(1, n_dp)) + [0]:
                to = lax.rem(z + i, n_dp)
                expert = lax.rem(to, inner)

                def go(i=i, to=to, expert=expert):
                    for h in range(2):
                        src = e_in[m].at[lax.rem(expert, local_experts), pl.ds(h * hh, hh)]
                        dst = w_out[m].at[pl.ds(h * hh, hh), z]

                        def far(src=src, dst=dst, h=h):
                            copy = remote(
                                src, dst, we_s.at[m, i, h], we_r.at[m, z], (to, 2 * c + h)
                            )
                            if start:
                                copy.start()
                            else:
                                copy.wait_send()

                        if i:
                            far()
                        else:
                            pl.when(k != h)(far)
                            if start:

                                @pl.when(k == h)
                                def _(src=src, dst=dst):
                                    pltpu.make_async_copy(src, dst, we_r.at[m, z]).start()

                pl.when(expert // local_experts == k)(go)

        def expert_arrivals(m):
            for i in range(n_dp):
                d = lax.rem(z + n_dp - i, n_dp)
                region = w_out[m].at[pl.ds(k * hh, hh), d]
                if i:
                    wait_recv(region, we_r.at[m, d], sibling)
                else:
                    from_here = my_l // local_experts == k

                    @pl.when(from_here)
                    def _(region=region, d=d):
                        src = e_in[m].at[lax.rem(my_l, local_experts), pl.ds(k * hh, hh)]
                        pltpu.make_async_copy(src, region, we_r.at[m, d]).wait()

                    @pl.when(jnp.logical_not(from_here))
                    def _(region=region, d=d):
                        wait_recv(region, we_r.at[m, d], sibling)

                remote(region, region, wf_s.at[m, i], wf_r.at[m, i], sibling).start()

        near = []
        for i in list(range(1, chips)) + [0]:
            chip = lax.rem(c + i, chips)
            copy = remote(
                x_ref.at[chip * 2 + 1 - k], from_sib.at[chip], near_s.at[i], near_r.at[i], sibling
            )
            copy.start()
            near.append(copy)
        shared_copies = []
        for i in range(1, n_dp):
            for m in range(3):
                copy = remote(
                    s_in[m].at[lax.rem(lax.rem(z + i, n_dp), inner)], s_out[m].at[e, z],
                    sh_s.at[m, i], sh_r.at[m, i], column[i - 1],
                )
                copy.start()
                shared_copies.append(copy)
        own = [
            pltpu.make_async_copy(s_in[m].at[my_l], s_out[m].at[e, z], local.at[m])
            for m in range(3)
        ]
        own.append(pltpu.make_async_copy(slot_ref.at[0], slot_out.at[0], local.at[3]))
        for copy in own:
            copy.start()
        expert_sends(0, True)
        expert_sends(1, True)
        far = []
        for i in range(1, chips):
            chip = lax.rem(c + i, chips)
            near[i - 1].wait_recv()
            out_buf[i] = (
                x_ref[chip * 2 + k].astype(F32) + from_sib[chip].astype(F32)
            ).astype(BF)
            copy = remote(out_buf.at[i], from_far.at[i], far_s.at[i], far_r.at[i], same_core[i - 1])
            copy.start()
            far.append(copy)
        slot_copies = []
        for i in range(1, chips):
            copy = remote(slot_ref.at[i], slot_out.at[i], g_s.at[i], g_r.at[i], same_core[i - 1])
            copy.start()
            slot_copies.append(copy)
        near[chips - 1].wait_recv()
        res_ref[...] = x_ref[e].astype(F32) + from_sib[c].astype(F32) + tok_ref[...].astype(F32)
        for i in range(1, chips):
            far[i - 1].wait_recv()
            res_ref[...] += from_far[i].astype(F32)
        residual = res_ref[...]
        scale = lax.rsqrt(jnp.mean(residual * residual, axis=-1, keepdims=True) + norm_eps)
        xbuf[...] = (residual * scale * gain_ref[...]).astype(BF)
        x_copies = []
        for i in range(1, inner):
            copy = remote(xbuf, xcol_ref.at[i], x_s.at[i], x_r.at[i], group[i])
            copy.start()
            x_copies.append(copy)
        x_own = pltpu.make_async_copy(xbuf, xcol_ref.at[0], local.at[4])
        x_own.start()
        expert_sends(2, True)
        for copy in own:
            copy.wait()
        for copy in shared_copies:
            copy.wait_recv()
        plane, to_sib = [], []
        for m in range(3):
            block = s_out[m].at[e]
            for i in range(1, chips):
                copy = remote(block, block, sp_s.at[m, i], sp_r.at[m, i], same_core[i - 1])
                copy.start()
                plane.append(copy)
            copy = remote(block, block, sf_s.at[m, 0], sf_r.at[m, 0], sibling)
            copy.start()
            to_sib.append(copy)
        for m in range(3):
            for i in range(1, chips):
                plane[m * (chips - 1) + i - 1].wait_recv()
                block = s_out[m].at[lax.rem(c + chips - i, chips) * 2 + k]
                copy = remote(block, block, sf_s.at[m, i], sf_r.at[m, i], sibling)
                copy.start()
                to_sib.append(copy)
        for m in range(3):
            expert_arrivals(m)
        for copy in x_copies + slot_copies + to_sib:
            copy.wait()
        x_own.wait()
        for copy in plane + shared_copies + near + far:
            copy.wait_send()
        for m in range(3):
            expert_sends(m, False)
            for i in range(n_dp):
                d = lax.rem(z + n_dp - i, n_dp)
                mine = w_out[m].at[pl.ds(k * hh, hh), d]
                remote(mine, mine, wf_s.at[m, i], wf_r.at[m, i], sibling).wait_send()
                region = w_out[m].at[pl.ds((1 - k) * hh, hh), d]
                wait_recv(region, wf_r.at[m, i], sibling)

    dma = pltpu.SemaphoreType.DMA
    r, ff = experts[0].shape[2:]
    ff_s = shared[0].shape[2]
    outs = pl.pallas_call(
        kernel,
        out_shape=[
            jax.ShapeDtypeStruct((rows, width), F32),
            jax.ShapeDtypeStruct((inner, rows, width), BF),
            jax.ShapeDtypeStruct(slots.shape, BF),
        ]
        + [jax.ShapeDtypeStruct((n_ex, n_dp, r, ff), BF)] * 3
        + [jax.ShapeDtypeStruct((n_ex, n_dp, r, ff_s), BF)] * 3,
        in_specs=[VMEM] * 3 + [ANY] * 7,
        out_specs=[VMEM] + [ANY] * 8,
        scratch_shapes=[pltpu.VMEM((chips, rows, width), BF)] * 3
        + [pltpu.VMEM((rows, width), BF)]
        + [dma((chips,))] * 4
        + [dma((inner,))] * 2
        + [dma((chips,))] * 2
        + [dma((3, n_dp, 2)), dma((3, n_dp)), dma((3, n_dp)), dma((3, n_dp))]
        + [dma((3, n_dp))] * 2
        + [dma((3, chips))] * 4
        + [dma((5,))],
        compiler_params=params(collective_id),
    )(parts, tok, gain, slots, *experts, *shared)
    return outs[0], outs[1], outs[2], outs[3:6], outs[6:9]


class ExpertsBack:
    @staticmethod
    def scratch(total, n_dp, inner):
        n_ex, _, r, ff = total.shape
        dma = pltpu.SemaphoreType.DMA
        return [
            pltpu.VMEM((n_ex // 2, n_dp, r, ff), BF),
            pltpu.VMEM((n_ex // 2, n_dp, r, ff), BF),
            dma((n_dp,)),
            dma((n_dp,)),
            dma((n_dp,)),
            dma((n_dp,)),
            dma((n_dp // inner, 2, 2)),
        ]

    @staticmethod
    def out(total, n_dp, inner):
        n_ex, _, r, ff = total.shape
        return jax.ShapeDtypeStruct((n_dp // inner, 2, n_ex, r, ff), BF)

    def __init__(self, total, out, scratch, n_dp, n_ex, inner):
        self.total, self.out, self.n_dp, self.inner = total, out, n_dp, inner
        self.own, self.sib, self.near_s, self.near_r, self.load, self.send, self.recv = scratch
        self.z, self.e, self.c, self.k, self.sibling, _, _ = places(n_dp, n_ex)
        self.hh = n_ex // 2

    def near(self, i):
        d = lax.rem(self.z + i, self.n_dp)
        return remote(
            self.total.at[pl.ds((1 - self.k) * self.hh, self.hh), d],
            self.sib.at[:, d], self.near_s.at[i], self.near_r.at[i], self.sibling,
        )

    def loads(self, i):
        d = lax.rem(self.z + i, self.n_dp)
        return pltpu.make_async_copy(
            self.total.at[pl.ds(self.k * self.hh, self.hh), d], self.own.at[:, d], self.load.at[i]
        )

    def order(self):
        return list(range(1, self.n_dp)) + [0]

    def begin(self):
        for i in self.order():
            self.near(i).start()
            self.loads(i).start()

    def route(self, i):
        d = lax.rem(self.z + i, self.n_dp)
        expert = lax.rem(self.z, self.inner)
        dst = self.out.at[
            self.z // self.inner, lax.rem(expert, 2), pl.ds(self.k * self.hh, self.hh)
        ]
        sem = self.recv.at[self.z // self.inner, lax.rem(expert, 2), self.k]
        return self.own.at[:, d], dst, sem, d, expert // 2

    def stay(self):
        src, dst, sem, _, _ = self.route(0)
        return pltpu.make_async_copy(src, dst, sem)

    def go(self, i):
        src, dst, sem, d, core = self.route(i)
        return remote(src, dst, self.send.at[i], sem, (d, 2 * self.c + core))

    def here(self):
        return lax.rem(self.z, self.inner) // 2 == self.k

    def middle(self):
        for i in self.order():
            d = lax.rem(self.z + i, self.n_dp)
            self.near(i).wait_recv()
            self.loads(i).wait()
            for j in range(self.hh):
                self.own[j, d] = (
                    self.own[j, d].astype(F32) + self.sib[j, d].astype(F32)
                ).astype(BF)
            if i:
                self.go(i).start()
            else:
                pl.when(self.here())(lambda: self.stay().start())
                pl.when(jnp.logical_not(self.here()))(lambda: self.go(0).start())

    def end(self):
        for i in self.order():
            self.near(i).wait_send()
            if i:
                self.go(i).wait_send()
            else:
                pl.when(jnp.logical_not(self.here()))(lambda: self.go(0).wait_send())
        for o in range(self.n_dp // self.inner):
            for j in range(2):
                for h in range(2):
                    region = self.out.at[o, j, pl.ds(h * self.hh, self.hh)]
                    source = o * self.inner + 2 * self.k + j
                    here = jnp.logical_and(source == self.z, self.k == h)

                    @pl.when(here)
                    def _(region=region, o=o, j=j, h=h):
                        d = self.z
                        pltpu.make_async_copy(
                            self.own.at[:, d], region, self.recv.at[o, j, h]
                        ).wait()

                    @pl.when(jnp.logical_not(here))
                    def _(region=region, o=o, j=j, h=h):
                        wait_recv(region, self.recv.at[o, j, h], self.sibling)


def gather_and_sum(block, blocks, n_dp, n_ex, inner, collective_id):
    chips = n_ex // 2

    def kernel(x_ref, y_ref, o_ref, sum_ref, buf, send, recv, sib_send, sib_recv, c_send, c_recv, local):
        z, e, c, k, sibling, same_core, _ = places(n_dp, n_ex)
        group = column_group(z, e, inner)
        greet(same_core + [sibling] + group[1:])
        far, column = [], []
        for i in range(1, chips):
            copy = remote(x_ref, o_ref.at[e], send.at[i], recv.at[i], same_core[i - 1])
            copy.start()
            far.append(copy)
        for i in range(1, inner):
            copy = remote(y_ref.at[i], buf.at[i], c_send.at[i], c_recv.at[i], group[inner - i])
            copy.start()
            column.append(copy)
        near = [remote(x_ref, o_ref.at[e], sib_send.at[0], sib_recv.at[0], sibling)]
        near[0].start()
        own = pltpu.make_async_copy(x_ref, o_ref.at[e], local)
        own.start()
        for i in range(1, chips):
            source = lax.rem(c + chips - i, chips) * 2 + k
            far[i - 1].wait_recv()
            copy = remote(
                o_ref.at[source], o_ref.at[source], sib_send.at[i], sib_recv.at[i], sibling
            )
            copy.start()
            near.append(copy)
        sum_ref[...] = y_ref[0].astype(F32)
        for i in range(1, inner):
            column[i - 1].wait_recv()
            sum_ref[...] += buf[i].astype(F32)
        own.wait()
        for copy in far + column:
            copy.wait_send()
        for copy in near:
            copy.wait()

    dma = pltpu.SemaphoreType.DMA
    return pl.pallas_call(
        kernel,
        out_shape=[
            jax.ShapeDtypeStruct((n_ex,) + block.shape, block.dtype),
            jax.ShapeDtypeStruct(blocks.shape[1:], F32),
        ],
        in_specs=[ANY, VMEM],
        out_specs=[ANY, VMEM],
        scratch_shapes=[pltpu.VMEM(blocks.shape, BF)]
        + [dma((chips,))] * 4
        + [dma((inner,))] * 2
        + [dma],
        compiler_params=params(collective_id),
    )(block, blocks)


def plane_sum(arrays, totals, n_dp, n_ex, inner, collective_id):
    chips = n_ex // 2
    count, extra = len(arrays), len(totals)

    def kernel(*refs):
        x_refs, t_refs = refs[:count], refs[count : count + extra]
        refs = refs[count + extra :]
        o_refs, back_refs = refs[:count], refs[count : count + extra]
        refs = refs[count + extra :]
        bufs, sems, rest = refs[: 3 * count], refs[3 * count : 7 * count], refs[7 * count :]
        z, e, c, k, sibling, same_core, column = places(n_dp, n_ex)
        greet(
            same_core + [sibling] + (column + [(d[0], sibling[1]) for d in column] if extra else [])
        )
        backs = [
            ExpertsBack(t_refs[m], back_refs[m], rest[7 * m : 7 * m + 7], n_dp, n_ex, inner)
            for m in range(extra)
        ]
        near, far = {}, {}
        for i in list(range(1, chips)) + [0]:
            chip = lax.rem(c + i, chips)
            for j in range(count):
                near[i, j] = remote(
                    x_refs[j].at[chip * 2 + 1 - k],
                    bufs[3 * j].at[chip],
                    sems[4 * j].at[i],
                    sems[4 * j + 1].at[i],
                    sibling,
                )
                near[i, j].start()
        for back in backs:
            back.begin()
        for i in range(1, chips):
            chip = lax.rem(c + i, chips)
            for j in range(count):
                from_sib, out_buf, from_far = bufs[3 * j : 3 * j + 3]
                near[i, j].wait_recv()
                out_buf[i] = (
                    x_refs[j][chip * 2 + k].astype(F32) + from_sib[chip].astype(F32)
                ).astype(BF)
                far[i, j] = remote(
                    out_buf.at[i],
                    from_far.at[i],
                    sems[4 * j + 2].at[i],
                    sems[4 * j + 3].at[i],
                    same_core[i - 1],
                )
                far[i, j].start()
        for back in backs:
            back.middle()
        for j in range(count):
            near[0, j].wait_recv()
            o_refs[j][...] = x_refs[j][e].astype(F32) + bufs[3 * j][c].astype(F32)
        for i in range(1, chips):
            for j in range(count):
                far[i, j].wait_recv()
                o_refs[j][...] += bufs[3 * j + 2][i].astype(F32)
        for copy in list(near.values()) + list(far.values()):
            copy.wait_send()
        for back in backs:
            back.end()

    scratch = []
    for array in arrays:
        scratch += [pltpu.VMEM((chips,) + array.shape[1:], BF)] * 3
    scratch += [pltpu.SemaphoreType.DMA((chips,))] * (4 * count)
    for total in totals:
        scratch += ExpertsBack.scratch(total, n_dp, inner)
    outs = pl.pallas_call(
        kernel,
        out_shape=[jax.ShapeDtypeStruct(array.shape[1:], F32) for array in arrays]
        + [ExpertsBack.out(total, n_dp, inner) for total in totals],
        in_specs=[VMEM] * count + [ANY] * extra,
        out_specs=[VMEM] * count + [ANY] * extra,
        scratch_shapes=scratch,
        compiler_params=params(collective_id),
    )(*arrays, *totals)
    return outs[:count], outs[count:]


def last_exchange(arrays, totals, n_dp, n_ex, inner, collective_id):
    count, extra = len(arrays), len(totals)

    def kernel(*refs):
        x_refs, t_refs = refs[:count], refs[count : count + extra]
        refs = refs[count + extra :]
        o_refs, back_refs = refs[:count], refs[count : count + extra]
        refs = refs[count + extra :]
        sems, local, rest = refs[: 2 * count], refs[2 * count], refs[2 * count + 1 :]
        z, e, c, k, sibling, same_core, column = places(n_dp, n_ex)
        greet([sibling] + column + [(d[0], sibling[1]) for d in column])
        backs = [
            ExpertsBack(t_refs[m], back_refs[m], rest[7 * m : 7 * m + 7], n_dp, n_ex, inner)
            for m in range(extra)
        ]
        for back in backs:
            back.begin()
        copies = []
        for j in range(count):
            for i in range(1, n_dp):
                copy = remote(
                    x_refs[j].at[lax.rem(z + i, n_dp)], o_refs[j].at[z],
                    sems[2 * j].at[i], sems[2 * j + 1].at[i], column[i - 1],
                )
                copy.start()
                copies.append(copy)
            copy = pltpu.make_async_copy(x_refs[j].at[z], o_refs[j].at[z], local.at[j])
            copy.start()
            copies.append(copy)
        for back in backs:
            back.middle()
        for copy in copies:
            copy.wait()
        for back in backs:
            back.end()

    dma = pltpu.SemaphoreType.DMA
    scratch = [dma((n_dp,))] * (2 * count) + [dma((count,))]
    for total in totals:
        scratch += ExpertsBack.scratch(total, n_dp, inner)
    outs = pl.pallas_call(
        kernel,
        out_shape=[jax.ShapeDtypeStruct(array.shape, array.dtype) for array in arrays]
        + [ExpertsBack.out(total, n_dp, inner) for total in totals],
        in_specs=[ANY] * (count + extra),
        out_specs=[ANY] * (count + extra),
        scratch_shapes=scratch,
        compiler_params=params(collective_id),
    )(*arrays, *totals)
    return outs[:count], outs[count:]


def shards(
    tokens,
    cotangent,
    lengths,
    routes,
    place_order,
    attn_gain,
    w_query,
    w_latent,
    latent_gain,
    w_expand,
    w_out,
    ffn_gain,
    w_router,
    shared_gate,
    shared_up,
    shared_down,
    expert_gate,
    expert_up,
    expert_down,
):
    rows, width = tokens.shape
    n_dp = lax.axis_size("dp")
    n_ex = lax.axis_size("expert")
    chips = n_ex // 2
    z = lax.axis_index("dp")
    e = lax.axis_index("expert")
    chip = e // 2
    n_experts = w_router.shape[1]
    top_k = routes.shape[1]
    capacity = (rows * top_k * 5 + 4 * n_experts - 1) // (4 * n_experts)
    cap = (capacity + 15) // 16 * 16
    seq = rows * n_ex
    r = w_query.shape[0]
    rl = w_expand.shape[0]
    hp = H // n_ex
    parts = DV // r
    heads = [
        (d * n_ex + (j // parts) * parts) * r // DV
        for j in range(n_ex)
        for d in range(j % parts * hp, j % parts * hp + hp)
    ]
    heads_back = [heads.index(h) for h in range(H)]
    inner = n_experts // chips
    my_local = lax.rem(z, inner)
    part_groups = [[i * parts + m for m in range(parts)] for i in range(n_ex // parts)]
    ff_e = expert_gate.shape[2]
    ff_s = shared_gate.shape[1] // inner
    lat = KVR + DR
    head_cols = hp * (DH + DR)
    kv_cols = hp * (DH + DV)

    def to_owner_order(values):
        cut = values.reshape(values.shape[0], n_dp, n_ex, r)
        return cut.transpose(0, 2, 1, 3).reshape(values.shape)

    def from_owner_order(values):
        cut = values.reshape(values.shape[0], n_ex, n_dp, r)
        return cut.transpose(0, 2, 1, 3).reshape(values.shape)

    def pick(values, index, axis=0):
        return lax.dynamic_index_in_dim(values, index, axis, keepdims=False)

    wq_send = jnp.take(w_query.reshape(r, H, DH + DR), jnp.array(heads), axis=1)
    wq_send = wq_send.reshape(r, n_ex, head_cols).transpose(1, 0, 2)
    we_send = jnp.take(w_expand.reshape(rl, H, DH + DV), jnp.array(heads), axis=1)
    we_send = we_send.reshape(rl, n_ex, kv_cols).transpose(1, 0, 2)
    we_send = we_send.reshape(n_ex, r, rl * kv_cols // r)
    wa_send = jnp.concatenate([wq_send, we_send], axis=-1)
    pack_cols = (lat + n_experts + 3 + 127) // 128 * 128
    pack = jnp.concatenate(
        [
            w_latent,
            w_router,
            attn_gain[:, None],
            ffn_gain[:, None],
            jnp.pad(latent_gain, (0, r - rl))[:, None],
            jnp.zeros((r, pack_cols - lat - n_experts - 3), BF),
        ],
        axis=1,
    )
    slot_own = jnp.pad(
        slot_places(routes, place_order[0], capacity), ((0, 0), (0, 128 - top_k))
    )
    cot_owner = to_owner_order(cotangent)
    tok_all, wa_all, pk_all, slot_col, cot_col = first_exchange(
        tokens, wa_send, pack, slot_own, cot_owner, n_dp, n_ex, inner, 1
    )
    wq = wa_all[..., :head_cols].reshape(width, head_cols)
    wexp = wa_all[..., head_cols:].reshape(KVR, kv_cols)
    pk_flat = pk_all.reshape(width, pack_cols)
    w_lat = pk_flat[:, :lat]
    gain_one = pk_flat[:, lat + n_experts].astype(F32)
    gain_two = pk_all[..., lat + n_experts + 1].transpose(1, 0, 2).reshape(width).astype(F32)
    router = pk_all[..., lat : lat + n_experts].transpose(1, 0, 2, 3).reshape(width, n_experts)
    gain_lat = (
        pk_all[..., lat + n_experts + 2].reshape(n_dp * n_ex, r)[:, :rl].reshape(KVR).astype(F32)
    )
    wo_send, _ = lax.optimization_barrier((to_owner_order(w_out), pk_all))
    wo_col = lax.all_gather(wo_send, "dp", axis=0, tiled=False)
    wo_rows = lax.all_to_all(
        wo_col.reshape(parts, hp, r, width),
        "expert",
        0,
        0,
        axis_index_groups=part_groups,
        tiled=True,
    )
    wo_rows = wo_rows.transpose(1, 0, 2, 3).reshape(hp * DV, width)

    cot_col = cot_col.reshape(inner * rows, width)
    slots_all = n_experts * capacity
    slot_ids = slot_col[..., :top_k]
    slot_ids = jnp.where(
        slot_ids >= 0, slot_ids + (jnp.arange(inner) * slots_all)[:, None, None], -1
    ).reshape(inner * rows, top_k)
    place = jnp.arange(cap)
    far_experts = [lax.rem(chip + m, chips) * inner + my_local for m in range(chips)]
    wanted = (
        jnp.stack(far_experts)[:, None, None] * capacity
        + (jnp.arange(inner) * slots_all)[None, :, None]
        + place[None, None, :]
    )
    wanted = jnp.where(place[None, None, :] < capacity, wanted, -2).reshape(-1)
    n_slots = wanted.shape[0]
    per_far = n_slots // chips
    hot = sum((wanted[:, None] == slot_ids[None, :, j]).astype(BF) for j in range(top_k))
    hot_t = sum((slot_ids[:, j][:, None] == wanted[None, :]).astype(BF) for j in range(top_k))

    def between(values, way):
        cut = values.reshape(chips, per_far, -1)
        got = [cut[0]]
        for m in range(1, chips):
            perm = [(i, (i + 2 * m * way) % n_ex) for i in range(n_ex)]
            got.append(lax.ppermute(cut[m], "expert", perm))
        return jnp.concatenate(got, axis=0)

    grad_send = mm(hot, cot_col).astype(BF).reshape(chips, per_far, width)

    tok_plane = tok_all.reshape(seq, width)
    hidden_one = rms_norm(tok_plane.astype(F32), gain_one).astype(BF)
    positions = jnp.arange(seq)
    cos_table, sine_table = rope_tables(positions)
    query_raw = mm(hidden_one, wq).reshape(seq, hp, DH + DR)

    def make_queries(query_in):
        return jnp.concatenate(
            [
                query_in[..., :DH],
                rotate(query_in[..., DH:], cos_table[:, None, :], sine_table[:, None, :]),
            ],
            axis=-1,
        )

    query_rot, query_back = jax.vjp(make_queries, query_raw)
    queries = query_rot.astype(BF)
    latent_raw = mm(hidden_one, w_lat)
    latent_low = rms_norm(latent_raw[:, :KVR], gain_lat).astype(BF)
    rope_low = rotate(latent_raw[:, KVR:], cos_table, sine_table).astype(BF)
    expanded = mm(latent_low, wexp).astype(BF).reshape(seq, hp, DH + DV)
    score_scale = (DH + DR) ** (-0.5)
    allowed = (positions[None, :] <= positions[:, None]) & (positions[None, :] < lengths[0])
    attn_probs, probs_low, keys, attended = [], [], [], []
    for h in range(hp):
        key = jnp.concatenate([expanded[:, h, :DH], rope_low], axis=1)
        scores = jnp.where(allowed, mm_cols(queries[:, h], key) * score_scale, masked_score)
        top = jnp.max(scores, axis=-1, keepdims=True)
        exp_scores = jnp.exp(scores - top)
        probs = exp_scores / jnp.sum(exp_scores, axis=-1, keepdims=True)
        low = probs.astype(BF)
        attn_probs.append(probs)
        probs_low.append(low)
        keys.append(key)
        attended.append(mm(low, expanded[:, h, DH:]).astype(BF))
    attended = jnp.concatenate(attended, axis=1)
    out_part = mm(attended, wo_rows).astype(BF)
    residual, x_col, grad_in, (wg, wu, wd), (sgate, sup, sdown) = forward_exchange(
        out_part.reshape(n_ex, rows, width),
        to_owner_order(tokens),
        gain_two[None],
        grad_send,
        [w.reshape(-1, n_ex, r, ff_e) for w in (expert_gate, expert_up, expert_down)],
        [w.reshape(r, inner, ff_s).transpose(1, 0, 2) for w in (shared_gate, shared_up, shared_down)],
        n_dp,
        n_ex,
        inner,
        2,
    )
    wg, wu, wd = (w.reshape(width, ff_e) for w in (wg, wu, wd))
    sgate, sup, sdown = (w.reshape(width, ff_s) for w in (sgate, sup, sdown))
    hidden_two = x_col[0]
    x_col = x_col.reshape(inner * rows, width)
    grad_in = grad_in.reshape(n_slots, width)

    x_in = between(mm(hot, x_col).astype(BF), 1)

    def probs_of(logits):
        top = jnp.max(logits, axis=-1, keepdims=True)
        exp_logits = jnp.exp(logits - top)
        return exp_logits / jnp.sum(exp_logits, axis=-1, keepdims=True)

    shared_a = mm(x_col, sgate)
    shared_b = mm(x_col, sup)
    shared_hidden, shared_back = jax.vjp(swiglu, shared_a, shared_b)
    shared_hidden = shared_hidden.astype(BF)
    shared_out = mm_cols(shared_hidden, sdown)
    grad_sa, grad_sb = (v.astype(BF) for v in shared_back(mm(cot_col, sdown)))
    shared_grads = [
        mm_rows(x_col, grad_sa).astype(BF),
        mm_rows(x_col, grad_sb).astype(BF),
        mm_rows(cot_col, shared_hidden).astype(BF),
    ]
    shared_sums = [
        lax.psum_scatter(
            grad.reshape(n_ex, n_dp, r, ff_s), "expert", scatter_dimension=0, tiled=True
        ).reshape(n_dp, r, ff_s)
        for grad in shared_grads
    ]
    shared_dx = mm_cols(grad_sa, sgate) + mm_cols(grad_sb, sup)

    slot_probs = probs_of(mm(x_in, router))
    slot_gate = jnp.sum(
        jnp.where(jnp.arange(n_experts)[None, :] == far_experts[0], slot_probs, 0.0),
        axis=1,
        keepdims=True,
    )
    expert_a = mm(x_in, wg)
    expert_b = mm(x_in, wu)
    expert_hidden, expert_back = jax.vjp(swiglu, expert_a, expert_b)
    expert_hidden = expert_hidden.astype(BF)
    rows_back = between(mm_cols(expert_hidden, wd).astype(BF), -1)
    slot_grad = (slot_gate * grad_in.astype(F32)).astype(BF)
    grad_ea, grad_eb = (v.astype(BF) for v in expert_back(mm(slot_grad, wd)))
    dx_back = between((mm_cols(grad_ea, wg) + mm_cols(grad_eb, wu)).astype(BF), -1)
    expert_totals = [
        mm_rows(left, right).astype(BF).reshape(n_ex, n_dp, r, ff_e)
        for left, right in ((x_in, grad_ea), (x_in, grad_eb), (slot_grad, expert_hidden))
    ]

    col_probs = probs_of(mm(x_col, router))
    expert_axis = jnp.arange(n_experts)[None, :]
    gates = [
        jnp.sum(jnp.where(expert_axis == expert, col_probs, 0.0), axis=1, keepdims=True)
        for expert in far_experts
    ]
    gate_hot = jnp.concatenate(
        [hot_t[:, m * per_far : (m + 1) * per_far] * gates[m].astype(BF) for m in range(chips)],
        axis=1,
    )
    out_col = (mm(gate_hot, rows_back) + shared_out).astype(BF)
    dots = mm_cols(cot_col, rows_back) * hot_t.astype(F32)
    dots = jnp.sum(dots.reshape(inner * rows, chips, per_far), axis=-1)
    grad_probs_col = sum(
        jnp.where(expert_axis == far_experts[m], dots[:, m : m + 1], 0.0) for m in range(chips)
    )
    dx_col = mm(hot_t, dx_back) + shared_dx
    dx_send = jnp.concatenate(
        [dx_col, grad_probs_col, jnp.zeros((inner * rows, 128 - n_experts), F32)], axis=1
    ).astype(BF)
    dx_sum = column_sum(dx_send.reshape(inner, rows, width + 128), n_dp, n_ex, inner, 3)
    router_probs = col_probs[:rows]
    grad_probs = dx_sum[:, width : width + n_experts]
    grad_logits = (
        router_probs * (grad_probs - jnp.sum(grad_probs * router_probs, axis=-1, keepdims=True))
    ).astype(BF)
    grad_router = mm_rows(hidden_two, grad_logits)
    grad_hidden_two = dx_sum[:, :width] + mm_cols(grad_logits, router)
    _, norm_two_back = jax.vjp(rms_norm, residual, gain_two)
    grad_resid_norm, grad_gain_two = norm_two_back(grad_hidden_two)
    grad_residual = cot_owner.astype(F32) + grad_resid_norm

    grad_attn, out_sum = gather_and_sum(
        grad_residual.astype(BF), out_col.reshape(inner, rows, width), n_dp, n_ex, inner, 4
    )
    out_tokens = from_owner_order((residual + out_sum).astype(BF))
    grad_attn = grad_attn.reshape(seq, width)
    grad_attended = mm_cols(grad_attn, wo_rows).astype(BF)
    grad_wout = mm_rows(attended, grad_attn).astype(BF)
    grad_rope = 0.0
    grad_queries, grad_expanded = [], []
    for h in range(hp):
        gat = grad_attended[:, h * DV : (h + 1) * DV]
        probs = attn_probs[h]
        dp = mm_cols(gat, expanded[:, h, DH:])
        grad_scores = probs * (dp - jnp.sum(dp * probs, axis=-1, keepdims=True))
        grad_raw = jnp.where(allowed, grad_scores * score_scale, 0.0).astype(BF)
        grad_queries.append(mm(grad_raw, keys[h]))
        grad_key = mm_rows(grad_raw, queries[:, h])
        grad_rope = grad_rope + grad_key[:, DH:]
        grad_expanded += [grad_key[:, :DH], mm_rows(probs_low[h], gat)]
    grad_expanded = jnp.concatenate(grad_expanded, axis=1).astype(BF)
    (grad_query_raw,) = query_back(jnp.stack(grad_queries, axis=1))
    grad_query_low = grad_query_raw.reshape(seq, head_cols).astype(BF)
    grad_latent_part = jnp.concatenate([mm_cols(grad_expanded, wexp), grad_rope], axis=1)
    grad_latent_part = jnp.pad(grad_latent_part, ((0, 0), (0, -lat % 128))).astype(BF)
    grad_query_part = mm_cols(grad_query_low, wq).astype(BF)
    (grad_query_sum, grad_latent_sum), (down_back,) = plane_sum(
        [grad_query_part.reshape(n_ex, rows, width), grad_latent_part.reshape(n_ex, rows, -1)],
        expert_totals[2:],
        n_dp,
        n_ex,
        inner,
        5,
    )
    own_start = e * rows
    latent_own = lax.dynamic_slice_in_dim(latent_raw, own_start, rows, 0)
    cos_own = lax.dynamic_slice_in_dim(cos_table, own_start, rows, 0)
    sine_own = lax.dynamic_slice_in_dim(sine_table, own_start, rows, 0)

    def make_latent(latent_in, gain_in):
        return (
            rms_norm(latent_in[:, :KVR], gain_in),
            rotate(latent_in[:, KVR:], cos_own, sine_own),
        )

    _, latent_back = jax.vjp(make_latent, latent_own, gain_lat)
    grad_latent_raw, grad_gain_lat = latent_back(
        (grad_latent_sum[:, :KVR], grad_latent_sum[:, KVR:lat])
    )
    grad_latent_low = grad_latent_raw.astype(BF)
    _, norm_one_back = jax.vjp(rms_norm, tokens.astype(F32), gain_one)
    grad_hidden_one = grad_query_sum + mm_cols(grad_latent_low, w_lat)
    grad_tokens_norm, grad_gain_one = norm_one_back(grad_hidden_one)
    grad_tokens = from_owner_order(grad_residual) + grad_tokens_norm

    wout_back = lax.all_to_all(
        grad_wout.reshape(hp, parts, r, width).transpose(1, 0, 2, 3),
        "expert",
        0,
        0,
        axis_index_groups=part_groups,
        tiled=True,
    ).reshape(n_dp, r, width)
    grad_wq = mm_rows(hidden_one, grad_query_low).astype(BF).reshape(n_dp, n_ex, r, head_cols)
    grad_we = mm_rows(latent_low, grad_expanded).astype(BF)
    grad_we = grad_we.reshape(n_dp, n_ex, r, rl * kv_cols // r)
    heads_grad = jnp.concatenate([grad_wq, grad_we], axis=-1)
    latent_plane = plane_gather(grad_latent_low, n_dp, n_ex, 6).reshape(seq, lat)
    grad_wlat = pick(mm_rows(hidden_one, latent_plane).reshape(n_dp, n_ex, r, lat), e, 1)

    def by_owner(values):
        return values.reshape(n_ex, n_dp, r, -1).transpose(1, 0, 2, 3)

    small = jnp.concatenate(
        [
            by_owner(grad_router),
            grad_gain_one.reshape(n_dp, n_ex, r, 1),
            by_owner(grad_gain_two),
            jnp.pad(grad_gain_lat.reshape(n_dp, n_ex, rl, 1), ((0, 0),) * 2 + ((0, r - rl), (0, 0))),
            jnp.zeros((n_dp, n_ex, r, pack_cols - lat - n_experts - 3), F32),
        ],
        axis=-1,
    ).transpose(1, 0, 2, 3)
    small = jnp.sum(lax.all_to_all(small, "expert", 0, 0, tiled=True), axis=0)
    pack_grad = jnp.concatenate([grad_wlat, small], axis=-1).astype(BF)
    (heads_got, wout_got, pack_got, *shared_got), (gate_back, up_back) = last_exchange(
        [heads_grad, wout_back, pack_grad] + shared_sums, expert_totals[:2], n_dp, n_ex, inner, 7
    )

    def added(values):
        return jnp.sum(values.astype(F32), axis=0)

    heads_sum = added(heads_got).astype(BF)
    heads_all = lax.all_to_all(heads_sum, "expert", 0, 0, tiled=True).astype(F32)
    sum_wq = heads_all[..., :head_cols].transpose(1, 0, 2).reshape(r, H, DH + DR)
    sum_wq = jnp.take(sum_wq, jnp.array(heads_back), axis=1).reshape(r, H * (DH + DR))
    sum_we = heads_all[..., head_cols:].reshape(n_ex, rl, kv_cols).transpose(1, 0, 2)
    sum_we = jnp.take(sum_we.reshape(rl, H, DH + DV), jnp.array(heads_back), axis=1)
    sum_we = sum_we.reshape(rl, H * (DH + DV))
    sum_wout = from_owner_order(added(wout_got))
    pack_sum = added(pack_got)
    sum_sgate, sum_sup, sum_sdown = (
        added(got.reshape(n_dp // inner, inner, r, ff_s)).transpose(1, 0, 2).reshape(r, -1)
        for got in shared_got
    )
    sum_egate, sum_eup, sum_edown = (
        added(back).reshape(-1, n_ex * r, ff_e) for back in (gate_back, up_back, down_back)
    )
    return (
        out_tokens,
        grad_tokens,
        pack_sum[:, lat + n_experts],
        sum_wq,
        pack_sum[:, :lat],
        pack_sum[:rl, lat + n_experts + 2],
        sum_we,
        sum_wout,
        pack_sum[:, lat + n_experts + 1],
        pack_sum[:, lat : lat + n_experts],
        sum_sgate,
        sum_sup,
        sum_sdown,
        sum_egate,
        sum_eup,
        sum_edown,
    )


def solution(mesh):
    both = ("dp", "expert")
    in_specs = (
        P(both, None),
        P(both, None),
        P("dp"),
        P(both, None),
        P(both, None),
        P(both),
        P(both, None),
        P(both, None),
        P(both),
        P(both, None),
        P(both, None),
        P(both),
        P(both, None),
        P(both, None),
        P(both, None),
        P(both, None),
        P("expert", "dp", None),
        P("expert", "dp", None),
        P("expert", "dp", None),
    )
    out_specs = (
        P(both, None),
        P(both, None),
        P(both),
        P(both, None),
        P(both, None),
        P(both),
        P(both, None),
        P(both, None),
        P(both),
        P(both, None),
        P(both, None),
        P(both, None),
        P(both, None),
        P("expert", "dp", None),
        P("expert", "dp", None),
        P("expert", "dp", None),
    )
    return jax.shard_map(shards, mesh=mesh, in_specs=in_specs, out_specs=out_specs, check_vma=False)
```

time: 1450 us -> 1360 us (0.938)
  Pallas kernels: 264 us -> 798 us
  waiting for transfers between devices: 364 us -> 66.7 us
  local copies, waits for them, and re-layouts: 307 us -> 139 us
  starting transfers between devices: 165 us -> 23.9 us
    pallas_call x3 -> x5, Pallas kernels: 166 us -> 679 us  [the longest x1 265 us: forward_exchange(): pl.pallas_call(kernel, out_shape=[jax.ShapeDtypeStruct((rows, width), F32...]
    ppermute x69 -> x0, waiting for transfers between devices: 288 us -> none  [the longest x57 288 us: shift(): lax.ppermute(values, 'dp', [(i, (i + step) % n_dp) for i in range(n_dp)])]
    ppermute x69 -> x0, starting transfers between devices: 131 us -> none  [the longest x57 87.3 us: shift(): lax.ppermute(values, 'dp', [(i, (i + step) % n_dp) for i in range(n_dp)])]
    dynamic_update_slice x48 -> x0, local copies, waits for them, and re-layouts: 66.6 us -> none  [the longest x12 49.2 us: shared_sum(): back = lax.dynamic_update_index_in_dim(back, block, after(i), 0)]
    pallas_call x1, Pallas kernels: 57.6 us -> 107 us  [first_exchange(): pl.pallas_call(kernel, out_shape=[jax.ShapeDtypeStruct((n_ex,) + tok.shap...]
    pallas_call x2 -> x1, Pallas kernels: 40.3 us -> 12.1 us  [plane_gather(): pl.pallas_call(kernel, out_shape=jax.ShapeDtypeStruct((n_ex,) + block.sha...]
    dynamic_slice x9 -> x0, local copies, waits for them, and re-layouts: 17.2 us -> none  [pick(): return lax.dynamic_index_in_dim(values, index, axis, keepdims=False)]
    unnamed x527 -> x352, local copies, waits for them, and re-layouts: 53.2 us -> 37.7 us
  transfers between devices with their start and end apart: 102 -> 16, of which waited for: 37 -> 4; matrix products, arithmetic and copies ran while one was open for 40% -> 27% of each run, Pallas kernels for 14% -> 15%
where the time goes in v4:
time: 1360 us; the launch traced here: 1350 us
  Pallas kernels  798 us (59%)
  matrix products  220 us (16%)
  local copies, waits for them, and re-layouts  139 us (10%)
  other arithmetic  73.4 us (5%)
  waiting for transfers between devices  66.7 us (5%)
  starting transfers between devices  23.9 us (2%)
  between operations  17.5 us (1%)
    pallas_call x1, Pallas kernels, forward_exchange(): pl.pallas_call(kernel, out_shape=[jax.ShapeDtypeStruct((rows, width), F32...  265 us
    pallas_call x1, Pallas kernels, last_exchange(): pl.pallas_call(kernel, out_shape=[jax.ShapeDtypeStruct(array.shape, array...  227 us
    pallas_call x1, Pallas kernels, first_exchange(): pl.pallas_call(kernel, out_shape=[jax.ShapeDtypeStruct((n_ex,) + tok.shap...  107 us
    dot_general x20, matrix products, mm(): return jnp.dot(left, right, preferred_element_type=F32)  93.5 us
    pallas_call x1, Pallas kernels, plane_sum(): pl.pallas_call(kernel, out_shape=[jax.ShapeDtypeStruct(array.shape[1:], F...  79.8 us
    dot_general x16, matrix products, mm_cols(): lax.dot_general(left, right, (((1,), (1,)), ((), ())), preferred_element_...  67.9 us
    ppermute x9, waiting for transfers between devices, between(): got.append(lax.ppermute(cut[m], 'expert', perm))  66.6 us
    dot_general x15, matrix products, mm_rows(): lax.dot_general(left, right, (((0,), (0,)), ((), ())), preferred_element_...  58.6 us
  transfers between devices with their start and end apart: 16, of which 4 were waited for; matrix products, arithmetic and copies ran while one was open for 27% of the time, Pallas kernels for 15%

profile of v4, /device:TPU:11, one launch (start us, length us, event | category | flops | bytes accessed | tf_op | source)
XLA Modules:
  0.0 1345.2 jit_solution(1371111012506849802)
XLA Ops:
  20.4 107.3 %shard_map.342 = (bf16[8,128,2048]{2,1,0:T(8,128)(2,1)}, bf16[4,8,64,512]{3,2,1,0:T(8,128)(2,1)S(1)}, bf16[4,8,64,640]{3,2,1,0:T(8,128)(2,1)}, s32[4,128,128]{2,1,0:T(8,128)S(1)}, bf16[4,128,2048]{2,1,0:T(8,128)(2,1)S(1)}) custom-call(bf16[128,2048]{1,0:T(8,128)(2,1)S(1)} %copy-done.2, bf16[8,64,512]{2,1,0:T(8,128)(2,1)S(1)} %copy-done.11, ...), custom_call_target="tpu_custom_call" | custom-call | tf_op jit(solution)/shard_map/pallas_call | solution.py:279
  150.0 4.7 subtract_convert_fusion
  167.3 4.5 fusion.112
  180.5 5.5 fusion.18
  206.2 5.1 convolution_convert_fusion.6
  211.3 6.4 all_to_all.20
  221.2 264.8 %shard_map.343 = (f32[128,2048]{1,0:T(8,128)S(1)}, bf16[4,128,2048]{2,1,0:T(8,128)(2,1)S(1)}, bf16[4,256,2048]{2,1,0:T(8,128)(2,1)}, bf16[8,4,64,1408]{3,2,1,0:T...) custom-call(bf16[8,128,2048]{2,1,0:T(8,128)(2,1)} %bitcast.282, ...), custom_call_target="tpu_custom_call" | custom-call | tf_op jit(solution)/shard_map/pallas_call | solution.py:469
  486.0 4.7 fusion.115
  499.8 4.6 copy.513
  508.1 6.5 copy.504
  514.6 5.0 convolution_convert_fusion.9
  519.7 4.6 copy.514
  527.6 5.2 convolution_convert_fusion.5
  541.4 5.1 convolution_convert_fusion.8
  546.5 5.0 copy.515
  551.9 5.9 fusion.117
  560.7 5.9 fusion.118
  566.6 4.0 fusion.119
  570.6 17.1 %collective-permute-done.1 = bf16[256,2048]{1,0:T(8,128)(2,1)} collective-permute-done((bf16[256,2048]{1,0:T(8,128)(2,1)}, bf16[256,2048]{1,0:T(8,128)(2,1)}, u32[]{:S(2)}, u32[]{:S(2)}) %collective-permute-start.1) | collective-permute-done | bytes 1048608 | tf_op jit(solution)/shard_map/ppermute | solution.py:923
  595.8 8.4 fusion.113
  604.3 13.0 fusion.99
  617.3 16.2 %multiply_convert_fusion.2 = (bf16[1024,1408]{1,0:T(8,128)(2,1)}, bf16[1024,1408]{1,0:T(8,128)(2,1)S(1)}, bf16[1024,1408]{1,0:T(8,128)(2,1)}) fusion(f32[1024,1408]{1,0:T(8,128)} %fusion.99, f32[1024,1408]{1,0:T(8,128)} %fusion.113, bf16[2048,1408]{1,0:T(8,128)(2,1)} %bitcast.393, bf16[256,2048]{1,0:T(8,128)(2,1)} %collective-permute-done.2, ...), kind=kOutput, calls=%fused_computation.20 | convolution fusion | flops 5945425920 | bytes 30146560 | tf_op jit(solution)/shard_map/dot_general | solution.py:56
  633.4 11.8 fusion.114
  645.2 11.1 add_convert_fusion
  660.6 7.3 convolution_convert_fusion.4
  670.2 8.7 convolution_convert_fusion.2
  678.8 10.6 convolution_convert_fusion.1
  689.5 10.6 convolution_convert_fusion
  700.1 13.0 collective-permute-done.8
  715.7 23.0 %collective-permute-done.6 = bf16[256,2048]{1,0:T(8,128)(2,1)S(1)} collective-permute-done((bf16[256,2048]{1,0:T(8,128)(2,1)S(1)}, bf16[256,2048]{1,0:T(8,128)(2,1)S(1)}, u32[]{:S(2)}, u32[]{:S(2)}) %collective-permute-start.6) | collective-permute-done | bytes 1048608 | tf_op jit(solution)/shard_map/ppermute | solution.py:923
  739.8 4.3 convert_multiply_fusion
  748.6 13.5 collective-permute-done.3
  762.1 8.9 add_convert_fusion.2
  771.6 3.6 concatenate.74.x_ref
  775.3 49.7 %shard_map.344 = f32[128,2176]{1,0:T(8,128)S(1)} custom-call(bf16[4,128,2176]{2,1,0:T(8,128)(2,1)S(1)} %concatenate.74.x_ref), custom_call_target="tpu_custom_call" | custom-call | tf_op jit(solution)/shard_map/pallas_call | solution.py:173
  827.9 4.2 add_convert_fusion.1
  832.2 57.5 %shard_map.345 = (bf16[8,128,2048]{2,1,0:T(8,128)(2,1)}, f32[128,2048]{1,0:T(8,128)S(1)}) custom-call(bf16[128,2048]{1,0:T(8,128)(2,1)S(1)} %get-tuple-element.203.x_ref, bf16[4,128,2048]{2,1,0:T(8,128)(2,1)S(1)} %bitcast.272), custom_call_target="tpu_custom_call" | custom-call | tf_op jit(solution)/shard_map/pallas_call | solution.py:641
  889.7 3.6 convolution_convert_fusion.16
  929.6 4.4 convolution_convert_fusion.3
  934.0 79.8 %shard_map.346 = (f32[128,2048]{1,0:T(8,128)S(1)}, f32[128,640]{1,0:T(8,128)S(1)}, bf16[1,2,8,64,1408]{4,3,2,1,0:T(8,128)(2,1)S(1)}) custom-call(bf16[8,128,2048]{2,1,0:T(8,128)(2,1)} %bitcast.305, bf16[8,128,640]{2,1,0:T(8,128)(2,1)S(1)} %bitcast.263, bf16[8,4,64,1408]{3,2,1,0:T(8,128)(2,1)} %bitcast.290), custom_call_target="tpu_custom_call" | custom-call | tf_op jit(solution)/shard_map/pallas_call | solution.py:725
  1016.9 12.1 shard_map.347
  1037.5 4.9 concatenate.79
  1045.1 5.0 all-to-all-start.2
  1054.8 3.6 fusion.15
  1064.5 3.9 all-to-all-start.1
  1075.5 227.1 %shard_map.348 = (bf16[4,8,64,512]{3,2,1,0:T(8,128)(2,1)}, bf16[4,64,2048]{2,1,0:T(8,128)(2,1)S(1)}, bf16[4,64,640]{2,1,0:T(8,128)(2,1)S(1)}, bf16[4,64,704]{2,1...) custom-call(bf16[4,8,64,512]{3,2,1,0:T(8,128)(2,1)} %pad_maximum_fus, ...), custom_call_target="tpu_custom_call" | custom-call | tf_op jit(solution)/shard_map/pallas_call | solution.py:777
  1306.3 4.4 all-to-all-start.3
  1321.3 4.9 convert.89
  (599 shorter events, 226.6 us)
Async XLA Ops:
  7.2 204.1 %all-gather.3.cloned.1.call-start = ((), (), s32[]{:S(2)}) async-start(), calls=%async_computation.10 | async-start | bytes 1310720 | tf_op jit(solution)/shard_map/all_gather | solution.py:888
  18.3 119.5 %copy-start.5 = (bf16[128,2048]{1,0:T(8,128)(2,1)}, bf16[128,2048]{1,0:T(8,128)(2,1)S(1)}, u32[]{:S(2)}) copy-start(bf16[128,2048]{1,0:T(8,128)(2,1)S(1)} %copy.465.co_ref) | copy-start | bytes 1572868
  129.1 943.4 %reduce-scatter.4.cloned.1.call-start = ((), (), s32[]{:S(2)}) async-start(), calls=%async_computation.7 | async-start | bytes 3538944 | tf_op jit(solution)/shard_map/reduce_scatter | solution.py:1002
  189.4 338.2 %copy-start.101 = (s32[512,1]{0,1:T(1,128)}, s32[512,1]{0,1:T(1,128)S(1)}, u32[]{:S(2)}) copy-start(s32[512,1]{0,1:T(1,128)S(1)} %copy.543) | copy-start | bytes 6148
  194.9 332.7 %copy-start.95 = (s32[1024]{0:T(1024)}, s32[1024]{0:T(1024)S(1)}, u32[]{:S(2)}) copy-start(s32[1024]{0:T(1024)S(1)} %select_n.131) | copy-start | bytes 12292
  221.2 264.8 %copy-start.21 = (bf16[4,128,2048]{2,1,0:T(8,128)(2,1)S(1)}, bf16[4,128,2048]{2,1,0:T(8,128)(2,1)}, u32[]{:S(2)}) copy-start(bf16[4,128,2048]{2,1,0:T(8,128)(2,1)} %copy-done.19) | copy-start | bytes 6291460
  486.0 65.8 %copy-start = (f32[128,2048]{1,0:T(8,128)}, f32[128,2048]{1,0:T(8,128)S(1)}, u32[]{:S(2)}) copy-start(f32[128,2048]{1,0:T(8,128)S(1)} %get-tuple-element.50) | copy-start | bytes 3145732
  504.5 568.0 %reduce-scatter.6.cloned.1.call-start = ((), (), s32[]{:S(2)}) async-start(), calls=%async_computation.8 | async-start | bytes 3538944 | tf_op jit(solution)/shard_map/reduce_scatter | solution.py:1002
  506.9 80.7 %copy-start.70 = (bf16[2048,16]{0,1:T(8,128)(2,1)}, bf16[2048,16]{0,1:T(8,128)(2,1)S(1)}, u32[]{:S(2)}) copy-start(bf16[2048,16]{0,1:T(8,128)(2,1)S(1)} %reshape.819) | copy-start | bytes 196612
  524.3 548.2 %reduce-scatter.8.cloned.1.call-start = ((), (), s32[]{:S(2)}) async-start(), calls=%async_computation.9 | async-start | bytes 3538944 | tf_op jit(solution)/shard_map/reduce_scatter | solution.py:1002
  524.6 33.2 %copy-start.130 = (pred[16]{0:T(512)(128)(4,1)}, pred[16]{0:T(512)(128)(4,1)S(1)}, u32[]{:S(2)}) copy-start(pred[16]{0:T(512)(128)(4,1)S(1)} %iota_compare_fusion.4) | copy-start | bytes 52
  524.6 33.2 %copy-start.120 = (pred[16]{0:T(512)(128)(4,1)}, pred[16]{0:T(512)(128)(4,1)S(1)}, u32[]{:S(2)}) copy-start(pred[16]{0:T(512)(128)(4,1)S(1)} %get-tuple-element.270) | copy-start | bytes 52
  524.7 33.2 %copy-start.122 = (pred[16]{0:T(512)(128)(4,1)}, pred[16]{0:T(512)(128)(4,1)S(1)}, u32[]{:S(2)}) copy-start(pred[16]{0:T(512)(128)(4,1)S(1)} %get-tuple-element.271) | copy-start | bytes 52
  535.0 35.6 %collective-permute-start.2 = (bf16[256,2048]{1,0:T(8,128)(2,1)}, bf16[256,2048]{1,0:T(8,128)(2,1)}, u32[]{:S(2)}, u32[]{:S(2)}) collective-permute-start(bf16[256,2048]{1,0:T(8,128)(2,1)} %get-tuple-element.217), channel_id=1, source_target_pairs={{0,6},{1,7},{2,0},{3,1},{4,2},{5,3},{6,4},{7,5},{8,14},{9,15},{10,... | collective-permute-start | bytes 3145736 | tf_op jit(solution)/shard_map/ppermute | solution.py:923
  535.6 52.0 %collective-permute-start.1 = (bf16[256,2048]{1,0:T(8,128)(2,1)}, bf16[256,2048]{1,0:T(8,128)(2,1)}, u32[]{:S(2)}, u32[]{:S(2)}) collective-permute-start(bf16[256,2048]{1,0:T(8,128)(2,1)} %get-tuple-element.218), channel_id=1, source_target_pairs={{0,4},{1,5},{2,6},{3,7},{4,0},{5,1},{6,2},{7,3},{8,12},{9,13},{10,... | collective-permute-start | bytes 3145736 | tf_op jit(solution)/shard_map/ppermute | solution.py:923
  536.5 51.2 %collective-permute-start = (bf16[256,2048]{1,0:T(8,128)(2,1)}, bf16[256,2048]{1,0:T(8,128)(2,1)}, u32[]{:S(2)}, u32[]{:S(2)}) collective-permute-start(bf16[256,2048]{1,0:T(8,128)(2,1)} %get-tuple-element.219), channel_id=1, source_target_pairs={{0,2},{1,3},{2,4},{3,5},{4,6},{5,7},{6,0},{7,1},{8,10},{9,11},{10,... | collective-permute-start | bytes 3145736 | tf_op jit(solution)/shard_map/ppermute | solution.py:923
  658.3 90.4 %collective-permute-start.5 = (bf16[256,2048]{1,0:T(8,128)(2,1)}, bf16[256,2048]{1,0:T(8,128)(2,1)}, u32[]{:S(2)}, u32[]{:S(2)}) collective-permute-start(bf16[256,2048]{1,0:T(8,128)(2,1)} %get-tuple-element.213), channel_id=1, source_target_pairs={{0,2},{1,3},{2,4},{3,5},{4,6},{5,7},{6,0},{7,1},{8,10},{9,11},{10,... | collective-permute-start | bytes 3145736 | tf_op jit(solution)/shard_map/ppermute | solution.py:923
  659.3 89.3 %collective-permute-start.4 = (bf16[256,2048]{1,0:T(8,128)(2,1)}, bf16[256,2048]{1,0:T(8,128)(2,1)}, u32[]{:S(2)}, u32[]{:S(2)}) collective-permute-start(bf16[256,2048]{1,0:T(8,128)(2,1)} %get-tuple-element.214), channel_id=1, source_target_pairs={{0,4},{1,5},{2,6},{3,7},{4,0},{5,1},{6,2},{7,3},{8,12},{9,13},{10,... | collective-permute-start | bytes 3145736 | tf_op jit(solution)/shard_map/ppermute | solution.py:923
  668.5 70.3 %copy-start.64 = (bf16[256,2048]{1,0:T(8,128)(2,1)}, bf16[256,2048]{1,0:T(8,128)(2,1)S(1)}, u32[]{:S(2)}) copy-start(bf16[256,2048]{1,0:T(8,128)(2,1)S(1)} %get-tuple-element.208) | copy-start | bytes 3145732
  668.5 44.7 %collective-permute-start.8 = (bf16[256,2048]{1,0:T(8,128)(2,1)S(1)}, bf16[256,2048]{1,0:T(8,128)(2,1)S(1)}, u32[]{:S(2)}, u32[]{:S(2)}) collective-permute-start(bf16[256,2048]{1,0:T(8,128)(2,1)S(1)} %get-tuple-element.209), channel_id=1, source_target_pairs={{0,2},{1,3},{2,4},{3,5},{4,6},{5,7},{6,0},{7,1},{8,10},{9,11},{10,... | collective-permute-start | bytes 3145736 | tf_op jit(solution)/shard_map/ppermute | solution.py:923
  668.8 46.9 %collective-permute-start.7 = (bf16[256,2048]{1,0:T(8,128)(2,1)S(1)}, bf16[256,2048]{1,0:T(8,128)(2,1)S(1)}, u32[]{:S(2)}, u32[]{:S(2)}) collective-permute-start(bf16[256,2048]{1,0:T(8,128)(2,1)S(1)} %get-tuple-element.210), channel_id=1, source_target_pairs={{0,4},{1,5},{2,6},{3,7},{4,0},{5,1},{6,2},{7,3},{8,12},{9,13},{10,... | collective-permute-start | bytes 3145736 | tf_op jit(solution)/shard_map/ppermute | solution.py:923
  669.6 69.2 %collective-permute-start.6 = (bf16[256,2048]{1,0:T(8,128)(2,1)S(1)}, bf16[256,2048]{1,0:T(8,128)(2,1)S(1)}, u32[]{:S(2)}, u32[]{:S(2)}) collective-permute-start(bf16[256,2048]{1,0:T(8,128)(2,1)S(1)} %get-tuple-element.211), channel_id=1, source_target_pairs={{0,6},{1,7},{2,0},{3,1},{4,2},{5,3},{6,4},{7,5},{8,14},{9,15},{10,... | collective-permute-start | bytes 3145736 | tf_op jit(solution)/shard_map/ppermute | solution.py:923
  689.5 50.3 %copy-start.22 = (bf16[4,128,2048]{2,1,0:T(8,128)(2,1)S(1)}, bf16[4,128,2048]{2,1,0:T(8,128)(2,1)}, u32[]{:S(2)}) copy-start(bf16[4,128,2048]{2,1,0:T(8,128)(2,1)} %copy-done.19) | copy-start | bytes 6291460
  689.5 50.3 %copy-start.96 = (s32[1024]{0:T(1024)S(1)}, s32[1024]{0:T(1024)}, u32[]{:S(2)}) copy-start(s32[1024]{0:T(1024)} %copy-done.95) | copy-start | bytes 12292
  689.5 50.3 %copy-start.102 = (s32[512,1]{0,1:T(1,128)S(1)}, s32[512,1]{0,1:T(1,128)}, u32[]{:S(2)}) copy-start(s32[512,1]{0,1:T(1,128)} %copy-done.101) | copy-start | bytes 6148
  689.5 50.3 %copy-start.105 = (s32[512,1]{0,1:T(1,128)S(1)}, s32[512,1]{0,1:T(1,128)}, u32[]{:S(2)}) copy-start(s32[512,1]{0,1:T(1,128)} %copy.542) | copy-start | bytes 6148
  689.5 50.3 %copy-start.108 = (s32[512,1]{0,1:T(1,128)S(1)}, s32[512,1]{0,1:T(1,128)}, u32[]{:S(2)}) copy-start(s32[512,1]{0,1:T(1,128)} %copy.541) | copy-start | bytes 6148
  689.5 50.3 %copy-start.111 = (s32[512,1]{0,1:T(1,128)S(1)}, s32[512,1]{0,1:T(1,128)}, u32[]{:S(2)}) copy-start(s32[512,1]{0,1:T(1,128)} %copy.540) | copy-start | bytes 6148
  689.5 50.3 %copy-start.114 = (s32[512,1]{0,1:T(1,128)S(1)}, s32[512,1]{0,1:T(1,128)}, u32[]{:S(2)}) copy-start(s32[512,1]{0,1:T(1,128)} %copy.539) | copy-start | bytes 6148
  689.5 50.3 %copy-start.117 = (s32[512,1]{0,1:T(1,128)S(1)}, s32[512,1]{0,1:T(1,128)}, u32[]{:S(2)}) copy-start(s32[512,1]{0,1:T(1,128)} %copy.538) | copy-start | bytes 6148
  713.2 48.9 %collective-permute-start.3 = (bf16[256,2048]{1,0:T(8,128)(2,1)}, bf16[256,2048]{1,0:T(8,128)(2,1)}, u32[]{:S(2)}, u32[]{:S(2)}) collective-permute-start(bf16[256,2048]{1,0:T(8,128)(2,1)} %get-tuple-element.215), channel_id=1, source_target_pairs={{0,6},{1,7},{2,0},{3,1},{4,2},{5,3},{6,4},{7,5},{8,14},{9,15},{10,... | collective-permute-start | bytes 3145736 | tf_op jit(solution)/shard_map/ppermute | solution.py:923
  771.0 54.1 %copy-start.66 = (f32[512,16]{1,0:T(8,128)S(1)}, f32[512,16]{1,0:T(8,128)}, u32[]{:S(2)}) copy-start(f32[512,16]{1,0:T(8,128)} %get-tuple-element.202) | copy-start | bytes 98308
  771.0 54.3 %copy-start.1 = (f32[128,2048]{1,0:T(8,128)S(1)}, f32[128,2048]{1,0:T(8,128)}, u32[]{:S(2)}) copy-start(f32[128,2048]{1,0:T(8,128)} %copy-done) | copy-start | bytes 3145732
  771.0 54.3 %copy-start.88 = (f32[2048]{0:T(1024)S(1)}, f32[2048]{0:T(1024)}, u32[]{:S(2)}) copy-start(f32[2048]{0:T(1024)} %reshape.873) | copy-start | bytes 24580
  775.2 51.9 %copy-start.138 = (f32[128]{0:T(128)S(1)}, f32[128]{0:T(128)}, u32[]{:S(2)}) copy-start(f32[128]{0:T(128)} %copy-done.137) | copy-start | bytes 1540
  775.3 51.9 %copy-start.6 = (bf16[128,2048]{1,0:T(8,128)(2,1)S(1)}, bf16[128,2048]{1,0:T(8,128)(2,1)}, u32[]{:S(2)}) copy-start(bf16[128,2048]{1,0:T(8,128)(2,1)} %copy-done.5) | copy-start | bytes 1572868
  775.3 51.9 %copy-start.128 = (f32[128]{0:T(128)S(1)}, f32[128]{0:T(128)}, u32[]{:S(2)}) copy-start(f32[128]{0:T(128)} %fusion.83) | copy-start | bytes 1540
  827.9 61.7 %copy-start.33 = (bf16[2,2,64,2048]{3,2,0,1:T(8,128)(2,1)S(1)}, bf16[2,2,64,2048]{3,2,0,1:T(8,128)(2,1)}, u32[]{:S(2)}) copy-start(bf16[2,2,64,2048]{3,2,0,1:T(8,128)(2,1)} %copy-done.32) | copy-start | bytes 3145732
  934.0 82.5 %copy-start.37 = (f32[128,512]{1,0:T(8,128)S(1)}, f32[128,512]{1,0:T(8,128)}, u32[]{:S(2)}) copy-start(f32[128,512]{1,0:T(8,128)} %copy-done.36) | copy-start | bytes 786436
  934.0 82.6 %copy-start.129 = (f32[128]{0:T(128)S(1)}, f32[128]{0:T(128)}, u32[]{:S(2)}) copy-start(f32[128]{0:T(128)} %fusion.84) | copy-start | bytes 1540
  934.0 82.7 %copy-start.136 = (f32[128]{0:T(128)S(1)}, f32[128]{0:T(128)}, u32[]{:S(2)}) copy-start(f32[128]{0:T(128)} %copy-done.135) | copy-start | bytes 1540
  934.0 96.0 %copy-start.3 = (bf16[128,2048]{1,0:T(8,128)(2,1)S(1)}, bf16[128,2048]{1,0:T(8,128)(2,1)}, u32[]{:S(2)}) copy-start(bf16[128,2048]{1,0:T(8,128)(2,1)} %tok_ref.1) | copy-start | bytes 1572868
  934.0 96.0 %copy-start.53 = (bf16[4,8,64,640]{3,2,1,0:T(8,128)(2,1)S(1)}, bf16[4,8,64,640]{3,2,1,0:T(8,128)(2,1)}, u32[]{:S(2)}) copy-start(bf16[4,8,64,640]{3,2,1,0:T(8,128)(2,1)} %get-tuple-element.45) | copy-start | bytes 7864324
  934.0 96.0 %copy-start.86 = (f32[2048,1]{0,1:T(1,128)S(1)}, f32[2048,1]{0,1:T(1,128)}, u32[]{:S(2)}) copy-start(f32[2048,1]{0,1:T(1,128)} %copy-done.85) | copy-start | bytes 24580
  934.0 96.0 %copy-start.132 = (f32[128]{0:T(128)S(1)}, f32[128]{0:T(128)}, u32[]{:S(2)}) copy-start(f32[128]{0:T(128)} %fusion.85) | copy-start | bytes 1540
  1045.1 19.4 %all-to-all-start.2 = ((f32[8,1,16384]{2,1,0:T(1,128)}), f32[8,1,16384]{2,1,0:T(1,128)}, u32[]{:S(2)}, u32[]{:S(2)}) async-start(f32[8,1,16384]{2,1,0:T(1,128)} %reshape.942), calls=%async_computation.2 | async-start | bytes 1048576 | tf_op jit(solution)/shard_map/all_to_all | solution.py:1142
  1064.5 8.0 all-to-all-start.1
  1306.3 24.2 %all-to-all-start.3 = ((bf16[8,64,512]{2,1,0:T(8,128)(2,1)}), bf16[8,64,512]{2,1,0:T(8,128)(2,1)}, u32[]{:S(2)}, u32[]{:S(2)}) async-start(bf16[8,64,512]{2,1,0:T(8,128)(2,1)} %reduce_sum.342), calls=%async_computation.6 | async-start | bytes 1048576 | tf_op jit(solution)/shard_map/all_to_all | solution.py:1152
  (134 other events, 779.4 us)
Sparse Core Ops, SparseCore 0:
  129.2 28.2 all-gather.2
  504.6 76.6 reduce-scatter.3
  585.1 54.3 reduce-scatter.5
  642.7 123.1 reduce-scatter.7

commit v5 on v4

--- a/solution.py
+++ b/solution.py
@@ -160,10 +160,11 @@
         greet(group[1:])
         copies = []
         for i in range(1, inner):
-            copy = remote(x_ref.at[i], buf.at[i], send.at[i], recv.at[i], group[inner - i])
+            to = lax.rem(z + i, inner)
+            copy = remote(x_ref.at[to], buf.at[i], send.at[i], recv.at[i], group[i])
             copy.start()
             copies.append(copy)
-        o_ref[...] = x_ref[0].astype(F32)
+        o_ref[...] = x_ref[lax.rem(z, inner)].astype(F32)
         for i in range(1, inner):
             copies[i - 1].wait_recv()
             o_ref[...] += buf[i].astype(F32)
@@ -185,17 +186,16 @@
     return [(start + lax.rem(z - start + i, inner), e) for i in range(inner)]
 
 
-def first_exchange(tok, heads_w, pack, slot, cot, n_dp, n_ex, inner, collective_id):
+def first_exchange(tok, heads_w, pack, n_dp, n_ex, collective_id):
     chips = n_ex // 2
 
     def kernel(
-        tok_ref, wa_ref, pk_ref, sl_ref, co_ref, tok_out, wa_out, pk_out, sl_out, co_out,
+        tok_ref, wa_ref, pk_ref, tok_out, wa_out, pk_out,
         t_send, t_recv, ts_send, ts_recv, a_send, a_recv, az_send, az_recv,
-        p_send, p_recv, pf_send, pf_recv, ps_send, ps_recv, s_send, s_recv, c_send, c_recv, local,
+        p_send, p_recv, pf_send, pf_recv, ps_send, ps_recv, local,
     ):
         z, e, c, k, sibling, same_core, column = places(n_dp, n_ex)
         plane = [(z, lax.rem(e + i, n_ex)) for i in range(1, n_ex)]
-        group = column_group(z, e, inner)
         greet(plane + column)
         wa_far, pk_col, tok_far, near = [], [], [], []
         for i in range(1, n_ex):
@@ -209,10 +209,6 @@
             copy = remote(pk_ref, pk_out.at[z, e], p_send.at[i], p_recv.at[i], column[i - 1])
             copy.start()
             pk_col.append(copy)
-        for i in range(1, inner):
-            copy = remote(sl_ref, sl_out.at[i], s_send.at[i], s_recv.at[i], group[i])
-            copy.start()
-            near.append(copy)
         for i in range(1, chips):
             copy = remote(tok_ref, tok_out.at[e], t_send.at[i], t_recv.at[i], same_core[i - 1])
             copy.start()
@@ -224,8 +220,6 @@
             pltpu.make_async_copy(wa_ref.at[e], wa_out.at[z, e], local.at[0]),
             pltpu.make_async_copy(pk_ref, pk_out.at[z, e], local.at[1]),
             pltpu.make_async_copy(tok_ref, tok_out.at[e], local.at[2]),
-            pltpu.make_async_copy(sl_ref, sl_out.at[0], local.at[3]),
-            pltpu.make_async_copy(co_ref, co_out.at[0], local.at[4]),
         ]
         for copy in own:
             copy.start()
@@ -240,10 +234,6 @@
             )
             copy.start()
             wa_col.append(copy)
-        for i in range(1, inner):
-            copy = remote(co_ref, co_out.at[i], c_send.at[i], c_recv.at[i], group[i])
-            copy.start()
-            near.append(copy)
         for copy in pk_col:
             copy.wait_recv()
         pk_far = []
@@ -282,93 +272,130 @@
             jax.ShapeDtypeStruct((n_ex,) + tok.shape, tok.dtype),
             jax.ShapeDtypeStruct((n_dp,) + heads_w.shape, heads_w.dtype),
             jax.ShapeDtypeStruct((n_dp, n_ex) + pack.shape, pack.dtype),
-            jax.ShapeDtypeStruct((inner,) + slot.shape, slot.dtype),
-            jax.ShapeDtypeStruct((inner,) + cot.shape, cot.dtype),
         ],
-        in_specs=[ANY] * 5,
-        out_specs=[ANY] * 5,
+        in_specs=[ANY] * 3,
+        out_specs=[ANY] * 3,
         scratch_shapes=[dma((chips,))] * 4
         + [dma((n_ex,))] * 2
         + [dma((n_dp,))] * 4
         + [dma((chips,))] * 4
-        + [dma((inner,))] * 4
-        + [dma((5,))],
+        + [dma((3,))],
         compiler_params=params(collective_id),
-    )(tok, heads_w, pack, slot, cot)
+    )(tok, heads_w, pack)
+
+
+class ExpertsIn:
+    @staticmethod
+    def scratch(n_dp):
+        dma = pltpu.SemaphoreType.DMA
+        return [dma((n_dp, 2)), dma((n_dp,)), dma((n_dp,)), dma((n_dp,))]
+
+    @staticmethod
+    def out(weight, n_dp, n_ex):
+        return jax.ShapeDtypeStruct((n_ex, n_dp) + weight.shape[2:], BF)
+
+    def __init__(self, weight, out, scratch, n_dp, n_ex, inner):
+        self.weight, self.out, self.n_dp, self.inner = weight, out, n_dp, inner
+        self.send, self.recv, self.sib_send, self.sib_recv = scratch
+        self.z, self.e, self.c, self.k, self.sibling, _, _ = places(n_dp, n_ex)
+        self.hh = n_ex // 2
+        self.local = weight.shape[0]
+
+    def sends(self, start):
+        for i in list(range(1, self.n_dp)) + [0]:
+            to = lax.rem(self.z + i, self.n_dp)
+            expert = lax.rem(to, self.inner)
+
+            def go(i=i, to=to, expert=expert):
+                for h in range(2):
+                    src = self.weight.at[lax.rem(expert, self.local), pl.ds(h * self.hh, self.hh)]
+                    dst = self.out.at[pl.ds(h * self.hh, self.hh), self.z]
+                    sem = self.recv.at[self.z]
+
+                    def far(src=src, dst=dst, h=h):
+                        copy = remote(src, dst, self.send.at[i, h], sem, (to, 2 * self.c + h))
+                        if start:
+                            copy.start()
+                        else:
+                            copy.wait_send()
+
+                    if i:
+                        far()
+                    else:
+                        pl.when(self.k != h)(far)
+                        if start:
+
+                            @pl.when(self.k == h)
+                            def _(src=src, dst=dst):
+                                pltpu.make_async_copy(src, dst, sem).start()
+
+            pl.when(expert // self.local == self.k)(go)
+
+    def begin(self):
+        self.sends(True)
+
+    def pass_on(self):
+        mine = lax.rem(self.z, self.inner)
+        for i in range(self.n_dp):
+            d = lax.rem(self.z + self.n_dp - i, self.n_dp)
+            region = self.out.at[pl.ds(self.k * self.hh, self.hh), d]
+            if i:
+                wait_recv(region, self.recv.at[d], self.sibling)
+            else:
+                from_here = mine // self.local == self.k
+
+                @pl.when(from_here)
+                def _(region=region, d=d):
+                    src = self.weight.at[
+                        lax.rem(mine, self.local), pl.ds(self.k * self.hh, self.hh)
+                    ]
+                    pltpu.make_async_copy(src, region, self.recv.at[d]).wait()
+
+                @pl.when(jnp.logical_not(from_here))
+                def _(region=region, d=d):
+                    wait_recv(region, self.recv.at[d], self.sibling)
+
+            remote(
+                region, region, self.sib_send.at[i], self.sib_recv.at[i], self.sibling
+            ).start()
+
+    def end(self):
+        self.sends(False)
+        for i in range(self.n_dp):
+            d = lax.rem(self.z + self.n_dp - i, self.n_dp)
+            mine = self.out.at[pl.ds(self.k * self.hh, self.hh), d]
+            remote(
+                mine, mine, self.sib_send.at[i], self.sib_recv.at[i], self.sibling
+            ).wait_send()
+            region = self.out.at[pl.ds((1 - self.k) * self.hh, self.hh), d]
+            wait_recv(region, self.sib_recv.at[i], self.sibling)
 
 
 def forward_exchange(parts, tok, gain, slots, experts, shared, n_dp, n_ex, inner, collective_id):
     chips = n_ex // 2
-    hh = n_ex // 2
-    local_experts = experts[0].shape[0]
     rows, width = tok.shape
+    count = len(experts)
 
     def kernel(x_ref, tok_ref, gain_ref, slot_ref, *refs):
-        e_in, s_in = refs[:3], refs[3:6]
-        res_ref, xcol_ref, slot_out = refs[6:9]
-        w_out, s_out = refs[9:12], refs[12:15]
-        from_sib, out_buf, from_far, xbuf = refs[15:19]
+        e_in, s_in = refs[:count], refs[count : count + 3]
+        refs = refs[count + 3 :]
+        res_ref, xcol_ref, slot_out = refs[:3]
+        w_out, s_out = refs[3 : 3 + count], refs[3 + count : 6 + count]
+        refs = refs[6 + count :]
+        from_sib, out_buf, from_far, xbuf = refs[:4]
         (
-            near_s, near_r, far_s, far_r, x_s, x_r, g_s, g_r, we_s, we_r, wf_s, wf_r,
+            near_s, near_r, far_s, far_r, x_s, x_r, g_s, g_r,
             sh_s, sh_r, sp_s, sp_r, sf_s, sf_r, local,
-        ) = refs[19:]
+        ) = refs[4:19]
+        refs = refs[19:]
         z, e, c, k, sibling, same_core, column = places(n_dp, n_ex)
         group = column_group(z, e, inner)
-        sib_column = [(device[0], sibling[1]) for device in column]
-        greet(same_core + [sibling] + column + sib_column)
+        greet(same_core + [sibling] + column + [(device[0], sibling[1]) for device in column])
         my_l = lax.rem(z, inner)
-
-        def expert_sends(m, start):
-            for i in list(range(1, n_dp)) + [0]:
-                to = lax.rem(z + i, n_dp)
-                expert = lax.rem(to, inner)
-
-                def go(i=i, to=to, expert=expert):
-                    for h in range(2):
-                        src = e_in[m].at[lax.rem(expert, local_experts), pl.ds(h * hh, hh)]
-                        dst = w_out[m].at[pl.ds(h * hh, hh), z]
-
-                        def far(src=src, dst=dst, h=h):
-                            copy = remote(
-                                src, dst, we_s.at[m, i, h], we_r.at[m, z], (to, 2 * c + h)
-                            )
-                            if start:
-                                copy.start()
-                            else:
-                                copy.wait_send()
-
-                        if i:
-                            far()
-                        else:
-                            pl.when(k != h)(far)
-                            if start:
-
-                                @pl.when(k == h)
-                                def _(src=src, dst=dst):
-                                    pltpu.make_async_copy(src, dst, we_r.at[m, z]).start()
-
-                pl.when(expert // local_experts == k)(go)
-
-        def expert_arrivals(m):
-            for i in range(n_dp):
-                d = lax.rem(z + n_dp - i, n_dp)
-                region = w_out[m].at[pl.ds(k * hh, hh), d]
-                if i:
-                    wait_recv(region, we_r.at[m, d], sibling)
-                else:
-                    from_here = my_l // local_experts == k
-
-                    @pl.when(from_here)
-                    def _(region=region, d=d):
-                        src = e_in[m].at[lax.rem(my_l, local_experts), pl.ds(k * hh, hh)]
-                        pltpu.make_async_copy(src, region, we_r.at[m, d]).wait()
-
-                    @pl.when(jnp.logical_not(from_here))
-                    def _(region=region, d=d):
-                        wait_recv(region, we_r.at[m, d], sibling)
-
-                remote(region, region, wf_s.at[m, i], wf_r.at[m, i], sibling).start()
-
+        matrices = [
+            ExpertsIn(e_in[m], w_out[m], refs[4 * m : 4 * m + 4], n_dp, n_ex, inner)
+            for m in range(count)
+        ]
         near = []
         for i in list(range(1, chips)) + [0]:
             chip = lax.rem(c + i, chips)
@@ -393,8 +420,7 @@
         own.append(pltpu.make_async_copy(slot_ref.at[0], slot_out.at[0], local.at[3]))
         for copy in own:
             copy.start()
-        expert_sends(0, True)
-        expert_sends(1, True)
+        matrices[0].begin()
         far = []
         for i in range(1, chips):
             chip = lax.rem(c + i, chips)
@@ -405,11 +431,6 @@
             copy = remote(out_buf.at[i], from_far.at[i], far_s.at[i], far_r.at[i], same_core[i - 1])
             copy.start()
             far.append(copy)
-        slot_copies = []
-        for i in range(1, chips):
-            copy = remote(slot_ref.at[i], slot_out.at[i], g_s.at[i], g_r.at[i], same_core[i - 1])
-            copy.start()
-            slot_copies.append(copy)
         near[chips - 1].wait_recv()
         res_ref[...] = x_ref[e].astype(F32) + from_sib[c].astype(F32) + tok_ref[...].astype(F32)
         for i in range(1, chips):
@@ -420,12 +441,18 @@
         xbuf[...] = (residual * scale * gain_ref[...]).astype(BF)
         x_copies = []
         for i in range(1, inner):
-            copy = remote(xbuf, xcol_ref.at[i], x_s.at[i], x_r.at[i], group[i])
+            copy = remote(xbuf, xcol_ref.at[my_l], x_s.at[i], x_r.at[i], group[i])
             copy.start()
             x_copies.append(copy)
-        x_own = pltpu.make_async_copy(xbuf, xcol_ref.at[0], local.at[4])
+        x_own = pltpu.make_async_copy(xbuf, xcol_ref.at[my_l], local.at[4])
         x_own.start()
-        expert_sends(2, True)
+        for matrix in matrices[1:]:
+            matrix.begin()
+        slot_copies = []
+        for i in range(1, chips):
+            copy = remote(slot_ref.at[i], slot_out.at[i], g_s.at[i], g_r.at[i], same_core[i - 1])
+            copy.start()
+            slot_copies.append(copy)
         for copy in own:
             copy.wait()
         for copy in shared_copies:
@@ -447,25 +474,22 @@
                 copy = remote(block, block, sf_s.at[m, i], sf_r.at[m, i], sibling)
                 copy.start()
                 to_sib.append(copy)
-        for m in range(3):
-            expert_arrivals(m)
+        for matrix in matrices:
+            matrix.pass_on()
         for copy in x_copies + slot_copies + to_sib:
             copy.wait()
         x_own.wait()
         for copy in plane + shared_copies + near + far:
             copy.wait_send()
-        for m in range(3):
-            expert_sends(m, False)
-            for i in range(n_dp):
-                d = lax.rem(z + n_dp - i, n_dp)
-                mine = w_out[m].at[pl.ds(k * hh, hh), d]
-                remote(mine, mine, wf_s.at[m, i], wf_r.at[m, i], sibling).wait_send()
-                region = w_out[m].at[pl.ds((1 - k) * hh, hh), d]
-                wait_recv(region, wf_r.at[m, i], sibling)
+        for matrix in matrices:
+            matrix.end()
 
     dma = pltpu.SemaphoreType.DMA
-    r, ff = experts[0].shape[2:]
+    r = shared[0].shape[1]
     ff_s = shared[0].shape[2]
+    scratch = []
+    for _ in experts:
+        scratch += ExpertsIn.scratch(n_dp)
     outs = pl.pallas_call(
         kernel,
         out_shape=[
@@ -473,22 +497,81 @@
             jax.ShapeDtypeStruct((inner, rows, width), BF),
             jax.ShapeDtypeStruct(slots.shape, BF),
         ]
-        + [jax.ShapeDtypeStruct((n_ex, n_dp, r, ff), BF)] * 3
+        + [ExpertsIn.out(w, n_dp, n_ex) for w in experts]
         + [jax.ShapeDtypeStruct((n_ex, n_dp, r, ff_s), BF)] * 3,
-        in_specs=[VMEM] * 3 + [ANY] * 7,
-        out_specs=[VMEM] + [ANY] * 8,
+        in_specs=[VMEM] * 3 + [ANY] * (4 + count),
+        out_specs=[VMEM] + [ANY] * (5 + count),
         scratch_shapes=[pltpu.VMEM((chips, rows, width), BF)] * 3
         + [pltpu.VMEM((rows, width), BF)]
         + [dma((chips,))] * 4
         + [dma((inner,))] * 2
         + [dma((chips,))] * 2
-        + [dma((3, n_dp, 2)), dma((3, n_dp)), dma((3, n_dp)), dma((3, n_dp))]
         + [dma((3, n_dp))] * 2
         + [dma((3, chips))] * 4
-        + [dma((5,))],
+        + [dma((5,))]
+        + scratch,
         compiler_params=params(collective_id),
     )(parts, tok, gain, slots, *experts, *shared)
-    return outs[0], outs[1], outs[2], outs[3:6], outs[6:9]
+    return outs[0], outs[1], outs[2], outs[3 : 3 + count], outs[3 + count :]
+
+
+def between(blocks, way, weights, totals, n_dp, n_ex, inner, collective_id):
+    chips = n_ex // 2
+    n_in, n_back = len(weights), len(totals)
+
+    def kernel(x_ref, *refs):
+        w_in, t_in = refs[:n_in], refs[n_in : n_in + n_back]
+        refs = refs[n_in + n_back :]
+        o_ref, w_out, t_out = refs[0], refs[1 : 1 + n_in], refs[1 + n_in : 1 + n_in + n_back]
+        refs = refs[1 + n_in + n_back :]
+        send, recv, local = refs[:3]
+        z, e, c, k, sibling, same_core, column = places(n_dp, n_ex)
+        greet(same_core + [sibling] + column + [(device[0], sibling[1]) for device in column])
+        refs = refs[3:]
+        works = [
+            ExpertsIn(w_in[m], w_out[m], refs[4 * m : 4 * m + 4], n_dp, n_ex, inner)
+            for m in range(n_in)
+        ]
+        refs = refs[4 * n_in :]
+        works += [
+            ExpertsBack(t_in[m], t_out[m], refs[7 * m : 7 * m + 7], n_dp, n_ex, inner)
+            for m in range(n_back)
+        ]
+        copies = []
+        for i in range(1, chips):
+            to = same_core[i - 1] if way > 0 else same_core[chips - i - 1]
+            copy = remote(x_ref.at[i], o_ref.at[i], send.at[i], recv.at[i], to)
+            copy.start()
+            copies.append(copy)
+        copy = pltpu.make_async_copy(x_ref.at[0], o_ref.at[0], local)
+        copy.start()
+        copies.append(copy)
+        for work in works:
+            work.begin()
+        for work in works:
+            work.pass_on()
+        for copy in copies:
+            copy.wait()
+        for work in works:
+            work.end()
+
+    dma = pltpu.SemaphoreType.DMA
+    scratch = [dma((chips,)), dma((chips,)), dma]
+    for _ in weights:
+        scratch += ExpertsIn.scratch(n_dp)
+    for total in totals:
+        scratch += ExpertsBack.scratch(total, n_dp, inner)
+    outs = pl.pallas_call(
+        kernel,
+        out_shape=[jax.ShapeDtypeStruct(blocks.shape, BF)]
+        + [ExpertsIn.out(w, n_dp, n_ex) for w in weights]
+        + [ExpertsBack.out(total, n_dp, inner) for total in totals],
+        in_specs=[ANY] * (1 + n_in + n_back),
+        out_specs=[ANY] * (1 + n_in + n_back),
+        scratch_shapes=scratch,
+        compiler_params=params(collective_id),
+    )(blocks, *weights, *totals)
+    return outs[0], outs[1:]
 
 
 class ExpertsBack:
@@ -558,7 +641,7 @@
     def here(self):
         return lax.rem(self.z, self.inner) // 2 == self.k
 
-    def middle(self):
+    def pass_on(self):
         for i in self.order():
             d = lax.rem(self.z + i, self.n_dp)
             self.near(i).wait_recv()
@@ -597,61 +680,6 @@
                     @pl.when(jnp.logical_not(here))
                     def _(region=region, o=o, j=j, h=h):
                         wait_recv(region, self.recv.at[o, j, h], self.sibling)
-
-
-def gather_and_sum(block, blocks, n_dp, n_ex, inner, collective_id):
-    chips = n_ex // 2
-
-    def kernel(x_ref, y_ref, o_ref, sum_ref, buf, send, recv, sib_send, sib_recv, c_send, c_recv, local):
-        z, e, c, k, sibling, same_core, _ = places(n_dp, n_ex)
-        group = column_group(z, e, inner)
-        greet(same_core + [sibling] + group[1:])
-        far, column = [], []
-        for i in range(1, chips):
-            copy = remote(x_ref, o_ref.at[e], send.at[i], recv.at[i], same_core[i - 1])
-            copy.start()
-            far.append(copy)
-        for i in range(1, inner):
-            copy = remote(y_ref.at[i], buf.at[i], c_send.at[i], c_recv.at[i], group[inner - i])
-            copy.start()
-            column.append(copy)
-        near = [remote(x_ref, o_ref.at[e], sib_send.at[0], sib_recv.at[0], sibling)]
-        near[0].start()
-        own = pltpu.make_async_copy(x_ref, o_ref.at[e], local)
-        own.start()
-        for i in range(1, chips):
-            source = lax.rem(c + chips - i, chips) * 2 + k
-            far[i - 1].wait_recv()
-            copy = remote(
-                o_ref.at[source], o_ref.at[source], sib_send.at[i], sib_recv.at[i], sibling
-            )
-            copy.start()
-            near.append(copy)
-        sum_ref[...] = y_ref[0].astype(F32)
-        for i in range(1, inner):
-            column[i - 1].wait_recv()
-            sum_ref[...] += buf[i].astype(F32)
-        own.wait()
-        for copy in far + column:
-            copy.wait_send()
-        for copy in near:
-            copy.wait()
-
-    dma = pltpu.SemaphoreType.DMA
-    return pl.pallas_call(
-        kernel,
-        out_shape=[
-            jax.ShapeDtypeStruct((n_ex,) + block.shape, block.dtype),
-            jax.ShapeDtypeStruct(blocks.shape[1:], F32),
-        ],
-        in_specs=[ANY, VMEM],
-        out_specs=[ANY, VMEM],
-        scratch_shapes=[pltpu.VMEM(blocks.shape, BF)]
-        + [dma((chips,))] * 4
-        + [dma((inner,))] * 2
-        + [dma],
-        compiler_params=params(collective_id),
-    )(block, blocks)
 
 
 def plane_sum(arrays, totals, n_dp, n_ex, inner, collective_id):
@@ -703,7 +731,7 @@
                 )
                 far[i, j].start()
         for back in backs:
-            back.middle()
+            back.pass_on()
         for j in range(count):
             near[0, j].wait_recv()
             o_refs[j][...] = x_refs[j][e].astype(F32) + bufs[3 * j][c].astype(F32)
@@ -734,56 +762,147 @@
     return outs[:count], outs[count:]
 
 
-def last_exchange(arrays, totals, n_dp, n_ex, inner, collective_id):
-    count, extra = len(arrays), len(totals)
-
-    def kernel(*refs):
-        x_refs, t_refs = refs[:count], refs[count : count + extra]
-        refs = refs[count + extra :]
-        o_refs, back_refs = refs[:count], refs[count : count + extra]
-        refs = refs[count + extra :]
-        sems, local, rest = refs[: 2 * count], refs[2 * count], refs[2 * count + 1 :]
+def last_exchange(heads, wout, pack, shared, totals, n_dp, n_ex, inner, collective_id):
+    chips = n_ex // 2
+    extra = len(totals)
+    rows, cols = pack.shape[1:]
+    r = rows // n_dp
+
+    def kernel(heads_ref, wout_ref, pack_ref, *refs):
+        sh_in, t_refs = refs[:3], refs[3 : 3 + extra]
+        refs = refs[3 + extra :]
+        heads_out, wout_out, pack_out = refs[:3]
+        sh_out, back_refs = refs[3:6], refs[6 : 6 + extra]
+        refs = refs[6 + extra :]
+        hbuf, hsum, wbuf, psib, pout, pfar, psum, pbuf = refs[:8]
+        (
+            h_s, h_r, hp_s, hp_r, w_s, w_r, pn_s, pn_r, pf_s, pf_r, pc_s, pc_r, s_s, s_r, local,
+        ) = refs[8:23]
+        rest = refs[23:]
         z, e, c, k, sibling, same_core, column = places(n_dp, n_ex)
-        greet([sibling] + column + [(d[0], sibling[1]) for d in column])
+        plane = [(z, lax.rem(e + i, n_ex)) for i in range(1, n_ex)]
+        greet(plane + column + [(d[0], sibling[1]) for d in column])
         backs = [
             ExpertsBack(t_refs[m], back_refs[m], rest[7 * m : 7 * m + 7], n_dp, n_ex, inner)
             for m in range(extra)
         ]
+        near, far = [], []
+        for i in list(range(1, chips)) + [0]:
+            chip = lax.rem(c + i, chips)
+            copy = remote(
+                pack_ref.at[chip * 2 + 1 - k], psib.at[chip], pn_s.at[i], pn_r.at[i], sibling
+            )
+            copy.start()
+            near.append(copy)
+        heads_col, others = [], []
+        for i in range(1, n_dp):
+            to = lax.rem(z + i, n_dp)
+            copy = remote(heads_ref.at[to], hbuf.at[i], h_s.at[i], h_r.at[i], column[i - 1])
+            copy.start()
+            heads_col.append(copy)
         for back in backs:
             back.begin()
-        copies = []
-        for j in range(count):
-            for i in range(1, n_dp):
+        for i in range(1, chips):
+            chip = lax.rem(c + i, chips)
+            near[i - 1].wait_recv()
+            pout[i] = (
+                pack_ref[chip * 2 + k].astype(F32) + psib[chip].astype(F32)
+            ).astype(BF)
+            copy = remote(pout.at[i], pfar.at[i], pf_s.at[i], pf_r.at[i], same_core[i - 1])
+            copy.start()
+            far.append(copy)
+        near[chips - 1].wait_recv()
+        total = pack_ref[e].astype(F32) + psib[c].astype(F32)
+        for i in range(1, chips):
+            far[i - 1].wait_recv()
+            total = total + pfar[i].astype(F32)
+        psum[...] = total.astype(BF).reshape(n_dp, r, cols)
+        pack_col, wout_col = [], []
+        for i in range(1, n_dp):
+            to = lax.rem(z + i, n_dp)
+            copy = remote(psum.at[to], pbuf.at[i], pc_s.at[i], pc_r.at[i], column[i - 1])
+            copy.start()
+            pack_col.append(copy)
+            copy = remote(wout_ref.at[to], wbuf.at[i], w_s.at[i], w_r.at[i], column[i - 1])
+            copy.start()
+            wout_col.append(copy)
+            for m in range(3):
                 copy = remote(
-                    x_refs[j].at[lax.rem(z + i, n_dp)], o_refs[j].at[z],
-                    sems[2 * j].at[i], sems[2 * j + 1].at[i], column[i - 1],
+                    sh_in[m].at[to], sh_out[m].at[z], s_s.at[m, i], s_r.at[m, i], column[i - 1]
                 )
                 copy.start()
-                copies.append(copy)
-            copy = pltpu.make_async_copy(x_refs[j].at[z], o_refs[j].at[z], local.at[j])
-            copy.start()
-            copies.append(copy)
+                others.append(copy)
+        for m in range(3):
+            copy = pltpu.make_async_copy(sh_in[m].at[z], sh_out[m].at[z], local.at[m])
+            copy.start()
+            others.append(copy)
+        for copy in heads_col:
+            copy.wait_recv()
+        for j in range(n_ex):
+            block = heads_ref[z, j].astype(F32)
+            for i in range(1, n_dp):
+                block = block + hbuf[i, j].astype(F32)
+            hsum[j] = block.astype(BF)
+        heads_plane = []
+        for i in range(1, n_ex):
+            copy = remote(
+                hsum.at[lax.rem(e + i, n_ex)], heads_out.at[e], hp_s.at[i], hp_r.at[i],
+                plane[i - 1],
+            )
+            copy.start()
+            heads_plane.append(copy)
+        keep = pltpu.make_async_copy(hsum.at[e], heads_out.at[e], local.at[3])
+        keep.start()
         for back in backs:
-            back.middle()
-        for copy in copies:
+            back.pass_on()
+        for copy in wout_col + pack_col:
+            copy.wait_recv()
+        wout_sum = wout_ref[z].astype(F32)
+        pack_sum = psum[z].astype(F32)
+        for i in range(1, n_dp):
+            wout_sum = wout_sum + wbuf[i].astype(F32)
+            pack_sum = pack_sum + pbuf[i].astype(F32)
+        wout_out[...] = wout_sum
+        pack_out[...] = pack_sum
+        for copy in near + far + heads_col + wout_col + pack_col:
+            copy.wait_send()
+        keep.wait()
+        for copy in heads_plane + others:
             copy.wait()
         for back in backs:
             back.end()
 
     dma = pltpu.SemaphoreType.DMA
-    scratch = [dma((n_dp,))] * (2 * count) + [dma((count,))]
+    scratch = [
+        pltpu.VMEM(heads.shape, BF),
+        pltpu.VMEM(heads.shape[1:], BF),
+        pltpu.VMEM(wout.shape, BF),
+        pltpu.VMEM((chips, rows, cols), BF),
+        pltpu.VMEM((chips, rows, cols), BF),
+        pltpu.VMEM((chips, rows, cols), BF),
+        pltpu.VMEM((n_dp, r, cols), BF),
+        pltpu.VMEM((n_dp, r, cols), BF),
+        dma((n_dp,)), dma((n_dp,)), dma((n_ex,)), dma((n_ex,)), dma((n_dp,)), dma((n_dp,)),
+        dma((chips,)), dma((chips,)), dma((chips,)), dma((chips,)), dma((n_dp,)), dma((n_dp,)),
+        dma((3, n_dp)), dma((3, n_dp)), dma((4,)),
+    ]
     for total in totals:
         scratch += ExpertsBack.scratch(total, n_dp, inner)
     outs = pl.pallas_call(
         kernel,
-        out_shape=[jax.ShapeDtypeStruct(array.shape, array.dtype) for array in arrays]
+        out_shape=[
+            jax.ShapeDtypeStruct(heads.shape[1:], BF),
+            jax.ShapeDtypeStruct(wout.shape[1:], F32),
+            jax.ShapeDtypeStruct((r, cols), F32),
+        ]
+        + [jax.ShapeDtypeStruct(array.shape, BF) for array in shared]
         + [ExpertsBack.out(total, n_dp, inner) for total in totals],
-        in_specs=[ANY] * (count + extra),
-        out_specs=[ANY] * (count + extra),
+        in_specs=[VMEM] * 3 + [ANY] * (3 + extra),
+        out_specs=[ANY, VMEM, VMEM] + [ANY] * (3 + extra),
         scratch_shapes=scratch,
         compiler_params=params(collective_id),
-    )(*arrays, *totals)
-    return outs[:count], outs[count:]
+    )(heads, wout, pack, *shared, *totals)
+    return outs[0], outs[1], outs[2], outs[3:6], outs[6:]
 
 
 def shards(
@@ -855,7 +974,12 @@
     we_send = we_send.reshape(rl, n_ex, kv_cols).transpose(1, 0, 2)
     we_send = we_send.reshape(n_ex, r, rl * kv_cols // r)
     wa_send = jnp.concatenate([wq_send, we_send], axis=-1)
-    pack_cols = (lat + n_experts + 3 + 127) // 128 * 128
+    slot_own = slot_places(routes, place_order[0], capacity)
+    slot_place = jnp.where(slot_own >= 0, slot_own - routes * capacity, -1)
+    slot_cols = 2 * rows * top_k // r
+    slot_pack = jnp.stack([routes, slot_place]).astype(BF).reshape(2, r, slot_cols // 2)
+    small_cols = lat + n_experts + 3
+    pack_cols = (small_cols + slot_cols + 127) // 128 * 128
     pack = jnp.concatenate(
         [
             w_latent,
@@ -863,17 +987,14 @@
             attn_gain[:, None],
             ffn_gain[:, None],
             jnp.pad(latent_gain, (0, r - rl))[:, None],
-            jnp.zeros((r, pack_cols - lat - n_experts - 3), BF),
+            slot_pack[0],
+            slot_pack[1],
+            jnp.zeros((r, pack_cols - small_cols - slot_cols), BF),
         ],
         axis=1,
     )
-    slot_own = jnp.pad(
-        slot_places(routes, place_order[0], capacity), ((0, 0), (0, 128 - top_k))
-    )
     cot_owner = to_owner_order(cotangent)
-    tok_all, wa_all, pk_all, slot_col, cot_col = first_exchange(
-        tokens, wa_send, pack, slot_own, cot_owner, n_dp, n_ex, inner, 1
-    )
+    tok_all, wa_all, pk_all = first_exchange(tokens, wa_send, pack, n_dp, n_ex, 1)
     wq = wa_all[..., :head_cols].reshape(width, head_cols)
     wexp = wa_all[..., head_cols:].reshape(KVR, kv_cols)
     pk_flat = pk_all.reshape(width, pack_cols)
@@ -896,11 +1017,18 @@
     )
     wo_rows = wo_rows.transpose(1, 0, 2, 3).reshape(hp * DV, width)
 
-    cot_col = cot_col.reshape(inner * rows, width)
+    col_groups = [[o * inner + i for i in range(inner)] for o in range(n_dp // inner)]
+    cot_send, _ = lax.optimization_barrier((cot_owner, wo_col))
+    cot_col = lax.all_gather(cot_send, "dp", axis=0, tiled=True, axis_index_groups=col_groups)
     slots_all = n_experts * capacity
-    slot_ids = slot_col[..., :top_k]
+    slot_col = pick(pk_all[..., small_cols : small_cols + slot_cols], e, 1)
+    slot_col = lax.dynamic_slice_in_dim(slot_col, z - my_local, inner, 0).astype(jnp.int32)
+    slot_col = slot_col.reshape(inner, r, 2, slot_cols // 2).transpose(2, 0, 1, 3)
+    slot_col = slot_col.reshape(2, inner, rows, top_k)
     slot_ids = jnp.where(
-        slot_ids >= 0, slot_ids + (jnp.arange(inner) * slots_all)[:, None, None], -1
+        slot_col[1] >= 0,
+        slot_col[0] * capacity + slot_col[1] + (jnp.arange(inner) * slots_all)[:, None, None],
+        -1,
     ).reshape(inner * rows, top_k)
     place = jnp.arange(cap)
     far_experts = [lax.rem(chip + m, chips) * inner + my_local for m in range(chips)]
@@ -915,11 +1043,11 @@
     hot = sum((wanted[:, None] == slot_ids[None, :, j]).astype(BF) for j in range(top_k))
     hot_t = sum((slot_ids[:, j][:, None] == wanted[None, :]).astype(BF) for j in range(top_k))
 
-    def between(values, way):
+    def through(values):
         cut = values.reshape(chips, per_far, -1)
         got = [cut[0]]
         for m in range(1, chips):
-            perm = [(i, (i + 2 * m * way) % n_ex) for i in range(n_ex)]
+            perm = [(i, (i - 2 * m) % n_ex) for i in range(n_ex)]
             got.append(lax.ppermute(cut[m], "expert", perm))
         return jnp.concatenate(got, axis=0)
 
@@ -962,25 +1090,35 @@
         attended.append(mm(low, expanded[:, h, DH:]).astype(BF))
     attended = jnp.concatenate(attended, axis=1)
     out_part = mm(attended, wo_rows).astype(BF)
-    residual, x_col, grad_in, (wg, wu, wd), (sgate, sup, sdown) = forward_exchange(
+    residual, x_col, grad_in, (wg, wu), (sgate, sup, sdown) = forward_exchange(
         out_part.reshape(n_ex, rows, width),
         to_owner_order(tokens),
         gain_two[None],
         grad_send,
-        [w.reshape(-1, n_ex, r, ff_e) for w in (expert_gate, expert_up, expert_down)],
+        [w.reshape(-1, n_ex, r, ff_e) for w in (expert_gate, expert_up)],
         [w.reshape(r, inner, ff_s).transpose(1, 0, 2) for w in (shared_gate, shared_up, shared_down)],
         n_dp,
         n_ex,
         inner,
         2,
     )
-    wg, wu, wd = (w.reshape(width, ff_e) for w in (wg, wu, wd))
     sgate, sup, sdown = (w.reshape(width, ff_s) for w in (sgate, sup, sdown))
-    hidden_two = x_col[0]
+    hidden_two = pick(x_col, my_local)
     x_col = x_col.reshape(inner * rows, width)
     grad_in = grad_in.reshape(n_slots, width)
 
-    x_in = between(mm(hot, x_col).astype(BF), 1)
+    x_in, (wd,) = between(
+        mm(hot, x_col).astype(BF).reshape(chips, per_far, width),
+        1,
+        [expert_down.reshape(-1, n_ex, r, ff_e)],
+        [],
+        n_dp,
+        n_ex,
+        inner,
+        8,
+    )
+    x_in = x_in.reshape(n_slots, width)
+    wg, wu, wd = (w.reshape(width, ff_e) for w in (wg, wu, wd))
 
     def probs_of(logits):
         top = jnp.max(logits, axis=-1, keepdims=True)
@@ -998,12 +1136,6 @@
         mm_rows(x_col, grad_sb).astype(BF),
         mm_rows(cot_col, shared_hidden).astype(BF),
     ]
-    shared_sums = [
-        lax.psum_scatter(
-            grad.reshape(n_ex, n_dp, r, ff_s), "expert", scatter_dimension=0, tiled=True
-        ).reshape(n_dp, r, ff_s)
-        for grad in shared_grads
-    ]
     shared_dx = mm_cols(grad_sa, sgate) + mm_cols(grad_sb, sup)
 
     slot_probs = probs_of(mm(x_in, router))
@@ -1016,14 +1148,24 @@
     expert_b = mm(x_in, wu)
     expert_hidden, expert_back = jax.vjp(swiglu, expert_a, expert_b)
     expert_hidden = expert_hidden.astype(BF)
-    rows_back = between(mm_cols(expert_hidden, wd).astype(BF), -1)
+    rows_back = through(mm_cols(expert_hidden, wd).astype(BF))
     slot_grad = (slot_gate * grad_in.astype(F32)).astype(BF)
     grad_ea, grad_eb = (v.astype(BF) for v in expert_back(mm(slot_grad, wd)))
-    dx_back = between((mm_cols(grad_ea, wg) + mm_cols(grad_eb, wu)).astype(BF), -1)
     expert_totals = [
         mm_rows(left, right).astype(BF).reshape(n_ex, n_dp, r, ff_e)
         for left, right in ((x_in, grad_ea), (x_in, grad_eb), (slot_grad, expert_hidden))
     ]
+    dx_back, (down_back,) = between(
+        (mm_cols(grad_ea, wg) + mm_cols(grad_eb, wu)).astype(BF).reshape(chips, per_far, width),
+        -1,
+        [],
+        expert_totals[2:],
+        n_dp,
+        n_ex,
+        inner,
+        9,
+    )
+    dx_back = dx_back.reshape(n_slots, width)
 
     col_probs = probs_of(mm(x_col, router))
     expert_axis = jnp.arange(n_experts)[None, :]
@@ -1046,7 +1188,7 @@
         [dx_col, grad_probs_col, jnp.zeros((inner * rows, 128 - n_experts), F32)], axis=1
     ).astype(BF)
     dx_sum = column_sum(dx_send.reshape(inner, rows, width + 128), n_dp, n_ex, inner, 3)
-    router_probs = col_probs[:rows]
+    router_probs = lax.dynamic_slice_in_dim(col_probs, my_local * rows, rows, 0)
     grad_probs = dx_sum[:, width : width + n_experts]
     grad_logits = (
         router_probs * (grad_probs - jnp.sum(grad_probs * router_probs, axis=-1, keepdims=True))
@@ -1057,11 +1199,18 @@
     grad_resid_norm, grad_gain_two = norm_two_back(grad_hidden_two)
     grad_residual = cot_owner.astype(F32) + grad_resid_norm
 
-    grad_attn, out_sum = gather_and_sum(
-        grad_residual.astype(BF), out_col.reshape(inner, rows, width), n_dp, n_ex, inner, 4
-    )
-    out_tokens = from_owner_order((residual + out_sum).astype(BF))
-    grad_attn = grad_attn.reshape(seq, width)
+    grad_attn = plane_gather(grad_residual.astype(BF), n_dp, n_ex, 4).reshape(seq, width)
+    out_sum = lax.psum_scatter(
+        out_col, "dp", scatter_dimension=0, tiled=True, axis_index_groups=col_groups
+    )
+    out_tokens = from_owner_order((residual + out_sum.astype(F32)).astype(BF))
+    shared_grads, _ = lax.optimization_barrier((shared_grads, grad_attn))
+    shared_sums = [
+        lax.psum_scatter(
+            grad.reshape(n_ex, n_dp, r, ff_s), "expert", scatter_dimension=0, tiled=True
+        ).reshape(n_dp, r, ff_s)
+        for grad in shared_grads
+    ]
     grad_attended = mm_cols(grad_attn, wo_rows).astype(BF)
     grad_wout = mm_rows(attended, grad_attn).astype(BF)
     grad_rope = 0.0
@@ -1082,9 +1231,9 @@
     grad_latent_part = jnp.concatenate([mm_cols(grad_expanded, wexp), grad_rope], axis=1)
     grad_latent_part = jnp.pad(grad_latent_part, ((0, 0), (0, -lat % 128))).astype(BF)
     grad_query_part = mm_cols(grad_query_low, wq).astype(BF)
-    (grad_query_sum, grad_latent_sum), (down_back,) = plane_sum(
+    (grad_query_sum, grad_latent_sum), (gate_back,) = plane_sum(
         [grad_query_part.reshape(n_ex, rows, width), grad_latent_part.reshape(n_ex, rows, -1)],
-        expert_totals[2:],
+        expert_totals[:1],
         n_dp,
         n_ex,
         inner,
@@ -1123,40 +1272,37 @@
     grad_we = mm_rows(latent_low, grad_expanded).astype(BF)
     grad_we = grad_we.reshape(n_dp, n_ex, r, rl * kv_cols // r)
     heads_grad = jnp.concatenate([grad_wq, grad_we], axis=-1)
-    latent_plane = plane_gather(grad_latent_low, n_dp, n_ex, 6).reshape(seq, lat)
-    grad_wlat = pick(mm_rows(hidden_one, latent_plane).reshape(n_dp, n_ex, r, lat), e, 1)
+    hidden_own = lax.dynamic_slice_in_dim(hidden_one, own_start, rows, 0)
 
     def by_owner(values):
         return values.reshape(n_ex, n_dp, r, -1).transpose(1, 0, 2, 3)
 
-    small = jnp.concatenate(
+    pack_grad = jnp.concatenate(
         [
+            mm_rows(hidden_own, grad_latent_low).reshape(n_dp, n_ex, r, lat),
             by_owner(grad_router),
             grad_gain_one.reshape(n_dp, n_ex, r, 1),
             by_owner(grad_gain_two),
             jnp.pad(grad_gain_lat.reshape(n_dp, n_ex, rl, 1), ((0, 0),) * 2 + ((0, r - rl), (0, 0))),
-            jnp.zeros((n_dp, n_ex, r, pack_cols - lat - n_experts - 3), F32),
+            jnp.zeros((n_dp, n_ex, r, -small_cols % 128), F32),
         ],
         axis=-1,
-    ).transpose(1, 0, 2, 3)
-    small = jnp.sum(lax.all_to_all(small, "expert", 0, 0, tiled=True), axis=0)
-    pack_grad = jnp.concatenate([grad_wlat, small], axis=-1).astype(BF)
-    (heads_got, wout_got, pack_got, *shared_got), (gate_back, up_back) = last_exchange(
-        [heads_grad, wout_back, pack_grad] + shared_sums, expert_totals[:2], n_dp, n_ex, inner, 7
+    ).astype(BF)
+    pack_grad = pack_grad.transpose(1, 0, 2, 3).reshape(n_ex, n_dp * r, -1)
+    heads_all, sum_wout, pack_sum, shared_got, (up_back,) = last_exchange(
+        heads_grad, wout_back, pack_grad, shared_sums, expert_totals[1:2], n_dp, n_ex, inner, 7
     )
 
     def added(values):
         return jnp.sum(values.astype(F32), axis=0)
 
-    heads_sum = added(heads_got).astype(BF)
-    heads_all = lax.all_to_all(heads_sum, "expert", 0, 0, tiled=True).astype(F32)
+    heads_all = heads_all.astype(F32)
     sum_wq = heads_all[..., :head_cols].transpose(1, 0, 2).reshape(r, H, DH + DR)
     sum_wq = jnp.take(sum_wq, jnp.array(heads_back), axis=1).reshape(r, H * (DH + DR))
     sum_we = heads_all[..., head_cols:].reshape(n_ex, rl, kv_cols).transpose(1, 0, 2)
     sum_we = jnp.take(sum_we.reshape(rl, H, DH + DV), jnp.array(heads_back), axis=1)
     sum_we = sum_we.reshape(rl, H * (DH + DV))
-    sum_wout = from_owner_order(added(wout_got))
-    pack_sum = added(pack_got)
+    sum_wout = from_owner_order(sum_wout)
     sum_sgate, sum_sup, sum_sdown = (
         added(got.reshape(n_dp // inner, inner, r, ff_s)).transpose(1, 0, 2).reshape(r, -1)
         for got in shared_got

time: 1360 us -> 1210 us (0.89)
  waiting for transfers between devices: 66.7 us -> 15.1 us
  Pallas kernels: 798 us -> 756 us
  starting transfers between devices: 23.9 us -> 6.41 us
  matrix products: 220 us -> 203 us
    pallas_call x1, Pallas kernels: 265 us -> 203 us  [forward_exchange(): pl.pallas_call(kernel, out_shape=[jax.ShapeDtypeStruct((rows, width), F32...]
    pallas_call x2 -> x3, Pallas kernels: 285 us -> 343 us  [the longest x2 174 us: between(): pl.pallas_call(kernel, out_shape=[jax.ShapeDtypeStruct(blocks.shape, BF)]...]
    ppermute x9 -> x3, waiting for transfers between devices: 66.6 us -> 14.9 us  [through(): got.append(lax.ppermute(cut[m], 'expert', perm))]
    pallas_call x1, Pallas kernels: 107 us -> 57.6 us  [first_exchange(): pl.pallas_call(kernel, out_shape=[jax.ShapeDtypeStruct((n_ex,) + tok.shap...]
    pallas_call x1, Pallas kernels: 12.1 us -> 28 us  [plane_gather(): pl.pallas_call(kernel, out_shape=jax.ShapeDtypeStruct((n_ex,) + block.sha...]
    convert_element_type x4 -> x1, local copies, waits for them, and re-layouts: 14.6 us -> 0.27 us  [shards(): out_tokens = from_owner_order((residual + out_sum.astype(F32)).astype(BF))]
    optimization_barrier x0 -> x3, local copies, waits for them, and re-layouts: none -> 14.1 us  [shards(): shared_grads, _ = lax.optimization_barrier((shared_grads, grad_attn))]
    unnamed x352 -> x314, local copies, waits for them, and re-layouts: 37.7 us -> 36.5 us
  transfers between devices with their start and end apart: 16 -> 10, of which waited for: 4 -> 1; matrix products, arithmetic and copies ran while one was open for 27% -> 20% of each run, Pallas kernels for 15% -> 19%
where the time goes in v5:
time: 1210 us
  Pallas kernels  756 us (62%)
  matrix products  203 us (17%)
  local copies, waits for them, and re-layouts  140 us (12%)
  other arithmetic  62 us (5%)
  between operations  17.8 us (1%)
  waiting for transfers between devices  15.1 us (1%)
    pallas_call x1, Pallas kernels, forward_exchange(): pl.pallas_call(kernel, out_shape=[jax.ShapeDtypeStruct((rows, width), F32...  203 us
    pallas_call x2, Pallas kernels, between(): pl.pallas_call(kernel, out_shape=[jax.ShapeDtypeStruct(blocks.shape, BF)]...  174 us
    pallas_call x1, Pallas kernels, last_exchange(): pl.pallas_call(kernel, out_shape=[jax.ShapeDtypeStruct(heads.shape[1:], B...  169 us
    dot_general x20, matrix products, mm(): return jnp.dot(left, right, preferred_element_type=F32)  85.4 us
    pallas_call x1, Pallas kernels, plane_sum(): pl.pallas_call(kernel, out_shape=[jax.ShapeDtypeStruct(array.shape[1:], F...  74.5 us
    dot_general x16, matrix products, mm_cols(): lax.dot_general(left, right, (((1,), (1,)), ((), ())), preferred_element_...  62.4 us
    pallas_call x1, Pallas kernels, first_exchange(): pl.pallas_call(kernel, out_shape=[jax.ShapeDtypeStruct((n_ex,) + tok.shap...  57.6 us
    dot_general x15, matrix products, mm_rows(): lax.dot_general(left, right, (((0,), (0,)), ((), ())), preferred_element_...  55.3 us
  transfers between devices with their start and end apart: 10, of which 1 were waited for; matrix products, arithmetic and copies ran while one was open for 20% of the time, Pallas kernels for 19%

profile of v5, /device:TPU:11, one launch (start us, length us, event | category | flops | bytes accessed | tf_op | source)
XLA Modules:
  0.0 1205.6 jit_solution(17632489784715909800)
XLA Ops:
  20.0 57.6 %shard_map.342 = (bf16[8,128,2048]{2,1,0:T(8,128)(2,1)}, bf16[4,8,64,512]{3,2,1,0:T(8,128)(2,1)S(1)}, bf16[4,8,64,640]{3,2,1,0:T(8,128)(2,1)S(1)}) custom-call(bf16[128,2048]{1,0:T(8,128)(2,1)S(1)} %copy-done, bf16[8,64,512]{2,1,0:T(8,128)(2,1)S(1)} %copy-done.10, bf16[64,640]{1,0:T(8,128)(2,1)S(1)} %concatenate.56.pk_ref), custom_call_target="tpu_custom_call" | custom-call | tf_op jit(solution)/shard_map/pallas_call | solution.py:269
  114.8 4.4 subtract_convert_fusion
  132.5 4.6 fusion.101
  164.5 5.3 all_to_all.10
  170.0 3.3 convolution_convert_fusion.7
  173.4 6.8 convolution_convert_fusion.6
  180.2 203.3 %shard_map.343 = (f32[128,2048]{1,0:T(8,128)S(1)}, bf16[4,128,2048]{2,1,0:T(8,128)(2,1)S(1)}, bf16[4,256,2048]{2,1,0:T(8,128)(2,1)}, bf16[8,4,64,1408]{3,2,1,0:T...) custom-call(bf16[8,128,2048]{2,1,0:T(8,128)(2,1)} %bitcast.295, ...), custom_call_target="tpu_custom_call" | custom-call | tf_op jit(solution)/shard_map/pallas_call | solution.py:493
  383.6 5.1 convolution_convert_fusion.5
  389.4 69.6 %shard_map.344 = (bf16[4,256,2048]{2,1,0:T(8,128)(2,1)}, bf16[8,4,64,1408]{3,2,1,0:T(8,128)(2,1)}) custom-call(bf16[4,256,2048]{2,1,0:T(8,128)(2,1)} %bitcast.316, bf16[2,8,64,1408]{3,2,1,0:T(8,128)(2,1)S(1)} %bitcast.284), custom_call_target="tpu_custom_call" | custom-call | tf_op jit(solution)/shard_map/pallas_call | solution.py:564
  459.0 3.5 fusion.99
  462.6 10.7 fusion.102
  473.3 8.4 fusion.103
  486.1 14.9 %multiply_convert_fusion.2 = (bf16[1024,1408]{1,0:T(8,128)(2,1)}, bf16[1024,1408]{1,0:T(8,128)(2,1)S(1)}, bf16[1024,1408]{1,0:T(8,128)(2,1)}) fusion(f32[1024,1408]{1,0:T(8,128)} %fusion.102, f32[1024,1408]{1,0:T(8,128)} %fusion.103, bf16[1024,2048]{1,0:T(8,128)(2,1)S(1)} %bitcast.326, bf16[2048,1408]{1,0:T(8,128)(2,1)} %bitcast.385), kind=kOutput, calls=%fused_computation.20 | convolution fusion | flops 5928648704 | bytes 30146560 | tf_op jit(solution)/shard_map/dot_general | solution.py:56
  501.0 8.9 fusion.107
  509.9 9.1 convolution_convert_fusion.4
  519.1 8.6 convolution_convert_fusion.2
  537.3 5.5 multiply_convert_fusion.5
  542.9 3.3 convolution_convert_fusion.9
  546.2 3.3 convolution_convert_fusion.8
  549.5 10.7 add_convert_fusion
  562.4 3.4 fusion.12
  567.7 14.9 %collective-permute-done = bf16[256,2048]{1,0:T(8,128)(2,1)} collective-permute-done((bf16[256,2048]{1,0:T(8,128)(2,1)}, bf16[256,2048]{1,0:T(8,128)(2,1)}, u32[]{:S(2)}, u32[]{:S(2)}) %collective-permute-start) | collective-permute-done | bytes 1048608 | tf_op jit(solution)/shard_map/ppermute | solution.py:1051
  582.6 5.6 add_convert_fusion.2
  590.2 104.0 %shard_map.345 = (bf16[4,256,2048]{2,1,0:T(8,128)(2,1)}, bf16[1,2,8,64,1408]{4,3,2,1,0:T(8,128)(2,1)S(1)}) custom-call(bf16[4,256,2048]{2,1,0:T(8,128)(2,1)} %bitcast.322, bf16[8,4,64,1408]{3,2,1,0:T(8,128)(2,1)} %bitcast.312), custom_call_target="tpu_custom_call" | custom-call | tf_op jit(solution)/shard_map/pallas_call | solution.py:564
  706.8 5.9 bitcast_reduce_fusion
  713.8 3.6 concatenate.64.x_ref
  717.4 50.0 %shard_map.346 = f32[128,2176]{1,0:T(8,128)S(1)} custom-call(bf16[4,128,2176]{2,1,0:T(8,128)(2,1)S(1)} %concatenate.64.x_ref), custom_call_target="tpu_custom_call" | custom-call | tf_op jit(solution)/shard_map/pallas_call | solution.py:174
  771.5 28.0 %shard_map.347 = bf16[8,128,2048]{2,1,0:T(8,128)(2,1)S(1)} custom-call(bf16[128,2048]{1,0:T(8,128)(2,1)S(1)} %get-tuple-element.192.x_ref), custom_call_target="tpu_custom_call" | custom-call | tf_op jit(solution)/shard_map/pallas_call | solution.py:140
  801.6 4.6 copy.423
  806.7 11.1 convolution_convert_fusion.1
  817.8 8.7 convolution_convert_fusion
  833.4 4.7 copy.424
  838.1 3.5 convolution_convert_fusion.17
  842.8 3.4 multiply_reduce_fusion.2
  848.8 3.3 select_convert_fusion.1
  863.4 3.8 convolution_convert_fusion.13
  868.2 3.8 all-to-all-start.1
  872.1 4.8 copy.425
  881.6 4.4 convolution_convert_fusion.3
  886.0 74.5 %shard_map.348 = (f32[128,2048]{1,0:T(8,128)S(1)}, f32[128,640]{1,0:T(8,128)S(1)}, bf16[1,2,8,64,1408]{4,3,2,1,0:T(8,128)(2,1)S(1)}) custom-call(bf16[8,128,2048]{2,1,0:T(8,128)(2,1)} %bitcast.327, bf16[8,128,640]{2,1,0:T(8,128)(2,1)S(1)} %bitcast.274, bf16[8,4,64,1408]{3,2,1,0:T(8,128)(2,1)} %bitcast.311), custom_call_target="tpu_custom_call" | custom-call | tf_op jit(solution)/shard_map/pallas_call | solution.py:753
  963.5 3.3 convolution_convert_fusion.11
  966.9 4.6 copy.415
  971.5 3.8 fusion.31
  977.6 6.7 concatenate.68
  984.3 3.7 copy.422
  988.0 3.3 convert.121
  1001.5 169.0 %shard_map.349 = (bf16[8,64,512]{2,1,0:T(8,128)(2,1)S(1)}, f32[64,2048]{1,0:T(8,128)S(1)}, f32[64,640]{1,0:T(8,128)S(1)}, bf16[4,64,704]{2,1,0:T(8,128)(2,1)S(1)...) custom-call(bf16[4,8,64,512]{3,2,1,0:T(8,128)(2,1)} %pad_maximum_fusion.2.h, ...), custom_call_target="tpu_custom_call" | custom-call | tf_op jit(solution)/shard_map/pallas_call | solution.py:891
  1192.9 4.7 convert.122
  (550 shorter events, 195.7 us)
Async XLA Ops:
  7.2 157.3 %all-gather.6.cloned.1.call-start = ((), (), s32[]{:S(2)}) async-start(), calls=%async_computation.11 | async-start | bytes 1310720 | tf_op jit(solution)/shard_map/all_gather | solution.py:1009
  79.0 29.6 %copy-start.6 = (bf16[4,8,64,640]{3,2,1,0:T(8,128)(2,1)}, bf16[4,8,64,640]{3,2,1,0:T(8,128)(2,1)S(1)}, u32[]{:S(2)}) copy-start(bf16[4,8,64,640]{3,2,1,0:T(8,128)(2,1)S(1)} %get-tuple-element.47) | copy-start | bytes 7864324
  79.0 94.3 %all-gather.4.cloned.1.call-start = ((), (), s32[]{:S(2)}) async-start(), calls=%async_computation.6 | async-start | bytes 2621440 | tf_op jit(solution)/shard_map/all_gather | solution.py:1022
  83.4 685.7 %reduce-scatter.5.cloned.1.call-start = ((), (), s32[]{:S(2)}) async-start(), calls=%async_computation.7 | async-start | bytes 2621440 | tf_op jit(solution)/shard_map/reduce_scatter | solution.py:1203
  88.6 37.6 %copy-start.84 = (f32[2048,1]{0,1:T(1,128)}, f32[2048,1]{0,1:T(1,128)S(1)}, u32[]{:S(2)}) copy-start(f32[2048,1]{0,1:T(1,128)S(1)} %copy.448) | copy-start | bytes 24580
  111.6 12.5 %copy-start.92 = (bf16[4,8,64]{2,1,0:T(8,128)(2,1)S(1)}, bf16[4,8,64]{2,1,0:T(8,128)(2,1)}, u32[]{:S(2)}) copy-start(bf16[4,8,64]{2,1,0:T(8,128)(2,1)} %slice_reduce_fusion) | copy-start | bytes 12292
  111.6 12.6 %copy-start.96 = (f32[1024]{0:T(1024)S(1)}, f32[1024]{0:T(1024)}, u32[]{:S(2)}) copy-start(f32[1024]{0:T(1024)} %multiply_reduce_fusion.3) | copy-start | bytes 12292
  111.6 12.6 %copy-start.44 = (f32[1024,576]{0,1:T(8,128)S(1)}, f32[1024,576]{0,1:T(8,128)}, u32[]{:S(2)}) copy-start(f32[1024,576]{0,1:T(8,128)} %copy-done.43) | copy-start | bytes 7077892
  119.2 12.9 %copy-start.45 = (f32[1024,32]{1,0:T(8,128)}, f32[1024,32]{1,0:T(8,128)S(1)}, u32[]{:S(2)}) copy-start(f32[1024,32]{1,0:T(8,128)S(1)} %get-tuple-element.226) | copy-start | bytes 393220
  132.3 14.5 %copy-start.57 = (f32[1024,32]{0,1:T(8,128)}, f32[1024,32]{0,1:T(8,128)S(1)}, u32[]{:S(2)}) copy-start(f32[1024,32]{0,1:T(8,128)S(1)} %copy.382) | copy-start | bytes 393220
  132.4 14.3 %copy-start.59 = (f32[1024,32]{0,1:T(8,128)}, f32[1024,32]{0,1:T(8,128)S(1)}, u32[]{:S(2)}) copy-start(f32[1024,32]{0,1:T(8,128)S(1)} %copy.381) | copy-start | bytes 393220
  141.5 31.8 %copy-start.100 = (s32[512]{0:T(512)}, s32[512]{0:T(512)S(1)}, u32[]{:S(2)}) copy-start(s32[512]{0:T(512)S(1)} %get-tuple-element.183) | copy-start | bytes 6148
  141.5 31.8 %copy-start.103 = (s32[512]{0:T(512)}, s32[512]{0:T(512)S(1)}, u32[]{:S(2)}) copy-start(s32[512]{0:T(512)S(1)} %get-tuple-element.184) | copy-start | bytes 6148
  141.5 31.8 %copy-start.106 = (s32[512]{0:T(512)}, s32[512]{0:T(512)S(1)}, u32[]{:S(2)}) copy-start(s32[512]{0:T(512)S(1)} %get-tuple-element.185) | copy-start | bytes 6148
  141.5 31.8 %copy-start.109 = (s32[512]{0:T(512)}, s32[512]{0:T(512)S(1)}, u32[]{:S(2)}) copy-start(s32[512]{0:T(512)S(1)} %get-tuple-element.186) | copy-start | bytes 6148
  141.5 31.8 %copy-start.112 = (s32[512]{0:T(512)}, s32[512]{0:T(512)S(1)}, u32[]{:S(2)}) copy-start(s32[512]{0:T(512)S(1)} %get-tuple-element.187) | copy-start | bytes 6148
  180.2 203.4 %copy-start.101 = (s32[512]{0:T(512)S(1)}, s32[512]{0:T(512)}, u32[]{:S(2)}) copy-start(s32[512]{0:T(512)} %copy-done.100) | copy-start | bytes 6148
  180.2 203.4 %copy-start.104 = (s32[512]{0:T(512)S(1)}, s32[512]{0:T(512)}, u32[]{:S(2)}) copy-start(s32[512]{0:T(512)} %copy-done.103) | copy-start | bytes 6148
  180.2 203.4 %copy-start.107 = (s32[512]{0:T(512)S(1)}, s32[512]{0:T(512)}, u32[]{:S(2)}) copy-start(s32[512]{0:T(512)} %copy-done.106) | copy-start | bytes 6148
  180.2 203.4 %copy-start.110 = (s32[512]{0:T(512)S(1)}, s32[512]{0:T(512)}, u32[]{:S(2)}) copy-start(s32[512]{0:T(512)} %copy-done.109) | copy-start | bytes 6148
  180.2 203.4 %copy-start.113 = (s32[512]{0:T(512)S(1)}, s32[512]{0:T(512)}, u32[]{:S(2)}) copy-start(s32[512]{0:T(512)} %copy-done.112) | copy-start | bytes 6148
  459.0 14.3 %slice-start = ((s8[5767168]{0:T(1024)(128)(4,1)}), s8[4194304]{0:T(1024)(128)(4,1)S(1)}, s32[]{:S(2)}) async-start(s8[5767168]{0:T(1024)(128)(4,1)} %bitcast.375), calls=%async_computation.12 | async-start | bytes 8388608
  462.6 10.7 slice-start.1
  485.3 15.7 %slice-start.4 = ((s8[5767168]{0:T(1024)(128)(4,1)}), s8[4194304]{0:T(1024)(128)(4,1)S(1)}, s32[]{:S(2)}) async-start(s8[5767168]{0:T(1024)(128)(4,1)} %bitcast.382), calls=%async_computation.16 | async-start | bytes 8388608
  486.1 14.9 %slice-start.5 = ((s8[5767168]{0:T(1024)(128)(4,1)}), s8[1572864]{0:T(1024)(128)(4,1)S(1)}, s32[]{:S(2)}) async-start(s8[5767168]{0:T(1024)(128)(4,1)} %bitcast.382), calls=%async_computation.17 | async-start | bytes 3145728
  501.0 9.0 copy-start.141
  501.0 8.9 copy-start.144
  535.4 32.3 %collective-permute-start.2 = (bf16[256,2048]{1,0:T(8,128)(2,1)}, bf16[256,2048]{1,0:T(8,128)(2,1)}, u32[]{:S(2)}, u32[]{:S(2)}) collective-permute-start(bf16[256,2048]{1,0:T(8,128)(2,1)} %get-tuple-element.199), channel_id=1, source_target_pairs={{0,2},{1,3},{2,4},{3,5},{4,6},{5,7},{6,0},{7,1},{8,10},{9,11},{10,... | collective-permute-start | bytes 3145736 | tf_op jit(solution)/shard_map/ppermute | solution.py:1051
  536.6 31.1 %collective-permute-start.1 = (bf16[256,2048]{1,0:T(8,128)(2,1)}, bf16[256,2048]{1,0:T(8,128)(2,1)}, u32[]{:S(2)}, u32[]{:S(2)}) collective-permute-start(bf16[256,2048]{1,0:T(8,128)(2,1)} %get-tuple-element.200), channel_id=1, source_target_pairs={{0,4},{1,5},{2,6},{3,7},{4,0},{5,1},{6,2},{7,3},{8,12},{9,13},{10,... | collective-permute-start | bytes 3145736 | tf_op jit(solution)/shard_map/ppermute | solution.py:1051
  536.9 45.7 %collective-permute-start = (bf16[256,2048]{1,0:T(8,128)(2,1)}, bf16[256,2048]{1,0:T(8,128)(2,1)}, u32[]{:S(2)}, u32[]{:S(2)}) collective-permute-start(bf16[256,2048]{1,0:T(8,128)(2,1)} %get-tuple-element.201), channel_id=1, source_target_pairs={{0,6},{1,7},{2,0},{3,1},{4,2},{5,3},{6,4},{7,5},{8,14},{9,15},{10,... | collective-permute-start | bytes 3145736 | tf_op jit(solution)/shard_map/ppermute | solution.py:1051
  549.5 11.0 copy-start.116
  549.5 11.0 copy-start.117
  549.5 11.0 copy-start.118
  549.5 12.0 copy-start.35
  565.8 16.8 %copy-start.68 = (bf16[256,2048]{1,0:T(8,128)(2,1)S(1)}, bf16[256,2048]{1,0:T(8,128)(2,1)}, u32[]{:S(2)}) copy-start(bf16[256,2048]{1,0:T(8,128)(2,1)} %get-tuple-element.198) | copy-start | bytes 3145732
  588.2 410.3 %reduce-scatter.7.cloned.1.call-start = ((), (), s32[]{:S(2)}) async-start(), calls=%async_computation.8 | async-start | bytes 3538944 | tf_op jit(solution)/shard_map/reduce_scatter | solution.py:1209
  713.8 54.6 %copy-start.66 = (bf16[2048,16]{0,1:T(8,128)(2,1)S(1)}, bf16[2048,16]{0,1:T(8,128)(2,1)}, u32[]{:S(2)}) copy-start(bf16[2048,16]{0,1:T(8,128)(2,1)} %reshape.831) | copy-start | bytes 196612
  713.8 54.6 %copy-start.87 = (f32[2048]{0:T(1024)S(1)}, f32[2048]{0:T(1024)}, u32[]{:S(2)}) copy-start(f32[2048]{0:T(1024)} %reshape.891) | copy-start | bytes 24580
  717.4 50.0 %copy-start.69 = (f32[512,16]{1,0:T(8,128)S(1)}, f32[512,16]{1,0:T(8,128)}, u32[]{:S(2)}) copy-start(f32[512,16]{1,0:T(8,128)} %get-tuple-element.194) | copy-start | bytes 98308
  806.2 192.3 %reduce-scatter.9.cloned.1.call-start = ((), (), s32[]{:S(2)}) async-start(), calls=%async_computation.9 | async-start | bytes 3538944 | tf_op jit(solution)/shard_map/reduce_scatter | solution.py:1209
  806.6 11.2 copy-start.28
  806.6 11.2 copy-start.143
  817.8 12.5 %copy-start.50 = (bf16[128,2048]{1,0:T(8,128)(2,1)S(1)}, bf16[128,2048]{1,0:T(8,128)(2,1)}, u32[]{:S(2)}) copy-start(bf16[128,2048]{1,0:T(8,128)(2,1)} %get-tuple-element.215) | copy-start | bytes 1572868
  868.2 130.3 %all-to-all-start.1 = ((bf16[2,2,64,2048]{3,2,1,0:T(8,128)(2,1)}), bf16[2,2,64,2048]{3,2,1,0:T(8,128)(2,1)S(1)}, u32[]{:S(2)}, u32[]{:S(2)}) async-start(bf16[2,2,64,2048]{3,2,1,0:T(8,128)(2,1)} %bitcast.266), calls=%async_computation.2 | async-start | bytes 2097152 | tf_op jit(solution)/shard_map/all_to_all | solution.py:1263
  872.0 126.5 %reduce-scatter.11.cloned.1.call-start = ((), (), s32[]{:S(2)}) async-start(), calls=%async_computation.10 | async-start | bytes 3538944 | tf_op jit(solution)/shard_map/reduce_scatter | solution.py:1209
  886.0 77.2 %copy-start.37 = (f32[128,512]{1,0:T(8,128)S(1)}, f32[128,512]{1,0:T(8,128)}, u32[]{:S(2)}) copy-start(f32[128,512]{1,0:T(8,128)} %copy-done.36) | copy-start | bytes 786436
  886.0 77.2 %copy-start.123 = (f32[128]{0:T(128)S(1)}, f32[128]{0:T(128)}, u32[]{:S(2)}) copy-start(f32[128]{0:T(128)} %fusion.76) | copy-start | bytes 1540
  886.0 77.3 %copy-start.129 = (f32[128]{0:T(128)S(1)}, f32[128]{0:T(128)}, u32[]{:S(2)}) copy-start(f32[128]{0:T(128)} %copy-done.128) | copy-start | bytes 1540
  (113 other events, 401.9 us)
Sparse Core Ops, SparseCore 0:
  79.1 27.0 all-gather.5
  108.3 43.2 all-gather.3
  588.3 98.1 reduce-scatter.4
  806.3 44.7 reduce-scatter.6
  854.3 49.8 reduce-scatter.8
  907.8 59.6 reduce-scatter.10

commit v6 on v5

--- a/solution.py
+++ b/solution.py
@@ -73,9 +73,129 @@
     return slot_index.reshape(route_rows.shape)
 
 
+def turn(values, cos, sin, sign):
+    half = DR // 2
+    first = lax.rem(lax.broadcasted_iota(jnp.int32, values.shape, 1), DR) < half
+    partner = jnp.where(
+        first, -pltpu.roll(values, 2 * DR - half, 1), pltpu.roll(values, half, 1)
+    )
+    return values * cos + sign * (partner * sin)
+
+
+def causal(i, tile, keep_ref):
+    shape = (tile, (i + 1) * tile)
+    query = lax.broadcasted_iota(jnp.int32, shape, 0) + i * tile
+    key = lax.broadcasted_iota(jnp.int32, shape, 1)
+    return (key <= query) & (keep_ref[:, : shape[1]] > 0.5)
+
+
+def attend_forward(
+    tok, gain, wq, wl, gain_lat, we, cos, sin, keep,
+    hidden, latent, latent_low, qcat, kcat, value, lse, attended,
+):
+    per, rows, width = tok.shape
+    seq = per * rows
+    tile = 2 * rows
+    scale = (DH + DR) ** (-0.5)
+
+    def project(i, carry):
+        at = pl.ds(pl.multiple_of(i * tile, tile), tile)
+        x = tok[pl.ds(2 * i, 2)].reshape(tile, width).astype(F32)
+        root = lax.rsqrt(jnp.mean(x * x, axis=-1, keepdims=True) + norm_eps)
+        hid = (x * root * gain[...]).astype(BF)
+        hidden[at, :] = hid
+        c, s = cos[at, :], sin[at, :]
+        query = mm(hid, wq[...])
+        rope_q = turn(query[:, 2 * DH :], c, s, 1.0).astype(BF)
+        lat = mm(hid, wl[...])
+        latent[at, :] = lat
+        plain = lat[:, :KVR]
+        root = lax.rsqrt(jnp.mean(plain * plain, axis=-1, keepdims=True) + norm_eps)
+        low = (plain * root * gain_lat[...]).astype(BF)
+        latent_low[at, :] = low
+        rope = lat[:, KVR : KVR + 2 * DR]
+        lane = lax.broadcasted_iota(jnp.int32, rope.shape, 1)
+        rope = jnp.where(lane < DR, rope, pltpu.roll(rope, DR, 1))
+        rope = turn(rope, c, s, 1.0)
+        expanded = mm(low, we[...]).astype(BF)
+        for h in range(2):
+            qcat[h, at, :DH] = query[:, h * DH : (h + 1) * DH].astype(BF)
+            qcat[h, at, DH:] = rope_q
+            mine = (lane < DR) if h == 0 else (lane >= DR)
+            kcat[h, at, :DH] = expanded[:, h * (DH + DV) : h * (DH + DV) + DH]
+            kcat[h, at, DH:] = jnp.where(mine, rope, 0.0).astype(BF)
+            value[h, at, :] = expanded[:, h * (DH + DV) + DH : (h + 1) * (DH + DV)]
+        return carry
+
+    lax.fori_loop(0, seq // tile, project, 0)
+    for h in range(2):
+        for i in range(seq // tile):
+            at, upto = slice(i * tile, (i + 1) * tile), slice(0, (i + 1) * tile)
+            scores = mm_cols(qcat[h, at, :], kcat[h, upto, :]) * scale
+            scores = jnp.where(causal(i, tile, keep), scores, masked_score)
+            top = jnp.max(scores, axis=-1, keepdims=True)
+            exp_scores = jnp.exp(scores - top)
+            total = jnp.sum(exp_scores, axis=-1, keepdims=True)
+            probs = (exp_scores / total).astype(BF)
+            attended[at, h * DV : (h + 1) * DV] = mm(probs, value[h, upto, :]).astype(BF)
+            lse[h, at, :] = jnp.broadcast_to(top + jnp.log(total), (tile, lse.shape[2]))
+
+
+def attend_backward(
+    grad, wo, wq, we, cos, sin, keep, qcat, kcat, value, lse, attended,
+    gat, grad_wout, dk, dv, grad_query, grad_expanded, grad_rope,
+):
+    per, rows, width = grad.shape
+    seq = per * rows
+    tile = 2 * rows
+    scale = (DH + DR) ** (-0.5)
+    count = seq // tile
+    grad_wout[...] = jnp.zeros_like(grad_wout)
+
+    def project(i, carry):
+        at = pl.ds(pl.multiple_of(i * tile, tile), tile)
+        block = grad[pl.ds(2 * i, 2)].reshape(tile, width)
+        gat[at, :] = mm_cols(block, wo[...]).astype(BF)
+        grad_wout[...] += mm_rows(attended[at, :], block)
+        return carry
+
+    lax.fori_loop(0, count, project, 0)
+    for h in range(2):
+        dk[...] = jnp.zeros_like(dk)
+        dv[...] = jnp.zeros_like(dv)
+        for i in range(count):
+            at, upto = slice(i * tile, (i + 1) * tile), slice(0, (i + 1) * tile)
+            g = gat[at, h * DV : (h + 1) * DV]
+            scores = mm_cols(qcat[h, at, :], kcat[h, upto, :]) * scale
+            scores = jnp.where(causal(i, tile, keep), scores, masked_score)
+            probs = jnp.exp(scores - lse[h, at, 0:1])
+            grad_probs = mm_cols(g, value[h, upto, :])
+            inner = jnp.sum(grad_probs * probs, axis=-1, keepdims=True)
+            raw = (probs * (grad_probs - inner) * scale).astype(BF)
+            grad_q = mm(raw, kcat[h, upto, :])
+            grad_query[at, h * DH : (h + 1) * DH] = grad_q[:, :DH].astype(BF)
+            rope = grad_q[:, DH:]
+            lane = lax.broadcasted_iota(jnp.int32, rope.shape, 1)
+            mine = (lane < DR) if h == 0 else (lane >= DR)
+            rope = turn(rope, cos[at, :], sin[at, :], -1.0).astype(BF)
+            if h == 0:
+                grad_query[at, 2 * DH :] = rope
+            else:
+                grad_query[at, 2 * DH :] = jnp.where(mine, rope, grad_query[at, 2 * DH :])
+            dk[upto, :] += mm_rows(raw, qcat[h, at, :])
+            dv[upto, :] += mm_rows(probs.astype(BF), g)
+        grad_expanded[:, h * (DH + DV) : h * (DH + DV) + DH] = dk[:, :DH].astype(BF)
+        grad_expanded[:, h * (DH + DV) + DH : (h + 1) * (DH + DV)] = dv[...].astype(BF)
+        rope = dk[:, DH:]
+        if h == 0:
+            grad_rope[...] = rope
+        else:
+            grad_rope[...] += pltpu.roll(rope, DR, 1)
+
+
 def params(collective_id):
     return pltpu.CompilerParams(
-        collective_id=collective_id, has_side_effects=True, vmem_limit_bytes=48 << 20
+        collective_id=collective_id, has_side_effects=True, vmem_limit_bytes=60 << 20
     )
 
 
@@ -106,45 +226,6 @@
     same_core = [(z, lax.rem(c + i, chips) * 2 + k) for i in range(1, chips)]
     column = [(lax.rem(z + i, n_dp), e) for i in range(1, n_dp)]
     return z, e, c, k, sibling, same_core, column
-
-
-def plane_gather(block, n_dp, n_ex, collective_id):
-    chips = n_ex // 2
-
-    def kernel(x_ref, o_ref, send, recv, sib_send, sib_recv, local):
-        z, e, c, k, sibling, same_core, _ = places(n_dp, n_ex)
-        greet(same_core + [sibling])
-        far = []
-        for i in range(1, chips):
-            copy = remote(x_ref, o_ref.at[e], send.at[i], recv.at[i], same_core[i - 1])
-            copy.start()
-            far.append(copy)
-        near = [remote(x_ref, o_ref.at[e], sib_send.at[0], sib_recv.at[0], sibling)]
-        near[0].start()
-        own = pltpu.make_async_copy(x_ref, o_ref.at[e], local)
-        own.start()
-        for i in range(1, chips):
-            source = lax.rem(c + chips - i, chips) * 2 + k
-            far[i - 1].wait_recv()
-            copy = remote(
-                o_ref.at[source], o_ref.at[source], sib_send.at[i], sib_recv.at[i], sibling
-            )
-            copy.start()
-            near.append(copy)
-        own.wait()
-        for copy in far:
-            copy.wait_send()
-        for copy in near:
-            copy.wait()
-
-    return pl.pallas_call(
-        kernel,
-        out_shape=jax.ShapeDtypeStruct((n_ex,) + block.shape, block.dtype),
-        in_specs=[ANY],
-        out_specs=ANY,
-        scratch_shapes=[pltpu.SemaphoreType.DMA((chips,))] * 4 + [pltpu.SemaphoreType.DMA],
-        compiler_params=params(collective_id),
-    )(block)
 
 
 def wait_recv(region, sem, device):
@@ -371,39 +452,81 @@
             wait_recv(region, self.sib_recv.at[i], self.sibling)
 
 
-def forward_exchange(parts, tok, gain, slots, experts, shared, n_dp, n_ex, inner, collective_id):
+def forward_exchange(attend, w_out, tok, gain, experts, shared, n_dp, n_ex, inner, collective_id):
     chips = n_ex // 2
     rows, width = tok.shape
     count = len(experts)
-
-    def kernel(x_ref, tok_ref, gain_ref, slot_ref, *refs):
-        e_in, s_in = refs[:count], refs[count : count + 3]
-        refs = refs[count + 3 :]
-        res_ref, xcol_ref, slot_out = refs[:3]
+    r = w_out.shape[0]
+    parts = DV // r
+    hp = n_dp // parts
+    seq = n_ex * rows
+
+    def kernel(*refs):
+        att_in, refs = refs[:9], refs[9:]
+        wo_in, tok_ref, gain_ref = refs[:3]
+        e_in, s_in = refs[3 : 3 + count], refs[3 + count : 6 + count]
+        refs = refs[6 + count :]
+        att_out, refs = refs[:8], refs[8:]
+        wo_out, res_ref, xcol_ref = refs[:3]
         w_out, s_out = refs[3 : 3 + count], refs[3 + count : 6 + count]
         refs = refs[6 + count :]
-        from_sib, out_buf, from_far, xbuf = refs[:4]
+        x_ref, from_sib, out_buf, from_far, xbuf = refs[:5]
         (
-            near_s, near_r, far_s, far_r, x_s, x_r, g_s, g_r,
-            sh_s, sh_r, sp_s, sp_r, sf_s, sf_r, local,
-        ) = refs[4:19]
-        refs = refs[19:]
+            near_s, near_r, far_s, far_r, x_s, x_r,
+            sh_s, sh_r, sp_s, sp_r, sf_s, sf_r, wo_s, wo_r, local,
+        ) = refs[5:20]
+        refs = refs[20:]
         z, e, c, k, sibling, same_core, column = places(n_dp, n_ex)
         group = column_group(z, e, inner)
-        greet(same_core + [sibling] + column + [(device[0], sibling[1]) for device in column])
+        part = lax.rem(e, parts)
+        members = [
+            (lax.rem(z + i, n_dp), e - part + lax.rem(part + j, parts))
+            for i in range(n_dp)
+            for j in range(parts)
+        ]
+        greet(same_core + column + [(device[0], sibling[1]) for device in column] + members[1:])
+
+        def wo_sends(start):
+            for i in range(n_dp):
+                target = (lax.rem(z + i, n_dp), e - part + z // hp)
+                dst, sem = wo_out.at[lax.rem(z, hp), part], wo_r.at[lax.rem(z, hp), part]
+
+                def far(i=i, target=target, dst=dst, sem=sem):
+                    copy = remote(wo_in, dst, wo_s.at[i], sem, target)
+                    if start:
+                        copy.start()
+                    else:
+                        copy.wait_send()
+
+                if i:
+                    far()
+                else:
+                    pl.when(z // hp != part)(far)
+                    if start:
+
+                        @pl.when(z // hp == part)
+                        def _(dst=dst, sem=sem):
+                            pltpu.make_async_copy(wo_in, dst, sem).start()
+
+        def wo_arrivals():
+            for h in range(hp):
+                for p in range(parts):
+                    here = jnp.logical_and(part * hp + h == z, part == p)
+
+                    @pl.when(here)
+                    def _(h=h, p=p):
+                        pltpu.make_async_copy(wo_in, wo_out.at[h, p], wo_r.at[h, p]).wait()
+
+                    @pl.when(jnp.logical_not(here))
+                    def _(h=h, p=p):
+                        wait_recv(wo_out.at[h, p], wo_r.at[h, p], sibling)
+
         my_l = lax.rem(z, inner)
         matrices = [
             ExpertsIn(e_in[m], w_out[m], refs[4 * m : 4 * m + 4], n_dp, n_ex, inner)
             for m in range(count)
         ]
-        near = []
-        for i in list(range(1, chips)) + [0]:
-            chip = lax.rem(c + i, chips)
-            copy = remote(
-                x_ref.at[chip * 2 + 1 - k], from_sib.at[chip], near_s.at[i], near_r.at[i], sibling
-            )
-            copy.start()
-            near.append(copy)
+        wo_sends(True)
         shared_copies = []
         for i in range(1, n_dp):
             for m in range(3):
@@ -417,10 +540,28 @@
             pltpu.make_async_copy(s_in[m].at[my_l], s_out[m].at[e, z], local.at[m])
             for m in range(3)
         ]
-        own.append(pltpu.make_async_copy(slot_ref.at[0], slot_out.at[0], local.at[3]))
         for copy in own:
             copy.start()
         matrices[0].begin()
+        attend_forward(*att_in, *att_out)
+        wo_arrivals()
+        wo = wo_out[...].reshape(hp * DV, width)
+
+        def project(i, carry):
+            at = pl.ds(pl.multiple_of(i * 2 * rows, 2 * rows), 2 * rows)
+            block = mm(att_out[7][at, :], wo).astype(BF)
+            x_ref[pl.ds(2 * i, 2)] = block.reshape(2, rows, width)
+            return carry
+
+        lax.fori_loop(0, chips, project, 0)
+        near = []
+        for i in list(range(1, chips)) + [0]:
+            chip = lax.rem(c + i, chips)
+            copy = remote(
+                x_ref.at[chip * 2 + 1 - k], from_sib.at[chip], near_s.at[i], near_r.at[i], sibling
+            )
+            copy.start()
+            near.append(copy)
         far = []
         for i in range(1, chips):
             chip = lax.rem(c + i, chips)
@@ -444,15 +585,10 @@
             copy = remote(xbuf, xcol_ref.at[my_l], x_s.at[i], x_r.at[i], group[i])
             copy.start()
             x_copies.append(copy)
-        x_own = pltpu.make_async_copy(xbuf, xcol_ref.at[my_l], local.at[4])
+        x_own = pltpu.make_async_copy(xbuf, xcol_ref.at[my_l], local.at[3])
         x_own.start()
         for matrix in matrices[1:]:
             matrix.begin()
-        slot_copies = []
-        for i in range(1, chips):
-            copy = remote(slot_ref.at[i], slot_out.at[i], g_s.at[i], g_r.at[i], same_core[i - 1])
-            copy.start()
-            slot_copies.append(copy)
         for copy in own:
             copy.wait()
         for copy in shared_copies:
@@ -476,43 +612,52 @@
                 to_sib.append(copy)
         for matrix in matrices:
             matrix.pass_on()
-        for copy in x_copies + slot_copies + to_sib:
+        for copy in x_copies + to_sib:
             copy.wait()
         x_own.wait()
         for copy in plane + shared_copies + near + far:
             copy.wait_send()
+        wo_sends(False)
         for matrix in matrices:
             matrix.end()
 
     dma = pltpu.SemaphoreType.DMA
-    r = shared[0].shape[1]
     ff_s = shared[0].shape[2]
     scratch = []
     for _ in experts:
         scratch += ExpertsIn.scratch(n_dp)
+    sds = jax.ShapeDtypeStruct
     outs = pl.pallas_call(
         kernel,
         out_shape=[
-            jax.ShapeDtypeStruct((rows, width), F32),
-            jax.ShapeDtypeStruct((inner, rows, width), BF),
-            jax.ShapeDtypeStruct(slots.shape, BF),
+            sds((seq, width), BF),
+            sds((seq, attend[3].shape[1]), F32),
+            sds((seq, KVR), BF),
+            sds((2, seq, 2 * DH), BF),
+            sds((2, seq, 2 * DH), BF),
+            sds((2, seq, DV), BF),
+            sds((2, seq, 128), F32),
+            sds((seq, 2 * DV), BF),
+            sds((hp, parts, r, width), BF),
+            sds((rows, width), F32),
+            sds((inner, rows, width), BF),
         ]
         + [ExpertsIn.out(w, n_dp, n_ex) for w in experts]
-        + [jax.ShapeDtypeStruct((n_ex, n_dp, r, ff_s), BF)] * 3,
-        in_specs=[VMEM] * 3 + [ANY] * (4 + count),
-        out_specs=[VMEM] + [ANY] * (5 + count),
-        scratch_shapes=[pltpu.VMEM((chips, rows, width), BF)] * 3
+        + [sds((n_ex, n_dp, r, ff_s), BF)] * 3,
+        in_specs=[VMEM] * 9 + [ANY] + [VMEM] * 2 + [ANY] * (3 + count),
+        out_specs=[VMEM] * 10 + [ANY] * (4 + count),
+        scratch_shapes=[pltpu.VMEM((n_ex, rows, width), BF)]
+        + [pltpu.VMEM((chips, rows, width), BF)] * 3
         + [pltpu.VMEM((rows, width), BF)]
         + [dma((chips,))] * 4
         + [dma((inner,))] * 2
-        + [dma((chips,))] * 2
         + [dma((3, n_dp))] * 2
         + [dma((3, chips))] * 4
-        + [dma((5,))]
+        + [dma((n_dp,)), dma((hp, parts)), dma((4,))]
         + scratch,
         compiler_params=params(collective_id),
-    )(parts, tok, gain, slots, *experts, *shared)
-    return outs[0], outs[1], outs[2], outs[3 : 3 + count], outs[3 + count :]
+    )(*attend, w_out, tok, gain, *experts, *shared)
+    return outs[:8], outs[8], outs[9], outs[10], outs[11 : 11 + count], outs[11 + count :]
 
 
 def between(blocks, way, weights, totals, n_dp, n_ex, inner, collective_id):
@@ -682,28 +827,73 @@
                         wait_recv(region, self.recv.at[o, j, h], self.sibling)
 
 
-def plane_sum(arrays, totals, n_dp, n_ex, inner, collective_id):
+def backward_exchange(grad, attend, hidden, latent_low, totals, n_dp, n_ex, inner, collective_id):
     chips = n_ex // 2
-    count, extra = len(arrays), len(totals)
+    rows, width = grad.shape
+    seq = n_ex * rows
+    extra = len(totals)
+    wq, we = attend[1], attend[2]
+    lat_cols = KVR + 2 * DR
 
     def kernel(*refs):
-        x_refs, t_refs = refs[:count], refs[count : count + extra]
-        refs = refs[count + extra :]
-        o_refs, back_refs = refs[:count], refs[count : count + extra]
-        refs = refs[count + extra :]
-        bufs, sems, rest = refs[: 3 * count], refs[3 * count : 7 * count], refs[7 * count :]
+        grad_ref, att_in, refs = refs[0], refs[1:12], refs[12:]
+        hidden_ref, low_ref, t_refs = refs[0], refs[1], refs[2 : 2 + extra]
+        refs = refs[2 + extra :]
+        sums, wout_ref, wq_ref, we_ref = refs[:2], refs[2], refs[3], refs[4]
+        back_refs, refs = refs[5 : 5 + extra], refs[5 + extra :]
+        gbuf, att_tmp, refs = refs[0], refs[1:8], refs[8:]
+        x_refs, bufs, refs = refs[:2], refs[2:8], refs[8:]
+        t_s, t_r, ts_s, ts_r, local = refs[:5]
+        sems, rest = refs[5:13], refs[13:]
         z, e, c, k, sibling, same_core, column = places(n_dp, n_ex)
-        greet(
-            same_core + [sibling] + (column + [(d[0], sibling[1]) for d in column] if extra else [])
-        )
+        greet(same_core + [sibling] + column + [(d[0], sibling[1]) for d in column])
         backs = [
             ExpertsBack(t_refs[m], back_refs[m], rest[7 * m : 7 * m + 7], n_dp, n_ex, inner)
             for m in range(extra)
         ]
+        gather, to_sib = [], []
+        for i in range(1, chips):
+            copy = remote(grad_ref, gbuf.at[e], t_s.at[i], t_r.at[i], same_core[i - 1])
+            copy.start()
+            gather.append(copy)
+        copy = remote(grad_ref, gbuf.at[e], ts_s.at[0], ts_r.at[0], sibling)
+        copy.start()
+        to_sib.append(copy)
+        own = pltpu.make_async_copy(grad_ref, gbuf.at[e], local)
+        own.start()
+        for back in backs:
+            back.begin()
+        for i in range(1, chips):
+            gather[i - 1].wait_recv()
+            block = gbuf.at[lax.rem(c + chips - i, chips) * 2 + k]
+            copy = remote(block, block, ts_s.at[i], ts_r.at[i], sibling)
+            copy.start()
+            to_sib.append(copy)
+        for back in backs:
+            back.pass_on()
+        own.wait()
+        for copy in to_sib:
+            copy.wait_recv()
+        for copy in gather + to_sib:
+            copy.wait_send()
+        gat, grad_wout, dk, dv, grad_query, grad_expanded, grad_rope = att_tmp
+        attend_backward(gbuf, *att_in, *att_tmp)
+
+        def spread(i, carry):
+            at = pl.ds(pl.multiple_of(i * 2 * rows, 2 * rows), 2 * rows)
+            block = mm_cols(grad_query[at, :], att_in[1][...]).astype(BF)
+            x_refs[0][pl.ds(2 * i, 2)] = block.reshape(2, rows, width)
+            block = mm_cols(grad_expanded[at, :], att_in[2][...]).astype(BF)
+            x_refs[1][pl.ds(2 * i, 2), :, :KVR] = block.reshape(2, rows, KVR)
+            block = grad_rope[at, :].astype(BF)
+            x_refs[1][pl.ds(2 * i, 2), :, KVR:] = block.reshape(2, rows, 2 * DR)
+            return carry
+
+        lax.fori_loop(0, chips, spread, 0)
         near, far = {}, {}
         for i in list(range(1, chips)) + [0]:
             chip = lax.rem(c + i, chips)
-            for j in range(count):
+            for j in range(2):
                 near[i, j] = remote(
                     x_refs[j].at[chip * 2 + 1 - k],
                     bufs[3 * j].at[chip],
@@ -712,11 +902,9 @@
                     sibling,
                 )
                 near[i, j].start()
-        for back in backs:
-            back.begin()
         for i in range(1, chips):
             chip = lax.rem(c + i, chips)
-            for j in range(count):
+            for j in range(2):
                 from_sib, out_buf, from_far = bufs[3 * j : 3 * j + 3]
                 near[i, j].wait_recv()
                 out_buf[i] = (
@@ -730,36 +918,62 @@
                     same_core[i - 1],
                 )
                 far[i, j].start()
-        for back in backs:
-            back.pass_on()
-        for j in range(count):
+        wout_ref[...] = grad_wout[...].astype(BF)
+        we_ref[...] = mm_rows(low_ref[...], grad_expanded[...]).astype(BF)
+
+        def wq_rows(i, carry):
+            at = pl.ds(pl.multiple_of(i * 256, 256), 256)
+            wq_ref[at, :] = mm_rows(hidden_ref[:, at], grad_query[...]).astype(BF)
+            return carry
+
+        lax.fori_loop(0, width // 256, wq_rows, 0)
+        for j in range(2):
             near[0, j].wait_recv()
-            o_refs[j][...] = x_refs[j][e].astype(F32) + bufs[3 * j][c].astype(F32)
+            sums[j][...] = x_refs[j][e].astype(F32) + bufs[3 * j][c].astype(F32)
         for i in range(1, chips):
-            for j in range(count):
+            for j in range(2):
                 far[i, j].wait_recv()
-                o_refs[j][...] += bufs[3 * j + 2][i].astype(F32)
+                sums[j][...] += bufs[3 * j + 2][i].astype(F32)
         for copy in list(near.values()) + list(far.values()):
             copy.wait_send()
         for back in backs:
             back.end()
 
-    scratch = []
-    for array in arrays:
-        scratch += [pltpu.VMEM((chips,) + array.shape[1:], BF)] * 3
-    scratch += [pltpu.SemaphoreType.DMA((chips,))] * (4 * count)
+    dma = pltpu.SemaphoreType.DMA
+    sds = jax.ShapeDtypeStruct
+    vmem = pltpu.VMEM
+    scratch = [
+        vmem((n_ex, rows, width), BF),
+        vmem((seq, 2 * DV), BF),
+        vmem((2 * DV, width), F32),
+        vmem((seq, 2 * DH), F32),
+        vmem((seq, DV), F32),
+        vmem((seq, wq.shape[1]), BF),
+        vmem((seq, we.shape[1]), BF),
+        vmem((seq, 2 * DR), F32),
+        vmem((n_ex, rows, width), BF),
+        vmem((n_ex, rows, lat_cols), BF),
+    ]
+    scratch += [vmem((chips, rows, width), BF)] * 3 + [vmem((chips, rows, lat_cols), BF)] * 3
+    scratch += [dma((chips,))] * 4 + [dma] + [dma((chips,))] * 8
     for total in totals:
         scratch += ExpertsBack.scratch(total, n_dp, inner)
     outs = pl.pallas_call(
         kernel,
-        out_shape=[jax.ShapeDtypeStruct(array.shape[1:], F32) for array in arrays]
+        out_shape=[
+            sds((rows, width), F32),
+            sds((rows, lat_cols), F32),
+            sds((2 * DV, width), BF),
+            sds(wq.shape, BF),
+            sds(we.shape, BF),
+        ]
         + [ExpertsBack.out(total, n_dp, inner) for total in totals],
-        in_specs=[VMEM] * count + [ANY] * extra,
-        out_specs=[VMEM] * count + [ANY] * extra,
+        in_specs=[ANY] + [VMEM] * 13 + [ANY] * extra,
+        out_specs=[VMEM] * 5 + [ANY] * extra,
         scratch_shapes=scratch,
         compiler_params=params(collective_id),
-    )(*arrays, *totals)
-    return outs[:count], outs[count:]
+    )(grad, *attend, hidden, latent_low, *totals)
+    return outs[:5], outs[5:]
 
 
 def last_exchange(heads, wout, pack, shared, totals, n_dp, n_ex, inner, collective_id):
@@ -969,7 +1183,14 @@
         return lax.dynamic_index_in_dim(values, index, axis, keepdims=False)
 
     wq_send = jnp.take(w_query.reshape(r, H, DH + DR), jnp.array(heads), axis=1)
-    wq_send = wq_send.reshape(r, n_ex, head_cols).transpose(1, 0, 2)
+    wq_send = wq_send.reshape(r, n_ex, hp, DH + DR)
+    wq_send = jnp.concatenate(
+        [
+            wq_send[..., :DH].reshape(r, n_ex, hp * DH),
+            wq_send[..., DH:].reshape(r, n_ex, hp * DR),
+        ],
+        axis=-1,
+    ).transpose(1, 0, 2)
     we_send = jnp.take(w_expand.reshape(rl, H, DH + DV), jnp.array(heads), axis=1)
     we_send = we_send.reshape(rl, n_ex, kv_cols).transpose(1, 0, 2)
     we_send = we_send.reshape(n_ex, r, rl * kv_cols // r)
@@ -1005,20 +1226,8 @@
     gain_lat = (
         pk_all[..., lat + n_experts + 2].reshape(n_dp * n_ex, r)[:, :rl].reshape(KVR).astype(F32)
     )
-    wo_send, _ = lax.optimization_barrier((to_owner_order(w_out), pk_all))
-    wo_col = lax.all_gather(wo_send, "dp", axis=0, tiled=False)
-    wo_rows = lax.all_to_all(
-        wo_col.reshape(parts, hp, r, width),
-        "expert",
-        0,
-        0,
-        axis_index_groups=part_groups,
-        tiled=True,
-    )
-    wo_rows = wo_rows.transpose(1, 0, 2, 3).reshape(hp * DV, width)
-
     col_groups = [[o * inner + i for i in range(inner)] for o in range(n_dp // inner)]
-    cot_send, _ = lax.optimization_barrier((cot_owner, wo_col))
+    cot_send, _ = lax.optimization_barrier((cot_owner, pk_all))
     cot_col = lax.all_gather(cot_send, "dp", axis=0, tiled=True, axis_index_groups=col_groups)
     slots_all = n_experts * capacity
     slot_col = pick(pk_all[..., small_cols : small_cols + slot_cols], e, 1)
@@ -1043,58 +1252,23 @@
     hot = sum((wanted[:, None] == slot_ids[None, :, j]).astype(BF) for j in range(top_k))
     hot_t = sum((slot_ids[:, j][:, None] == wanted[None, :]).astype(BF) for j in range(top_k))
 
-    def through(values):
+    def through(values, way):
         cut = values.reshape(chips, per_far, -1)
         got = [cut[0]]
         for m in range(1, chips):
-            perm = [(i, (i - 2 * m) % n_ex) for i in range(n_ex)]
+            perm = [(i, (i + 2 * m * way) % n_ex) for i in range(n_ex)]
             got.append(lax.ppermute(cut[m], "expert", perm))
         return jnp.concatenate(got, axis=0)
 
-    grad_send = mm(hot, cot_col).astype(BF).reshape(chips, per_far, width)
-
-    tok_plane = tok_all.reshape(seq, width)
-    hidden_one = rms_norm(tok_plane.astype(F32), gain_one).astype(BF)
     positions = jnp.arange(seq)
     cos_table, sine_table = rope_tables(positions)
-    query_raw = mm(hidden_one, wq).reshape(seq, hp, DH + DR)
-
-    def make_queries(query_in):
-        return jnp.concatenate(
-            [
-                query_in[..., :DH],
-                rotate(query_in[..., DH:], cos_table[:, None, :], sine_table[:, None, :]),
-            ],
-            axis=-1,
-        )
-
-    query_rot, query_back = jax.vjp(make_queries, query_raw)
-    queries = query_rot.astype(BF)
-    latent_raw = mm(hidden_one, w_lat)
-    latent_low = rms_norm(latent_raw[:, :KVR], gain_lat).astype(BF)
-    rope_low = rotate(latent_raw[:, KVR:], cos_table, sine_table).astype(BF)
-    expanded = mm(latent_low, wexp).astype(BF).reshape(seq, hp, DH + DV)
-    score_scale = (DH + DR) ** (-0.5)
-    allowed = (positions[None, :] <= positions[:, None]) & (positions[None, :] < lengths[0])
-    attn_probs, probs_low, keys, attended = [], [], [], []
-    for h in range(hp):
-        key = jnp.concatenate([expanded[:, h, :DH], rope_low], axis=1)
-        scores = jnp.where(allowed, mm_cols(queries[:, h], key) * score_scale, masked_score)
-        top = jnp.max(scores, axis=-1, keepdims=True)
-        exp_scores = jnp.exp(scores - top)
-        probs = exp_scores / jnp.sum(exp_scores, axis=-1, keepdims=True)
-        low = probs.astype(BF)
-        attn_probs.append(probs)
-        probs_low.append(low)
-        keys.append(key)
-        attended.append(mm(low, expanded[:, h, DH:]).astype(BF))
-    attended = jnp.concatenate(attended, axis=1)
-    out_part = mm(attended, wo_rows).astype(BF)
-    residual, x_col, grad_in, (wg, wu), (sgate, sup, sdown) = forward_exchange(
-        out_part.reshape(n_ex, rows, width),
+    cos_wide, sine_wide = jnp.tile(cos_table, (1, 4)), jnp.tile(sine_table, (1, 4))
+    keep = (positions < lengths[0]).astype(F32)[None]
+    attend_out, wo_rows, residual, x_col, (wg, wu), (sgate, sup, sdown) = forward_exchange(
+        [tok_all, gain_one[None], wq, pk_flat, gain_lat[None], wexp, cos_wide, sine_wide, keep],
+        to_owner_order(w_out),
         to_owner_order(tokens),
         gain_two[None],
-        grad_send,
         [w.reshape(-1, n_ex, r, ff_e) for w in (expert_gate, expert_up)],
         [w.reshape(r, inner, ff_s).transpose(1, 0, 2) for w in (shared_gate, shared_up, shared_down)],
         n_dp,
@@ -1102,10 +1276,11 @@
         inner,
         2,
     )
+    hidden_one, latent_raw, latent_low, qcat, kcat, value, lse, attended = attend_out
+    wo_rows = wo_rows.reshape(hp * DV, width)
     sgate, sup, sdown = (w.reshape(width, ff_s) for w in (sgate, sup, sdown))
     hidden_two = pick(x_col, my_local)
     x_col = x_col.reshape(inner * rows, width)
-    grad_in = grad_in.reshape(n_slots, width)
 
     x_in, (wd,) = between(
         mm(hot, x_col).astype(BF).reshape(chips, per_far, width),
@@ -1118,6 +1293,7 @@
         8,
     )
     x_in = x_in.reshape(n_slots, width)
+    grad_in = through(mm(hot, cot_col).astype(BF), 1)
     wg, wu, wd = (w.reshape(width, ff_e) for w in (wg, wu, wd))
 
     def probs_of(logits):
@@ -1148,7 +1324,7 @@
     expert_b = mm(x_in, wu)
     expert_hidden, expert_back = jax.vjp(swiglu, expert_a, expert_b)
     expert_hidden = expert_hidden.astype(BF)
-    rows_back = through(mm_cols(expert_hidden, wd).astype(BF))
+    rows_back = through(mm_cols(expert_hidden, wd).astype(BF), -1)
     slot_grad = (slot_gate * grad_in.astype(F32)).astype(BF)
     grad_ea, grad_eb = (v.astype(BF) for v in expert_back(mm(slot_grad, wd)))
     expert_totals = [
@@ -1199,48 +1375,31 @@
     grad_resid_norm, grad_gain_two = norm_two_back(grad_hidden_two)
     grad_residual = cot_owner.astype(F32) + grad_resid_norm
 
-    grad_attn = plane_gather(grad_residual.astype(BF), n_dp, n_ex, 4).reshape(seq, width)
+    out_col, shared_grads, _ = lax.optimization_barrier((out_col, shared_grads, dx_sum))
     out_sum = lax.psum_scatter(
         out_col, "dp", scatter_dimension=0, tiled=True, axis_index_groups=col_groups
     )
     out_tokens = from_owner_order((residual + out_sum.astype(F32)).astype(BF))
-    shared_grads, _ = lax.optimization_barrier((shared_grads, grad_attn))
     shared_sums = [
         lax.psum_scatter(
             grad.reshape(n_ex, n_dp, r, ff_s), "expert", scatter_dimension=0, tiled=True
         ).reshape(n_dp, r, ff_s)
         for grad in shared_grads
     ]
-    grad_attended = mm_cols(grad_attn, wo_rows).astype(BF)
-    grad_wout = mm_rows(attended, grad_attn).astype(BF)
-    grad_rope = 0.0
-    grad_queries, grad_expanded = [], []
-    for h in range(hp):
-        gat = grad_attended[:, h * DV : (h + 1) * DV]
-        probs = attn_probs[h]
-        dp = mm_cols(gat, expanded[:, h, DH:])
-        grad_scores = probs * (dp - jnp.sum(dp * probs, axis=-1, keepdims=True))
-        grad_raw = jnp.where(allowed, grad_scores * score_scale, 0.0).astype(BF)
-        grad_queries.append(mm(grad_raw, keys[h]))
-        grad_key = mm_rows(grad_raw, queries[:, h])
-        grad_rope = grad_rope + grad_key[:, DH:]
-        grad_expanded += [grad_key[:, :DH], mm_rows(probs_low[h], gat)]
-    grad_expanded = jnp.concatenate(grad_expanded, axis=1).astype(BF)
-    (grad_query_raw,) = query_back(jnp.stack(grad_queries, axis=1))
-    grad_query_low = grad_query_raw.reshape(seq, head_cols).astype(BF)
-    grad_latent_part = jnp.concatenate([mm_cols(grad_expanded, wexp), grad_rope], axis=1)
-    grad_latent_part = jnp.pad(grad_latent_part, ((0, 0), (0, -lat % 128))).astype(BF)
-    grad_query_part = mm_cols(grad_query_low, wq).astype(BF)
-    (grad_query_sum, grad_latent_sum), (gate_back,) = plane_sum(
-        [grad_query_part.reshape(n_ex, rows, width), grad_latent_part.reshape(n_ex, rows, -1)],
+    attend_grads, (gate_back,) = backward_exchange(
+        grad_residual.astype(BF),
+        [wo_rows, wq, wexp, cos_wide, sine_wide, keep, qcat, kcat, value, lse, attended],
+        hidden_one,
+        latent_low,
         expert_totals[:1],
         n_dp,
         n_ex,
         inner,
         5,
     )
+    grad_query_sum, grad_latent_sum, grad_wout, grad_wq, grad_we = attend_grads
     own_start = e * rows
-    latent_own = lax.dynamic_slice_in_dim(latent_raw, own_start, rows, 0)
+    latent_own = lax.dynamic_slice_in_dim(latent_raw, own_start, rows, 0)[:, :lat]
     cos_own = lax.dynamic_slice_in_dim(cos_table, own_start, rows, 0)
     sine_own = lax.dynamic_slice_in_dim(sine_table, own_start, rows, 0)
 
@@ -1268,8 +1427,7 @@
         axis_index_groups=part_groups,
         tiled=True,
     ).reshape(n_dp, r, width)
-    grad_wq = mm_rows(hidden_one, grad_query_low).astype(BF).reshape(n_dp, n_ex, r, head_cols)
-    grad_we = mm_rows(latent_low, grad_expanded).astype(BF)
+    grad_wq = grad_wq.reshape(n_dp, n_ex, r, head_cols)
     grad_we = grad_we.reshape(n_dp, n_ex, r, rl * kv_cols // r)
     heads_grad = jnp.concatenate([grad_wq, grad_we], axis=-1)
     hidden_own = lax.dynamic_slice_in_dim(hidden_one, own_start, rows, 0)
@@ -1297,7 +1455,14 @@
         return jnp.sum(values.astype(F32), axis=0)
 
     heads_all = heads_all.astype(F32)
-    sum_wq = heads_all[..., :head_cols].transpose(1, 0, 2).reshape(r, H, DH + DR)
+    sum_wq = heads_all[..., :head_cols].transpose(1, 0, 2)
+    sum_wq = jnp.concatenate(
+        [
+            sum_wq[..., : hp * DH].reshape(r, n_ex, hp, DH),
+            sum_wq[..., hp * DH :].reshape(r, n_ex, hp, DR),
+        ],
+        axis=-1,
+    ).reshape(r, H, DH + DR)
     sum_wq = jnp.take(sum_wq, jnp.array(heads_back), axis=1).reshape(r, H * (DH + DR))
     sum_we = heads_all[..., head_cols:].reshape(n_ex, rl, kv_cols).transpose(1, 0, 2)
     sum_we = jnp.take(sum_we.reshape(rl, H, DH + DV), jnp.array(heads_back), axis=1)

time: 1210 us -> 1160 us (0.959)
  local copies, waits for them, and re-layouts: 140 us -> 102 us
  matrix products: 203 us -> 171 us
  other arithmetic: 62 us -> 38.7 us
  waiting for transfers between devices: 15.1 us -> 37.2 us
  Pallas kernels: 756 us -> 776 us
    pallas_call x3 -> x2, Pallas kernels: 306 us -> 341 us  [the longest x1 236 us: forward_exchange(): pl.pallas_call(kernel, out_shape=[sds((seq, width), BF), sds((seq, attend...]
    pallas_call x2, Pallas kernels: 174 us -> 140 us  [between(): pl.pallas_call(kernel, out_shape=[jax.ShapeDtypeStruct(blocks.shape, BF)]...]
    unnamed x314 -> x173, local copies, waits for them, and re-layouts: 36.5 us -> 7.79 us
    dot_general x16 -> x9, matrix products: 62.4 us -> 48.1 us  [mm_cols(): lax.dot_general(left, right, (((1,), (1,)), ((), ())), preferred_element_...]
    pallas_call x1, Pallas kernels: 57.6 us -> 71.3 us  [first_exchange(): pl.pallas_call(kernel, out_shape=[jax.ShapeDtypeStruct((n_ex,) + tok.shap...]
    reduce_scatter x3, waiting for transfers between devices: 0.02 us -> 13.2 us  [shards(): lax.psum_scatter(grad.reshape(n_ex, n_dp, r, ff_s), 'expert', scatter_dim...]
    dot_general x20 -> x12, matrix products: 85.4 us -> 75.2 us  [mm(): return jnp.dot(left, right, preferred_element_type=F32)]
    dot_general x15 -> x8, matrix products: 55.3 us -> 47.9 us  [mm_rows(): lax.dot_general(left, right, (((0,), (0,)), ((), ())), preferred_element_...]
  transfers between devices with their start and end apart: 10 -> 12, of which waited for: 1 -> 4; matrix products, arithmetic and copies ran while one was open for 20% -> 18% of each run, Pallas kernels for 19% -> 42%
where the time goes in v6:
time: 1160 us; the launch traced here: 1150 us
  Pallas kernels  776 us (67%)
  matrix products  171 us (15%)
  local copies, waits for them, and re-layouts  102 us (9%)
  other arithmetic  38.7 us (3%)
  waiting for transfers between devices  37.2 us (3%)
  between operations  16.3 us (1%)
  starting transfers between devices  11.6 us (1%)
    pallas_call x1, Pallas kernels, forward_exchange(): pl.pallas_call(kernel, out_shape=[sds((seq, width), BF), sds((seq, attend...  236 us
    pallas_call x1, Pallas kernels, last_exchange(): pl.pallas_call(kernel, out_shape=[jax.ShapeDtypeStruct(heads.shape[1:], B...  170 us
    pallas_call x2, Pallas kernels, between(): pl.pallas_call(kernel, out_shape=[jax.ShapeDtypeStruct(blocks.shape, BF)]...  140 us
    pallas_call x1, Pallas kernels, backward_exchange(): pl.pallas_call(kernel, out_shape=[sds((rows, width), F32), sds((rows, lat...  105 us
    dot_general x12, matrix products, mm(): return jnp.dot(left, right, preferred_element_type=F32)  75.2 us
    pallas_call x1, Pallas kernels, first_exchange(): pl.pallas_call(kernel, out_shape=[jax.ShapeDtypeStruct((n_ex,) + tok.shap...  71.3 us
    pallas_call x1, Pallas kernels, column_sum(): pl.pallas_call(kernel, out_shape=jax.ShapeDtypeStruct(shape, F32), in_spe...  53.9 us
    dot_general x9, matrix products, mm_cols(): lax.dot_general(left, right, (((1,), (1,)), ((), ())), preferred_element_...  48.1 us
  transfers between devices with their start and end apart: 12, of which 4 were waited for; matrix products, arithmetic and copies ran while one was open for 18% of the time, Pallas kernels for 42%

profile of v6, /device:TPU:11, one launch (start us, length us, event | category | flops | bytes accessed | tf_op | source)
XLA Modules:
  0.0 1153.4 jit_solution(3434449912239818805)
XLA Ops:
  16.5 71.3 %shard_map.342 = (bf16[8,128,2048]{2,1,0:T(8,128)(2,1)}, bf16[4,8,64,512]{3,2,1,0:T(8,128)(2,1)}, bf16[4,8,64,640]{3,2,1,0:T(8,128)(2,1)}) custom-call(bf16[128,2048]{1,0:T(8,128)(2,1)} %tok_ref.1, bf16[8,64,512]{2,1,0:T(8,128)(2,1)} %pad_maximum_fusion.5.wa_ref, bf16[64,640]{1,0:T(8,128)(2,1)} %concatenate.46.pk_ref), custom_call_target="tpu_custom_call" | custom-call | tf_op jit(solution)/shard_map/pallas_call | solution.py:350
  90.1 2.8 slice.173
  123.2 235.5 %shard_map.343 = (bf16[1024,2048]{1,0:T(8,128)(2,1)}, f32[1024,640]{1,0:T(8,128)}, bf16[1024,512]{1,0:T(8,128)(2,1)}, bf16[2,1024,256]{2,1,0:T(8,128)(2,1)}, bf1...) custom-call(bf16[8,128,2048]{2,1,0:T(8,128)(2,1)} %get-tuple-element, ...), custom_call_target="tpu_custom_call" | custom-call | tf_op jit(solution)/shard_map/pallas_call | solution.py:630
  358.7 6.8 convolution_convert_fusion.5
  366.2 67.9 %shard_map.344 = (bf16[4,256,2048]{2,1,0:T(8,128)(2,1)}, bf16[8,4,64,1408]{3,2,1,0:T(8,128)(2,1)}) custom-call(bf16[4,256,2048]{2,1,0:T(8,128)(2,1)} %bitcast.216, bf16[2,8,64,1408]{3,2,1,0:T(8,128)(2,1)} %bitcast.232), custom_call_target="tpu_custom_call" | custom-call | tf_op jit(solution)/shard_map/pallas_call | solution.py:709
  434.1 3.5 fusion.61
  437.7 10.5 fusion.63
  451.5 5.2 fusion.65
  456.7 2.8 fusion.66
  459.6 8.4 fusion.64
  468.0 4.7 convolution_convert_fusion.3
  474.7 2.5 collective-permute-start.3
  479.6 3.3 convolution_convert_fusion.7
  482.9 3.3 convolution_convert_fusion.6
  486.2 3.2 convolution_convert_fusion.8
  489.4 3.9 fusion.69
  493.3 3.9 fusion.67
  498.6 22.0 %collective-permute-done.4 = bf16[256,2048]{1,0:T(8,128)(2,1)S(1)} collective-permute-done((bf16[256,2048]{1,0:T(8,128)(2,1)S(1)}, bf16[256,2048]{1,0:T(8,128)(2,1)S(1)}, u32[]{:S(2)}, u32[]{:S(2)}) %collective-permute-start.4) | collective-permute-done | bytes 1048608 | tf_op jit(solution)/shard_map/ppermute | solution.py:1260
  522.1 17.5 %multiply_convert_fusion.1 = (bf16[1024,1408]{1,0:T(8,128)(2,1)}, bf16[1024,1408]{1,0:T(8,128)(2,1)}, bf16[1024,1408]{1,0:T(8,128)(2,1)}) fusion(f32[1024,1408]{1,0:T(8,128)} %fusion.63, f32[1024,1408]{1,0:T(8,128)} %fusion.64, bf16[2048,1408]{1,0:T(8,128)(2,1)} %bitcast.284, bf16[256,2048]{1,0:T(8,128)(2,1)} %copy-done.66, ...), kind=kOutput, calls=%fused_computation.13 | convolution fusion | flops 5949620224 | bytes 30150656 | tf_op jit(solution)/shard_map/dot_general | solution.py:56
  539.6 8.7 fusion.68
  548.3 8.9 convolution_convert_fusion.4
  561.4 8.2 add_convert_fusion
  569.6 11.1 convolution_convert_fusion.2
  580.7 72.1 %shard_map.345 = (bf16[4,256,2048]{2,1,0:T(8,128)(2,1)}, bf16[1,2,8,64,1408]{4,3,2,1,0:T(8,128)(2,1)}) custom-call(bf16[4,256,2048]{2,1,0:T(8,128)(2,1)} %bitcast.218, bf16[8,4,64,1408]{3,2,1,0:T(8,128)(2,1)} %bitcast.212), custom_call_target="tpu_custom_call" | custom-call | tf_op jit(solution)/shard_map/pallas_call | solution.py:709
  652.8 5.5 fusion.53
  660.2 6.7 convert_multiply_fusion
  666.9 3.2 reshape.800
  673.3 3.0 concatenate.51.x_ref
  676.4 53.9 %shard_map.346 = f32[128,2176]{1,0:T(8,128)} custom-call(bf16[4,128,2176]{2,1,0:T(8,128)(2,1)} %concatenate.51.x_ref), custom_call_target="tpu_custom_call" | custom-call | tf_op jit(solution)/shard_map/pallas_call | solution.py:255
  730.3 7.3 add_convert_fusion.2
  737.7 2.9 copy.455
  740.6 4.7 copy.456
  748.9 11.1 convolution_convert_fusion.1
  760.0 4.6 copy.457
  764.6 11.2 convolution_convert_fusion
  775.9 2.9 convert.74
  782.2 2.7 multiply_reduce_fusion
  786.1 2.7 fusion.56
  792.9 105.2 %shard_map.347 = (f32[128,2048]{1,0:T(8,128)}, f32[128,640]{1,0:T(8,128)}, bf16[256,2048]{1,0:T(8,128)(2,1)}, bf16[2048,384]{1,0:T(8,128)(2,1)}, bf16[512,512]{1...) custom-call(bf16[128,2048]{1,0:T(8,128)(2,1)} %get-tuple-element.232.refs_0_, bf16[256,2048]{1,0:T(8,128)(2,1)} %bitcast.253, ...), custom_call_target="tpu_custom_call" | custom-call | tf_op jit(solution)/shard_map/pallas_call | solution.py:961
  902.8 4.5 all-to-all-start
  910.5 3.3 convolution_convert_fusion.9
  913.8 4.5 copy.447
  918.3 3.4 fusion.19
  925.6 5.7 concatenate.53
  934.1 2.9 convert.72
  940.6 13.2 %reduce-scatter.11.cloned.1.call-done = bf16[1,4,64,704]{3,2,1,0:T(8,128)(2,1)} async-done(((bf16[8,4,64,704]{3,2,1,0:T(8,128)(2,1)}), bf16[1,4,64,704]{3,2,1,0:T(8,128)(2,1)}) %reduce-scatter.11.cloned.1.call-update) | async-done | bytes 360464 | tf_op jit(solution)/shard_map/reduce_scatter | solution.py:1384
  953.8 170.3 %shard_map.348 = (bf16[8,64,512]{2,1,0:T(8,128)(2,1)}, f32[64,2048]{1,0:T(8,128)}, f32[64,640]{1,0:T(8,128)}, bf16[4,64,704]{2,1,0:T(8,128)(2,1)}, bf16[4,64,704...) custom-call(bf16[4,8,64,512]{3,2,1,0:T(8,128)(2,1)} %pad_maximum_fusion.1.heads_ref, ...), custom_call_target="tpu_custom_call" | custom-call | tf_op jit(solution)/shard_map/pallas_call | solution.py:1105
  1141.3 4.7 convert.73
  (375 shorter events, 109.2 us)
Async XLA Ops:
  7.2 460.8 %all-gather.2.cloned.1.call-start = ((), (), s32[]{:S(2)}) async-start(), calls=%async_computation.5 | async-start | bytes 2621440 | tf_op jit(solution)/shard_map/all_gather | solution.py:1231
  16.5 78.3 %copy-start.3 = (bf16[128,2048]{1,0:T(8,128)(2,1)S(1)}, bf16[128,2048]{1,0:T(8,128)(2,1)}, u32[]{:S(2)}) copy-start(bf16[128,2048]{1,0:T(8,128)(2,1)} %tok_ref.1) | copy-start | bytes 1572868
  87.8 8.0 copy-start
  87.8 698.3 %reduce-scatter.5.cloned.1.call-start = ((), (), s32[]{:S(2)}) async-start(), calls=%async_computation.6 | async-start | bytes 2621440 | tf_op jit(solution)/shard_map/reduce_scatter | solution.py:1379
  105.0 6.4 copy-start.18
  106.2 7.5 copy-start.36
  114.2 6.4 copy-start.61
  118.3 315.8 %copy-start.23 = (bf16[2048,16]{0,1:T(8,128)(2,1)}, bf16[2048,16]{0,1:T(8,128)(2,1)S(1)}, u32[]{:S(2)}) copy-start(bf16[2048,16]{0,1:T(8,128)(2,1)S(1)} %reshape.785) | copy-start | bytes 196612
  118.9 329.7 %copy-start.50 = (pred[16]{0:T(512)(128)(4,1)}, pred[16]{0:T(512)(128)(4,1)S(1)}, u32[]{:S(2)}) copy-start(pred[16]{0:T(512)(128)(4,1)S(1)} %iota_compare_fusion.3) | copy-start | bytes 52
  119.4 329.2 %copy-start.52 = (pred[16]{0:T(512)(128)(4,1)}, pred[16]{0:T(512)(128)(4,1)S(1)}, u32[]{:S(2)}) copy-start(pred[16]{0:T(512)(128)(4,1)S(1)} %get-tuple-element.270) | copy-start | bytes 52
  119.4 329.2 %copy-start.54 = (pred[16]{0:T(512)(128)(4,1)}, pred[16]{0:T(512)(128)(4,1)S(1)}, u32[]{:S(2)}) copy-start(pred[16]{0:T(512)(128)(4,1)S(1)} %get-tuple-element.271) | copy-start | bytes 52
  358.7 6.9 copy-start.10
  450.2 9.4 slice-start
  451.5 8.1 slice-start.1
  473.2 25.4 %collective-permute-start.5 = (bf16[256,2048]{1,0:T(8,128)(2,1)S(1)}, bf16[256,2048]{1,0:T(8,128)(2,1)S(1)}, u32[]{:S(2)}, u32[]{:S(2)}) collective-permute-start(bf16[256,2048]{1,0:T(8,128)(2,1)S(1)} %get-tuple-element.239), channel_id=1, source_target_pairs={{0,6},{1,7},{2,0},{3,1},{4,2},{5,3},{6,4},{7,5},{8,14},{9,15},{10,... | collective-permute-start | bytes 3145736 | tf_op jit(solution)/shard_map/ppermute | solution.py:1260
  473.6 47.0 %collective-permute-start.4 = (bf16[256,2048]{1,0:T(8,128)(2,1)S(1)}, bf16[256,2048]{1,0:T(8,128)(2,1)S(1)}, u32[]{:S(2)}, u32[]{:S(2)}) collective-permute-start(bf16[256,2048]{1,0:T(8,128)(2,1)S(1)} %get-tuple-element.240), channel_id=1, source_target_pairs={{0,4},{1,5},{2,6},{3,7},{4,0},{5,1},{6,2},{7,3},{8,12},{9,13},{10,... | collective-permute-start | bytes 3145736 | tf_op jit(solution)/shard_map/ppermute | solution.py:1260
  474.7 46.3 %collective-permute-start.3 = (bf16[256,2048]{1,0:T(8,128)(2,1)S(1)}, bf16[256,2048]{1,0:T(8,128)(2,1)S(1)}, u32[]{:S(2)}, u32[]{:S(2)}) collective-permute-start(bf16[256,2048]{1,0:T(8,128)(2,1)S(1)} %get-tuple-element.241), channel_id=1, source_target_pairs={{0,2},{1,3},{2,4},{3,5},{4,6},{5,7},{6,0},{7,1},{8,10},{9,11},{10,... | collective-permute-start | bytes 3145736 | tf_op jit(solution)/shard_map/ppermute | solution.py:1260
  493.3 46.2 %slice-start.4 = ((s8[5767168]{0:T(1024)(128)(4,1)}), s8[4194304]{0:T(1024)(128)(4,1)S(1)}, s32[]{:S(2)}) async-start(s8[5767168]{0:T(1024)(128)(4,1)} %bitcast.281), calls=%async_computation.14 | async-start | bytes 8388608
  498.6 22.5 %copy-start.66 = (bf16[256,2048]{1,0:T(8,128)(2,1)}, bf16[256,2048]{1,0:T(8,128)(2,1)S(1)}, u32[]{:S(2)}) copy-start(bf16[256,2048]{1,0:T(8,128)(2,1)S(1)} %collective-permute-done.5) | copy-start | bytes 3145732
  522.1 17.5 %slice-start.5 = ((s8[5767168]{0:T(1024)(128)(4,1)}), s8[1572864]{0:T(1024)(128)(4,1)S(1)}, s32[]{:S(2)}) async-start(s8[5767168]{0:T(1024)(128)(4,1)} %bitcast.281), calls=%async_computation.15 | async-start | bytes 3145728
  539.6 8.7 copy-start.76
  539.6 21.7 %slice-start.2 = ((s8[5767168]{0:T(1024)(128)(4,1)}), s8[4194304]{0:T(1024)(128)(4,1)S(1)}, s32[]{:S(2)}) async-start(s8[5767168]{0:T(1024)(128)(4,1)} %bitcast.277), calls=%async_computation.12 | async-start | bytes 8388608
  548.2 13.1 %slice-start.3 = ((s8[5767168]{0:T(1024)(128)(4,1)}), s8[1572864]{0:T(1024)(128)(4,1)S(1)}, s32[]{:S(2)}) async-start(s8[5767168]{0:T(1024)(128)(4,1)} %bitcast.277), calls=%async_computation.13 | async-start | bytes 3145728
  558.9 101.4 %copy-start.26 = (bf16[256,2048]{1,0:T(8,128)(2,1)}, bf16[256,2048]{1,0:T(8,128)(2,1)S(1)}, u32[]{:S(2)}) copy-start(bf16[256,2048]{1,0:T(8,128)(2,1)S(1)} %get-tuple-element.242) | copy-start | bytes 3145732
  558.9 101.3 %collective-permute-start.2 = (bf16[256,2048]{1,0:T(8,128)(2,1)}, bf16[256,2048]{1,0:T(8,128)(2,1)}, u32[]{:S(2)}, u32[]{:S(2)}) collective-permute-start(bf16[256,2048]{1,0:T(8,128)(2,1)} %get-tuple-element.243), channel_id=1, source_target_pairs={{0,2},{1,3},{2,4},{3,5},{4,6},{5,7},{6,0},{7,1},{8,10},{9,11},{10,... | collective-permute-start | bytes 3145736 | tf_op jit(solution)/shard_map/ppermute | solution.py:1260
  559.2 101.0 %collective-permute-start.1 = (bf16[256,2048]{1,0:T(8,128)(2,1)}, bf16[256,2048]{1,0:T(8,128)(2,1)}, u32[]{:S(2)}, u32[]{:S(2)}) collective-permute-start(bf16[256,2048]{1,0:T(8,128)(2,1)} %get-tuple-element.244), channel_id=1, source_target_pairs={{0,4},{1,5},{2,6},{3,7},{4,0},{5,1},{6,2},{7,3},{8,12},{9,13},{10,... | collective-permute-start | bytes 3145736 | tf_op jit(solution)/shard_map/ppermute | solution.py:1260
  560.3 99.9 %collective-permute-start = (bf16[256,2048]{1,0:T(8,128)(2,1)}, bf16[256,2048]{1,0:T(8,128)(2,1)}, u32[]{:S(2)}, u32[]{:S(2)}) collective-permute-start(bf16[256,2048]{1,0:T(8,128)(2,1)} %get-tuple-element.245), channel_id=1, source_target_pairs={{0,6},{1,7},{2,0},{3,1},{4,2},{5,3},{6,4},{7,5},{8,14},{9,15},{10,... | collective-permute-start | bytes 3145736 | tf_op jit(solution)/shard_map/ppermute | solution.py:1260
  561.3 8.3 copy-start.67
  561.3 8.3 copy-start.69
  561.3 8.3 copy-start.71
  652.7 5.6 copy-start.8
  652.7 5.5 copy-start.12
  666.9 6.0 copy-start.51
  666.9 6.0 copy-start.53
  666.9 6.0 copy-start.55
  666.9 6.0 copy-start.58
  673.3 57.0 %copy-start.37 = (bf16[512,256]{1,0:T(8,128)(2,1)S(1)}, bf16[512,256]{1,0:T(8,128)(2,1)}, u32[]{:S(2)}) copy-start(bf16[512,256]{1,0:T(8,128)(2,1)} %get-tuple-element.252) | copy-start | bytes 786436
  673.3 57.0 %copy-start.38 = (bf16[512,256]{1,0:T(8,128)(2,1)S(1)}, bf16[512,256]{1,0:T(8,128)(2,1)}, u32[]{:S(2)}) copy-start(bf16[512,256]{1,0:T(8,128)(2,1)} %get-tuple-element.253) | copy-start | bytes 786436
  676.3 53.9 %copy-start.39 = (bf16[512,256]{1,0:T(8,128)(2,1)S(1)}, bf16[512,256]{1,0:T(8,128)(2,1)}, u32[]{:S(2)}) copy-start(bf16[512,256]{1,0:T(8,128)(2,1)} %get-tuple-element.254) | copy-start | bytes 786436
  676.4 53.9 %copy-start.40 = (bf16[512,256]{1,0:T(8,128)(2,1)S(1)}, bf16[512,256]{1,0:T(8,128)(2,1)}, u32[]{:S(2)}) copy-start(bf16[512,256]{1,0:T(8,128)(2,1)} %get-tuple-element.255) | copy-start | bytes 786436
  730.3 7.3 copy-start.14
  737.6 203.0 %reduce-scatter.7.cloned.1.call-start = ((), (), s32[]{:S(2)}) async-start(), calls=%async_computation.7 | async-start | bytes 3538944 | tf_op jit(solution)/shard_map/reduce_scatter | solution.py:1384
  740.6 200.1 %reduce-scatter.9.cloned.1.call-start = ((), (), s32[]{:S(2)}) async-start(), calls=%async_computation.8 | async-start | bytes 3538944 | tf_op jit(solution)/shard_map/reduce_scatter | solution.py:1384
  745.3 208.5 %reduce-scatter.11.cloned.1.call-start = ((), (), s32[]{:S(2)}) async-start(), calls=%async_computation.9 | async-start | bytes 3538944 | tf_op jit(solution)/shard_map/reduce_scatter | solution.py:1384
  764.6 11.2 copy-start.13
  775.8 6.3 copy-start.24
  898.2 9.1 copy-start.21
  902.8 37.9 %all-to-all-start = ((bf16[2,2,64,2048]{3,2,1,0:T(8,128)(2,1)}), bf16[2,2,64,2048]{3,2,1,0:T(8,128)(2,1)}, u32[]{:S(2)}, u32[]{:S(2)}) async-start(bf16[2,2,64,2048]{3,2,1,0:T(8,128)(2,1)} %bitcast.187), calls=%async_computation.1 | async-start | bytes 2097152 | tf_op jit(solution)/shard_map/all_to_all | solution.py:1422
  (47 other events, 161.9 us)
Sparse Core Ops, SparseCore 0:
  87.9 44.0 all-gather.1
  737.7 41.5 reduce-scatter.4
  783.1 63.6 reduce-scatter.6
  850.0 53.9 reduce-scatter.8
  907.6 46.2 reduce-scatter.10

commit v7 on v6

--- a/solution.py
+++ b/solution.py
@@ -232,34 +232,106 @@
     remote(region, region, sem, sem, device).wait_recv()
 
 
-def column_sum(array, n_dp, n_ex, inner, collective_id):
+def column_sum(array, shared, totals, n_dp, n_ex, inner, collective_id):
+    chips = n_ex // 2
     shape = array.shape[1:]
-
-    def kernel(x_ref, o_ref, buf, send, recv):
-        z, e, c, k, sibling, same_core, _ = places(n_dp, n_ex)
+    extra = len(totals)
+    _, _, r, ff_s = shared[0].shape
+
+    def kernel(x_ref, *refs):
+        s_in, t_refs, refs = refs[:3], refs[3 : 3 + extra], refs[3 + extra :]
+        o_ref, s_out, back_refs = refs[0], refs[1:4], refs[4 : 4 + extra]
+        refs = refs[4 + extra :]
+        buf, from_sib, out_buf, from_far = refs[:4]
+        send, recv, near_s, near_r, far_s, far_r = refs[4:10]
+        rest = refs[10:]
+        z, e, c, k, sibling, same_core, column = places(n_dp, n_ex)
         group = column_group(z, e, inner)
-        greet(group[1:])
+        greet(same_core + [sibling] + column + [(d[0], sibling[1]) for d in column])
+        backs = [
+            ExpertsBack(t_refs[m], back_refs[m], rest[7 * m : 7 * m + 7], n_dp, n_ex, inner)
+            for m in range(extra)
+        ]
         copies = []
         for i in range(1, inner):
             to = lax.rem(z + i, inner)
             copy = remote(x_ref.at[to], buf.at[i], send.at[i], recv.at[i], group[i])
             copy.start()
             copies.append(copy)
+        near, far = {}, {}
+        for i in list(range(1, chips)) + [0]:
+            chip = lax.rem(c + i, chips)
+            for m in range(3):
+                near[i, m] = remote(
+                    s_in[m].at[chip * 2 + 1 - k], from_sib.at[m, i],
+                    near_s.at[m, i], near_r.at[m, i], sibling,
+                )
+                near[i, m].start()
+        for back in backs:
+            back.begin()
+
+        def pair(i, m):
+            chip = lax.rem(c + i, chips)
+            near[i, m].wait_recv()
+
+            def row(d, carry):
+                out_buf[m, i, d] = (
+                    s_in[m][chip * 2 + k, d].astype(F32) + from_sib[m, i, d].astype(F32)
+                ).astype(BF)
+                return carry
+
+            lax.fori_loop(0, n_dp, row, 0)
+
+        for i in range(1, chips):
+            for m in range(3):
+                pair(i, m)
+                far[i, m] = remote(
+                    out_buf.at[m, i], from_far.at[m, i], far_s.at[m, i], far_r.at[m, i],
+                    same_core[i - 1],
+                )
+                far[i, m].start()
         o_ref[...] = x_ref[lax.rem(z, inner)].astype(F32)
+        for back in backs:
+            back.pass_on()
+        for m in range(3):
+            pair(0, m)
         for i in range(1, inner):
             copies[i - 1].wait_recv()
             o_ref[...] += buf[i].astype(F32)
-        for copy in copies:
+        for m in range(3):
+            for i in range(1, chips):
+                far[i, m].wait_recv()
+
+            def row(d, carry, m=m):
+                total = out_buf[m, 0, d].astype(F32)
+                for i in range(1, chips):
+                    total = total + from_far[m, i, d].astype(F32)
+                s_out[m][d] = total.astype(BF)
+                return carry
+
+            lax.fori_loop(0, n_dp, row, 0)
+        for copy in copies + list(near.values()) + list(far.values()):
             copy.wait_send()
-
-    return pl.pallas_call(
+        for back in backs:
+            back.end()
+
+    dma = pltpu.SemaphoreType.DMA
+    scratch = [pltpu.VMEM((inner,) + shape, BF)]
+    scratch += [pltpu.VMEM((3, chips, n_dp, r, ff_s), BF)] * 3
+    scratch += [dma((inner,))] * 2 + [dma((3, chips))] * 4
+    for total in totals:
+        scratch += ExpertsBack.scratch(total, n_dp, inner)
+    outs = pl.pallas_call(
         kernel,
-        out_shape=jax.ShapeDtypeStruct(shape, F32),
-        in_specs=[VMEM],
-        out_specs=VMEM,
-        scratch_shapes=[pltpu.VMEM((inner,) + shape, BF)] + [pltpu.SemaphoreType.DMA((inner,))] * 2,
+        out_shape=[jax.ShapeDtypeStruct(shape, F32)]
+        + [jax.ShapeDtypeStruct((n_dp, r, ff_s), BF)] * 3
+        + [ExpertsBack.out(total, n_dp, inner) for total in totals],
+        in_specs=[VMEM] * 4 + [ANY] * extra,
+        out_specs=[VMEM] * 4 + [ANY] * extra,
+        scratch_shapes=scratch,
         compiler_params=params(collective_id),
-    )(array)
+    )(array, *shared, *totals)
+    return outs[0], outs[1:4], outs[4:]
 
 
 def column_group(z, e, inner):
@@ -827,31 +899,64 @@
                         wait_recv(region, self.recv.at[o, j, h], self.sibling)
 
 
-def backward_exchange(grad, attend, hidden, latent_low, totals, n_dp, n_ex, inner, collective_id):
+def rms_back(x, gain, grad):
+    root = lax.rsqrt(jnp.mean(x * x, axis=-1, keepdims=True) + norm_eps)
+    scaled = grad * gain
+    along = jnp.mean(x * scaled, axis=-1, keepdims=True)
+    return root * scaled - x * (root * root * root) * along, grad * x * root
+
+
+def backward_exchange(
+    grad, attend, hidden, latent_low, own, shared, totals, n_dp, n_ex, inner, collective_id
+):
     chips = n_ex // 2
     rows, width = grad.shape
     seq = n_ex * rows
     extra = len(totals)
     wq, we = attend[1], attend[2]
     lat_cols = KVR + 2 * DR
+    r = width // (n_dp * n_ex)
+    rl = KVR // (n_dp * n_ex)
+    parts = DV // r
+    hp = n_dp // parts
+    n_dev = n_dp * n_ex
+    wq_cols = wq.shape[1]
+    we_cols = rl * we.shape[1] // r
+    head_cols = wq_cols + we_cols
 
     def kernel(*refs):
         grad_ref, att_in, refs = refs[0], refs[1:12], refs[12:]
-        hidden_ref, low_ref, t_refs = refs[0], refs[1], refs[2 : 2 + extra]
-        refs = refs[2 + extra :]
-        sums, wout_ref, wq_ref, we_ref = refs[:2], refs[2], refs[3], refs[4]
-        back_refs, refs = refs[5 : 5 + extra], refs[5 + extra :]
+        hidden_ref, low_ref, refs = refs[0], refs[1], refs[2:]
+        wl_ref, lat_ref, tok_ref, gain_ref, glat_ref, gnat_ref, router_ref, gtwo_ref = refs[:8]
+        sh_in, t_refs, refs = refs[8:11], refs[11 : 11 + extra], refs[11 + extra :]
+        tok_out, vec_out, pack_out, heads_mid, heads_out, wout_out = refs[:6]
+        sh_out, back_refs, refs = refs[6:9], refs[9 : 9 + extra], refs[9 + extra :]
         gbuf, att_tmp, refs = refs[0], refs[1:8], refs[8:]
-        x_refs, bufs, refs = refs[:2], refs[2:8], refs[8:]
+        part_l, bufs, sums, refs = refs[0], refs[1:7], refs[7:9], refs[9:]
+        hsrc, wsrc, pack, psib, pout, pfar, psum, pbuf, vec, vbuf, vzbuf = refs[:11]
+        refs = refs[11:]
         t_s, t_r, ts_s, ts_r, local = refs[:5]
-        sems, rest = refs[5:13], refs[13:]
+        sems, refs = refs[5:13], refs[13:]
+        (
+            h_s, h_r, hz_s, hz_r, w_s, w_r, pn_s, pn_r, pf_s, pf_r, pc_s, pc_r, s_s, s_r,
+            v_s, v_r, vz_s, vz_r,
+        ) = refs[:18]
+        rest = refs[18:]
+        x_refs = (gbuf, part_l)
         z, e, c, k, sibling, same_core, column = places(n_dp, n_ex)
-        greet(same_core + [sibling] + column + [(d[0], sibling[1]) for d in column])
+        plane = [(z, lax.rem(e + i, n_ex)) for i in range(1, n_ex)]
+        part = lax.rem(e, parts)
+        members = [
+            (lax.rem(z + i, n_dp), e - part + lax.rem(part + j, parts))
+            for i in range(n_dp)
+            for j in range(parts)
+        ]
+        greet(plane + column + [(d[0], sibling[1]) for d in column] + members[1:])
         backs = [
             ExpertsBack(t_refs[m], back_refs[m], rest[7 * m : 7 * m + 7], n_dp, n_ex, inner)
             for m in range(extra)
         ]
-        gather, to_sib = [], []
+        gather, to_sib, others = [], [], []
         for i in range(1, chips):
             copy = remote(grad_ref, gbuf.at[e], t_s.at[i], t_r.at[i], same_core[i - 1])
             copy.start()
@@ -859,10 +964,21 @@
         copy = remote(grad_ref, gbuf.at[e], ts_s.at[0], ts_r.at[0], sibling)
         copy.start()
         to_sib.append(copy)
-        own = pltpu.make_async_copy(grad_ref, gbuf.at[e], local)
-        own.start()
+        keep = pltpu.make_async_copy(grad_ref, gbuf.at[e], local.at[0])
+        keep.start()
         for back in backs:
             back.begin()
+        for m in range(3):
+            for i in range(1, n_dp):
+                copy = remote(
+                    sh_in[m].at[lax.rem(z + i, n_dp)], sh_out[m].at[z],
+                    s_s.at[m, i], s_r.at[m, i], column[i - 1],
+                )
+                copy.start()
+                others.append(copy)
+            copy = pltpu.make_async_copy(sh_in[m].at[z], sh_out[m].at[z], local.at[1 + m])
+            copy.start()
+            others.append(copy)
         for i in range(1, chips):
             gather[i - 1].wait_recv()
             block = gbuf.at[lax.rem(c + chips - i, chips) * 2 + k]
@@ -871,7 +987,7 @@
             to_sib.append(copy)
         for back in backs:
             back.pass_on()
-        own.wait()
+        keep.wait()
         for copy in to_sib:
             copy.wait_recv()
         for copy in gather + to_sib:
@@ -879,14 +995,42 @@
         gat, grad_wout, dk, dv, grad_query, grad_expanded, grad_rope = att_tmp
         attend_backward(gbuf, *att_in, *att_tmp)
 
+        wsrc[...] = grad_wout[...].astype(BF).reshape(hp, parts, r, width)
+
+        def wout_sends(start):
+            for h in range(hp):
+                for p in range(parts):
+                    target = (part * hp + h, e - part + p)
+                    here = jnp.logical_and(part * hp + h == z, p == part)
+
+                    def far(h=h, p=p, target=target):
+                        copy = remote(
+                            wsrc.at[h, p], wout_out.at[z], w_s.at[h, p], w_r.at[z], target
+                        )
+                        if start:
+                            copy.start()
+                        else:
+                            copy.wait_send()
+
+                    pl.when(jnp.logical_not(here))(far)
+                    if start:
+
+                        @pl.when(here)
+                        def _(h=h, p=p):
+                            pltpu.make_async_copy(
+                                wsrc.at[h, p], wout_out.at[z], w_r.at[z]
+                            ).start()
+
+        wout_sends(True)
+
         def spread(i, carry):
             at = pl.ds(pl.multiple_of(i * 2 * rows, 2 * rows), 2 * rows)
             block = mm_cols(grad_query[at, :], att_in[1][...]).astype(BF)
-            x_refs[0][pl.ds(2 * i, 2)] = block.reshape(2, rows, width)
+            gbuf[pl.ds(2 * i, 2)] = block.reshape(2, rows, width)
             block = mm_cols(grad_expanded[at, :], att_in[2][...]).astype(BF)
-            x_refs[1][pl.ds(2 * i, 2), :, :KVR] = block.reshape(2, rows, KVR)
+            part_l[pl.ds(2 * i, 2), :, :KVR] = block.reshape(2, rows, KVR)
             block = grad_rope[at, :].astype(BF)
-            x_refs[1][pl.ds(2 * i, 2), :, KVR:] = block.reshape(2, rows, 2 * DR)
+            part_l[pl.ds(2 * i, 2), :, KVR:] = block.reshape(2, rows, 2 * DR)
             return carry
 
         lax.fori_loop(0, chips, spread, 0)
@@ -918,15 +1062,37 @@
                     same_core[i - 1],
                 )
                 far[i, j].start()
-        wout_ref[...] = grad_wout[...].astype(BF)
-        we_ref[...] = mm_rows(low_ref[...], grad_expanded[...]).astype(BF)
+
+        per_tile = 256 // r
 
         def wq_rows(i, carry):
             at = pl.ds(pl.multiple_of(i * 256, 256), 256)
-            wq_ref[at, :] = mm_rows(hidden_ref[:, at], grad_query[...]).astype(BF)
+            block = mm_rows(hidden_ref[:, at], grad_query[...]).astype(BF)
+            hsrc[pl.ds(i * per_tile, per_tile), :, :wq_cols] = block.reshape(
+                per_tile, r, wq_cols
+            )
             return carry
 
         lax.fori_loop(0, width // 256, wq_rows, 0)
+        grad_we = mm_rows(low_ref[...], grad_expanded[...]).astype(BF)
+        for j in range(r // rl):
+            block = grad_we[:, j * we_cols : (j + 1) * we_cols]
+            hsrc[:, j * rl : (j + 1) * rl, wq_cols:] = block.reshape(n_dev, rl, we_cols)
+        heads_far = []
+        for i in range(1, n_ex):
+            for d in range(n_dp):
+                copy = remote(
+                    hsrc.at[d * n_ex + lax.rem(e + i, n_ex)], heads_mid.at[d, e],
+                    h_s.at[i, d], h_r.at[i, d], plane[i - 1],
+                )
+                copy.start()
+                heads_far.append(copy)
+        for d in range(n_dp):
+            copy = pltpu.make_async_copy(
+                hsrc.at[d * n_ex + e], heads_mid.at[d, e], h_r.at[0, d]
+            )
+            copy.start()
+            copy.wait()
         for j in range(2):
             near[0, j].wait_recv()
             sums[j][...] = x_refs[j][e].astype(F32) + bufs[3 * j][c].astype(F32)
@@ -934,8 +1100,112 @@
             for j in range(2):
                 far[i, j].wait_recv()
                 sums[j][...] += bufs[3 * j + 2][i].astype(F32)
-        for copy in list(near.values()) + list(far.values()):
+
+        at = pl.ds(pl.multiple_of(e * rows, rows), rows)
+        cos, sin = att_in[3][at, :], att_in[4][at, :]
+        lat_grad, lat_gain = rms_back(lat_ref[:, :KVR], glat_ref[...], sums[1][:, :KVR])
+        rope = turn(sums[1][:, KVR:], cos, sin, -1.0)
+        lane = lax.broadcasted_iota(jnp.int32, rope.shape, 1)
+        rope = jnp.where(lane < DR, rope, 0.0)
+        low = jnp.concatenate([lat_grad, rope], axis=1).astype(BF)
+        total = sums[0][...] + mm_cols(low, wl_ref[:, :lat_cols])
+        tok_grad, tok_gain = rms_back(tok_ref[...].astype(F32), gain_ref[...], total)
+        tok_out[...] = gnat_ref[...] + tok_grad
+        vec[...] = jnp.zeros_like(vec)
+        vec[0:1, :] = jnp.sum(tok_gain, axis=0, keepdims=True)
+        vec[1:2, :] = gtwo_ref[...]
+        vec[2:3, :KVR] = jnp.sum(lat_gain, axis=0, keepdims=True)
+        vec_far = []
+        for i in range(1, n_ex):
+            copy = remote(vec, vbuf.at[i], v_s.at[i], v_r.at[i], plane[i - 1])
+            copy.start()
+            vec_far.append(copy)
+        for d in range(n_dp):
+            block = hidden_ref[at, d * n_ex * r : (d + 1) * n_ex * r]
+            block = mm_rows(block, low).reshape(n_ex, r, lat_cols)
+            pack[:, d * r : (d + 1) * r, :KVR] = block[:, :, :KVR].astype(BF)
+            block = block[:, :, KVR:] + router_ref[:, d * r : (d + 1) * r].astype(F32)
+            pack[:, d * r : (d + 1) * r, KVR:] = block.astype(BF)
+        pack_near, pack_far = [], []
+        for i in list(range(1, chips)) + [0]:
+            chip = lax.rem(c + i, chips)
+            copy = remote(pack.at[chip * 2 + 1 - k], psib.at[chip], pn_s.at[i], pn_r.at[i], sibling)
+            copy.start()
+            pack_near.append(copy)
+        for copy in heads_far:
+            copy.wait_recv()
+        heads_col = []
+        for i in range(1, n_dp):
+            d = lax.rem(z + i, n_dp)
+            copy = remote(
+                heads_mid.at[d], heads_out.at[z], hz_s.at[i], hz_r.at[i], column[i - 1]
+            )
+            copy.start()
+            heads_col.append(copy)
+        copy = pltpu.make_async_copy(heads_mid.at[z], heads_out.at[z], local.at[4])
+        copy.start()
+        heads_col.append(copy)
+        for i in range(1, chips):
+            chip = lax.rem(c + i, chips)
+            pack_near[i - 1].wait_recv()
+            pout[i] = (pack[chip * 2 + k].astype(F32) + psib[chip].astype(F32)).astype(BF)
+            copy = remote(pout.at[i], pfar.at[i], pf_s.at[i], pf_r.at[i], same_core[i - 1])
+            copy.start()
+            pack_far.append(copy)
+        for copy in vec_far:
+            copy.wait_recv()
             copy.wait_send()
+        for i in range(1, n_ex):
+            vec[...] += vbuf[i]
+        vec_col = []
+        for i in range(1, n_dp):
+            copy = remote(vec, vzbuf.at[i], vz_s.at[i], vz_r.at[i], column[i - 1])
+            copy.start()
+            vec_col.append(copy)
+        pack_near[chips - 1].wait_recv()
+        total = pack[e].astype(F32) + psib[c].astype(F32)
+        for i in range(1, chips):
+            pack_far[i - 1].wait_recv()
+            total = total + pfar[i].astype(F32)
+        psum[...] = total.astype(BF).reshape(n_dp, r, lat_cols)
+        pack_col = []
+        for i in range(1, n_dp):
+            copy = remote(
+                psum.at[lax.rem(z + i, n_dp)], pbuf.at[i], pc_s.at[i], pc_r.at[i], column[i - 1]
+            )
+            copy.start()
+            pack_col.append(copy)
+        result = vec[...]
+        for i in range(1, n_dp):
+            vec_col[i - 1].wait_recv()
+            result = result + vzbuf[i]
+        vec_out[...] = result
+        result = psum[z].astype(F32)
+        for i in range(1, n_dp):
+            pack_col[i - 1].wait_recv()
+            result = result + pbuf[i].astype(F32)
+        pack_out[...] = result
+
+        for i in range(n_dp):
+            here = jnp.logical_and(z // hp == part, z == i)
+
+            @pl.when(here)
+            def _(i=i):
+                pltpu.make_async_copy(
+                    wsrc.at[lax.rem(z, hp), part], wout_out.at[i], w_r.at[i]
+                ).wait()
+
+            @pl.when(jnp.logical_not(here))
+            def _(i=i):
+                wait_recv(wout_out.at[i], w_r.at[i], sibling)
+
+        wout_sends(False)
+        for copy in list(near.values()) + list(far.values()) + heads_far:
+            copy.wait_send()
+        for copy in pack_near + pack_far + vec_col + pack_col:
+            copy.wait_send()
+        for copy in heads_col + others:
+            copy.wait()
         for back in backs:
             back.end()
 
@@ -951,172 +1221,48 @@
         vmem((seq, wq.shape[1]), BF),
         vmem((seq, we.shape[1]), BF),
         vmem((seq, 2 * DR), F32),
-        vmem((n_ex, rows, width), BF),
         vmem((n_ex, rows, lat_cols), BF),
     ]
     scratch += [vmem((chips, rows, width), BF)] * 3 + [vmem((chips, rows, lat_cols), BF)] * 3
-    scratch += [dma((chips,))] * 4 + [dma] + [dma((chips,))] * 8
+    scratch += [
+        vmem((rows, width), F32),
+        vmem((rows, lat_cols), F32),
+        vmem((n_dev, r, head_cols), BF),
+        vmem((hp, parts, r, width), BF),
+        vmem((n_ex, n_dp * r, lat_cols), BF),
+        vmem((chips, n_dp * r, lat_cols), BF),
+        vmem((chips, n_dp * r, lat_cols), BF),
+        vmem((chips, n_dp * r, lat_cols), BF),
+        vmem((n_dp, r, lat_cols), BF),
+        vmem((n_dp, r, lat_cols), BF),
+        vmem((8, width), F32),
+        vmem((n_ex, 8, width), F32),
+        vmem((n_dp, 8, width), F32),
+    ]
+    scratch += [dma((chips,))] * 4 + [dma((5,))] + [dma((chips,))] * 8
+    scratch += [dma((n_ex, n_dp))] * 2 + [dma((n_dp,))] * 2 + [dma((hp, parts)), dma((n_dp,))]
+    scratch += [dma((chips,))] * 4 + [dma((n_dp,))] * 2 + [dma((3, n_dp))] * 2
+    scratch += [dma((n_ex,))] * 2 + [dma((n_dp,))] * 2
     for total in totals:
         scratch += ExpertsBack.scratch(total, n_dp, inner)
     outs = pl.pallas_call(
         kernel,
         out_shape=[
             sds((rows, width), F32),
-            sds((rows, lat_cols), F32),
-            sds((2 * DV, width), BF),
-            sds(wq.shape, BF),
-            sds(we.shape, BF),
+            sds((8, width), F32),
+            sds((r, lat_cols), F32),
+            sds((n_dp, n_ex, r, head_cols), BF),
+            sds((n_dp, n_ex, r, head_cols), BF),
+            sds((n_dp, r, width), BF),
         ]
+        + [sds(array.shape, BF) for array in shared]
         + [ExpertsBack.out(total, n_dp, inner) for total in totals],
-        in_specs=[ANY] + [VMEM] * 13 + [ANY] * extra,
-        out_specs=[VMEM] * 5 + [ANY] * extra,
+        in_specs=[ANY] + [VMEM] * 21 + [ANY] * (3 + extra),
+        out_specs=[VMEM] * 3 + [ANY] * (6 + extra),
         scratch_shapes=scratch,
         compiler_params=params(collective_id),
-    )(grad, *attend, hidden, latent_low, *totals)
-    return outs[:5], outs[5:]
-
-
-def last_exchange(heads, wout, pack, shared, totals, n_dp, n_ex, inner, collective_id):
-    chips = n_ex // 2
-    extra = len(totals)
-    rows, cols = pack.shape[1:]
-    r = rows // n_dp
-
-    def kernel(heads_ref, wout_ref, pack_ref, *refs):
-        sh_in, t_refs = refs[:3], refs[3 : 3 + extra]
-        refs = refs[3 + extra :]
-        heads_out, wout_out, pack_out = refs[:3]
-        sh_out, back_refs = refs[3:6], refs[6 : 6 + extra]
-        refs = refs[6 + extra :]
-        hbuf, hsum, wbuf, psib, pout, pfar, psum, pbuf = refs[:8]
-        (
-            h_s, h_r, hp_s, hp_r, w_s, w_r, pn_s, pn_r, pf_s, pf_r, pc_s, pc_r, s_s, s_r, local,
-        ) = refs[8:23]
-        rest = refs[23:]
-        z, e, c, k, sibling, same_core, column = places(n_dp, n_ex)
-        plane = [(z, lax.rem(e + i, n_ex)) for i in range(1, n_ex)]
-        greet(plane + column + [(d[0], sibling[1]) for d in column])
-        backs = [
-            ExpertsBack(t_refs[m], back_refs[m], rest[7 * m : 7 * m + 7], n_dp, n_ex, inner)
-            for m in range(extra)
-        ]
-        near, far = [], []
-        for i in list(range(1, chips)) + [0]:
-            chip = lax.rem(c + i, chips)
-            copy = remote(
-                pack_ref.at[chip * 2 + 1 - k], psib.at[chip], pn_s.at[i], pn_r.at[i], sibling
-            )
-            copy.start()
-            near.append(copy)
-        heads_col, others = [], []
-        for i in range(1, n_dp):
-            to = lax.rem(z + i, n_dp)
-            copy = remote(heads_ref.at[to], hbuf.at[i], h_s.at[i], h_r.at[i], column[i - 1])
-            copy.start()
-            heads_col.append(copy)
-        for back in backs:
-            back.begin()
-        for i in range(1, chips):
-            chip = lax.rem(c + i, chips)
-            near[i - 1].wait_recv()
-            pout[i] = (
-                pack_ref[chip * 2 + k].astype(F32) + psib[chip].astype(F32)
-            ).astype(BF)
-            copy = remote(pout.at[i], pfar.at[i], pf_s.at[i], pf_r.at[i], same_core[i - 1])
-            copy.start()
-            far.append(copy)
-        near[chips - 1].wait_recv()
-        total = pack_ref[e].astype(F32) + psib[c].astype(F32)
-        for i in range(1, chips):
-            far[i - 1].wait_recv()
-            total = total + pfar[i].astype(F32)
-        psum[...] = total.astype(BF).reshape(n_dp, r, cols)
-        pack_col, wout_col = [], []
-        for i in range(1, n_dp):
-            to = lax.rem(z + i, n_dp)
-            copy = remote(psum.at[to], pbuf.at[i], pc_s.at[i], pc_r.at[i], column[i - 1])
-            copy.start()
-            pack_col.append(copy)
-            copy = remote(wout_ref.at[to], wbuf.at[i], w_s.at[i], w_r.at[i], column[i - 1])
-            copy.start()
-            wout_col.append(copy)
-            for m in range(3):
-                copy = remote(
-                    sh_in[m].at[to], sh_out[m].at[z], s_s.at[m, i], s_r.at[m, i], column[i - 1]
-                )
-                copy.start()
-                others.append(copy)
-        for m in range(3):
-            copy = pltpu.make_async_copy(sh_in[m].at[z], sh_out[m].at[z], local.at[m])
-            copy.start()
-            others.append(copy)
-        for copy in heads_col:
-            copy.wait_recv()
-        for j in range(n_ex):
-            block = heads_ref[z, j].astype(F32)
-            for i in range(1, n_dp):
-                block = block + hbuf[i, j].astype(F32)
-            hsum[j] = block.astype(BF)
-        heads_plane = []
-        for i in range(1, n_ex):
-            copy = remote(
-                hsum.at[lax.rem(e + i, n_ex)], heads_out.at[e], hp_s.at[i], hp_r.at[i],
-                plane[i - 1],
-            )
-            copy.start()
-            heads_plane.append(copy)
-        keep = pltpu.make_async_copy(hsum.at[e], heads_out.at[e], local.at[3])
-        keep.start()
-        for back in backs:
-            back.pass_on()
-        for copy in wout_col + pack_col:
-            copy.wait_recv()
-        wout_sum = wout_ref[z].astype(F32)
-        pack_sum = psum[z].astype(F32)
-        for i in range(1, n_dp):
-            wout_sum = wout_sum + wbuf[i].astype(F32)
-            pack_sum = pack_sum + pbuf[i].astype(F32)
-        wout_out[...] = wout_sum
-        pack_out[...] = pack_sum
-        for copy in near + far + heads_col + wout_col + pack_col:
-            copy.wait_send()
-        keep.wait()
-        for copy in heads_plane + others:
-            copy.wait()
-        for back in backs:
-            back.end()
-
-    dma = pltpu.SemaphoreType.DMA
-    scratch = [
-        pltpu.VMEM(heads.shape, BF),
-        pltpu.VMEM(heads.shape[1:], BF),
-        pltpu.VMEM(wout.shape, BF),
-        pltpu.VMEM((chips, rows, cols), BF),
-        pltpu.VMEM((chips, rows, cols), BF),
-        pltpu.VMEM((chips, rows, cols), BF),
-        pltpu.VMEM((n_dp, r, cols), BF),
-        pltpu.VMEM((n_dp, r, cols), BF),
-        dma((n_dp,)), dma((n_dp,)), dma((n_ex,)), dma((n_ex,)), dma((n_dp,)), dma((n_dp,)),
-        dma((chips,)), dma((chips,)), dma((chips,)), dma((chips,)), dma((n_dp,)), dma((n_dp,)),
-        dma((3, n_dp)), dma((3, n_dp)), dma((4,)),
-    ]
-    for total in totals:
-        scratch += ExpertsBack.scratch(total, n_dp, inner)
-    outs = pl.pallas_call(
-        kernel,
-        out_shape=[
-            jax.ShapeDtypeStruct(heads.shape[1:], BF),
-            jax.ShapeDtypeStruct(wout.shape[1:], F32),
-            jax.ShapeDtypeStruct((r, cols), F32),
-        ]
-        + [jax.ShapeDtypeStruct(array.shape, BF) for array in shared]
-        + [ExpertsBack.out(total, n_dp, inner) for total in totals],
-        in_specs=[VMEM] * 3 + [ANY] * (3 + extra),
-        out_specs=[ANY, VMEM, VMEM] + [ANY] * (3 + extra),
-        scratch_shapes=scratch,
-        compiler_params=params(collective_id),
-    )(heads, wout, pack, *shared, *totals)
-    return outs[0], outs[1], outs[2], outs[3:6], outs[6:]
+    )(grad, *attend, hidden, latent_low, *own, *shared, *totals)
+    return outs[:3], outs[4], outs[5], outs[6:9], outs[9:]
 
 
 def shards(
@@ -1164,7 +1310,6 @@
     heads_back = [heads.index(h) for h in range(H)]
     inner = n_experts // chips
     my_local = lax.rem(z, inner)
-    part_groups = [[i * parts + m for m in range(parts)] for i in range(n_ex // parts)]
     ff_e = expert_gate.shape[2]
     ff_s = shared_gate.shape[1] // inner
     lat = KVR + DR
@@ -1192,8 +1337,9 @@
         axis=-1,
     ).transpose(1, 0, 2)
     we_send = jnp.take(w_expand.reshape(rl, H, DH + DV), jnp.array(heads), axis=1)
-    we_send = we_send.reshape(rl, n_ex, kv_cols).transpose(1, 0, 2)
-    we_send = we_send.reshape(n_ex, r, rl * kv_cols // r)
+    we_cols = rl * kv_cols // r
+    we_send = we_send.reshape(rl, n_ex, r // rl, we_cols).transpose(1, 2, 0, 3)
+    we_send = we_send.reshape(n_ex, r, we_cols)
     wa_send = jnp.concatenate([wq_send, we_send], axis=-1)
     slot_own = slot_places(routes, place_order[0], capacity)
     slot_place = jnp.where(slot_own >= 0, slot_own - routes * capacity, -1)
@@ -1217,7 +1363,8 @@
     cot_owner = to_owner_order(cotangent)
     tok_all, wa_all, pk_all = first_exchange(tokens, wa_send, pack, n_dp, n_ex, 1)
     wq = wa_all[..., :head_cols].reshape(width, head_cols)
-    wexp = wa_all[..., head_cols:].reshape(KVR, kv_cols)
+    wexp = wa_all[..., head_cols:].reshape(n_dp * n_ex, r // rl, rl, we_cols)
+    wexp = wexp.transpose(0, 2, 1, 3).reshape(KVR, kv_cols)
     pk_flat = pk_all.reshape(width, pack_cols)
     w_lat = pk_flat[:, :lat]
     gain_one = pk_flat[:, lat + n_experts].astype(F32)
@@ -1363,7 +1510,15 @@
     dx_send = jnp.concatenate(
         [dx_col, grad_probs_col, jnp.zeros((inner * rows, 128 - n_experts), F32)], axis=1
     ).astype(BF)
-    dx_sum = column_sum(dx_send.reshape(inner, rows, width + 128), n_dp, n_ex, inner, 3)
+    dx_sum, shared_sums, (gate_back,) = column_sum(
+        dx_send.reshape(inner, rows, width + 128),
+        [grad.reshape(n_ex, n_dp, r, ff_s) for grad in shared_grads],
+        expert_totals[:1],
+        n_dp,
+        n_ex,
+        inner,
+        3,
+    )
     router_probs = lax.dynamic_slice_in_dim(col_probs, my_local * rows, rows, 0)
     grad_probs = dx_sum[:, width : width + n_experts]
     grad_logits = (
@@ -1375,86 +1530,45 @@
     grad_resid_norm, grad_gain_two = norm_two_back(grad_hidden_two)
     grad_residual = cot_owner.astype(F32) + grad_resid_norm
 
-    out_col, shared_grads, _ = lax.optimization_barrier((out_col, shared_grads, dx_sum))
+    out_col, _ = lax.optimization_barrier((out_col, dx_sum))
     out_sum = lax.psum_scatter(
         out_col, "dp", scatter_dimension=0, tiled=True, axis_index_groups=col_groups
     )
     out_tokens = from_owner_order((residual + out_sum.astype(F32)).astype(BF))
-    shared_sums = [
-        lax.psum_scatter(
-            grad.reshape(n_ex, n_dp, r, ff_s), "expert", scatter_dimension=0, tiled=True
-        ).reshape(n_dp, r, ff_s)
-        for grad in shared_grads
-    ]
-    attend_grads, (gate_back,) = backward_exchange(
-        grad_residual.astype(BF),
-        [wo_rows, wq, wexp, cos_wide, sine_wide, keep, qcat, kcat, value, lse, attended],
-        hidden_one,
-        latent_low,
-        expert_totals[:1],
-        n_dp,
-        n_ex,
-        inner,
-        5,
-    )
-    grad_query_sum, grad_latent_sum, grad_wout, grad_wq, grad_we = attend_grads
-    own_start = e * rows
-    latent_own = lax.dynamic_slice_in_dim(latent_raw, own_start, rows, 0)[:, :lat]
-    cos_own = lax.dynamic_slice_in_dim(cos_table, own_start, rows, 0)
-    sine_own = lax.dynamic_slice_in_dim(sine_table, own_start, rows, 0)
-
-    def make_latent(latent_in, gain_in):
-        return (
-            rms_norm(latent_in[:, :KVR], gain_in),
-            rotate(latent_in[:, KVR:], cos_own, sine_own),
+    latent_own = lax.dynamic_slice_in_dim(latent_raw, e * rows, rows, 0)
+    router_back = jnp.pad(
+        grad_router.reshape(n_ex, n_dp * r, n_experts),
+        ((0, 0), (0, 0), (DR, DR - n_experts)),
+    ).astype(BF)
+    (grad_tokens, vec_sum, pack_sum), heads_got, wout_got, shared_got, (up_back,) = (
+        backward_exchange(
+            grad_residual.astype(BF),
+            [wo_rows, wq, wexp, cos_wide, sine_wide, keep, qcat, kcat, value, lse, attended],
+            hidden_one,
+            latent_low,
+            [
+                pk_flat,
+                latent_own,
+                tokens,
+                gain_one[None],
+                gain_lat[None],
+                from_owner_order(grad_residual),
+                router_back,
+                grad_gain_two[None],
+            ],
+            shared_sums,
+            expert_totals[1:2],
+            n_dp,
+            n_ex,
+            inner,
+            5,
         )
-
-    _, latent_back = jax.vjp(make_latent, latent_own, gain_lat)
-    grad_latent_raw, grad_gain_lat = latent_back(
-        (grad_latent_sum[:, :KVR], grad_latent_sum[:, KVR:lat])
-    )
-    grad_latent_low = grad_latent_raw.astype(BF)
-    _, norm_one_back = jax.vjp(rms_norm, tokens.astype(F32), gain_one)
-    grad_hidden_one = grad_query_sum + mm_cols(grad_latent_low, w_lat)
-    grad_tokens_norm, grad_gain_one = norm_one_back(grad_hidden_one)
-    grad_tokens = from_owner_order(grad_residual) + grad_tokens_norm
-
-    wout_back = lax.all_to_all(
-        grad_wout.reshape(hp, parts, r, width).transpose(1, 0, 2, 3),
-        "expert",
-        0,
-        0,
-        axis_index_groups=part_groups,
-        tiled=True,
-    ).reshape(n_dp, r, width)
-    grad_wq = grad_wq.reshape(n_dp, n_ex, r, head_cols)
-    grad_we = grad_we.reshape(n_dp, n_ex, r, rl * kv_cols // r)
-    heads_grad = jnp.concatenate([grad_wq, grad_we], axis=-1)
-    hidden_own = lax.dynamic_slice_in_dim(hidden_one, own_start, rows, 0)
-
-    def by_owner(values):
-        return values.reshape(n_ex, n_dp, r, -1).transpose(1, 0, 2, 3)
-
-    pack_grad = jnp.concatenate(
-        [
-            mm_rows(hidden_own, grad_latent_low).reshape(n_dp, n_ex, r, lat),
-            by_owner(grad_router),
-            grad_gain_one.reshape(n_dp, n_ex, r, 1),
-            by_owner(grad_gain_two),
-            jnp.pad(grad_gain_lat.reshape(n_dp, n_ex, rl, 1), ((0, 0),) * 2 + ((0, r - rl), (0, 0))),
-            jnp.zeros((n_dp, n_ex, r, -small_cols % 128), F32),
-        ],
-        axis=-1,
-    ).astype(BF)
-    pack_grad = pack_grad.transpose(1, 0, 2, 3).reshape(n_ex, n_dp * r, -1)
-    heads_all, sum_wout, pack_sum, shared_got, (up_back,) = last_exchange(
-        heads_grad, wout_back, pack_grad, shared_sums, expert_totals[1:2], n_dp, n_ex, inner, 7
     )
 
     def added(values):
         return jnp.sum(values.astype(F32), axis=0)
 
-    heads_all = heads_all.astype(F32)
+    heads_all = added(heads_got)
     sum_wq = heads_all[..., :head_cols].transpose(1, 0, 2)
     sum_wq = jnp.concatenate(
         [
@@ -1464,10 +1578,14 @@
         axis=-1,
     ).reshape(r, H, DH + DR)
     sum_wq = jnp.take(sum_wq, jnp.array(heads_back), axis=1).reshape(r, H * (DH + DR))
-    sum_we = heads_all[..., head_cols:].reshape(n_ex, rl, kv_cols).transpose(1, 0, 2)
+    sum_we = heads_all[..., head_cols:].reshape(n_ex, r // rl, rl, we_cols).transpose(2, 0, 1, 3)
     sum_we = jnp.take(sum_we.reshape(rl, H, DH + DV), jnp.array(heads_back), axis=1)
     sum_we = sum_we.reshape(rl, H * (DH + DV))
-    sum_wout = from_owner_order(sum_wout)
+    sum_wout = from_owner_order(added(wout_got))
+    device = z * n_ex + e
+    sum_gain_one = lax.dynamic_slice_in_dim(vec_sum[0], device * r, r, 0)
+    sum_gain_two = lax.dynamic_slice_in_dim(vec_sum[1], (e * n_dp + z) * r, r, 0)
+    sum_gain_lat = lax.dynamic_slice_in_dim(vec_sum[2], device * rl, rl, 0)
     sum_sgate, sum_sup, sum_sdown = (
         added(got.reshape(n_dp // inner, inner, r, ff_s)).transpose(1, 0, 2).reshape(r, -1)
         for got in shared_got
@@ -1478,13 +1596,13 @@
     return (
         out_tokens,
         grad_tokens,
-        pack_sum[:, lat + n_experts],
+        sum_gain_one,
         sum_wq,
         pack_sum[:, :lat],
-        pack_sum[:rl, lat + n_experts + 2],
+        sum_gain_lat,
         sum_we,
         sum_wout,
-        pack_sum[:, lat + n_experts + 1],
+        sum_gain_two,
         pack_sum[:, lat : lat + n_experts],
         sum_sgate,
         sum_sup,

time: 1160 us -> 1080 us (0.931)
  Pallas kernels: 776 us -> 754 us
  local copies, waits for them, and re-layouts: 102 us -> 80.8 us
  waiting for transfers between devices: 37.2 us -> 22.2 us
  matrix products: 171 us -> 158 us
    pallas_call x3 -> x2, Pallas kernels: 329 us -> 302 us  [the longest x1 181 us: backward_exchange(): pl.pallas_call(kernel, out_shape=[sds((rows, width), F32), sds((8, width)...]
    ppermute x6, waiting for transfers between devices: 23.9 us -> 9.89 us  [through(): got.append(lax.ppermute(cut[m], 'expert', perm))]
    reduce_scatter x3 -> x0, waiting for transfers between devices: 13.2 us -> none  [shards(): lax.psum_scatter(grad.reshape(n_ex, n_dp, r, ff_s), 'expert', scatter_dim...]
    convert_element_type x0 -> x3, local copies, waits for them, and re-layouts: none -> 12.3 us  [the longest x1 4.81 us: shards(): mm_rows(x_col, grad_sa).astype(BF)]
    reduce_scatter x1, waiting for transfers between devices: 0.01 us -> 12.3 us  [shards(): lax.psum_scatter(out_col, 'dp', scatter_dimension=0, tiled=True, axis_ind...]
    optimization_barrier x3 -> x0, local copies, waits for them, and re-layouts: 12.2 us -> none  [shards(): lax.optimization_barrier((out_col, shared_grads, dx_sum))]
    dot_general x8 -> x7, matrix products: 47.9 us -> 38.9 us  [mm_rows(): lax.dot_general(left, right, (((0,), (0,)), ((), ())), preferred_element_...]
    dot_general x9 -> x8, matrix products: 48.1 us -> 44.5 us  [mm_cols(): lax.dot_general(left, right, (((1,), (1,)), ((), ())), preferred_element_...]
  transfers between devices with their start and end apart: 12 -> 8, of which waited for: 4 -> 3; matrix products, arithmetic and copies ran while one was open for 18% -> 15% of each run, Pallas kernels for 42% -> 36%
where the time goes in v7:
time: 1080 us; the launch traced here: 1070 us
  Pallas kernels  754 us (70%)
  matrix products  158 us (15%)
  local copies, waits for them, and re-layouts  80.8 us (7%)
  other arithmetic  35.4 us (3%)
  waiting for transfers between devices  22.2 us (2%)
  between operations  16.6 us (2%)
    pallas_call x1, Pallas kernels, forward_exchange(): pl.pallas_call(kernel, out_shape=[sds((seq, width), BF), sds((seq, attend...  241 us
    pallas_call x1, Pallas kernels, backward_exchange(): pl.pallas_call(kernel, out_shape=[sds((rows, width), F32), sds((8, width)...  181 us
    pallas_call x2, Pallas kernels, between(): pl.pallas_call(kernel, out_shape=[jax.ShapeDtypeStruct(blocks.shape, BF)]...  141 us
    pallas_call x1, Pallas kernels, column_sum(): pl.pallas_call(kernel, out_shape=[jax.ShapeDtypeStruct(shape, F32)] + [ja...  121 us
    dot_general x12, matrix products, mm(): return jnp.dot(left, right, preferred_element_type=F32)  74.1 us
    pallas_call x1, Pallas kernels, first_exchange(): pl.pallas_call(kernel, out_shape=[jax.ShapeDtypeStruct((n_ex,) + tok.shap...  71.3 us
    dot_general x8, matrix products, mm_cols(): lax.dot_general(left, right, (((1,), (1,)), ((), ())), preferred_element_...  44.5 us
    dot_general x7, matrix products, mm_rows(): lax.dot_general(left, right, (((0,), (0,)), ((), ())), preferred_element_...  38.9 us
  transfers between devices with their start and end apart: 8, of which 3 were waited for; matrix products, arithmetic and copies ran while one was open for 15% of the time, Pallas kernels for 36%

profile of v7, /device:TPU:11, one launch (start us, length us, event | category | flops | bytes accessed | tf_op | source)
XLA Modules:
  0.0 1073.3 jit_solution(17674706899245542876)
XLA Ops:
  16.4 71.3 %shard_map.342 = (bf16[8,128,2048]{2,1,0:T(8,128)(2,1)}, bf16[4,8,64,512]{3,2,1,0:T(8,128)(2,1)}, bf16[4,8,64,640]{3,2,1,0:T(8,128)(2,1)}) custom-call(bf16[128,2048]{1,0:T(8,128)(2,1)} %refs_16_.1, bf16[8,64,512]{2,1,0:T(8,128)(2,1)} %pad_maximum_fusion.4.wa_ref, bf16[64,640]{1,0:T(8,128)(2,1)} %concatenate.39.pk_ref), custom_call_target="tpu_custom_call" | custom-call | tf_op jit(solution)/shard_map/pallas_call | solution.py:422
  89.7 2.8 slice.159
  92.5 1.9 slice.162
  117.6 241.0 %shard_map.343 = (bf16[1024,2048]{1,0:T(8,128)(2,1)}, f32[1024,640]{1,0:T(8,128)}, bf16[1024,512]{1,0:T(8,128)(2,1)}, bf16[2,1024,256]{2,1,0:T(8,128)(2,1)}, bf1...) custom-call(bf16[8,128,2048]{2,1,0:T(8,128)(2,1)} %get-tuple-element, ...), custom_call_target="tpu_custom_call" | custom-call | tf_op jit(solution)/shard_map/pallas_call | solution.py:702
  358.6 6.8 convolution_convert_fusion.5
  366.1 67.9 %shard_map.344 = (bf16[4,256,2048]{2,1,0:T(8,128)(2,1)}, bf16[8,4,64,1408]{3,2,1,0:T(8,128)(2,1)}) custom-call(bf16[4,256,2048]{2,1,0:T(8,128)(2,1)} %bitcast.213, bf16[2,8,64,1408]{3,2,1,0:T(8,128)(2,1)} %bitcast.230), custom_call_target="tpu_custom_call" | custom-call | tf_op jit(solution)/shard_map/pallas_call | solution.py:781
  434.0 3.5 fusion.48
  437.6 10.4 fusion.50
  451.5 5.1 fusion.52
  456.6 2.9 fusion.53
  459.5 8.4 fusion.51
  467.9 4.7 convolution_convert_fusion.3
  472.6 2.2 fusion.45
  476.3 2.5 collective-permute-start.3
  478.7 2.3 multiply_convert_fusion.3
  481.1 3.2 convolution_convert_fusion.7
  484.3 3.2 convolution_convert_fusion.6
  487.5 3.3 convolution_convert_fusion.8
  490.9 4.8 copy.394
  495.7 2.9 copy.395
  498.5 4.7 copy.396
  503.2 5.9 fusion.56
  509.1 3.9 fusion.54
  513.0 9.7 collective-permute-done.4
  522.9 16.9 %multiply_convert_fusion.1 = (bf16[1024,1408]{1,0:T(8,128)(2,1)}, bf16[1024,1408]{1,0:T(8,128)(2,1)S(1)}, bf16[1024,1408]{1,0:T(8,128)(2,1)}) fusion(f32[1024,1408]{1,0:T(8,128)} %fusion.50, f32[1024,1408]{1,0:T(8,128)} %fusion.51, bf16[2048,1408]{1,0:T(8,128)(2,1)} %bitcast.280, bf16[256,2048]{1,0:T(8,128)(2,1)} %collective-permute-done.5, ...), kind=kOutput, calls=%fused_computation.13 | convolution fusion | flops 5949620224 | bytes 30150656 | tf_op jit(solution)/shard_map/dot_general | solution.py:56
  539.8 6.7 fusion.55
  546.6 8.7 convolution_convert_fusion.1
  555.3 8.9 convolution_convert_fusion.4
  568.1 8.2 add_convert_fusion
  576.3 10.6 convolution_convert_fusion.2
  586.9 72.7 %shard_map.345 = (bf16[4,256,2048]{2,1,0:T(8,128)(2,1)}, bf16[1,2,8,64,1408]{4,3,2,1,0:T(8,128)(2,1)}) custom-call(bf16[4,256,2048]{2,1,0:T(8,128)(2,1)} %bitcast.216, bf16[8,4,64,1408]{3,2,1,0:T(8,128)(2,1)} %bitcast.207), custom_call_target="tpu_custom_call" | custom-call | tf_op jit(solution)/shard_map/pallas_call | solution.py:781
  659.6 5.5 fusion.39
  665.2 1.9 add_convert_fusion.1
  667.1 6.7 convert_multiply_fusion
  673.8 3.2 reshape.722
  676.9 2.2 reduce_sum.149
  680.1 2.9 concatenate.44.x_ref
  683.0 120.7 %shard_map.346 = (f32[128,2176]{1,0:T(8,128)}, bf16[4,64,704]{2,1,0:T(8,128)(2,1)}, bf16[4,64,704]{2,1,0:T(8,128)(2,1)}, bf16[4,64,704]{2,1,0:T(8,128)(2,1)}, bf16[1,2,8,64,1408]{4,3,2,1,0:T(8,128)(2,1)}) custom-call(bf16[4,128,2176]{2,1,0:T(8,128)(2,1)} %concatenate.44.x_ref, bf16[8,4,64,704]{3,2,1,0:T(8,128)(2,1)} %bitcast.197, ...), custom_call_target="tpu_custom_call" | custom-call | tf_op jit(solution)/shard_map/pallas_call | solution.py:324
  803.7 6.9 add_convert_fusion.2
  815.0 5.2 convert.47
  821.1 8.7 convolution_convert_fusion
  833.2 4.8 convert.45
  838.0 2.4 multiply_reduce_fusion
  840.4 12.3 %reduce-scatter.2.cloned.1.call-done = bf16[128,2048]{1,0:T(8,128)(2,1)} async-done(((bf16[512,2048]{1,0:T(8,128)(2,1)}), bf16[128,2048]{1,0:T(8,128)(2,1)}) %reduce-scatter.2.cloned.1.call-update) | async-done | bytes 524304 | tf_op jit(solution)/shard_map/reduce_scatter | solution.py:1534
  852.7 2.6 fusion.42
  857.0 181.0 %shard_map.347 = (f32[128,2048]{1,0:T(8,128)}, f32[8,2048]{1,0:T(8,128)}, f32[64,640]{1,0:T(8,128)}, bf16[4,8,64,512]{3,2,1,0:T(8,128)(2,1)}, bf16[4,8,64,512]{3...) custom-call(bf16[128,2048]{1,0:T(8,128)(2,1)} %get-tuple-element.222, ...), custom_call_target="tpu_custom_call" | custom-call | tf_op jit(solution)/shard_map/pallas_call | solution.py:1248
  1038.0 2.1 convert_reduce_fusion
  1057.9 4.8 convert.46
  (325 shorter events, 75.3 us)
Async XLA Ops:
  7.2 460.7 %all-gather.2.cloned.1.call-start = ((), (), s32[]{:S(2)}) async-start(), calls=%async_computation.1 | async-start | bytes 2621440 | tf_op jit(solution)/shard_map/all_gather | solution.py:1378
  16.4 78.0 %copy-start.6 = (bf16[128,2048]{1,0:T(8,128)(2,1)S(1)}, bf16[128,2048]{1,0:T(8,128)(2,1)}, u32[]{:S(2)}) copy-start(bf16[128,2048]{1,0:T(8,128)(2,1)} %refs_16_.1) | copy-start | bytes 1572868
  87.7 7.7 copy-start
  87.7 765.0 %reduce-scatter.2.cloned.1.call-start = ((), (), s32[]{:S(2)}) async-start(), calls=%async_computation.2 | async-start | bytes 2621440 | tf_op jit(solution)/shard_map/reduce_scatter | solution.py:1534
  98.7 7.7 copy-start.31
  102.5 5.8 copy-start.15
  104.1 6.0 copy-start.28
  112.7 321.3 %copy-start.16 = (bf16[2048,16]{0,1:T(8,128)(2,1)}, bf16[2048,16]{0,1:T(8,128)(2,1)S(1)}, u32[]{:S(2)}) copy-start(bf16[2048,16]{0,1:T(8,128)(2,1)S(1)} %reshape.707) | copy-start | bytes 196612
  113.3 335.2 %copy-start.43 = (pred[16]{0:T(512)(128)(4,1)}, pred[16]{0:T(512)(128)(4,1)S(1)}, u32[]{:S(2)}) copy-start(pred[16]{0:T(512)(128)(4,1)S(1)} %iota_compare_fusion.3) | copy-start | bytes 52
  113.8 334.7 %copy-start.45 = (pred[16]{0:T(512)(128)(4,1)}, pred[16]{0:T(512)(128)(4,1)S(1)}, u32[]{:S(2)}) copy-start(pred[16]{0:T(512)(128)(4,1)S(1)} %get-tuple-element.260) | copy-start | bytes 52
  113.8 334.7 %copy-start.47 = (pred[16]{0:T(512)(128)(4,1)}, pred[16]{0:T(512)(128)(4,1)S(1)}, u32[]{:S(2)}) copy-start(pred[16]{0:T(512)(128)(4,1)S(1)} %get-tuple-element.261) | copy-start | bytes 52
  358.6 6.9 copy-start.10
  450.1 9.3 slice-start.1
  451.5 8.0 slice-start.2
  472.6 6.2 copy-start.55
  472.6 6.2 copy-start.57
  472.6 6.2 copy-start.64
  472.6 6.1 copy-start.65
  474.8 38.2 %collective-permute-start.5 = (bf16[256,2048]{1,0:T(8,128)(2,1)}, bf16[256,2048]{1,0:T(8,128)(2,1)}, u32[]{:S(2)}, u32[]{:S(2)}) collective-permute-start(bf16[256,2048]{1,0:T(8,128)(2,1)} %get-tuple-element.229), channel_id=1, source_target_pairs={{0,6},{1,7},{2,0},{3,1},{4,2},{5,3},{6,4},{7,5},{8,14},{9,15},{10,... | collective-permute-start | bytes 3145736 | tf_op jit(solution)/shard_map/ppermute | solution.py:1407
  475.3 47.4 %collective-permute-start.4 = (bf16[256,2048]{1,0:T(8,128)(2,1)}, bf16[256,2048]{1,0:T(8,128)(2,1)}, u32[]{:S(2)}, u32[]{:S(2)}) collective-permute-start(bf16[256,2048]{1,0:T(8,128)(2,1)} %get-tuple-element.230), channel_id=1, source_target_pairs={{0,4},{1,5},{2,6},{3,7},{4,0},{5,1},{6,2},{7,3},{8,12},{9,13},{10,... | collective-permute-start | bytes 3145736 | tf_op jit(solution)/shard_map/ppermute | solution.py:1407
  476.3 46.6 %collective-permute-start.3 = (bf16[256,2048]{1,0:T(8,128)(2,1)}, bf16[256,2048]{1,0:T(8,128)(2,1)}, u32[]{:S(2)}, u32[]{:S(2)}) collective-permute-start(bf16[256,2048]{1,0:T(8,128)(2,1)} %get-tuple-element.231), channel_id=1, source_target_pairs={{0,2},{1,3},{2,4},{3,5},{4,6},{5,7},{6,0},{7,1},{8,10},{9,11},{10,... | collective-permute-start | bytes 3145736 | tf_op jit(solution)/shard_map/ppermute | solution.py:1407
  481.0 6.5 copy-start.60
  503.2 5.9 copy-start.56
  503.2 5.9 copy-start.61
  509.1 13.8 %copy-start.20 = (bf16[256,2048]{1,0:T(8,128)(2,1)S(1)}, bf16[256,2048]{1,0:T(8,128)(2,1)}, u32[]{:S(2)}) copy-start(bf16[256,2048]{1,0:T(8,128)(2,1)} %get-tuple-element.228) | copy-start | bytes 3145732
  509.1 30.7 %slice-start.5 = ((s8[5767168]{0:T(1024)(128)(4,1)}), s8[4194304]{0:T(1024)(128)(4,1)S(1)}, s32[]{:S(2)}) async-start(s8[5767168]{0:T(1024)(128)(4,1)} %bitcast.277), calls=%async_computation.8 | async-start | bytes 8388608
  522.9 16.9 %slice-start.6 = ((s8[5767168]{0:T(1024)(128)(4,1)}), s8[1572864]{0:T(1024)(128)(4,1)S(1)}, s32[]{:S(2)}) async-start(s8[5767168]{0:T(1024)(128)(4,1)} %bitcast.277), calls=%async_computation.9 | async-start | bytes 3145728
  539.8 6.7 copy-start.4
  546.5 8.7 copy-start.68
  546.6 21.5 %slice-start.3 = ((s8[5767168]{0:T(1024)(128)(4,1)}), s8[4194304]{0:T(1024)(128)(4,1)S(1)}, s32[]{:S(2)}) async-start(s8[5767168]{0:T(1024)(128)(4,1)} %bitcast.273), calls=%async_computation.6 | async-start | bytes 8388608
  555.3 12.8 %slice-start.4 = ((s8[5767168]{0:T(1024)(128)(4,1)}), s8[1572864]{0:T(1024)(128)(4,1)S(1)}, s32[]{:S(2)}) async-start(s8[5767168]{0:T(1024)(128)(4,1)} %bitcast.273), calls=%async_computation.7 | async-start | bytes 3145728
  566.0 101.1 %collective-permute-start.2 = (bf16[256,2048]{1,0:T(8,128)(2,1)}, bf16[256,2048]{1,0:T(8,128)(2,1)}, u32[]{:S(2)}, u32[]{:S(2)}) collective-permute-start(bf16[256,2048]{1,0:T(8,128)(2,1)} %get-tuple-element.233), channel_id=1, source_target_pairs={{0,2},{1,3},{2,4},{3,5},{4,6},{5,7},{6,0},{7,1},{8,10},{9,11},{10,... | collective-permute-start | bytes 3145736 | tf_op jit(solution)/shard_map/ppermute | solution.py:1407
  566.4 100.6 %collective-permute-start.1 = (bf16[256,2048]{1,0:T(8,128)(2,1)}, bf16[256,2048]{1,0:T(8,128)(2,1)}, u32[]{:S(2)}, u32[]{:S(2)}) collective-permute-start(bf16[256,2048]{1,0:T(8,128)(2,1)} %get-tuple-element.234), channel_id=1, source_target_pairs={{0,4},{1,5},{2,6},{3,7},{4,0},{5,1},{6,2},{7,3},{8,12},{9,13},{10,... | collective-permute-start | bytes 3145736 | tf_op jit(solution)/shard_map/ppermute | solution.py:1407
  567.4 99.6 %collective-permute-start = (bf16[256,2048]{1,0:T(8,128)(2,1)}, bf16[256,2048]{1,0:T(8,128)(2,1)}, u32[]{:S(2)}, u32[]{:S(2)}) collective-permute-start(bf16[256,2048]{1,0:T(8,128)(2,1)} %get-tuple-element.235), channel_id=1, source_target_pairs={{0,6},{1,7},{2,0},{3,1},{4,2},{5,3},{6,4},{7,5},{8,14},{9,15},{10,... | collective-permute-start | bytes 3145736 | tf_op jit(solution)/shard_map/ppermute | solution.py:1407
  673.7 6.0 copy-start.44
  673.7 6.0 copy-start.46
  673.7 6.0 copy-start.48
  673.8 6.0 copy-start.51
  683.0 120.7 %copy-start.32 = (bf16[512,256]{1,0:T(8,128)(2,1)S(1)}, bf16[512,256]{1,0:T(8,128)(2,1)}, u32[]{:S(2)}) copy-start(bf16[512,256]{1,0:T(8,128)(2,1)} %get-tuple-element.240) | copy-start | bytes 786436
  683.0 120.7 %copy-start.33 = (bf16[512,256]{1,0:T(8,128)(2,1)S(1)}, bf16[512,256]{1,0:T(8,128)(2,1)}, u32[]{:S(2)}) copy-start(bf16[512,256]{1,0:T(8,128)(2,1)} %get-tuple-element.241) | copy-start | bytes 786436
  683.0 120.7 %copy-start.34 = (bf16[512,256]{1,0:T(8,128)(2,1)S(1)}, bf16[512,256]{1,0:T(8,128)(2,1)}, u32[]{:S(2)}) copy-start(bf16[512,256]{1,0:T(8,128)(2,1)} %get-tuple-element.242) | copy-start | bytes 786436
  683.0 120.7 %copy-start.35 = (bf16[512,256]{1,0:T(8,128)(2,1)S(1)}, bf16[512,256]{1,0:T(8,128)(2,1)}, u32[]{:S(2)}) copy-start(bf16[512,256]{1,0:T(8,128)(2,1)} %get-tuple-element.243) | copy-start | bytes 786436
  803.7 7.0 copy-start.38
  803.7 7.1 copy-start.7
  815.0 6.1 copy-start.67
  821.1 8.7 copy-start.21
  1057.8 6.6 copy-start.19
  1057.9 7.5 copy-start.36
  (36 other events, 144.8 us)
Sparse Core Ops, SparseCore 0:
  87.8 52.3 all-gather.1
  810.8 41.8 reduce-scatter.1

commit v8 on v7

--- a/solution.py
+++ b/solution.py
@@ -232,19 +232,19 @@
     remote(region, region, sem, sem, device).wait_recv()
 
 
-def column_sum(array, shared, totals, n_dp, n_ex, inner, collective_id):
+def column_sum(array, rows_out, shared, totals, n_dp, n_ex, inner, collective_id):
     chips = n_ex // 2
     shape = array.shape[1:]
     extra = len(totals)
     _, _, r, ff_s = shared[0].shape
 
     def kernel(x_ref, *refs):
-        s_in, t_refs, refs = refs[:3], refs[3 : 3 + extra], refs[3 + extra :]
-        o_ref, s_out, back_refs = refs[0], refs[1:4], refs[4 : 4 + extra]
-        refs = refs[4 + extra :]
+        s_in, r_ref, t_refs, refs = refs[:3], refs[3], refs[4 : 4 + extra], refs[4 + extra :]
+        o_ref, s_out, r_out, back_refs = refs[0], refs[1:4], refs[4], refs[5 : 5 + extra]
+        refs = refs[5 + extra :]
         buf, from_sib, out_buf, from_far = refs[:4]
-        send, recv, near_s, near_r, far_s, far_r = refs[4:10]
-        rest = refs[10:]
+        send, recv, near_s, near_r, far_s, far_r, r_s, r_r, local = refs[4:13]
+        rest = refs[13:]
         z, e, c, k, sibling, same_core, column = places(n_dp, n_ex)
         group = column_group(z, e, inner)
         greet(same_core + [sibling] + column + [(d[0], sibling[1]) for d in column])
@@ -252,7 +252,7 @@
             ExpertsBack(t_refs[m], back_refs[m], rest[7 * m : 7 * m + 7], n_dp, n_ex, inner)
             for m in range(extra)
         ]
-        copies = []
+        copies, rows_back = [], []
         for i in range(1, inner):
             to = lax.rem(z + i, inner)
             copy = remote(x_ref.at[to], buf.at[i], send.at[i], recv.at[i], group[i])
@@ -269,6 +269,15 @@
                 near[i, m].start()
         for back in backs:
             back.begin()
+        for i in range(1, chips):
+            copy = remote(
+                r_ref.at[i], r_out.at[i], r_s.at[i], r_r.at[i], same_core[chips - i - 1]
+            )
+            copy.start()
+            rows_back.append(copy)
+        copy = pltpu.make_async_copy(r_ref.at[0], r_out.at[0], local)
+        copy.start()
+        rows_back.append(copy)
 
         def pair(i, m):
             chip = lax.rem(c + i, chips)
@@ -312,26 +321,29 @@
             lax.fori_loop(0, n_dp, row, 0)
         for copy in copies + list(near.values()) + list(far.values()):
             copy.wait_send()
+        for copy in rows_back:
+            copy.wait()
         for back in backs:
             back.end()
 
     dma = pltpu.SemaphoreType.DMA
     scratch = [pltpu.VMEM((inner,) + shape, BF)]
     scratch += [pltpu.VMEM((3, chips, n_dp, r, ff_s), BF)] * 3
-    scratch += [dma((inner,))] * 2 + [dma((3, chips))] * 4
+    scratch += [dma((inner,))] * 2 + [dma((3, chips))] * 4 + [dma((chips,))] * 2 + [dma]
     for total in totals:
         scratch += ExpertsBack.scratch(total, n_dp, inner)
     outs = pl.pallas_call(
         kernel,
         out_shape=[jax.ShapeDtypeStruct(shape, F32)]
         + [jax.ShapeDtypeStruct((n_dp, r, ff_s), BF)] * 3
+        + [jax.ShapeDtypeStruct(rows_out.shape, BF)]
         + [ExpertsBack.out(total, n_dp, inner) for total in totals],
-        in_specs=[VMEM] * 4 + [ANY] * extra,
-        out_specs=[VMEM] * 4 + [ANY] * extra,
+        in_specs=[VMEM] * 4 + [ANY] * (1 + extra),
+        out_specs=[VMEM] * 4 + [ANY] * (1 + extra),
         scratch_shapes=scratch,
         compiler_params=params(collective_id),
-    )(array, *shared, *totals)
-    return outs[0], outs[1:4], outs[4:]
+    )(array, *shared, rows_out, *totals)
+    return outs[0], outs[1:4], outs[4], outs[5:]
 
 
 def column_group(z, e, inner):
@@ -732,63 +744,226 @@
     return outs[:8], outs[8], outs[9], outs[10], outs[11 : 11 + count], outs[11 + count :]
 
 
-def between(blocks, way, weights, totals, n_dp, n_ex, inner, collective_id):
+def silu_parts(a):
+    sig = 1.0 / (1.0 + jnp.exp(-a))
+    return a * sig, sig * (1.0 + a * (1.0 - sig))
+
+
+def dispatch(blocks, x, cot, shared, weight, n_dp, n_ex, inner, collective_id):
     chips = n_ex // 2
-    n_in, n_back = len(weights), len(totals)
-
-    def kernel(x_ref, *refs):
-        w_in, t_in = refs[:n_in], refs[n_in : n_in + n_back]
-        refs = refs[n_in + n_back :]
-        o_ref, w_out, t_out = refs[0], refs[1 : 1 + n_in], refs[1 + n_in : 1 + n_in + n_back]
-        refs = refs[1 + n_in + n_back :]
-        send, recv, local = refs[:3]
+    rows, width = x.shape
+    ff = shared[0].shape[1]
+    tile = 256
+
+    def kernel(
+        b_ref, x_hbm, c_hbm, g_hbm, u_hbm, d_hbm, w_ref,
+        o_ref, w_out, out_ref, dx_ref, gg_ref, gu_ref, gd_ref,
+        x_v, c_v, g_v, u_v, d_v, hid, ga, gb, send, recv, loads, *rest,
+    ):
         z, e, c, k, sibling, same_core, column = places(n_dp, n_ex)
         greet(same_core + [sibling] + column + [(device[0], sibling[1]) for device in column])
-        refs = refs[3:]
-        works = [
-            ExpertsIn(w_in[m], w_out[m], refs[4 * m : 4 * m + 4], n_dp, n_ex, inner)
-            for m in range(n_in)
-        ]
-        refs = refs[4 * n_in :]
-        works += [
-            ExpertsBack(t_in[m], t_out[m], refs[7 * m : 7 * m + 7], n_dp, n_ex, inner)
-            for m in range(n_back)
-        ]
+        matrix = ExpertsIn(w_ref, w_out, rest, n_dp, n_ex, inner)
         copies = []
         for i in range(1, chips):
-            to = same_core[i - 1] if way > 0 else same_core[chips - i - 1]
-            copy = remote(x_ref.at[i], o_ref.at[i], send.at[i], recv.at[i], to)
+            copy = remote(b_ref.at[i], o_ref.at[i], send.at[i], recv.at[i], same_core[i - 1])
             copy.start()
             copies.append(copy)
-        copy = pltpu.make_async_copy(x_ref.at[0], o_ref.at[0], local)
+        copy = pltpu.make_async_copy(b_ref.at[0], o_ref.at[0], loads.at[0])
         copy.start()
         copies.append(copy)
-        for work in works:
-            work.begin()
-        for work in works:
-            work.pass_on()
+        matrix.begin()
+        moves = [
+            pltpu.make_async_copy(src, dst, loads.at[1 + j])
+            for j, (src, dst) in enumerate(
+                [(x_hbm, x_v), (g_hbm, g_v), (u_hbm, u_v), (c_hbm, c_v), (d_hbm, d_v)]
+            )
+        ]
+        for copy in moves:
+            copy.start()
+        for copy in moves:
+            copy.wait()
+
+        def rows_of(i, carry):
+            at = pl.ds(pl.multiple_of(i * tile, tile), tile)
+            first = mm(x_v[at, :], g_v[...])
+            second = mm(x_v[at, :], u_v[...])
+            silu, slope = silu_parts(first)
+            low = (silu * second).astype(BF)
+            hid[at, :] = low
+            out_ref[at, :] = mm_cols(low, d_v[...])
+            back = mm(c_v[at, :], d_v[...])
+            low_a = (back * second * slope).astype(BF)
+            low_b = (back * silu).astype(BF)
+            ga[at, :] = low_a
+            gb[at, :] = low_b
+            dx_ref[at, :] = mm_cols(low_a, g_v[...]) + mm_cols(low_b, u_v[...])
+            return carry
+
+        lax.fori_loop(0, rows // tile, rows_of, 0)
+
+        def columns_of(j, carry):
+            at = pl.ds(pl.multiple_of(j * tile, tile), tile)
+            gg_ref[at, :] = mm_rows(x_v[:, at], ga[...]).astype(BF)
+            gu_ref[at, :] = mm_rows(x_v[:, at], gb[...]).astype(BF)
+            gd_ref[at, :] = mm_rows(c_v[:, at], hid[...]).astype(BF)
+            return carry
+
+        lax.fori_loop(0, width // tile, columns_of, 0)
+        matrix.pass_on()
         for copy in copies:
             copy.wait()
-        for work in works:
-            work.end()
+        matrix.end()
 
     dma = pltpu.SemaphoreType.DMA
-    scratch = [dma((chips,)), dma((chips,)), dma]
-    for _ in weights:
-        scratch += ExpertsIn.scratch(n_dp)
-    for total in totals:
-        scratch += ExpertsBack.scratch(total, n_dp, inner)
+    sds = jax.ShapeDtypeStruct
+    vmem = pltpu.VMEM
     outs = pl.pallas_call(
         kernel,
-        out_shape=[jax.ShapeDtypeStruct(blocks.shape, BF)]
-        + [ExpertsIn.out(w, n_dp, n_ex) for w in weights]
-        + [ExpertsBack.out(total, n_dp, inner) for total in totals],
-        in_specs=[ANY] * (1 + n_in + n_back),
-        out_specs=[ANY] * (1 + n_in + n_back),
-        scratch_shapes=scratch,
+        out_shape=[sds(blocks.shape, BF), ExpertsIn.out(weight, n_dp, n_ex)]
+        + [sds((rows, width), F32)] * 2
+        + [sds((width, ff), BF)] * 3,
+        in_specs=[ANY] * 7,
+        out_specs=[ANY] * 2 + [VMEM] * 5,
+        scratch_shapes=[vmem((rows, width), BF)] * 2
+        + [vmem((width, ff), BF)] * 3
+        + [vmem((rows, ff), BF)] * 3
+        + [dma((chips,)), dma((chips,)), dma((6,))]
+        + ExpertsIn.scratch(n_dp),
         compiler_params=params(collective_id),
-    )(blocks, *weights, *totals)
-    return outs[0], outs[1:]
+    )(blocks, x, cot, *shared, weight)
+    return outs[0], outs[1], outs[2], outs[3], outs[4:]
+
+
+def experts_back(values, weights, dots, n_dp, n_ex, inner, collective_id):
+    chips = n_ex // 2
+    n_slots, width = values[0].shape
+    ff = values[2].shape[1]
+    per_far = n_slots // chips
+    r = width // (n_dp * n_ex)
+    tile = 256
+    span = n_dp * r
+
+    def kernel(*refs):
+        v_hbm, w_hbm, dots_ref, refs = refs[:5], refs[5:8], refs[8], refs[9:]
+        dx_out, dots_out, back_out, g_out, refs = refs[0], refs[1], refs[2], refs[3:5], refs[5:]
+        x_v, s_v, a_v, b_v, h_v, wg, wu, wd, dx_v, total, stage = refs[:11]
+        loads, send, recv, d_send, d_recv, local, out_sem = refs[11:18]
+        z, e, c, k, sibling, same_core, column = places(n_dp, n_ex)
+        moves = [
+            pltpu.make_async_copy(src, dst, loads.at[j])
+            for j, (src, dst) in enumerate(
+                zip((*v_hbm, *w_hbm), (x_v, s_v, a_v, b_v, h_v, wg, wu, wd))
+            )
+        ]
+        for j in (1, 4, 7, 2, 3, 5, 6, 0):
+            moves[j].start()
+        greet(same_core + [sibling] + column + [(device[0], sibling[1]) for device in column])
+        back = ExpertsBack(total, back_out, refs[18:], n_dp, n_ex, inner)
+        dot_copies = []
+        for i in range(1, chips):
+            copy = remote(
+                dots_ref.at[i], dots_out.at[i], d_send.at[i], d_recv.at[i],
+                same_core[chips - i - 1],
+            )
+            copy.start()
+            dot_copies.append(copy)
+        copy = pltpu.make_async_copy(dots_ref.at[0], dots_out.at[0], local.at[0])
+        copy.start()
+        dot_copies.append(copy)
+        moves[1].wait()
+        moves[4].wait()
+
+        def down_rows(t, carry):
+            j = lax.rem(t + (1 - k) * (n_ex // 2), n_ex)
+            at = pl.ds(pl.multiple_of(j * span, span), span)
+            block = mm_rows(s_v[:, at], h_v[...]).astype(BF)
+            total[j] = block.reshape(n_dp, r, ff)
+            return carry
+
+        lax.fori_loop(0, n_ex, down_rows, 0)
+        back.begin()
+        for j in (7, 2, 3):
+            moves[j].wait()
+
+        def hidden_rows(i, carry):
+            at = pl.ds(pl.multiple_of(i * tile, tile), tile)
+            grad = mm(s_v[at, :], wd[...])
+            silu, slope = silu_parts(a_v[at, :].astype(F32))
+            second = b_v[at, :].astype(F32)
+            a_v[at, :] = (grad * second * slope).astype(BF)
+            b_v[at, :] = (grad * silu).astype(BF)
+            return carry
+
+        lax.fori_loop(0, n_slots // tile, hidden_rows, 0)
+        moves[5].wait()
+        moves[6].wait()
+        copies = []
+        for i in list(range(1, chips)) + [0]:
+            at = slice(i * per_far, (i + 1) * per_far)
+            block = mm_cols(a_v[at, :], wg[...]) + mm_cols(b_v[at, :], wu[...])
+            dx_v[i] = block.astype(BF)
+            if i:
+                copy = remote(
+                    dx_v.at[i], dx_out.at[i], send.at[i], recv.at[i], same_core[chips - i - 1]
+                )
+            else:
+                copy = pltpu.make_async_copy(dx_v.at[0], dx_out.at[0], local.at[1])
+            copy.start()
+            copies.append(copy)
+            if i == 1:
+                back.pass_on()
+        moves[0].wait()
+
+        def other_rows(j, carry):
+            at = pl.ds(pl.multiple_of(j * span, span), span)
+            for m, side in enumerate((a_v, b_v)):
+
+                @pl.when(j > 0)
+                def _(m=m):
+                    pltpu.make_async_copy(stage.at[m], g_out[m].at[j - 1], out_sem.at[m]).wait()
+
+                block = mm_rows(x_v[:, at], side[...]).astype(BF)
+                stage[m] = block.reshape(n_dp, r, ff)
+                pltpu.make_async_copy(stage.at[m], g_out[m].at[j], out_sem.at[m]).start()
+            return carry
+
+        lax.fori_loop(0, n_ex, other_rows, 0)
+        for m in range(2):
+            pltpu.make_async_copy(stage.at[m], g_out[m].at[n_ex - 1], out_sem.at[m]).wait()
+        for copy in copies + dot_copies:
+            copy.wait()
+        back.end()
+
+    dma = pltpu.SemaphoreType.DMA
+    sds = jax.ShapeDtypeStruct
+    vmem = pltpu.VMEM
+    total = sds((n_ex, n_dp, r, ff), BF)
+    outs = pl.pallas_call(
+        kernel,
+        out_shape=[
+            sds((chips, per_far, width), BF),
+            sds(dots.shape, BF),
+            ExpertsBack.out(total, n_dp, inner),
+            total,
+            total,
+        ],
+        in_specs=[ANY] * 9,
+        out_specs=[ANY] * 5,
+        scratch_shapes=[vmem((n_slots, width), BF)] * 2
+        + [vmem((n_slots, ff), BF)] * 3
+        + [vmem((width, ff), BF)] * 3
+        + [
+            vmem((chips, per_far, width), BF),
+            vmem(total.shape, BF),
+            vmem((2, n_dp, r, ff), BF),
+            dma((8,)),
+        ]
+        + [dma((chips,))] * 4
+        + [dma((2,))] * 2
+        + ExpertsBack.scratch(total, n_dp, inner),
+        compiler_params=params(collective_id),
+    )(*values, *weights, dots)
+    return outs[0], outs[1], outs[2], outs[3:]
 
 
 class ExpertsBack:
@@ -907,7 +1082,7 @@
 
 
 def backward_exchange(
-    grad, attend, hidden, latent_low, own, shared, totals, n_dp, n_ex, inner, collective_id
+    grad, attend, hidden, latent_low, own, out, shared, totals, n_dp, n_ex, inner, collective_id
 ):
     chips = n_ex // 2
     rows, width = grad.shape
@@ -928,9 +1103,10 @@
         grad_ref, att_in, refs = refs[0], refs[1:12], refs[12:]
         hidden_ref, low_ref, refs = refs[0], refs[1], refs[2:]
         wl_ref, lat_ref, tok_ref, gain_ref, glat_ref, gnat_ref, router_ref, gtwo_ref = refs[:8]
-        sh_in, t_refs, refs = refs[8:11], refs[11 : 11 + extra], refs[11 + extra :]
-        tok_out, vec_out, pack_out, heads_mid, heads_out, wout_out = refs[:6]
-        sh_out, back_refs, refs = refs[6:9], refs[9 : 9 + extra], refs[9 + extra :]
+        out_ref, sh_in, refs = refs[8], refs[9:12], refs[12:]
+        t_refs, refs = refs[:extra], refs[extra:]
+        tok_out, vec_out, pack_out, heads_mid, heads_out, wout_out, out_got = refs[:7]
+        sh_out, back_refs, refs = refs[7:10], refs[10 : 10 + extra], refs[10 + extra :]
         gbuf, att_tmp, refs = refs[0], refs[1:8], refs[8:]
         part_l, bufs, sums, refs = refs[0], refs[1:7], refs[7:9], refs[9:]
         hsrc, wsrc, pack, psib, pout, pfar, psum, pbuf, vec, vbuf, vzbuf = refs[:11]
@@ -939,10 +1115,11 @@
         sems, refs = refs[5:13], refs[13:]
         (
             h_s, h_r, hz_s, hz_r, w_s, w_r, pn_s, pn_r, pf_s, pf_r, pc_s, pc_r, s_s, s_r,
-            v_s, v_r, vz_s, vz_r,
-        ) = refs[:18]
-        rest = refs[18:]
+            v_s, v_r, vz_s, vz_r, o_s, o_r,
+        ) = refs[:20]
+        rest = refs[20:]
         x_refs = (gbuf, part_l)
+        group = column_group(lax.axis_index("dp"), lax.axis_index("expert"), inner)
         z, e, c, k, sibling, same_core, column = places(n_dp, n_ex)
         plane = [(z, lax.rem(e + i, n_ex)) for i in range(1, n_ex)]
         part = lax.rem(e, parts)
@@ -979,6 +1156,17 @@
             copy = pltpu.make_async_copy(sh_in[m].at[z], sh_out[m].at[z], local.at[1 + m])
             copy.start()
             others.append(copy)
+        mine = lax.rem(z, inner)
+        for i in range(1, inner):
+            copy = remote(
+                out_ref.at[lax.rem(mine + i, inner)], out_got.at[mine], o_s.at[i], o_r.at[i],
+                group[i],
+            )
+            copy.start()
+            others.append(copy)
+        copy = pltpu.make_async_copy(out_ref.at[mine], out_got.at[mine], local.at[5])
+        copy.start()
+        others.append(copy)
         for i in range(1, chips):
             gather[i - 1].wait_recv()
             block = gbuf.at[lax.rem(c + chips - i, chips) * 2 + k]
@@ -1239,10 +1427,10 @@
         vmem((n_ex, 8, width), F32),
         vmem((n_dp, 8, width), F32),
     ]
-    scratch += [dma((chips,))] * 4 + [dma((5,))] + [dma((chips,))] * 8
+    scratch += [dma((chips,))] * 4 + [dma((6,))] + [dma((chips,))] * 8
     scratch += [dma((n_ex, n_dp))] * 2 + [dma((n_dp,))] * 2 + [dma((hp, parts)), dma((n_dp,))]
     scratch += [dma((chips,))] * 4 + [dma((n_dp,))] * 2 + [dma((3, n_dp))] * 2
-    scratch += [dma((n_ex,))] * 2 + [dma((n_dp,))] * 2
+    scratch += [dma((n_ex,))] * 2 + [dma((n_dp,))] * 2 + [dma((inner,))] * 2
     for total in totals:
         scratch += ExpertsBack.scratch(total, n_dp, inner)
     outs = pl.pallas_call(
@@ -1254,15 +1442,16 @@
             sds((n_dp, n_ex, r, head_cols), BF),
             sds((n_dp, n_ex, r, head_cols), BF),
             sds((n_dp, r, width), BF),
+            sds(out.shape, BF),
         ]
         + [sds(array.shape, BF) for array in shared]
         + [ExpertsBack.out(total, n_dp, inner) for total in totals],
-        in_specs=[ANY] + [VMEM] * 21 + [ANY] * (3 + extra),
-        out_specs=[VMEM] * 3 + [ANY] * (6 + extra),
+        in_specs=[ANY] + [VMEM] * 21 + [ANY] * (4 + extra),
+        out_specs=[VMEM] * 3 + [ANY] * (7 + extra),
         scratch_shapes=scratch,
         compiler_params=params(collective_id),
-    )(grad, *attend, hidden, latent_low, *own, *shared, *totals)
-    return outs[:3], outs[4], outs[5], outs[6:9], outs[9:]
+    )(grad, *attend, hidden, latent_low, *own, out, *shared, *totals)
+    return outs[:3], outs[4], outs[5], outs[6], outs[7:10], outs[10:]
 
 
 def shards(
@@ -1429,11 +1618,12 @@
     hidden_two = pick(x_col, my_local)
     x_col = x_col.reshape(inner * rows, width)
 
-    x_in, (wd,) = between(
+    x_in, wd, shared_out, shared_dx, shared_grads = dispatch(
         mm(hot, x_col).astype(BF).reshape(chips, per_far, width),
-        1,
-        [expert_down.reshape(-1, n_ex, r, ff_e)],
-        [],
+        x_col,
+        cot_col,
+        (sgate, sup, sdown),
+        expert_down.reshape(-1, n_ex, r, ff_e),
         n_dp,
         n_ex,
         inner,
@@ -1447,19 +1637,6 @@
         top = jnp.max(logits, axis=-1, keepdims=True)
         exp_logits = jnp.exp(logits - top)
         return exp_logits / jnp.sum(exp_logits, axis=-1, keepdims=True)
-
-    shared_a = mm(x_col, sgate)
-    shared_b = mm(x_col, sup)
-    shared_hidden, shared_back = jax.vjp(swiglu, shared_a, shared_b)
-    shared_hidden = shared_hidden.astype(BF)
-    shared_out = mm_cols(shared_hidden, sdown)
-    grad_sa, grad_sb = (v.astype(BF) for v in shared_back(mm(cot_col, sdown)))
-    shared_grads = [
-        mm_rows(x_col, grad_sa).astype(BF),
-        mm_rows(x_col, grad_sb).astype(BF),
-        mm_rows(cot_col, shared_hidden).astype(BF),
-    ]
-    shared_dx = mm_cols(grad_sa, sgate) + mm_cols(grad_sb, sup)
 
     slot_probs = probs_of(mm(x_in, router))
     slot_gate = jnp.sum(
@@ -1469,20 +1646,15 @@
     )
     expert_a = mm(x_in, wg)
     expert_b = mm(x_in, wu)
-    expert_hidden, expert_back = jax.vjp(swiglu, expert_a, expert_b)
-    expert_hidden = expert_hidden.astype(BF)
-    rows_back = through(mm_cols(expert_hidden, wd).astype(BF), -1)
+    expert_hidden = swiglu(expert_a, expert_b).astype(BF)
+    expert_rows = mm_cols(expert_hidden, wd).astype(BF)
+    slot_dots = jnp.sum(grad_in.astype(F32) * expert_rows.astype(F32), axis=-1, keepdims=True)
+    slot_dots = jnp.broadcast_to(slot_dots, (n_slots, 128)).astype(BF)
     slot_grad = (slot_gate * grad_in.astype(F32)).astype(BF)
-    grad_ea, grad_eb = (v.astype(BF) for v in expert_back(mm(slot_grad, wd)))
-    expert_totals = [
-        mm_rows(left, right).astype(BF).reshape(n_ex, n_dp, r, ff_e)
-        for left, right in ((x_in, grad_ea), (x_in, grad_eb), (slot_grad, expert_hidden))
-    ]
-    dx_back, (down_back,) = between(
-        (mm_cols(grad_ea, wg) + mm_cols(grad_eb, wu)).astype(BF).reshape(chips, per_far, width),
-        -1,
-        [],
-        expert_totals[2:],
+    dx_back, dots_back, down_back, expert_totals = experts_back(
+        [x_in, slot_grad, expert_a.astype(BF), expert_b.astype(BF), expert_hidden],
+        [wg, wu, wd],
+        slot_dots.reshape(chips, per_far, 128),
         n_dp,
         n_ex,
         inner,
@@ -1500,8 +1672,7 @@
         [hot_t[:, m * per_far : (m + 1) * per_far] * gates[m].astype(BF) for m in range(chips)],
         axis=1,
     )
-    out_col = (mm(gate_hot, rows_back) + shared_out).astype(BF)
-    dots = mm_cols(cot_col, rows_back) * hot_t.astype(F32)
+    dots = dots_back.reshape(n_slots, 128)[:, 0].astype(F32)[None] * hot_t.astype(F32)
     dots = jnp.sum(dots.reshape(inner * rows, chips, per_far), axis=-1)
     grad_probs_col = sum(
         jnp.where(expert_axis == far_experts[m], dots[:, m : m + 1], 0.0) for m in range(chips)
@@ -1510,8 +1681,9 @@
     dx_send = jnp.concatenate(
         [dx_col, grad_probs_col, jnp.zeros((inner * rows, 128 - n_experts), F32)], axis=1
     ).astype(BF)
-    dx_sum, shared_sums, (gate_back,) = column_sum(
+    dx_sum, shared_sums, rows_back, (gate_back,) = column_sum(
         dx_send.reshape(inner, rows, width + 128),
+        expert_rows.reshape(chips, per_far, width),
         [grad.reshape(n_ex, n_dp, r, ff_s) for grad in shared_grads],
         expert_totals[:1],
         n_dp,
@@ -1530,17 +1702,13 @@
     grad_resid_norm, grad_gain_two = norm_two_back(grad_hidden_two)
     grad_residual = cot_owner.astype(F32) + grad_resid_norm
 
-    out_col, _ = lax.optimization_barrier((out_col, dx_sum))
-    out_sum = lax.psum_scatter(
-        out_col, "dp", scatter_dimension=0, tiled=True, axis_index_groups=col_groups
-    )
-    out_tokens = from_owner_order((residual + out_sum.astype(F32)).astype(BF))
+    out_col = mm(gate_hot, rows_back.reshape(n_slots, width)) + shared_out
     latent_own = lax.dynamic_slice_in_dim(latent_raw, e * rows, rows, 0)
     router_back = jnp.pad(
         grad_router.reshape(n_ex, n_dp * r, n_experts),
         ((0, 0), (0, 0), (DR, DR - n_experts)),
     ).astype(BF)
-    (grad_tokens, vec_sum, pack_sum), heads_got, wout_got, shared_got, (up_back,) = (
+    (grad_tokens, vec_sum, pack_sum), heads_got, wout_got, out_got, shared_got, (up_back,) = (
         backward_exchange(
             grad_residual.astype(BF),
             [wo_rows, wq, wexp, cos_wide, sine_wide, keep, qcat, kcat, value, lse, attended],
@@ -1556,6 +1724,7 @@
                 router_back,
                 grad_gain_two[None],
             ],
+            out_col.astype(BF).reshape(inner, rows, width),
             shared_sums,
             expert_totals[1:2],
             n_dp,
@@ -1568,6 +1737,7 @@
     def added(values):
         return jnp.sum(values.astype(F32), axis=0)
 
+    out_tokens = from_owner_order((residual + added(out_got)).astype(BF))
     heads_all = added(heads_got)
     sum_wq = heads_all[..., :head_cols].transpose(1, 0, 2)
     sum_wq = jnp.concatenate(

time: 1080 us -> 1050 us (0.972)
  matrix products: 158 us -> 64.1 us
  Pallas kernels: 754 us -> 834 us
  waiting for transfers between devices: 22.2 us -> 0.03 us
    pallas_call x1, Pallas kernels: 181 us -> 226 us  [backward_exchange(): pl.pallas_call(kernel, out_shape=[sds((rows, width), F32), sds((8, width)...]
    pallas_call x2, Pallas kernels: 141 us -> 185 us  [the longest x1 95.9 us: dispatch(): pl.pallas_call(kernel, out_shape=[sds(blocks.shape, BF), ExpertsIn.out(we...]
    dot_general x7 -> x1, matrix products: 38.9 us -> 1.17 us  [mm_rows(): lax.dot_general(left, right, (((0,), (0,)), ((), ())), preferred_element_...]
    dot_general x8 -> x2, matrix products: 44.5 us -> 13.3 us  [mm_cols(): lax.dot_general(left, right, (((1,), (1,)), ((), ())), preferred_element_...]
    dot_general x12 -> x8, matrix products: 74.1 us -> 49.6 us  [mm(): return jnp.dot(left, right, preferred_element_type=F32)]
    convert_element_type x4 -> x3, local copies, waits for them, and re-layouts: 12.6 us -> 0.29 us  [the longest x1 0.27 us: shards(): out_tokens = from_owner_order((residual + added(out_got)).astype(BF))]
    reduce_scatter x1 -> x0, waiting for transfers between devices: 12.3 us -> none  [shards(): lax.psum_scatter(out_col, 'dp', scatter_dimension=0, tiled=True, axis_ind...]
  transfers between devices with their start and end apart: 8 -> 4, of which waited for: 3 -> 0; matrix products, arithmetic and copies ran while one was open for 15% -> 8% of each run, Pallas kernels for 36% -> 32%
where the time goes in v8:
time: 1050 us; the launch traced here: 1040 us
  Pallas kernels  834 us (79%)
  local copies, waits for them, and re-layouts  83.3 us (8%)
  matrix products  64.1 us (6%)
  other arithmetic  34.5 us (3%)
  between operations  16.2 us (2%)
    pallas_call x1, Pallas kernels, forward_exchange(): pl.pallas_call(kernel, out_shape=[sds((seq, width), BF), sds((seq, attend...  233 us
    pallas_call x1, Pallas kernels, backward_exchange(): pl.pallas_call(kernel, out_shape=[sds((rows, width), F32), sds((8, width)...  226 us
    pallas_call x1, Pallas kernels, column_sum(): pl.pallas_call(kernel, out_shape=[jax.ShapeDtypeStruct(shape, F32)] + [ja...  120 us
    pallas_call x1, Pallas kernels, dispatch(): pl.pallas_call(kernel, out_shape=[sds(blocks.shape, BF), ExpertsIn.out(we...  95.9 us
    pallas_call x1, Pallas kernels, experts_back(): pl.pallas_call(kernel, out_shape=[sds((chips, per_far, width), BF), sds(d...  89 us
    pallas_call x1, Pallas kernels, first_exchange(): pl.pallas_call(kernel, out_shape=[jax.ShapeDtypeStruct((n_ex,) + tok.shap...  71.3 us
    dot_general x8, matrix products, mm(): return jnp.dot(left, right, preferred_element_type=F32)  49.6 us
  transfers between devices with their start and end apart: 4, of which 0 were waited for; matrix products, arithmetic and copies ran while one was open for 8% of the time, Pallas kernels for 32%

profile of v8, /device:TPU:11, one launch (start us, length us, event | category | flops | bytes accessed | tf_op | source)
XLA Modules:
  0.0 1036.2 jit_solution(1175878652465801376)
XLA Ops:
  9.5 1.7 reshape.762
  17.8 71.3 %shard_map.342 = (bf16[8,128,2048]{2,1,0:T(8,128)(2,1)}, bf16[4,8,64,512]{3,2,1,0:T(8,128)(2,1)}, bf16[4,8,64,640]{3,2,1,0:T(8,128)(2,1)}) custom-call(bf16[128,2048]{1,0:T(8,128)(2,1)} %refs_16_.1, bf16[8,64,512]{2,1,0:T(8,128)(2,1)} %pad_maximum_fusion.2.wa_ref, bf16[64,640]{1,0:T(8,128)(2,1)} %concatenate.36.pk_ref), custom_call_target="tpu_custom_call" | custom-call | tf_op jit(solution)/shard_map/pallas_call | solution.py:434
  89.1 2.2 copy.263
  94.6 1.9 slice.149
  96.4 1.3 slice.146
  104.4 2.0 copy.255.refs_7_.refs_5_
  106.5 1.4 reshape.777
  108.7 1.4 reshape.778
  110.1 2.2 reshape.779
  112.3 1.7 tile.26
  114.1 2.0 copy.254.refs_6_.refs_4_
  116.1 2.3 reshape.771
  118.4 2.0 copy.307
  120.4 2.2 reshape.772.refs_9_
  122.6 1.9 copy.249
  124.5 2.0 copy.256.refs_10_
  129.7 1.3 copy.246
  133.4 233.0 %shard_map.343 = (bf16[1024,2048]{1,0:T(8,128)(2,1)}, f32[1024,640]{1,0:T(8,128)}, bf16[1024,512]{1,0:T(8,128)(2,1)}, bf16[2,1024,256]{2,1,0:T(8,128)(2,1)}, bf1...) custom-call(bf16[8,128,2048]{2,1,0:T(8,128)(2,1)} %get-tuple-element, ...), custom_call_target="tpu_custom_call" | custom-call | tf_op jit(solution)/shard_map/pallas_call | solution.py:714
  367.6 2.3 fusion.45
  372.9 1.7 constant_dynamic-slice_fusion.2.refs_15_
  376.7 1.4 fusion.7
  378.1 1.3 slice_multiply_fusion.3
  379.4 5.1 convolution_convert_fusion.2
  384.5 4.7 convolution_convert_fusion.1
  389.2 1.8 fusion.41
  392.4 2.1 collective-permute-start
  394.5 95.9 %shard_map.344 = (bf16[4,256,2048]{2,1,0:T(8,128)(2,1)}, bf16[8,4,64,1408]{3,2,1,0:T(8,128)(2,1)}, f32[512,2048]{1,0:T(8,128)}, f32[512,2048]{1,0:T(8,128)}, bf1...) custom-call(bf16[4,256,2048]{2,1,0:T(8,128)(2,1)} %bitcast.189, ...), custom_call_target="tpu_custom_call" | custom-call | tf_op jit(solution)/shard_map/pallas_call | solution.py:820
  490.5 11.0 %fusion.46 = f32[1024,1408]{1,0:T(8,128)S(1)} fusion(bf16[1024,2048]{1,0:T(8,128)(2,1)} %bitcast.168, bf16[2048,1408]{1,0:T(8,128)(2,1)} %bitcast.177), kind=kOutput, calls=%fused_computation.158 | convolution fusion | flops 5905580032 | bytes 15728640 | tf_op jit(solution)/shard_map/dot_general | solution.py:56
  501.5 11.6 %multiply_convert_fusion = (bf16[1024,1408]{1,0:T(8,128)(2,1)S(1)}, bf16[1024,1408]{1,0:T(8,128)(2,1)}, bf16[1024,1408]{1,0:T(8,128)(2,1)}) fusion(f32[1024,1408]{1,0:T(8,128)S(1)} %fusion.46, bf16[1024,2048]{1,0:T(8,128)(2,1)S(1)} %bitcast.170, bf16[2048,1408]{1,0:T(8,128)(2,1)} %bitcast.179), kind=kOutput, calls=%fused_computation.8 | convolution fusion | flops 5917114368 | bytes 24379392 | tf_op jit(solution)/shard_map/dot_general | solution.py:56
  514.5 10.9 %fusion.1 = (bf16[1024]{0:T(1024)(128)(2,1)S(1)}, bf16[1024,2048]{1,0:T(8,128)(2,1)}, bf16[1024,2048]{1,0:T(8,128)(2,1)}) fusion(bf16[256,2048]{1,0:T(8,128)(2,1)} %collective-permute-done.2, bf16[256,2048]{1,0:T(8,128)(2,1)} %collective-permute-done.1, bf16[256,2048]{1,0:T(8,128)(2,1)} %collective-permute-done, ...), kind=kOutput, calls=%fused_computation.7 | convolution fusion | flops 5934939136 | bytes 21239808 | tf_op jit(solution)/shard_map/dot_general | solution.py:64
  526.3 89.0 %shard_map.345 = (bf16[4,256,2048]{2,1,0:T(8,128)(2,1)}, bf16[4,256,128]{2,1,0:T(8,128)(2,1)}, bf16[1,2,8,64,1408]{4,3,2,1,0:T(8,128)(2,1)}, bf16[8,4,64,1408]{3,2,1,0:T(8,128)(2,1)}, bf16[8,4,64,1408]{3,2,1,0:T(8,128)(2,1)}) custom-call(bf16[1024,2048]{1,0:T(8,128)(2,1)} %bitcast.169, bf16[1024,2048]{1,0:T(8,128)(2,1)} %get-tuple-element.211.refs_1_, ...), custom_call_target="tpu_custom_call" | custom-call | tf_op jit(solution)/shard_map/pallas_call | solution.py:941
  616.5 1.6 multiply_reduce_fusion
  618.1 6.4 add_convert_fusion.1
  626.1 3.6 concatenate.39.x_ref
  629.7 119.8 %shard_map.346 = (f32[128,2176]{1,0:T(8,128)}, bf16[4,64,704]{2,1,0:T(8,128)(2,1)}, bf16[4,64,704]{2,1,0:T(8,128)(2,1)}, bf16[4,64,704]{2,1,0:T(8,128)(2,1)}, bf...) custom-call(bf16[4,128,2176]{2,1,0:T(8,128)(2,1)} %concatenate.39.x_ref, ...), custom_call_target="tpu_custom_call" | custom-call | tf_op jit(solution)/shard_map/pallas_call | solution.py:335
  751.7 2.4 multiply_reduce_fusion.1
  755.4 2.2 fusion.39
  758.0 1.3 copy.275.refs_19_
  759.3 7.4 add_convert_fusion
  766.7 225.6 %shard_map.347 = (f32[128,2048]{1,0:T(8,128)}, f32[8,2048]{1,0:T(8,128)}, f32[64,640]{1,0:T(8,128)}, bf16[4,8,64,512]{3,2,1,0:T(8,128)(2,1)}, bf16[4,8,64,512]{3...) custom-call(bf16[128,2048]{1,0:T(8,128)(2,1)} %get-tuple-element.205, ...), custom_call_target="tpu_custom_call" | custom-call | tf_op jit(solution)/shard_map/pallas_call | solution.py:1436
  992.3 2.2 convert_reduce_fusion
  999.5 1.4 convert_reduce_fusion.3
  1003.5 1.4 reshape.829
  1005.5 1.4 reshape.831
  1007.4 1.4 reshape.833
  1014.7 4.9 convert.47
  1019.6 2.9 convert.46
  1022.6 2.9 convert.48
  (231 shorter events, 58.7 us)
Async XLA Ops:
  7.2 4.9 copy-start.34
  7.2 5.0 copy-start.31
  7.2 5.1 copy-start.32
  7.2 5.2 copy-start.29
  7.2 5.8 copy-start.30
  7.2 6.6 copy-start.24
  7.2 377.3 %all-gather.2.cloned.1.call-start = ((), (), s32[]{:S(2)}) async-start(), calls=%async_computation | async-start | bytes 2621440 | tf_op jit(solution)/shard_map/all_gather | solution.py:1567
  9.5 4.4 copy-start.28
  9.5 5.1 copy-start.18
  14.4 2.6 copy-start.26
  15.7 76.1 %copy-start.4 = (bf16[128,2048]{1,0:T(8,128)(2,1)S(1)}, bf16[128,2048]{1,0:T(8,128)(2,1)}, u32[]{:S(2)}) copy-start(bf16[128,2048]{1,0:T(8,128)(2,1)} %refs_16_.1) | copy-start | bytes 1572868
  89.1 3.8 copy-start
  92.9 3.5 copy-start.11
  127.5 4.9 copy-start.14
  132.3 380.8 %copy-start.15 = (bf16[2048,16]{0,1:T(8,128)(2,1)}, bf16[2048,16]{0,1:T(8,128)(2,1)S(1)}, u32[]{:S(2)}) copy-start(bf16[2048,16]{0,1:T(8,128)(2,1)S(1)} %reshape.789) | copy-start | bytes 196612
  366.4 3.4 copy-start.33
  366.4 3.5 copy-start.5
  366.4 4.9 copy-start.27
  366.4 5.1 copy-start.25
  369.9 6.1 copy-start.2
  375.1 4.3 copy-start.3
  390.9 123.5 %collective-permute-start.2 = (bf16[256,2048]{1,0:T(8,128)(2,1)}, bf16[256,2048]{1,0:T(8,128)(2,1)}, u32[]{:S(2)}, u32[]{:S(2)}) collective-permute-start(bf16[256,2048]{1,0:T(8,128)(2,1)} %get-tuple-element.213), channel_id=1, source_target_pairs={{0,6},{1,7},{2,0},{3,1},{4,2},{5,3},{6,4},{7,5},{8,14},{9,15},{10,... | collective-permute-start | bytes 3145736 | tf_op jit(solution)/shard_map/ppermute | solution.py:1596
  391.9 122.6 %collective-permute-start.1 = (bf16[256,2048]{1,0:T(8,128)(2,1)}, bf16[256,2048]{1,0:T(8,128)(2,1)}, u32[]{:S(2)}, u32[]{:S(2)}) collective-permute-start(bf16[256,2048]{1,0:T(8,128)(2,1)} %get-tuple-element.214), channel_id=1, source_target_pairs={{0,4},{1,5},{2,6},{3,7},{4,0},{5,1},{6,2},{7,3},{8,12},{9,13},{10,... | collective-permute-start | bytes 3145736 | tf_op jit(solution)/shard_map/ppermute | solution.py:1596
  392.4 122.0 %collective-permute-start = (bf16[256,2048]{1,0:T(8,128)(2,1)S(1)}, bf16[256,2048]{1,0:T(8,128)(2,1)}, u32[]{:S(2)}, u32[]{:S(2)}) collective-permute-start(bf16[256,2048]{1,0:T(8,128)(2,1)S(1)} %get-tuple-element.215), channel_id=1, source_target_pairs={{0,2},{1,3},{2,4},{3,5},{4,6},{5,7},{6,0},{7,1},{8,10},{9,11},{10,... | collective-permute-start | bytes 3145736 | tf_op jit(solution)/shard_map/ppermute | solution.py:1596
  490.4 11.0 %copy-start.1 = (bf16[4,256,2048]{2,1,0:T(8,128)(2,1)S(1)}, bf16[4,256,2048]{2,1,0:T(8,128)(2,1)}, u32[]{:S(2)}) copy-start(bf16[4,256,2048]{2,1,0:T(8,128)(2,1)} %get-tuple-element.73) | copy-start | bytes 12582916
  490.4 24.0 %slice-start = ((s8[5767168]{0:T(1024)(128)(4,1)}), s8[4194304]{0:T(1024)(128)(4,1)S(1)}, s32[]{:S(2)}) async-start(s8[5767168]{0:T(1024)(128)(4,1)} %bitcast.182), calls=%async_computation.1 | async-start | bytes 8388608
  501.4 13.0 %slice-start.1 = ((s8[5767168]{0:T(1024)(128)(4,1)}), s8[1572864]{0:T(1024)(128)(4,1)S(1)}, s32[]{:S(2)}) async-start(s8[5767168]{0:T(1024)(128)(4,1)} %bitcast.182), calls=%async_computation.2 | async-start | bytes 3145728
  513.1 12.3 %copy-start.10 = (bf16[1024,1408]{1,0:T(8,128)(2,1)}, bf16[1024,1408]{1,0:T(8,128)(2,1)S(1)}, u32[]{:S(2)}) copy-start(bf16[1024,1408]{1,0:T(8,128)(2,1)S(1)} %get-tuple-element.207.refs_4_) | copy-start | bytes 8650756
  629.7 120.7 %copy-start.13 = (bf16[2048,128]{1,0:T(8,128)(2,1)S(1)}, bf16[2048,128]{1,0:T(8,128)(2,1)}, u32[]{:S(2)}) copy-start(bf16[2048,128]{1,0:T(8,128)(2,1)} %copy.270) | copy-start | bytes 1572868
  629.7 121.9 %copy-start.16 = (bf16[2048,16]{0,1:T(8,128)(2,1)S(1)}, bf16[2048,16]{0,1:T(8,128)(2,1)}, u32[]{:S(2)}) copy-start(bf16[2048,16]{0,1:T(8,128)(2,1)} %copy-done.15) | copy-start | bytes 196612
  757.6 1.8 copy-start.22
  992.3 2.3 copy-start.12
  994.5 1.0 copy-start.6
  994.6 1.1 copy-start.7
  1000.9 1.9 copy-start.21
  1001.7 3.1 copy-start.20
  1003.5 3.4 copy-start.19
  1005.4 3.4 slice-start.2
  1006.9 3.7 slice-start.4
  1008.8 2.7 slice-start.3
  1014.7 4.9 copy-start.9
  1019.6 3.0 copy-start.8
  1022.6 4.7 copy-start.17
  1022.6 5.6 copy-start.23
Sparse Core Ops, SparseCore 0:
  91.4 44.6 all-gather.1

commit v9 on v8

--- a/solution.py
+++ b/solution.py
@@ -26,26 +26,6 @@
         * lax.rsqrt(jnp.mean(values * values, axis=-1, keepdims=True) + norm_eps)
         * scale_gain
     )
-
-
-def rotate(values, cos_table, sine_table):
-    half_dim = values.shape[-1] // 2
-    first_half = values[..., :half_dim]
-    second_half = values[..., half_dim:]
-    return jnp.concatenate(
-        [
-            first_half * cos_table - second_half * sine_table,
-            second_half * cos_table + first_half * sine_table,
-        ],
-        axis=-1,
-    )
-
-
-def rope_tables(positions):
-    half_dim = DR // 2
-    inv_freq = 10000.0 ** (-(jnp.arange(half_dim).astype(F32) * 2.0) / DR)
-    angles = positions.astype(F32)[:, None] * inv_freq[None, :]
-    return (jnp.cos(angles), jnp.sin(angles))
 
 
 def swiglu(gate_in, up_in):
@@ -536,7 +516,7 @@
             wait_recv(region, self.sib_recv.at[i], self.sibling)
 
 
-def forward_exchange(attend, w_out, tok, gain, experts, shared, n_dp, n_ex, inner, collective_id):
+def forward_exchange(attend, w_out, tok, gain, cot, experts, shared, n_dp, n_ex, inner, collective_id):
     chips = n_ex // 2
     rows, width = tok.shape
     count = len(experts)
@@ -544,22 +524,25 @@
     parts = DV // r
     hp = n_dp // parts
     seq = n_ex * rows
+    rl = KVR // (n_dp * n_ex)
+    we_cols = rl * hp * (DH + DV) // r
+    wq_cols = hp * (DH + DR)
 
     def kernel(*refs):
-        att_in, refs = refs[:9], refs[9:]
-        wo_in, tok_ref, gain_ref = refs[:3]
-        e_in, s_in = refs[3 : 3 + count], refs[3 + count : 6 + count]
-        refs = refs[6 + count :]
+        att_in, refs = refs[:8], refs[8:]
+        wo_in, tok_ref, gain_ref, cot_in = refs[:4]
+        e_in, s_in = refs[4 : 4 + count], refs[4 + count : 7 + count]
+        refs = refs[7 + count :]
         att_out, refs = refs[:8], refs[8:]
-        wo_out, res_ref, xcol_ref = refs[:3]
-        w_out, s_out = refs[3 : 3 + count], refs[3 + count : 6 + count]
-        refs = refs[6 + count :]
+        wq_ref, we_ref, wo_out, res_ref, xcol_ref, cot_out = refs[:6]
+        w_out, s_out = refs[6 : 6 + count], refs[6 + count : 9 + count]
+        refs = refs[9 + count :]
         x_ref, from_sib, out_buf, from_far, xbuf = refs[:5]
         (
             near_s, near_r, far_s, far_r, x_s, x_r,
-            sh_s, sh_r, sp_s, sp_r, sf_s, sf_r, wo_s, wo_r, local,
-        ) = refs[5:20]
-        refs = refs[20:]
+            sh_s, sh_r, sp_s, sp_r, sf_s, sf_r, wo_s, wo_r, co_s, co_r, local,
+        ) = refs[5:22]
+        refs = refs[22:]
         z, e, c, k, sibling, same_core, column = places(n_dp, n_ex)
         group = column_group(z, e, inner)
         part = lax.rem(e, parts)
@@ -627,7 +610,22 @@
         for copy in own:
             copy.start()
         matrices[0].begin()
-        attend_forward(*att_in, *att_out)
+        cot_copies = []
+        for i in range(1, inner):
+            copy = remote(cot_in, cot_out.at[my_l], co_s.at[i], co_r.at[i], group[i])
+            copy.start()
+            cot_copies.append(copy)
+        copy = pltpu.make_async_copy(cot_in, cot_out.at[my_l], local.at[4])
+        copy.start()
+        cot_copies.append(copy)
+        tok_all, gain_one, wa_ref, wl_ref, gain_lat, cos, sin, keep = att_in
+        wq_ref[...] = wa_ref[:, :, :, :wq_cols].reshape(width, wq_cols)
+        for j in range(r // rl):
+            block = wa_ref[:, :, j * rl : (j + 1) * rl, wq_cols:].reshape(KVR, we_cols)
+            we_ref[:, j * we_cols : (j + 1) * we_cols] = block
+        attend_forward(
+            tok_all, gain_one, wq_ref, wl_ref, gain_lat, we_ref, cos, sin, keep, *att_out
+        )
         wo_arrivals()
         wo = wo_out[...].reshape(hp * DV, width)
 
@@ -696,7 +694,7 @@
                 to_sib.append(copy)
         for matrix in matrices:
             matrix.pass_on()
-        for copy in x_copies + to_sib:
+        for copy in x_copies + cot_copies + to_sib:
             copy.wait()
         x_own.wait()
         for copy in plane + shared_copies + near + far:
@@ -722,14 +720,17 @@
             sds((2, seq, DV), BF),
             sds((2, seq, 128), F32),
             sds((seq, 2 * DV), BF),
+            sds((width, wq_cols), BF),
+            sds((KVR, hp * (DH + DV)), BF),
             sds((hp, parts, r, width), BF),
             sds((rows, width), F32),
+            sds((inner, rows, width), BF),
             sds((inner, rows, width), BF),
         ]
         + [ExpertsIn.out(w, n_dp, n_ex) for w in experts]
         + [sds((n_ex, n_dp, r, ff_s), BF)] * 3,
-        in_specs=[VMEM] * 9 + [ANY] + [VMEM] * 2 + [ANY] * (3 + count),
-        out_specs=[VMEM] * 10 + [ANY] * (4 + count),
+        in_specs=[VMEM] * 8 + [ANY] + [VMEM] * 2 + [ANY] * (4 + count),
+        out_specs=[VMEM] * 12 + [ANY] * (5 + count),
         scratch_shapes=[pltpu.VMEM((n_ex, rows, width), BF)]
         + [pltpu.VMEM((chips, rows, width), BF)] * 3
         + [pltpu.VMEM((rows, width), BF)]
@@ -737,11 +738,13 @@
         + [dma((inner,))] * 2
         + [dma((3, n_dp))] * 2
         + [dma((3, chips))] * 4
-        + [dma((n_dp,)), dma((hp, parts)), dma((4,))]
+        + [dma((n_dp,)), dma((hp, parts))]
+        + [dma((inner,))] * 2
+        + [dma((5,))]
         + scratch,
         compiler_params=params(collective_id),
-    )(*attend, w_out, tok, gain, *experts, *shared)
-    return outs[:8], outs[8], outs[9], outs[10], outs[11 : 11 + count], outs[11 + count :]
+    )(*attend, w_out, tok, gain, cot, *experts, *shared)
+    return outs[:8], outs[8:11], outs[11], outs[12], outs[13], outs[14 : 14 + count], outs[14 + count :]
 
 
 def silu_parts(a):
@@ -749,38 +752,58 @@
     return a * sig, sig * (1.0 + a * (1.0 - sig))
 
 
-def dispatch(blocks, x, cot, shared, weight, n_dp, n_ex, inner, collective_id):
+def dispatch(hot, x, cot, shared, weights, n_dp, n_ex, inner, collective_id):
     chips = n_ex // 2
     rows, width = x.shape
     ff = shared[0].shape[1]
     tile = 256
 
-    def kernel(
-        b_ref, x_hbm, c_hbm, g_hbm, u_hbm, d_hbm, w_ref,
-        o_ref, w_out, out_ref, dx_ref, gg_ref, gu_ref, gd_ref,
-        x_v, c_v, g_v, u_v, d_v, hid, ga, gb, send, recv, loads, *rest,
-    ):
+    per_far = hot.shape[0] // chips
+    count = len(weights)
+
+    def kernel(hot_ref, x_hbm, c_hbm, g_hbm, u_hbm, d_hbm, *refs):
+        w_in, refs = refs[:count], refs[count:]
+        o_ref, go_ref, w_out, refs = refs[0], refs[1], refs[2 : 2 + count], refs[2 + count :]
+        out_ref, dx_ref, gg_ref, gu_ref, gd_ref = refs[:5]
+        hot_v, x_v, c_v, g_v, u_v, d_v, hid, ga, gb, b_v, send, recv, loads, keep = refs[5:19]
+        rest = refs[19:]
         z, e, c, k, sibling, same_core, column = places(n_dp, n_ex)
-        greet(same_core + [sibling] + column + [(device[0], sibling[1]) for device in column])
-        matrix = ExpertsIn(w_ref, w_out, rest, n_dp, n_ex, inner)
-        copies = []
-        for i in range(1, chips):
-            copy = remote(b_ref.at[i], o_ref.at[i], send.at[i], recv.at[i], same_core[i - 1])
-            copy.start()
-            copies.append(copy)
-        copy = pltpu.make_async_copy(b_ref.at[0], o_ref.at[0], loads.at[0])
-        copy.start()
-        copies.append(copy)
-        matrix.begin()
         moves = [
-            pltpu.make_async_copy(src, dst, loads.at[1 + j])
+            pltpu.make_async_copy(src, dst, loads.at[j])
             for j, (src, dst) in enumerate(
-                [(x_hbm, x_v), (g_hbm, g_v), (u_hbm, u_v), (c_hbm, c_v), (d_hbm, d_v)]
+                [
+                    (hot_ref, hot_v), (x_hbm, x_v), (c_hbm, c_v),
+                    (g_hbm, g_v), (u_hbm, u_v), (d_hbm, d_v),
+                ]
             )
         ]
         for copy in moves:
             copy.start()
-        for copy in moves:
+        greet(same_core + [sibling] + column + [(device[0], sibling[1]) for device in column])
+        matrices = [
+            ExpertsIn(w_in[m], w_out[m], rest[4 * m : 4 * m + 4], n_dp, n_ex, inner)
+            for m in range(count)
+        ]
+        for matrix in matrices:
+            matrix.begin()
+        copies = []
+        for j, (source, target) in enumerate(((x_v, o_ref), (c_v, go_ref))):
+            if not j:
+                moves[0].wait()
+            moves[1 + j].wait()
+            for i in list(range(1, chips)) + [0]:
+                block = mm(hot_v[i * per_far : (i + 1) * per_far, :], source[...])
+                b_v[j, i] = block.astype(BF)
+                if i:
+                    copy = remote(
+                        b_v.at[j, i], target.at[i], send.at[j, i], recv.at[j, i],
+                        same_core[i - 1],
+                    )
+                else:
+                    copy = pltpu.make_async_copy(b_v.at[j, 0], target.at[0], keep.at[j])
+                copy.start()
+                copies.append(copy)
+        for copy in moves[3:]:
             copy.wait()
 
         def rows_of(i, carry):
@@ -809,29 +832,37 @@
             return carry
 
         lax.fori_loop(0, width // tile, columns_of, 0)
-        matrix.pass_on()
+        for matrix in matrices:
+            matrix.pass_on()
         for copy in copies:
             copy.wait()
-        matrix.end()
+        for matrix in matrices:
+            matrix.end()
 
     dma = pltpu.SemaphoreType.DMA
     sds = jax.ShapeDtypeStruct
     vmem = pltpu.VMEM
+    scratch = []
+    for _ in weights:
+        scratch += ExpertsIn.scratch(n_dp)
     outs = pl.pallas_call(
         kernel,
-        out_shape=[sds(blocks.shape, BF), ExpertsIn.out(weight, n_dp, n_ex)]
+        out_shape=[sds((chips, per_far, width), BF)] * 2
+        + [ExpertsIn.out(weight, n_dp, n_ex) for weight in weights]
         + [sds((rows, width), F32)] * 2
         + [sds((width, ff), BF)] * 3,
-        in_specs=[ANY] * 7,
-        out_specs=[ANY] * 2 + [VMEM] * 5,
-        scratch_shapes=[vmem((rows, width), BF)] * 2
+        in_specs=[ANY] * (6 + count),
+        out_specs=[ANY] * (2 + count) + [VMEM] * 5,
+        scratch_shapes=[vmem(hot.shape, BF)]
+        + [vmem((rows, width), BF)] * 2
         + [vmem((width, ff), BF)] * 3
         + [vmem((rows, ff), BF)] * 3
-        + [dma((chips,)), dma((chips,)), dma((6,))]
-        + ExpertsIn.scratch(n_dp),
+        + [vmem((2, chips, per_far, width), BF)]
+        + [dma((2, chips)), dma((2, chips)), dma((6,)), dma((2,))]
+        + scratch,
         compiler_params=params(collective_id),
-    )(blocks, x, cot, *shared, weight)
-    return outs[0], outs[1], outs[2], outs[3], outs[4:]
+    )(hot, x, cot, *shared, *weights)
+    return outs[:2], outs[2 : 2 + count], outs[2 + count], outs[3 + count], outs[4 + count :]
 
 
 def experts_back(values, weights, dots, n_dp, n_ex, inner, collective_id):
@@ -971,14 +1002,15 @@
     def scratch(total, n_dp, inner):
         n_ex, _, r, ff = total.shape
         dma = pltpu.SemaphoreType.DMA
+        hh = n_ex // 2
         return [
-            pltpu.VMEM((n_ex // 2, n_dp, r, ff), BF),
-            pltpu.VMEM((n_ex // 2, n_dp, r, ff), BF),
-            dma((n_dp,)),
-            dma((n_dp,)),
-            dma((n_dp,)),
-            dma((n_dp,)),
-            dma((n_dp // inner, 2, 2)),
+            pltpu.VMEM((hh, n_dp, r, ff), BF),
+            pltpu.VMEM((hh, n_dp, r, ff), BF),
+            dma((hh,)),
+            dma((hh,)),
+            dma((hh,)),
+            dma((hh, n_dp)),
+            dma((n_dp // inner, 2, 2, hh)),
         ]
 
     @staticmethod
@@ -992,86 +1024,76 @@
         self.z, self.e, self.c, self.k, self.sibling, _, _ = places(n_dp, n_ex)
         self.hh = n_ex // 2
 
-    def near(self, i):
-        d = lax.rem(self.z + i, self.n_dp)
+    def near(self, j):
         return remote(
-            self.total.at[pl.ds((1 - self.k) * self.hh, self.hh), d],
-            self.sib.at[:, d], self.near_s.at[i], self.near_r.at[i], self.sibling,
+            self.total.at[(1 - self.k) * self.hh + j], self.sib.at[j],
+            self.near_s.at[j], self.near_r.at[j], self.sibling,
         )
 
-    def loads(self, i):
-        d = lax.rem(self.z + i, self.n_dp)
+    def loads(self, j):
         return pltpu.make_async_copy(
-            self.total.at[pl.ds(self.k * self.hh, self.hh), d], self.own.at[:, d], self.load.at[i]
+            self.total.at[self.k * self.hh + j], self.own.at[j], self.load.at[j]
         )
 
-    def order(self):
-        return list(range(1, self.n_dp)) + [0]
-
     def begin(self):
-        for i in self.order():
-            self.near(i).start()
-            self.loads(i).start()
-
-    def route(self, i):
+        for j in range(self.hh):
+            self.near(j).start()
+            self.loads(j).start()
+
+    def route(self, j, i):
         d = lax.rem(self.z + i, self.n_dp)
         expert = lax.rem(self.z, self.inner)
-        dst = self.out.at[
-            self.z // self.inner, lax.rem(expert, 2), pl.ds(self.k * self.hh, self.hh)
-        ]
-        sem = self.recv.at[self.z // self.inner, lax.rem(expert, 2), self.k]
-        return self.own.at[:, d], dst, sem, d, expert // 2
-
-    def stay(self):
-        src, dst, sem, _, _ = self.route(0)
+        o = self.z // self.inner
+        dst = self.out.at[o, lax.rem(expert, 2), self.k * self.hh + j]
+        sem = self.recv.at[o, lax.rem(expert, 2), self.k, j]
+        return self.own.at[j, d], dst, sem, (d, 2 * self.c + expert // 2)
+
+    def stay(self, j):
+        src, dst, sem, _ = self.route(j, 0)
         return pltpu.make_async_copy(src, dst, sem)
 
-    def go(self, i):
-        src, dst, sem, d, core = self.route(i)
-        return remote(src, dst, self.send.at[i], sem, (d, 2 * self.c + core))
+    def go(self, j, i):
+        src, dst, sem, device = self.route(j, i)
+        return remote(src, dst, self.send.at[j, i], sem, device)
 
     def here(self):
         return lax.rem(self.z, self.inner) // 2 == self.k
 
     def pass_on(self):
-        for i in self.order():
-            d = lax.rem(self.z + i, self.n_dp)
-            self.near(i).wait_recv()
-            self.loads(i).wait()
-            for j in range(self.hh):
+        for j in range(self.hh):
+            self.near(j).wait_recv()
+            self.loads(j).wait()
+            for d in range(self.n_dp):
                 self.own[j, d] = (
                     self.own[j, d].astype(F32) + self.sib[j, d].astype(F32)
                 ).astype(BF)
-            if i:
-                self.go(i).start()
-            else:
-                pl.when(self.here())(lambda: self.stay().start())
-                pl.when(jnp.logical_not(self.here()))(lambda: self.go(0).start())
+            for i in range(1, self.n_dp):
+                self.go(j, i).start()
+            pl.when(self.here())(lambda j=j: self.stay(j).start())
+            pl.when(jnp.logical_not(self.here()))(lambda j=j: self.go(j, 0).start())
 
     def end(self):
-        for i in self.order():
-            self.near(i).wait_send()
-            if i:
-                self.go(i).wait_send()
-            else:
-                pl.when(jnp.logical_not(self.here()))(lambda: self.go(0).wait_send())
+        for j in range(self.hh):
+            self.near(j).wait_send()
+            for i in range(1, self.n_dp):
+                self.go(j, i).wait_send()
+            pl.when(jnp.logical_not(self.here()))(lambda j=j: self.go(j, 0).wait_send())
         for o in range(self.n_dp // self.inner):
-            for j in range(2):
+            for i in range(2):
                 for h in range(2):
-                    region = self.out.at[o, j, pl.ds(h * self.hh, self.hh)]
-                    source = o * self.inner + 2 * self.k + j
+                    source = o * self.inner + 2 * self.k + i
                     here = jnp.logical_and(source == self.z, self.k == h)
-
-                    @pl.when(here)
-                    def _(region=region, o=o, j=j, h=h):
-                        d = self.z
-                        pltpu.make_async_copy(
-                            self.own.at[:, d], region, self.recv.at[o, j, h]
-                        ).wait()
-
-                    @pl.when(jnp.logical_not(here))
-                    def _(region=region, o=o, j=j, h=h):
-                        wait_recv(region, self.recv.at[o, j, h], self.sibling)
+                    for j in range(self.hh):
+                        region = self.out.at[o, i, h * self.hh + j]
+                        sem = self.recv.at[o, i, h, j]
+
+                        @pl.when(here)
+                        def _(region=region, sem=sem, j=j):
+                            pltpu.make_async_copy(self.own.at[j, self.z], region, sem).wait()
+
+                        @pl.when(jnp.logical_not(here))
+                        def _(region=region, sem=sem):
+                            wait_recv(region, sem, self.sibling)
 
 
 def rms_back(x, gain, grad):
@@ -1551,9 +1573,6 @@
     )
     cot_owner = to_owner_order(cotangent)
     tok_all, wa_all, pk_all = first_exchange(tokens, wa_send, pack, n_dp, n_ex, 1)
-    wq = wa_all[..., :head_cols].reshape(width, head_cols)
-    wexp = wa_all[..., head_cols:].reshape(n_dp * n_ex, r // rl, rl, we_cols)
-    wexp = wexp.transpose(0, 2, 1, 3).reshape(KVR, kv_cols)
     pk_flat = pk_all.reshape(width, pack_cols)
     w_lat = pk_flat[:, :lat]
     gain_one = pk_flat[:, lat + n_experts].astype(F32)
@@ -1562,9 +1581,6 @@
     gain_lat = (
         pk_all[..., lat + n_experts + 2].reshape(n_dp * n_ex, r)[:, :rl].reshape(KVR).astype(F32)
     )
-    col_groups = [[o * inner + i for i in range(inner)] for o in range(n_dp // inner)]
-    cot_send, _ = lax.optimization_barrier((cot_owner, pk_all))
-    cot_col = lax.all_gather(cot_send, "dp", axis=0, tiled=True, axis_index_groups=col_groups)
     slots_all = n_experts * capacity
     slot_col = pick(pk_all[..., small_cols : small_cols + slot_cols], e, 1)
     slot_col = lax.dynamic_slice_in_dim(slot_col, z - my_local, inner, 0).astype(jnp.int32)
@@ -1588,24 +1604,18 @@
     hot = sum((wanted[:, None] == slot_ids[None, :, j]).astype(BF) for j in range(top_k))
     hot_t = sum((slot_ids[:, j][:, None] == wanted[None, :]).astype(BF) for j in range(top_k))
 
-    def through(values, way):
-        cut = values.reshape(chips, per_far, -1)
-        got = [cut[0]]
-        for m in range(1, chips):
-            perm = [(i, (i + 2 * m * way) % n_ex) for i in range(n_ex)]
-            got.append(lax.ppermute(cut[m], "expert", perm))
-        return jnp.concatenate(got, axis=0)
-
     positions = jnp.arange(seq)
-    cos_table, sine_table = rope_tables(positions)
-    cos_wide, sine_wide = jnp.tile(cos_table, (1, 4)), jnp.tile(sine_table, (1, 4))
+    lane = jnp.arange(2 * DR) % (DR // 2)
+    angles = positions.astype(F32)[:, None] * (10000.0 ** (-(lane.astype(F32) * 2.0) / DR))[None, :]
+    cos_wide, sine_wide = jnp.cos(angles), jnp.sin(angles)
     keep = (positions < lengths[0]).astype(F32)[None]
-    attend_out, wo_rows, residual, x_col, (wg, wu), (sgate, sup, sdown) = forward_exchange(
-        [tok_all, gain_one[None], wq, pk_flat, gain_lat[None], wexp, cos_wide, sine_wide, keep],
+    attend_out, (wq, wexp, wo_rows), residual, x_col, cot_col, (wg,), shared_w = forward_exchange(
+        [tok_all, gain_one[None], wa_all, pk_flat, gain_lat[None], cos_wide, sine_wide, keep],
         to_owner_order(w_out),
         to_owner_order(tokens),
         gain_two[None],
-        [w.reshape(-1, n_ex, r, ff_e) for w in (expert_gate, expert_up)],
+        cot_owner,
+        [expert_gate.reshape(-1, n_ex, r, ff_e)],
         [w.reshape(r, inner, ff_s).transpose(1, 0, 2) for w in (shared_gate, shared_up, shared_down)],
         n_dp,
         n_ex,
@@ -1614,23 +1624,23 @@
     )
     hidden_one, latent_raw, latent_low, qcat, kcat, value, lse, attended = attend_out
     wo_rows = wo_rows.reshape(hp * DV, width)
-    sgate, sup, sdown = (w.reshape(width, ff_s) for w in (sgate, sup, sdown))
+    cot_col = cot_col.reshape(inner * rows, width)
     hidden_two = pick(x_col, my_local)
     x_col = x_col.reshape(inner * rows, width)
 
-    x_in, wd, shared_out, shared_dx, shared_grads = dispatch(
-        mm(hot, x_col).astype(BF).reshape(chips, per_far, width),
+    (x_in, grad_in), (wu, wd), shared_out, shared_dx, shared_grads = dispatch(
+        hot,
         x_col,
         cot_col,
-        (sgate, sup, sdown),
-        expert_down.reshape(-1, n_ex, r, ff_e),
+        [w.reshape(width, ff_s) for w in shared_w],
+        [w.reshape(-1, n_ex, r, ff_e) for w in (expert_up, expert_down)],
         n_dp,
         n_ex,
         inner,
         8,
     )
     x_in = x_in.reshape(n_slots, width)
-    grad_in = through(mm(hot, cot_col).astype(BF), 1)
+    grad_in = grad_in.reshape(n_slots, width)
     wg, wu, wd = (w.reshape(width, ff_e) for w in (wg, wu, wd))
 
     def probs_of(logits):

time: 1050 us -> 1020 us (0.971)
  local copies, waits for them, and re-layouts: 83.3 us -> 55.9 us
  Pallas kernels: 834 us -> 857 us
  between operations: 16.2 us -> 2.94 us
    pallas_call x1, Pallas kernels: 95.9 us -> 138 us  [dispatch(): pl.pallas_call(kernel, out_shape=[sds((chips, per_far, width), BF)] * 2 +...]
    pallas_call x1, Pallas kernels: 233 us -> 214 us  [forward_exchange(): pl.pallas_call(kernel, out_shape=[sds((seq, width), BF), sds((seq, attend...]
    dot_general x8 -> x6, matrix products: 49.6 us -> 42.4 us  [mm(): return jnp.dot(left, right, preferred_element_type=F32)]
  transfers between devices with their start and end apart: 4 -> 0, of which waited for: 0 -> 0; matrix products, arithmetic and copies ran while one was open for 8% -> 0% of each run, Pallas kernels for 32% -> 0%
where the time goes in v9:
time: 1020 us; the launch traced here: 1010 us
  Pallas kernels  857 us (84%)
  matrix products  56.1 us (6%)
  local copies, waits for them, and re-layouts  55.9 us (5%)
  other arithmetic  37 us (4%)
    pallas_call x1, Pallas kernels, backward_exchange(): pl.pallas_call(kernel, out_shape=[sds((rows, width), F32), sds((8, width)...  226 us
    pallas_call x1, Pallas kernels, forward_exchange(): pl.pallas_call(kernel, out_shape=[sds((seq, width), BF), sds((seq, attend...  214 us
    pallas_call x1, Pallas kernels, dispatch(): pl.pallas_call(kernel, out_shape=[sds((chips, per_far, width), BF)] * 2 +...  138 us
    pallas_call x1, Pallas kernels, column_sum(): pl.pallas_call(kernel, out_shape=[jax.ShapeDtypeStruct(shape, F32)] + [ja...  121 us
    pallas_call x1, Pallas kernels, experts_back(): pl.pallas_call(kernel, out_shape=[sds((chips, per_far, width), BF), sds(d...  88 us
    pallas_call x1, Pallas kernels, first_exchange(): pl.pallas_call(kernel, out_shape=[jax.ShapeDtypeStruct((n_ex,) + tok.shap...  71.3 us
    dot_general x6, matrix products, mm(): return jnp.dot(left, right, preferred_element_type=F32)  42.4 us

profile of v9, /device:TPU:11, one launch (start us, length us, event | category | flops | bytes accessed | tf_op | source)
XLA Modules:
  0.0 1008.9 jit_solution(15294643026040983161)
XLA Ops:
  10.0 1.6 concatenate.33.pk_ref
  13.3 1.4 reshape.707
  17.7 1.0 copy.240.refs_11_
  22.3 1.2 reshape.701.refs_8_
  23.8 1.0 copy.239.refs_9_
  24.8 3.2 multiply_sine_fusion
  28.0 71.3 %shard_map.342 = (bf16[8,128,2048]{2,1,0:T(8,128)(2,1)}, bf16[4,8,64,512]{3,2,1,0:T(8,128)(2,1)}, bf16[4,8,64,640]{3,2,1,0:T(8,128)(2,1)}) custom-call(bf16[128,2048]{1,0:T(8,128)(2,1)} %refs_16_.1, bf16[8,64,512]{2,1,0:T(8,128)(2,1)} %pad_maximum_fusion.1.wa_ref, bf16[64,640]{1,0:T(8,128)(2,1)} %concatenate.33.pk_ref), custom_call_target="tpu_custom_call" | custom-call | tf_op jit(solution)/shard_map/pallas_call | solution.py:414
  99.3 2.0 convert_reduce_fusion.5
  101.3 1.6 slice_reduce_fusion
  103.6 1.6 convert_reduce_fusion.4
  105.9 1.2 slice_bitcast_fusion.1
  107.6 1.3 slice.127
  110.5 2.3 fusion.12.hot_ref
  112.8 1.4 fusion.7
  114.2 213.7 %shard_map.343 = (bf16[1024,2048]{1,0:T(8,128)(2,1)}, f32[1024,640]{1,0:T(8,128)}, bf16[1024,512]{1,0:T(8,128)(2,1)}, bf16[2,1024,256]{2,1,0:T(8,128)(2,1)}, bf1...) custom-call(bf16[8,128,2048]{2,1,0:T(8,128)(2,1)} %get-tuple-element, ...), custom_call_target="tpu_custom_call" | custom-call | tf_op jit(solution)/shard_map/pallas_call | solution.py:712
  327.9 1.4 multiply_reduce_fusion.3
  329.3 2.3 fusion.47
  331.9 1.0 select_reduce_fusion.3
  332.9 1.3 slice_multiply_fusion.3
  334.2 1.7 constant_dynamic-slice_fusion.2.refs_15_
  335.9 1.1 dynamic-slice_bitcast_fusion
  337.3 137.7 %shard_map.344 = (bf16[4,256,2048]{2,1,0:T(8,128)(2,1)}, bf16[4,256,2048]{2,1,0:T(8,128)(2,1)}, bf16[8,4,64,1408]{3,2,1,0:T(8,128)(2,1)}, bf16[8,4,64,1408]{3,2,...) custom-call(bf16[1024,512]{1,0:T(8,128)(2,1)} %fusion.12.hot_ref, ...), custom_call_target="tpu_custom_call" | custom-call | tf_op jit(solution)/shard_map/pallas_call | solution.py:848
  475.0 3.5 fusion.46
  478.7 10.4 %fusion.48 = f32[1024,1408]{1,0:T(8,128)} fusion(bf16[1024,2048]{1,0:T(8,128)(2,1)S(1)} %bitcast.162, bf16[2048,1408]{1,0:T(8,128)(2,1)} %bitcast.166), kind=kOutput, calls=%fused_computation.158 | convolution fusion | flops 5905580032 | bytes 15728640 | tf_op jit(solution)/shard_map/dot_general | solution.py:36
  489.1 12.4 %multiply_convert_fusion = (bf16[1024,1408]{1,0:T(8,128)(2,1)S(1)}, bf16[1024,1408]{1,0:T(8,128)(2,1)}, bf16[1024,1408]{1,0:T(8,128)(2,1)}) fusion(f32[1024,1408]{1,0:T(8,128)} %fusion.48, bf16[1024,2048]{1,0:T(8,128)(2,1)S(1)} %bitcast.163, bf16[2048,1408]{1,0:T(8,128)(2,1)S(1)} %bitcast.171), kind=kOutput, calls=%fused_computation.8 | convolution fusion | flops 5917114368 | bytes 24379392 | tf_op jit(solution)/shard_map/dot_general | solution.py:36
  501.5 10.2 %fusion.1 = (bf16[1024]{0:T(1024)(128)(2,1)S(1)}, bf16[1024,2048]{1,0:T(8,128)(2,1)}, bf16[1024,2048]{1,0:T(8,128)(2,1)}) fusion(bf16[4,256,2048]{2,1,0:T(8,128)(2,1)S(1)} %copy-done.25, f32[1024]{0:T(1024)S(1)} %select_reduce_fusion.4, bf16[1024,1408]{1,0:T(8,128)(2,1)S(1)} %get-tuple-element.213.refs_4_, bf16[2048,1408]{1,0:T(8,128)(2,1)S(1)} %bitcast.175), kind=kOutput, calls=%fused_computation.7 | convolution fusion | flops 5920259072 | bytes 21239808 | tf_op jit(solution)/shard_map/dot_general | solution.py:44
  512.6 88.0 %shard_map.345 = (bf16[4,256,2048]{2,1,0:T(8,128)(2,1)}, bf16[4,256,128]{2,1,0:T(8,128)(2,1)}, bf16[1,2,8,64,1408]{4,3,2,1,0:T(8,128)(2,1)}, bf16[8,4,64,1408]{3,2,1,0:T(8,128)(2,1)}, bf16[8,4,64,1408]{3,2,1,0:T(8,128)(2,1)}) custom-call(bf16[1024,2048]{1,0:T(8,128)(2,1)} %bitcast.161, bf16[1024,2048]{1,0:T(8,128)(2,1)} %get-tuple-element.217.refs_1_, ...), custom_call_target="tpu_custom_call" | custom-call | tf_op jit(solution)/shard_map/pallas_call | solution.py:972
  600.6 6.6 add_convert_fusion.1
  607.3 1.6 multiply_reduce_fusion
  609.4 2.9 concatenate.35.x_ref
  612.2 120.6 %shard_map.346 = (f32[128,2176]{1,0:T(8,128)}, bf16[4,64,704]{2,1,0:T(8,128)(2,1)}, bf16[4,64,704]{2,1,0:T(8,128)(2,1)}, bf16[4,64,704]{2,1,0:T(8,128)(2,1)}, bf...) custom-call(bf16[4,128,2176]{2,1,0:T(8,128)(2,1)} %concatenate.35.x_ref, ...), custom_call_target="tpu_custom_call" | custom-call | tf_op jit(solution)/shard_map/pallas_call | solution.py:315
  732.9 7.2 add_convert_fusion
  741.1 1.2 convolution_convert_fusion.1
  742.3 2.4 multiply_reduce_fusion.1
  744.7 1.2 fusion.42
  746.2 1.0 pad.10.refs_20_
  747.7 1.3 copy.254.refs_19_
  749.0 225.7 %shard_map.347 = (f32[128,2048]{1,0:T(8,128)}, f32[8,2048]{1,0:T(8,128)}, f32[64,640]{1,0:T(8,128)}, bf16[4,8,64,512]{3,2,1,0:T(8,128)(2,1)}, bf16[4,8,64,512]{3...) custom-call(bf16[128,2048]{1,0:T(8,128)(2,1)} %get-tuple-element.211, ...), custom_call_target="tpu_custom_call" | custom-call | tf_op jit(solution)/shard_map/pallas_call | solution.py:1458
  974.7 2.1 convert_reduce_fusion.1
  977.3 1.0 copy.269
  982.8 1.2 reshape.739
  984.5 1.4 reshape.759
  986.5 1.4 reshape.761
  988.5 1.4 reshape.763
  994.7 1.3 gather.29
  996.0 4.9 convert.49
  1000.9 2.9 convert.48
  1003.9 2.9 convert.50
  (194 shorter events, 37.3 us)
Async XLA Ops:
  0.6 15.3 %copy-start.17 = (bf16[64,2816]{1,0:T(8,128)(2,1)S(1)}, bf16[64,2816]{1,0:T(8,128)(2,1)}, u32[]{:S(2)}) copy-start(bf16[64,2816]{1,0:T(8,128)(2,1)} %param.38) | copy-start | bytes 1081348
  0.7 14.8 %copy-start.16 = (bf16[64,2816]{1,0:T(8,128)(2,1)S(1)}, bf16[64,2816]{1,0:T(8,128)(2,1)}, u32[]{:S(2)}) copy-start(bf16[64,2816]{1,0:T(8,128)(2,1)} %param.37) | copy-start | bytes 1081348
  12.5 4.9 copy-start.11
  15.9 2.8 copy-start.12
  19.3 2.2 copy-start.18
  20.1 3.3 copy-start.2
  475.0 3.7 copy-start
  475.0 14.1 %slice-start = ((s8[5767168]{0:T(1024)(128)(4,1)}), s8[4194304]{0:T(1024)(128)(4,1)S(1)}, s32[]{:S(2)}) async-start(s8[5767168]{0:T(1024)(128)(4,1)} %bitcast.169), calls=%async_computation | async-start | bytes 8388608
  478.7 10.4 %slice-start.1 = ((s8[5767168]{0:T(1024)(128)(4,1)}), s8[1572864]{0:T(1024)(128)(4,1)S(1)}, s32[]{:S(2)}) async-start(s8[5767168]{0:T(1024)(128)(4,1)} %bitcast.169), calls=%async_computation.1 | async-start | bytes 3145728
  478.7 22.8 %slice-start.2 = ((s8[5767168]{0:T(1024)(128)(4,1)}), s8[4194304]{0:T(1024)(128)(4,1)S(1)}, s32[]{:S(2)}) async-start(s8[5767168]{0:T(1024)(128)(4,1)} %bitcast.173), calls=%async_computation.2 | async-start | bytes 8388608
  489.1 12.4 %slice-start.3 = ((s8[5767168]{0:T(1024)(128)(4,1)}), s8[1572864]{0:T(1024)(128)(4,1)S(1)}, s32[]{:S(2)}) async-start(s8[5767168]{0:T(1024)(128)(4,1)} %bitcast.173), calls=%async_computation.3 | async-start | bytes 3145728
  489.1 12.4 %copy-start.25 = (bf16[4,256,2048]{2,1,0:T(8,128)(2,1)S(1)}, bf16[4,256,2048]{2,1,0:T(8,128)(2,1)}, u32[]{:S(2)}) copy-start(bf16[4,256,2048]{2,1,0:T(8,128)(2,1)} %get-tuple-element.77) | copy-start | bytes 12582916
  501.5 10.2 %copy-start.6 = (bf16[1024,1408]{1,0:T(8,128)(2,1)}, bf16[1024,1408]{1,0:T(8,128)(2,1)S(1)}, u32[]{:S(2)}) copy-start(bf16[1024,1408]{1,0:T(8,128)(2,1)S(1)} %get-tuple-element.213.refs_4_) | copy-start | bytes 8650756
  600.6 6.6 copy-start.19
  612.2 120.6 %copy-start.20 = (bf16[512,256]{1,0:T(8,128)(2,1)S(1)}, bf16[512,256]{1,0:T(8,128)(2,1)}, u32[]{:S(2)}) copy-start(bf16[512,256]{1,0:T(8,128)(2,1)} %get-tuple-element.218) | copy-start | bytes 786436
  612.2 120.6 %copy-start.21 = (bf16[512,256]{1,0:T(8,128)(2,1)S(1)}, bf16[512,256]{1,0:T(8,128)(2,1)}, u32[]{:S(2)}) copy-start(bf16[512,256]{1,0:T(8,128)(2,1)} %get-tuple-element.219) | copy-start | bytes 786436
  612.2 120.6 %copy-start.22 = (bf16[512,256]{1,0:T(8,128)(2,1)S(1)}, bf16[512,256]{1,0:T(8,128)(2,1)}, u32[]{:S(2)}) copy-start(bf16[512,256]{1,0:T(8,128)(2,1)} %get-tuple-element.220) | copy-start | bytes 786436
  612.2 120.6 %copy-start.23 = (bf16[512,256]{1,0:T(8,128)(2,1)S(1)}, bf16[512,256]{1,0:T(8,128)(2,1)}, u32[]{:S(2)}) copy-start(bf16[512,256]{1,0:T(8,128)(2,1)} %get-tuple-element.221) | copy-start | bytes 786436
  732.9 7.2 copy-start.10
  732.9 9.4 copy-start.1
  740.1 4.6 copy-start.3
  976.8 4.2 copy-start.24
  976.9 5.0 copy-start.8
  982.0 1.9 copy-start.15
  982.8 3.1 copy-start.14
  984.5 3.4 copy-start.13
  986.5 3.4 copy-start.7
  996.0 4.9 copy-start.5
  1000.9 3.0 copy-start.4
  1003.9 2.9 copy-start.9

commit v10 on v9

--- a/solution.py
+++ b/solution.py
@@ -26,10 +26,6 @@
         * lax.rsqrt(jnp.mean(values * values, axis=-1, keepdims=True) + norm_eps)
         * scale_gain
     )
-
-
-def swiglu(gate_in, up_in):
-    return jax.nn.silu(gate_in) * up_in
 
 
 def mm(left, right):
@@ -326,6 +322,64 @@
     return outs[0], outs[1:4], outs[4], outs[5:]
 
 
+class Relay:
+    @staticmethod
+    def scratch(inner):
+        dma = pltpu.SemaphoreType.DMA
+        return [dma((inner,)), dma((inner,)), dma((inner,)), dma]
+
+    def __init__(self, block, out, scratch, n_dp, n_ex, inner):
+        self.block, self.out, self.inner = block, out, inner
+        self.up_s, self.down_s, self.recv, self.local = scratch
+        self.z, self.e, *_ = places(n_dp, n_ex)
+        self.mine = lax.rem(self.z, inner)
+
+    def copy(self, source, src, step):
+        sem = self.up_s if step > 0 else self.down_s
+        return remote(
+            src, self.out.at[source], sem.at[source], self.recv.at[source], (self.z + step, self.e)
+        )
+
+    def keep(self):
+        return pltpu.make_async_copy(self.block, self.out.at[self.mine], self.local)
+
+    def begin(self):
+        pl.when(self.mine < self.inner - 1)(lambda: self.copy(self.mine, self.block, 1).start())
+        pl.when(self.mine > 0)(lambda: self.copy(self.mine, self.block, -1).start())
+        self.keep().start()
+
+    def pass_on(self):
+        for t in range(1, self.inner):
+            for step in (1, -1):
+                source = self.mine - step * t
+                exists = source >= 0 if step > 0 else source < self.inner
+                more = self.mine < self.inner - 1 if step > 0 else self.mine > 0
+
+                @pl.when(exists)
+                def _(source=source, step=step):
+                    self.copy(source, self.out.at[source], step).wait_recv()
+
+                @pl.when(jnp.logical_and(exists, more))
+                def _(source=source, step=step):
+                    self.copy(source, self.out.at[source], step).start()
+
+    def end(self):
+        self.keep().wait()
+        pl.when(self.mine < self.inner - 1)(
+            lambda: self.copy(self.mine, self.block, 1).wait_send()
+        )
+        pl.when(self.mine > 0)(lambda: self.copy(self.mine, self.block, -1).wait_send())
+        for t in range(1, self.inner):
+            for step in (1, -1):
+                source = self.mine - step * t
+                exists = source >= 0 if step > 0 else source < self.inner
+                more = self.mine < self.inner - 1 if step > 0 else self.mine > 0
+
+                @pl.when(jnp.logical_and(exists, more))
+                def _(source=source, step=step):
+                    self.copy(source, self.out.at[source], step).wait_send()
+
+
 def column_group(z, e, inner):
     start = z // inner * inner
     return [(start + lax.rem(z - start + i, inner), e) for i in range(inner)]
@@ -539,12 +593,11 @@
         refs = refs[9 + count :]
         x_ref, from_sib, out_buf, from_far, xbuf = refs[:5]
         (
-            near_s, near_r, far_s, far_r, x_s, x_r,
-            sh_s, sh_r, sp_s, sp_r, sf_s, sf_r, wo_s, wo_r, co_s, co_r, local,
-        ) = refs[5:22]
-        refs = refs[22:]
+            near_s, near_r, far_s, far_r,
+            sh_s, sh_r, sp_s, sp_r, sf_s, sf_r, wo_s, wo_r, local,
+        ) = refs[5:18]
+        x_sems, co_sems, refs = refs[18:22], refs[22:26], refs[26:]
         z, e, c, k, sibling, same_core, column = places(n_dp, n_ex)
-        group = column_group(z, e, inner)
         part = lax.rem(e, parts)
         members = [
             (lax.rem(z + i, n_dp), e - part + lax.rem(part + j, parts))
@@ -610,14 +663,6 @@
         for copy in own:
             copy.start()
         matrices[0].begin()
-        cot_copies = []
-        for i in range(1, inner):
-            copy = remote(cot_in, cot_out.at[my_l], co_s.at[i], co_r.at[i], group[i])
-            copy.start()
-            cot_copies.append(copy)
-        copy = pltpu.make_async_copy(cot_in, cot_out.at[my_l], local.at[4])
-        copy.start()
-        cot_copies.append(copy)
         tok_all, gain_one, wa_ref, wl_ref, gain_lat, cos, sin, keep = att_in
         wq_ref[...] = wa_ref[:, :, :, :wq_cols].reshape(width, wq_cols)
         for j in range(r // rl):
@@ -662,13 +707,13 @@
         residual = res_ref[...]
         scale = lax.rsqrt(jnp.mean(residual * residual, axis=-1, keepdims=True) + norm_eps)
         xbuf[...] = (residual * scale * gain_ref[...]).astype(BF)
-        x_copies = []
-        for i in range(1, inner):
-            copy = remote(xbuf, xcol_ref.at[my_l], x_s.at[i], x_r.at[i], group[i])
-            copy.start()
-            x_copies.append(copy)
-        x_own = pltpu.make_async_copy(xbuf, xcol_ref.at[my_l], local.at[3])
-        x_own.start()
+        relays = [
+            Relay(xbuf, xcol_ref, x_sems, n_dp, n_ex, inner),
+            Relay(cot_in, cot_out, co_sems, n_dp, n_ex, inner),
+        ]
+        relays[0].begin()
+        relays[0].pass_on()
+        relays[1].begin()
         for matrix in matrices[1:]:
             matrix.begin()
         for copy in own:
@@ -692,11 +737,13 @@
                 copy = remote(block, block, sf_s.at[m, i], sf_r.at[m, i], sibling)
                 copy.start()
                 to_sib.append(copy)
+        relays[1].pass_on()
         for matrix in matrices:
             matrix.pass_on()
-        for copy in x_copies + cot_copies + to_sib:
+        for copy in to_sib:
             copy.wait()
-        x_own.wait()
+        for relay in relays:
+            relay.end()
         for copy in plane + shared_copies + near + far:
             copy.wait_send()
         wo_sends(False)
@@ -735,12 +782,10 @@
         + [pltpu.VMEM((chips, rows, width), BF)] * 3
         + [pltpu.VMEM((rows, width), BF)]
         + [dma((chips,))] * 4
-        + [dma((inner,))] * 2
         + [dma((3, n_dp))] * 2
         + [dma((3, chips))] * 4
-        + [dma((n_dp,)), dma((hp, parts))]
-        + [dma((inner,))] * 2
-        + [dma((5,))]
+        + [dma((n_dp,)), dma((hp, parts)), dma((3,))]
+        + Relay.scratch(inner) * 2
         + scratch,
         compiler_params=params(collective_id),
     )(*attend, w_out, tok, gain, cot, *experts, *shared)
@@ -865,44 +910,69 @@
     return outs[:2], outs[2 : 2 + count], outs[2 + count], outs[3 + count], outs[4 + count :]
 
 
-def experts_back(values, weights, dots, n_dp, n_ex, inner, collective_id):
+def experts_run(x_in, grad_in, weights, router, n_dp, n_ex, inner, collective_id):
     chips = n_ex // 2
-    n_slots, width = values[0].shape
-    ff = values[2].shape[1]
+    n_slots, width = x_in.shape
+    ff = weights[0].shape[1]
     per_far = n_slots // chips
     r = width // (n_dp * n_ex)
-    tile = 256
+    tile = per_far
     span = n_dp * r
+    n_experts = inner * chips
 
     def kernel(*refs):
-        v_hbm, w_hbm, dots_ref, refs = refs[:5], refs[5:8], refs[8], refs[9:]
-        dx_out, dots_out, back_out, g_out, refs = refs[0], refs[1], refs[2], refs[3:5], refs[5:]
-        x_v, s_v, a_v, b_v, h_v, wg, wu, wd, dx_v, total, stage = refs[:11]
-        loads, send, recv, d_send, d_recv, local, out_sem = refs[11:18]
+        in_hbm, refs = refs[:6], refs[6:]
+        dx_out, dots_out, rows_out, back_out, g_out, refs = *refs[:4], refs[4:6], refs[6:]
+        x_v, s_v, wg, wu, wd, route, a_v, b_v, h_v, dx_v, total, stage, dots_v = refs[:13]
+        loads, send, recv, d_send, d_recv, local, rows_sem, out_sem = refs[13:21]
         z, e, c, k, sibling, same_core, column = places(n_dp, n_ex)
         moves = [
             pltpu.make_async_copy(src, dst, loads.at[j])
-            for j, (src, dst) in enumerate(
-                zip((*v_hbm, *w_hbm), (x_v, s_v, a_v, b_v, h_v, wg, wu, wd))
-            )
+            for j, (src, dst) in enumerate(zip(in_hbm, (x_v, s_v, wg, wu, wd, route)))
         ]
-        for j in (1, 4, 7, 2, 3, 5, 6, 0):
+        for j in (5, 0, 2, 3, 4, 1):
             moves[j].start()
         greet(same_core + [sibling] + column + [(device[0], sibling[1]) for device in column])
-        back = ExpertsBack(total, back_out, refs[18:], n_dp, n_ex, inner)
+        back = ExpertsBack(total, back_out, refs[21:], n_dp, n_ex, inner)
+        expert = c * inner + lax.rem(z, inner)
+        for j in (5, 0, 2, 3, 4, 1):
+            moves[j].wait()
+
+        def forward(i, carry):
+            at = pl.ds(pl.multiple_of(i * tile, tile), tile)
+            x = x_v[at, :]
+            logits = mm(x, route[...])
+            lane = lax.broadcasted_iota(jnp.int32, logits.shape, 1)
+            logits = jnp.where(lane < n_experts, logits, masked_score)
+            chances = jnp.exp(logits - jnp.max(logits, axis=-1, keepdims=True))
+            gate = jnp.sum(jnp.where(lane == expert, chances, 0.0), axis=-1, keepdims=True)
+            gate = gate / jnp.sum(chances, axis=-1, keepdims=True)
+            first = mm(x, wg[...])
+            second = mm(x, wu[...])
+            a_v[at, :] = first.astype(BF)
+            b_v[at, :] = second.astype(BF)
+            hid = (silu_parts(first)[0] * second).astype(BF)
+            h_v[at, :] = hid
+            rows = mm_cols(hid, wd[...]).astype(BF)
+            dx_v[i] = rows
+            grad = s_v[at, :].astype(F32)
+            dots = jnp.sum(grad * rows.astype(F32), axis=-1, keepdims=True)
+            dots_v[i] = jnp.broadcast_to(dots, (tile, 128)).astype(BF)
+            s_v[at, :] = (gate * grad).astype(BF)
+            pltpu.make_async_copy(dx_v.at[i], rows_out.at[i], rows_sem.at[i]).start()
+            return carry
+
+        lax.fori_loop(0, chips, forward, 0)
         dot_copies = []
         for i in range(1, chips):
             copy = remote(
-                dots_ref.at[i], dots_out.at[i], d_send.at[i], d_recv.at[i],
-                same_core[chips - i - 1],
+                dots_v.at[i], dots_out.at[i], d_send.at[i], d_recv.at[i], same_core[chips - i - 1]
             )
             copy.start()
             dot_copies.append(copy)
-        copy = pltpu.make_async_copy(dots_ref.at[0], dots_out.at[0], local.at[0])
+        copy = pltpu.make_async_copy(dots_v.at[0], dots_out.at[0], local.at[0])
         copy.start()
         dot_copies.append(copy)
-        moves[1].wait()
-        moves[4].wait()
 
         def down_rows(t, carry):
             j = lax.rem(t + (1 - k) * (n_ex // 2), n_ex)
@@ -913,8 +983,6 @@
 
         lax.fori_loop(0, n_ex, down_rows, 0)
         back.begin()
-        for j in (7, 2, 3):
-            moves[j].wait()
 
         def hidden_rows(i, carry):
             at = pl.ds(pl.multiple_of(i * tile, tile), tile)
@@ -925,13 +993,13 @@
             b_v[at, :] = (grad * silu).astype(BF)
             return carry
 
-        lax.fori_loop(0, n_slots // tile, hidden_rows, 0)
-        moves[5].wait()
-        moves[6].wait()
+        lax.fori_loop(0, chips, hidden_rows, 0)
+        back.pass_on()
         copies = []
         for i in list(range(1, chips)) + [0]:
             at = slice(i * per_far, (i + 1) * per_far)
             block = mm_cols(a_v[at, :], wg[...]) + mm_cols(b_v[at, :], wu[...])
+            pltpu.make_async_copy(dx_v.at[i], rows_out.at[i], rows_sem.at[i]).wait()
             dx_v[i] = block.astype(BF)
             if i:
                 copy = remote(
@@ -941,9 +1009,6 @@
                 copy = pltpu.make_async_copy(dx_v.at[0], dx_out.at[0], local.at[1])
             copy.start()
             copies.append(copy)
-            if i == 1:
-                back.pass_on()
-        moves[0].wait()
 
         def other_rows(j, carry):
             at = pl.ds(pl.multiple_of(j * span, span), span)
@@ -969,32 +1034,30 @@
     sds = jax.ShapeDtypeStruct
     vmem = pltpu.VMEM
     total = sds((n_ex, n_dp, r, ff), BF)
+    blocks = sds((chips, per_far, width), BF)
+    dots = sds((chips, per_far, 128), BF)
     outs = pl.pallas_call(
         kernel,
-        out_shape=[
-            sds((chips, per_far, width), BF),
-            sds(dots.shape, BF),
-            ExpertsBack.out(total, n_dp, inner),
-            total,
-            total,
-        ],
-        in_specs=[ANY] * 9,
-        out_specs=[ANY] * 5,
+        out_shape=[blocks, dots, blocks, ExpertsBack.out(total, n_dp, inner), total, total],
+        in_specs=[ANY] * 6,
+        out_specs=[ANY] * 6,
         scratch_shapes=[vmem((n_slots, width), BF)] * 2
+        + [vmem((width, ff), BF)] * 3
+        + [vmem((width, 128), BF)]
         + [vmem((n_slots, ff), BF)] * 3
-        + [vmem((width, ff), BF)] * 3
         + [
-            vmem((chips, per_far, width), BF),
+            vmem(blocks.shape, BF),
             vmem(total.shape, BF),
             vmem((2, n_dp, r, ff), BF),
-            dma((8,)),
+            vmem(dots.shape, BF),
+            dma((6,)),
         ]
         + [dma((chips,))] * 4
-        + [dma((2,))] * 2
+        + [dma((2,)), dma((chips,)), dma((2,))]
         + ExpertsBack.scratch(total, n_dp, inner),
         compiler_params=params(collective_id),
-    )(*values, *weights, dots)
-    return outs[0], outs[1], outs[2], outs[3:]
+    )(x_in, grad_in, *weights, router)
+    return outs[0], outs[1], outs[2], outs[3], outs[4:]
 
 
 class ExpertsBack:
@@ -1648,23 +1711,11 @@
         exp_logits = jnp.exp(logits - top)
         return exp_logits / jnp.sum(exp_logits, axis=-1, keepdims=True)
 
-    slot_probs = probs_of(mm(x_in, router))
-    slot_gate = jnp.sum(
-        jnp.where(jnp.arange(n_experts)[None, :] == far_experts[0], slot_probs, 0.0),
-        axis=1,
-        keepdims=True,
-    )
-    expert_a = mm(x_in, wg)
-    expert_b = mm(x_in, wu)
-    expert_hidden = swiglu(expert_a, expert_b).astype(BF)
-    expert_rows = mm_cols(expert_hidden, wd).astype(BF)
-    slot_dots = jnp.sum(grad_in.astype(F32) * expert_rows.astype(F32), axis=-1, keepdims=True)
-    slot_dots = jnp.broadcast_to(slot_dots, (n_slots, 128)).astype(BF)
-    slot_grad = (slot_gate * grad_in.astype(F32)).astype(BF)
-    dx_back, dots_back, down_back, expert_totals = experts_back(
-        [x_in, slot_grad, expert_a.astype(BF), expert_b.astype(BF), expert_hidden],
+    dx_back, dots_back, expert_rows, down_back, expert_totals = experts_run(
+        x_in,
+        grad_in,
         [wg, wu, wd],
-        slot_dots.reshape(chips, per_far, 128),
+        jnp.pad(router, ((0, 0), (0, 128 - n_experts))),
         n_dp,
         n_ex,
         inner,
@@ -1693,7 +1744,7 @@
     ).astype(BF)
     dx_sum, shared_sums, rows_back, (gate_back,) = column_sum(
         dx_send.reshape(inner, rows, width + 128),
-        expert_rows.reshape(chips, per_far, width),
+        expert_rows,
         [grad.reshape(n_ex, n_dp, r, ff_s) for grad in shared_grads],
         expert_totals[:1],
         n_dp,

time: 1020 us -> 1000 us (0.980)
  matrix products: 56.1 us -> 20.4 us
  Pallas kernels: 857 us -> 881 us
    dot_general x6 -> x3, matrix products: 42.4 us -> 16.8 us  [mm(): return jnp.dot(left, right, preferred_element_type=F32)]
    pallas_call x1, Pallas kernels: 88 us -> 111 us  [experts_run(): pl.pallas_call(kernel, out_shape=[blocks, dots, blocks, ExpertsBack.out(t...]
where the time goes in v10:
time: 1000 us; the launch traced here: 996 us
  Pallas kernels  881 us (88%)
  local copies, waits for them, and re-layouts  56.8 us (6%)
  other arithmetic  35.8 us (4%)
  matrix products  20.4 us (2%)
    pallas_call x1, Pallas kernels, backward_exchange(): pl.pallas_call(kernel, out_shape=[sds((rows, width), F32), sds((8, width)...  226 us
    pallas_call x1, Pallas kernels, forward_exchange(): pl.pallas_call(kernel, out_shape=[sds((seq, width), BF), sds((seq, attend...  209 us
    pallas_call x1, Pallas kernels, dispatch(): pl.pallas_call(kernel, out_shape=[sds((chips, per_far, width), BF)] * 2 +...  143 us
    pallas_call x1, Pallas kernels, column_sum(): pl.pallas_call(kernel, out_shape=[jax.ShapeDtypeStruct(shape, F32)] + [ja...  121 us
    pallas_call x1, Pallas kernels, experts_run(): pl.pallas_call(kernel, out_shape=[blocks, dots, blocks, ExpertsBack.out(t...  111 us
    pallas_call x1, Pallas kernels, first_exchange(): pl.pallas_call(kernel, out_shape=[jax.ShapeDtypeStruct((n_ex,) + tok.shap...  71.3 us

profile of v10, /device:TPU:11, one launch (start us, length us, event | category | flops | bytes accessed | tf_op | source)
XLA Modules:
  0.0 996.4 jit_solution(18309790525398259101)
XLA Ops:
  10.0 1.6 concatenate.33.pk_ref
  11.6 0.9 copy.286
  15.5 1.0 copy_bitcast_fusion.1
  16.7 1.0 copy.241.refs_11_
  19.7 0.9 pad_maximum_fusion.1.wa_ref
  21.3 1.2 reshape.687.refs_8_
  22.8 1.0 copy.240.refs_9_
  23.8 3.6 multiply_sine_fusion
  27.4 71.3 %shard_map.342 = (bf16[8,128,2048]{2,1,0:T(8,128)(2,1)}, bf16[4,8,64,512]{3,2,1,0:T(8,128)(2,1)}, bf16[4,8,64,640]{3,2,1,0:T(8,128)(2,1)}) custom-call(bf16[128,2048]{1,0:T(8,128)(2,1)} %refs_16_.1, bf16[8,64,512]{2,1,0:T(8,128)(2,1)} %pad_maximum_fusion.1.wa_ref, bf16[64,640]{1,0:T(8,128)(2,1)} %concatenate.33.pk_ref), custom_call_target="tpu_custom_call" | custom-call | tf_op jit(solution)/shard_map/pallas_call | solution.py:468
  98.6 2.0 convert_reduce_fusion.5
  100.7 1.6 slice_reduce_fusion
  102.9 1.6 convert_reduce_fusion.4
  105.2 1.2 slice_bitcast_fusion.1
  106.5 0.9 pad.14.refs_5_
  107.4 1.2 slice.127
  110.3 2.3 fusion.10.hot_ref
  112.6 1.4 fusion.5
  114.0 209.4 %shard_map.343 = (bf16[1024,2048]{1,0:T(8,128)(2,1)}, f32[1024,640]{1,0:T(8,128)}, bf16[1024,512]{1,0:T(8,128)(2,1)}, bf16[2,1024,256]{2,1,0:T(8,128)(2,1)}, bf1...) custom-call(bf16[8,128,2048]{2,1,0:T(8,128)(2,1)} %get-tuple-element, ...), custom_call_target="tpu_custom_call" | custom-call | tf_op jit(solution)/shard_map/pallas_call | solution.py:759
  323.4 1.4 multiply_reduce_fusion.3
  324.8 2.3 fusion.43
  328.3 1.7 constant_dynamic-slice_fusion.2.refs_15_
  330.0 1.1 dynamic-slice_bitcast_fusion
  331.3 142.9 %shard_map.344 = (bf16[4,256,2048]{2,1,0:T(8,128)(2,1)}, bf16[4,256,2048]{2,1,0:T(8,128)(2,1)}, bf16[8,4,64,1408]{3,2,1,0:T(8,128)(2,1)}, bf16[8,4,64,1408]{3,2,...) custom-call(bf16[1024,512]{1,0:T(8,128)(2,1)} %fusion.10.hot_ref, ...), custom_call_target="tpu_custom_call" | custom-call | tf_op jit(solution)/shard_map/pallas_call | solution.py:893
  474.3 110.6 %shard_map.345 = (bf16[4,256,2048]{2,1,0:T(8,128)(2,1)}, bf16[4,256,128]{2,1,0:T(8,128)(2,1)}, bf16[4,256,2048]{2,1,0:T(8,128)(2,1)}, bf16[1,2,8,64,1408]{4,3,2,...) custom-call(bf16[1024,2048]{1,0:T(8,128)(2,1)} %bitcast.155, ...), custom_call_target="tpu_custom_call" | custom-call | tf_op jit(solution)/shard_map/pallas_call | solution.py:1039
  584.9 7.3 add_convert_fusion.1
  592.4 1.6 multiply_reduce_fusion
  594.4 4.6 concatenate.35.x_ref
  599.0 121.1 %shard_map.346 = (f32[128,2176]{1,0:T(8,128)}, bf16[4,64,704]{2,1,0:T(8,128)(2,1)}, bf16[4,64,704]{2,1,0:T(8,128)(2,1)}, bf16[4,64,704]{2,1,0:T(8,128)(2,1)}, bf...) custom-call(bf16[4,128,2176]{2,1,0:T(8,128)(2,1)} %concatenate.35.x_ref, ...), custom_call_target="tpu_custom_call" | custom-call | tf_op jit(solution)/shard_map/pallas_call | solution.py:311
  720.1 7.2 add_convert_fusion
  727.3 1.0 multiply_reduce_fusion.4
  728.3 1.2 convolution_convert_fusion
  729.5 2.4 multiply_reduce_fusion.1
  731.9 1.2 fusion.39
  733.4 1.0 pad.15.refs_20_
  734.9 1.3 copy.255.refs_19_
  736.2 225.7 %shard_map.347 = (f32[128,2048]{1,0:T(8,128)}, f32[8,2048]{1,0:T(8,128)}, f32[64,640]{1,0:T(8,128)}, bf16[4,8,64,512]{3,2,1,0:T(8,128)(2,1)}, bf16[4,8,64,512]{3...) custom-call(bf16[128,2048]{1,0:T(8,128)(2,1)} %get-tuple-element.213, ...), custom_call_target="tpu_custom_call" | custom-call | tf_op jit(solution)/shard_map/pallas_call | solution.py:1521
  961.9 2.1 convert_reduce_fusion.1
  964.5 1.0 copy.270
  965.5 1.0 fusion.41
  969.9 1.2 reshape.725
  971.7 1.4 reshape.744
  973.6 1.4 reshape.746
  975.6 1.4 reshape.748
  982.5 1.3 gather.29
  983.8 4.9 convert.47
  988.7 2.9 convert.46
  991.7 2.9 convert.48
  994.6 1.0 copy.290
  (165 shorter events, 32.1 us)
Async XLA Ops:
  0.6 13.9 %copy-start.15 = (bf16[64,2816]{1,0:T(8,128)(2,1)S(1)}, bf16[64,2816]{1,0:T(8,128)(2,1)}, u32[]{:S(2)}) copy-start(bf16[64,2816]{1,0:T(8,128)(2,1)} %param.37) | copy-start | bytes 1081348
  0.7 12.6 %copy-start.14 = (bf16[64,2816]{1,0:T(8,128)(2,1)S(1)}, bf16[64,2816]{1,0:T(8,128)(2,1)}, u32[]{:S(2)}) copy-start(bf16[64,2816]{1,0:T(8,128)(2,1)} %param.36) | copy-start | bytes 1081348
  9.7 5.3 copy-start.16
  13.7 2.7 copy-start.9
  15.4 2.3 copy-start.10
  19.1 1.5 copy-start.17
  19.7 2.8 copy-start.1
  584.9 7.4 copy-start.18
  720.1 9.4 copy-start
  727.3 4.6 copy-start.2
  964.2 4.1 copy-start.19
  964.2 4.8 copy-start.7
  969.8 1.2 copy-start.13
  971.1 2.0 copy-start.12
  973.0 2.0 copy-start.11
  975.0 2.0 copy-start.6
  977.4 1.8 copy-start.3
  979.8 1.0 slice-start
  983.8 4.9 copy-start.5
  988.7 3.0 copy-start.4
  991.7 2.9 copy-start.8

commit v11 on v10

--- a/solution.py
+++ b/solution.py
@@ -214,27 +214,22 @@
     extra = len(totals)
     _, _, r, ff_s = shared[0].shape
 
-    def kernel(x_ref, *refs):
+    def kernel(x_hbm, *refs):
         s_in, r_ref, t_refs, refs = refs[:3], refs[3], refs[4 : 4 + extra], refs[4 + extra :]
         o_ref, s_out, r_out, back_refs = refs[0], refs[1:4], refs[4], refs[5 : 5 + extra]
         refs = refs[5 + extra :]
-        buf, from_sib, out_buf, from_far = refs[:4]
-        send, recv, near_s, near_r, far_s, far_r, r_s, r_r, local = refs[4:13]
-        rest = refs[13:]
+        x_ref, s_v, from_sib, out_buf, from_far = refs[0], refs[1:4], *refs[4:7]
+        loads, near_s, near_r, far_s, far_r, r_s, r_r, local = refs[7:15]
+        relay_refs, rest = refs[15:18], refs[18:]
+        moves = stage([x_hbm, *s_in], [x_ref, *s_v], loads)
         z, e, c, k, sibling, same_core, column = places(n_dp, n_ex)
-        group = column_group(z, e, inner)
         greet(same_core + [sibling] + column + [(d[0], sibling[1]) for d in column])
         backs = [
             ExpertsBack(t_refs[m], back_refs[m], rest[7 * m : 7 * m + 7], n_dp, n_ex, inner)
             for m in range(extra)
         ]
-        copies, rows_back = [], []
-        for i in range(1, inner):
-            to = lax.rem(z + i, inner)
-            copy = remote(x_ref.at[to], buf.at[i], send.at[i], recv.at[i], group[i])
-            copy.start()
-            copies.append(copy)
-        near, far = {}, {}
+        relay = RelaySum(x_ref, relay_refs, n_dp, n_ex, inner)
+        near, far, rows_back = {}, {}, []
         for i in list(range(1, chips)) + [0]:
             chip = lax.rem(c + i, chips)
             for m in range(3):
@@ -254,6 +249,8 @@
         copy = pltpu.make_async_copy(r_ref.at[0], r_out.at[0], local)
         copy.start()
         rows_back.append(copy)
+        moves[0].wait()
+        relay.run()
 
         def pair(i, m):
             chip = lax.rem(c + i, chips)
@@ -261,12 +258,16 @@
 
             def row(d, carry):
                 out_buf[m, i, d] = (
-                    s_in[m][chip * 2 + k, d].astype(F32) + from_sib[m, i, d].astype(F32)
+                    s_v[m][chip * 2 + k, d].astype(F32) + from_sib[m, i, d].astype(F32)
                 ).astype(BF)
                 return carry
 
             lax.fori_loop(0, n_dp, row, 0)
 
+        for back in backs:
+            back.pass_on()
+        for move in moves[1:]:
+            move.wait()
         for i in range(1, chips):
             for m in range(3):
                 pair(i, m)
@@ -275,14 +276,9 @@
                     same_core[i - 1],
                 )
                 far[i, m].start()
-        o_ref[...] = x_ref[lax.rem(z, inner)].astype(F32)
-        for back in backs:
-            back.pass_on()
         for m in range(3):
             pair(0, m)
-        for i in range(1, inner):
-            copies[i - 1].wait_recv()
-            o_ref[...] += buf[i].astype(F32)
+        relay.finish(o_ref)
         for m in range(3):
             for i in range(1, chips):
                 far[i, m].wait_recv()
@@ -295,17 +291,19 @@
                 return carry
 
             lax.fori_loop(0, n_dp, row, 0)
-        for copy in copies + list(near.values()) + list(far.values()):
+        for copy in list(near.values()) + list(far.values()):
             copy.wait_send()
         for copy in rows_back:
             copy.wait()
+        relay.end()
         for back in backs:
             back.end()
 
     dma = pltpu.SemaphoreType.DMA
-    scratch = [pltpu.VMEM((inner,) + shape, BF)]
+    scratch = like([array, *shared])
     scratch += [pltpu.VMEM((3, chips, n_dp, r, ff_s), BF)] * 3
-    scratch += [dma((inner,))] * 2 + [dma((3, chips))] * 4 + [dma((chips,))] * 2 + [dma]
+    scratch += [dma((4,))] + [dma((3, chips))] * 4 + [dma((chips,))] * 2 + [dma]
+    scratch += RelaySum.scratch(shape, inner)
     for total in totals:
         scratch += ExpertsBack.scratch(total, n_dp, inner)
     outs = pl.pallas_call(
@@ -314,7 +312,7 @@
         + [jax.ShapeDtypeStruct((n_dp, r, ff_s), BF)] * 3
         + [jax.ShapeDtypeStruct(rows_out.shape, BF)]
         + [ExpertsBack.out(total, n_dp, inner) for total in totals],
-        in_specs=[VMEM] * 4 + [ANY] * (1 + extra),
+        in_specs=[ANY] * (5 + extra),
         out_specs=[VMEM] * 4 + [ANY] * (1 + extra),
         scratch_shapes=scratch,
         compiler_params=params(collective_id),
@@ -378,6 +376,111 @@
                 @pl.when(jnp.logical_and(exists, more))
                 def _(source=source, step=step):
                     self.copy(source, self.out.at[source], step).wait_send()
+
+
+class RelaySum:
+    @staticmethod
+    def scratch(shape, inner):
+        dma = pltpu.SemaphoreType.DMA
+        return [pltpu.VMEM((inner + 1,) + shape, BF), dma((inner,)), dma((inner + 1,))]
+
+    def __init__(self, blocks, scratch, n_dp, n_ex, inner):
+        self.blocks, self.inner = blocks, inner
+        self.buf, self.send, self.recv = scratch
+        self.z, self.e, *_ = places(n_dp, n_ex)
+        self.mine = lax.rem(self.z, inner)
+
+    def copy(self, t, src, slot, step):
+        return remote(
+            src, self.buf.at[slot], self.send.at[t], self.recv.at[slot], (self.z + step, self.e)
+        )
+
+    def routes(self, t, step):
+        inner, mine = self.inner, self.mine
+        if step > 0:
+            return [(mine < t, mine == 0, t)]
+        last = mine == inner - 1
+        return [
+            (jnp.logical_and(mine > t, mine - 1 != t), last, t),
+            (mine - 1 == t, last, inner),
+        ]
+
+    def hop(self, t, step, start):
+        for active, first, slot in self.routes(t, step):
+
+            @pl.when(jnp.logical_and(active, first))
+            def _(slot=slot):
+                copy = self.copy(t, self.blocks.at[t], slot, step)
+                if start:
+                    copy.start()
+                else:
+                    copy.wait_send()
+
+            @pl.when(jnp.logical_and(active, jnp.logical_not(first)))
+            def _(slot=slot):
+                copy = self.copy(t, self.buf.at[t], slot, step)
+                if start:
+                    self.copy(t, self.buf.at[t], t, step).wait_recv()
+                    total = self.buf[t].astype(F32) + self.blocks[t].astype(F32)
+                    self.buf[t] = total.astype(BF)
+                    copy.start()
+                else:
+                    copy.wait_send()
+
+    def run(self):
+        inner = self.inner
+
+        def up():
+            for t in range(inner - 1, 0, -1):
+                self.hop(t, 1, True)
+
+        def down():
+            for t in range(inner - 1):
+                self.hop(t, -1, True)
+
+        @pl.when(self.mine < inner // 2)
+        def _():
+            up()
+            down()
+
+        @pl.when(self.mine >= inner // 2)
+        def _():
+            down()
+            up()
+
+    def finish(self, out):
+        out[...] = self.blocks[self.mine].astype(F32)
+
+        @pl.when(self.mine > 0)
+        def _():
+            self.copy(0, self.buf.at[self.mine], self.mine, 1).wait_recv()
+            out[...] += self.buf[self.mine].astype(F32)
+
+        @pl.when(self.mine < self.inner - 1)
+        def _():
+            self.copy(0, self.buf.at[self.inner], self.inner, 1).wait_recv()
+            out[...] += self.buf[self.inner].astype(F32)
+
+    def end(self):
+        for t in range(self.inner):
+            if t:
+                self.hop(t, 1, False)
+            if t < self.inner - 1:
+                self.hop(t, -1, False)
+
+
+def stage(sources, targets, sems):
+    copies = [
+        pltpu.make_async_copy(source, target, sems.at[j])
+        for j, (source, target) in enumerate(zip(sources, targets))
+    ]
+    for copy in copies:
+        copy.start()
+    return copies
+
+
+def like(arrays):
+    return [pltpu.VMEM(array.shape, array.dtype) for array in arrays]
 
 
 def column_group(z, e, inner):
@@ -583,14 +686,23 @@
     wq_cols = hp * (DH + DR)
 
     def kernel(*refs):
-        att_in, refs = refs[:8], refs[8:]
+        att_hbm, refs = refs[:8], refs[8:]
         wo_in, tok_ref, gain_ref, cot_in = refs[:4]
         e_in, s_in = refs[4 : 4 + count], refs[4 + count : 7 + count]
         refs = refs[7 + count :]
-        att_out, refs = refs[:8], refs[8:]
-        wq_ref, we_ref, wo_out, res_ref, xcol_ref, cot_out = refs[:6]
-        w_out, s_out = refs[6 : 6 + count], refs[6 + count : 9 + count]
-        refs = refs[9 + count :]
+        kept_hbm, refs = refs[:11], refs[11:]
+        res_ref, xcol_ref, cot_out = refs[:3]
+        refs = refs[3:]
+        w_out, s_out = refs[:count], refs[count : 3 + count]
+        refs = refs[3 + count :]
+        staged, kept, refs = refs[:5], refs[5:16], refs[16:]
+        stage_sem, kept_sem, refs = refs[0], refs[1], refs[2:]
+        att_out, (wq_ref, we_ref, wo_out) = kept[:8], kept[8:]
+        big = (0, 2, 3, 5, 6)
+        moves = stage([att_hbm[j] for j in big], staged, stage_sem)
+        att_in = list(att_hbm)
+        for j, ref in zip(big, staged):
+            att_in[j] = ref
         x_ref, from_sib, out_buf, from_far, xbuf = refs[:5]
         (
             near_s, near_r, far_s, far_r,
@@ -664,6 +776,8 @@
             copy.start()
         matrices[0].begin()
         tok_all, gain_one, wa_ref, wl_ref, gain_lat, cos, sin, keep = att_in
+        for move in moves:
+            move.wait()
         wq_ref[...] = wa_ref[:, :, :, :wq_cols].reshape(width, wq_cols)
         for j in range(r // rl):
             block = wa_ref[:, :, j * rl : (j + 1) * rl, wq_cols:].reshape(KVR, we_cols)
@@ -672,6 +786,7 @@
             tok_all, gain_one, wq_ref, wl_ref, gain_lat, we_ref, cos, sin, keep, *att_out
         )
         wo_arrivals()
+        kept_moves = stage(kept, kept_hbm, kept_sem)
         wo = wo_out[...].reshape(hp * DV, width)
 
         def project(i, carry):
@@ -747,6 +862,8 @@
         for copy in plane + shared_copies + near + far:
             copy.wait_send()
         wo_sends(False)
+        for move in kept_moves:
+            move.wait()
         for matrix in matrices:
             matrix.end()
 
@@ -756,29 +873,39 @@
     for _ in experts:
         scratch += ExpertsIn.scratch(n_dp)
     sds = jax.ShapeDtypeStruct
+    kept = [
+        sds((seq, width), BF),
+        sds((seq, attend[3].shape[1]), F32),
+        sds((seq, KVR), BF),
+        sds((2, seq, 2 * DH), BF),
+        sds((2, seq, 2 * DH), BF),
+        sds((2, seq, DV), BF),
+        sds((2, seq, 128), F32),
+        sds((seq, 2 * DV), BF),
+        sds((width, wq_cols), BF),
+        sds((KVR, hp * (DH + DV)), BF),
+        sds((hp, parts, r, width), BF),
+    ]
+    big = (0, 2, 3, 5, 6)
     outs = pl.pallas_call(
         kernel,
-        out_shape=[
-            sds((seq, width), BF),
-            sds((seq, attend[3].shape[1]), F32),
-            sds((seq, KVR), BF),
-            sds((2, seq, 2 * DH), BF),
-            sds((2, seq, 2 * DH), BF),
-            sds((2, seq, DV), BF),
-            sds((2, seq, 128), F32),
-            sds((seq, 2 * DV), BF),
-            sds((width, wq_cols), BF),
-            sds((KVR, hp * (DH + DV)), BF),
-            sds((hp, parts, r, width), BF),
+        out_shape=kept
+        + [
             sds((rows, width), F32),
             sds((inner, rows, width), BF),
             sds((inner, rows, width), BF),
         ]
         + [ExpertsIn.out(w, n_dp, n_ex) for w in experts]
         + [sds((n_ex, n_dp, r, ff_s), BF)] * 3,
-        in_specs=[VMEM] * 8 + [ANY] + [VMEM] * 2 + [ANY] * (4 + count),
-        out_specs=[VMEM] * 12 + [ANY] * (5 + count),
-        scratch_shapes=[pltpu.VMEM((n_ex, rows, width), BF)]
+        in_specs=[ANY if j in big else VMEM for j in range(8)]
+        + [ANY]
+        + [VMEM] * 2
+        + [ANY] * (4 + count),
+        out_specs=[ANY] * 11 + [VMEM] + [ANY] * (5 + count),
+        scratch_shapes=like([attend[j] for j in big])
+        + like(kept)
+        + [dma((5,)), dma((11,))]
+        + [pltpu.VMEM((n_ex, rows, width), BF)]
         + [pltpu.VMEM((chips, rows, width), BF)] * 3
         + [pltpu.VMEM((rows, width), BF)]
         + [dma((chips,))] * 4
@@ -809,9 +936,10 @@
     def kernel(hot_ref, x_hbm, c_hbm, g_hbm, u_hbm, d_hbm, *refs):
         w_in, refs = refs[:count], refs[count:]
         o_ref, go_ref, w_out, refs = refs[0], refs[1], refs[2 : 2 + count], refs[2 + count :]
-        out_ref, dx_ref, gg_ref, gu_ref, gd_ref = refs[:5]
-        hot_v, x_v, c_v, g_v, u_v, d_v, hid, ga, gb, b_v, send, recv, loads, keep = refs[5:19]
-        rest = refs[19:]
+        results, refs = refs[:5], refs[5:]
+        hot_v, x_v, c_v, g_v, u_v, d_v, hid, ga, gb, b_v, send, recv, loads, keep = refs[:14]
+        out_ref, dx_ref, gg_ref, gu_ref, gd_ref = refs[14:19]
+        results_sem, rest = refs[19], refs[20:]
         z, e, c, k, sibling, same_core, column = places(n_dp, n_ex)
         moves = [
             pltpu.make_async_copy(src, dst, loads.at[j])
@@ -877,9 +1005,10 @@
             return carry
 
         lax.fori_loop(0, width // tile, columns_of, 0)
+        result_moves = stage([out_ref, dx_ref, gg_ref, gu_ref, gd_ref], results, results_sem)
         for matrix in matrices:
             matrix.pass_on()
-        for copy in copies:
+        for copy in copies + result_moves:
             copy.wait()
         for matrix in matrices:
             matrix.end()
@@ -890,20 +1019,22 @@
     scratch = []
     for _ in weights:
         scratch += ExpertsIn.scratch(n_dp)
+    results = [sds((rows, width), F32)] * 2 + [sds((width, ff), BF)] * 3
     outs = pl.pallas_call(
         kernel,
         out_shape=[sds((chips, per_far, width), BF)] * 2
         + [ExpertsIn.out(weight, n_dp, n_ex) for weight in weights]
-        + [sds((rows, width), F32)] * 2
-        + [sds((width, ff), BF)] * 3,
+        + results,
         in_specs=[ANY] * (6 + count),
-        out_specs=[ANY] * (2 + count) + [VMEM] * 5,
+        out_specs=[ANY] * (7 + count),
         scratch_shapes=[vmem(hot.shape, BF)]
         + [vmem((rows, width), BF)] * 2
         + [vmem((width, ff), BF)] * 3
         + [vmem((rows, ff), BF)] * 3
         + [vmem((2, chips, per_far, width), BF)]
         + [dma((2, chips)), dma((2, chips)), dma((6,)), dma((2,))]
+        + like(results)
+        + [dma((5,))]
         + scratch,
         compiler_params=params(collective_id),
     )(hot, x, cot, *shared, *weights)
@@ -1183,12 +1314,12 @@
     wq_cols = wq.shape[1]
     we_cols = rl * we.shape[1] // r
     head_cols = wq_cols + we_cols
+    given_arrays = [*attend, hidden, latent_low, *own]
+    big = [j for j, array in enumerate(given_arrays) if array.shape[0] > 1]
 
     def kernel(*refs):
-        grad_ref, att_in, refs = refs[0], refs[1:12], refs[12:]
-        hidden_ref, low_ref, refs = refs[0], refs[1], refs[2:]
-        wl_ref, lat_ref, tok_ref, gain_ref, glat_ref, gnat_ref, router_ref, gtwo_ref = refs[:8]
-        out_ref, sh_in, refs = refs[8], refs[9:12], refs[12:]
+        grad_ref, given, refs = refs[0], list(refs[1:22]), refs[22:]
+        out_ref, sh_in, refs = refs[0], refs[1:4], refs[4:]
         t_refs, refs = refs[:extra], refs[extra:]
         tok_out, vec_out, pack_out, heads_mid, heads_out, wout_out, out_got = refs[:7]
         sh_out, back_refs, refs = refs[7:10], refs[10 : 10 + extra], refs[10 + extra :]
@@ -1202,7 +1333,12 @@
             h_s, h_r, hz_s, hz_r, w_s, w_r, pn_s, pn_r, pf_s, pf_r, pc_s, pc_r, s_s, s_r,
             v_s, v_r, vz_s, vz_r, o_s, o_r,
         ) = refs[:20]
-        rest = refs[20:]
+        staged, stage_sem, rest = refs[20 : 20 + len(big)], refs[20 + len(big)], refs[21 + len(big) :]
+        moves = stage([given[j] for j in big], staged, stage_sem)
+        for j, ref in zip(big, staged):
+            given[j] = ref
+        att_in, hidden_ref, low_ref = given[:11], given[11], given[12]
+        wl_ref, lat_ref, tok_ref, gain_ref, glat_ref, gnat_ref, router_ref, gtwo_ref = given[13:]
         x_refs = (gbuf, part_l)
         group = column_group(lax.axis_index("dp"), lax.axis_index("expert"), inner)
         z, e, c, k, sibling, same_core, column = places(n_dp, n_ex)
@@ -1266,6 +1402,8 @@
         for copy in gather + to_sib:
             copy.wait_send()
         gat, grad_wout, dk, dv, grad_query, grad_expanded, grad_rope = att_tmp
+        for move in moves:
+            move.wait()
         attend_backward(gbuf, *att_in, *att_tmp)
 
         wsrc[...] = grad_wout[...].astype(BF).reshape(hp, parts, r, width)
@@ -1516,6 +1654,7 @@
     scratch += [dma((n_ex, n_dp))] * 2 + [dma((n_dp,))] * 2 + [dma((hp, parts)), dma((n_dp,))]
     scratch += [dma((chips,))] * 4 + [dma((n_dp,))] * 2 + [dma((3, n_dp))] * 2
     scratch += [dma((n_ex,))] * 2 + [dma((n_dp,))] * 2 + [dma((inner,))] * 2
+    scratch += like([given_arrays[j] for j in big]) + [dma((len(big),))]
     for total in totals:
         scratch += ExpertsBack.scratch(total, n_dp, inner)
     outs = pl.pallas_call(
@@ -1531,7 +1670,9 @@
         ]
         + [sds(array.shape, BF) for array in shared]
         + [ExpertsBack.out(total, n_dp, inner) for total in totals],
-        in_specs=[ANY] + [VMEM] * 21 + [ANY] * (4 + extra),
+        in_specs=[ANY]
+        + [ANY if j in big else VMEM for j in range(21)]
+        + [ANY] * (4 + extra),
         out_specs=[VMEM] * 3 + [ANY] * (7 + extra),
         scratch_shapes=scratch,
         compiler_params=params(collective_id),
@@ -1800,18 +1941,16 @@
 
     out_tokens = from_owner_order((residual + added(out_got)).astype(BF))
     heads_all = added(heads_got)
-    sum_wq = heads_all[..., :head_cols].transpose(1, 0, 2)
-    sum_wq = jnp.concatenate(
-        [
-            sum_wq[..., : hp * DH].reshape(r, n_ex, hp, DH),
-            sum_wq[..., hp * DH :].reshape(r, n_ex, hp, DR),
-        ],
-        axis=-1,
-    ).reshape(r, H, DH + DR)
-    sum_wq = jnp.take(sum_wq, jnp.array(heads_back), axis=1).reshape(r, H * (DH + DR))
-    sum_we = heads_all[..., head_cols:].reshape(n_ex, r // rl, rl, we_cols).transpose(2, 0, 1, 3)
-    sum_we = jnp.take(sum_we.reshape(rl, H, DH + DV), jnp.array(heads_back), axis=1)
-    sum_we = sum_we.reshape(rl, H * (DH + DV))
+    wq_parts, we_parts = [], []
+    for h in heads_back:
+        block, i = heads_all[h // hp], h % hp
+        wq_parts.append(block[:, i * DH : (i + 1) * DH])
+        wq_parts.append(block[:, hp * DH + i * DR : hp * DH + (i + 1) * DR])
+        per = (DH + DV) // we_cols
+        for j in range(i * per, (i + 1) * per):
+            we_parts.append(block[j * rl : (j + 1) * rl, head_cols:])
+    sum_wq = jnp.concatenate(wq_parts, axis=1)
+    sum_we = jnp.concatenate(we_parts, axis=1)
     sum_wout = from_owner_order(added(wout_got))
     device = z * n_ex + e
     sum_gain_one = lax.dynamic_slice_in_dim(vec_sum[0], device * r, r, 0)

time: 1000 us -> 987 us (0.987)
  Pallas kernels: 881 us -> 848 us
  local copies, waits for them, and re-layouts: 56.8 us -> 73 us
    pallas_call x1, Pallas kernels: 121 us -> 105 us  [column_sum(): pl.pallas_call(kernel, out_shape=[jax.ShapeDtypeStruct(shape, F32)] + [ja...]
where the time goes in v11:
time: 987 us; the launch traced here: 978 us
  Pallas kernels  848 us (86%)
  local copies, waits for them, and re-layouts  73 us (7%)
  other arithmetic  33.8 us (3%)
  matrix products  20.4 us (2%)
    pallas_call x1, Pallas kernels, backward_exchange(): pl.pallas_call(kernel, out_shape=[sds((rows, width), F32), sds((8, width)...  222 us
    pallas_call x1, Pallas kernels, forward_exchange(): pl.pallas_call(kernel, out_shape=kept + [sds((rows, width), F32), sds((in...  202 us
    pallas_call x1, Pallas kernels, dispatch(): pl.pallas_call(kernel, out_shape=[sds((chips, per_far, width), BF)] * 2 +...  137 us
    pallas_call x1, Pallas kernels, experts_run(): pl.pallas_call(kernel, out_shape=[blocks, dots, blocks, ExpertsBack.out(t...  111 us
    pallas_call x1, Pallas kernels, column_sum(): pl.pallas_call(kernel, out_shape=[jax.ShapeDtypeStruct(shape, F32)] + [ja...  105 us
    pallas_call x1, Pallas kernels, first_exchange(): pl.pallas_call(kernel, out_shape=[jax.ShapeDtypeStruct((n_ex,) + tok.shap...  71.3 us

profile of v11, /device:TPU:11, one launch (start us, length us, event | category | flops | bytes accessed | tf_op | source)
XLA Modules:
  0.0 977.7 jit_solution(14465079154598282668)
XLA Ops:
  10.0 1.6 concatenate.31.pk_ref
  11.6 0.9 copy.256
  15.5 1.0 copy_bitcast_fusion.1
  16.7 1.0 copy.220.refs_11_
  19.7 0.9 pad_maximum_fusion.wa_ref
  21.3 1.2 reshape.658.refs_8_
  22.8 1.0 copy.219.refs_9_
  23.8 3.5 multiply_sine_fusion
  27.3 71.3 %shard_map.324 = (bf16[8,128,2048]{2,1,0:T(8,128)(2,1)}, bf16[4,8,64,512]{3,2,1,0:T(8,128)(2,1)}, bf16[4,8,64,640]{3,2,1,0:T(8,128)(2,1)}) custom-call(bf16[128,2048]{1,0:T(8,128)(2,1)} %refs_16_.1, bf16[8,64,512]{2,1,0:T(8,128)(2,1)} %pad_maximum_fusion.wa_ref, bf16[64,640]{1,0:T(8,128)(2,1)} %concatenate.31.pk_ref), custom_call_target="tpu_custom_call" | custom-call | tf_op jit(solution)/shard_map/pallas_call | solution.py:571
  98.6 2.0 convert_reduce_fusion.5
  100.6 1.6 slice_reduce_fusion
  102.8 1.6 convert_reduce_fusion.4
  105.2 1.2 slice_bitcast_fusion
  106.5 0.9 pad.14.refs_5_
  107.4 1.2 slice.339
  110.3 2.3 fusion.10.hot_ref
  112.5 1.4 fusion.5
  113.9 201.9 %shard_map.325 = (bf16[1024,2048]{1,0:T(8,128)(2,1)}, f32[1024,640]{1,0:T(8,128)}, bf16[1024,512]{1,0:T(8,128)(2,1)}, bf16[2,1024,256]{2,1,0:T(8,128)(2,1)}, bf1...) custom-call(bf16[8,128,2048]{2,1,0:T(8,128)(2,1)} %get-tuple-element, ...), custom_call_target="tpu_custom_call" | custom-call | tf_op jit(solution)/shard_map/pallas_call | solution.py:890
  315.8 1.4 multiply_reduce_fusion.3
  317.2 2.3 fusion.59
  320.7 1.7 constant_dynamic-slice_fusion.2.refs_15_
  322.4 1.1 dynamic-slice_bitcast_fusion
  323.8 136.9 %shard_map.326 = (bf16[4,256,2048]{2,1,0:T(8,128)(2,1)}, bf16[4,256,2048]{2,1,0:T(8,128)(2,1)}, bf16[8,4,64,1408]{3,2,1,0:T(8,128)(2,1)}, bf16[8,4,64,1408]{3,2,...) custom-call(bf16[1024,512]{1,0:T(8,128)(2,1)} %fusion.10.hot_ref, ...), custom_call_target="tpu_custom_call" | custom-call | tf_op jit(solution)/shard_map/pallas_call | solution.py:1023
  460.7 110.6 %shard_map.327 = (bf16[4,256,2048]{2,1,0:T(8,128)(2,1)}, bf16[4,256,128]{2,1,0:T(8,128)(2,1)}, bf16[4,256,2048]{2,1,0:T(8,128)(2,1)}, bf16[1,2,8,64,1408]{4,3,2,...) custom-call(bf16[1024,2048]{1,0:T(8,128)(2,1)} %bitcast.162, ...), custom_call_target="tpu_custom_call" | custom-call | tf_op jit(solution)/shard_map/pallas_call | solution.py:1170
  571.3 7.4 add_convert_fusion.1
  578.8 1.6 multiply_reduce_fusion
  580.8 4.6 concatenate.33.x_hbm
  585.4 104.9 %shard_map.328 = (f32[128,2176]{1,0:T(8,128)}, bf16[4,64,704]{2,1,0:T(8,128)(2,1)}, bf16[4,64,704]{2,1,0:T(8,128)(2,1)}, bf16[4,64,704]{2,1,0:T(8,128)(2,1)}, bf...) custom-call(bf16[4,128,2176]{2,1,0:T(8,128)(2,1)} %concatenate.33.x_hbm, ...), custom_call_target="tpu_custom_call" | custom-call | tf_op jit(solution)/shard_map/pallas_call | solution.py:309
  690.4 7.2 add_convert_fusion
  697.6 1.0 multiply_reduce_fusion.4
  698.6 1.2 convolution_convert_fusion
  699.7 2.4 multiply_reduce_fusion.1
  702.2 1.2 fusion.39
  703.6 1.0 pad.15.refs_20_
  705.1 1.3 copy.234.refs_19_
  706.4 222.4 %shard_map.329 = (f32[128,2048]{1,0:T(8,128)}, f32[8,2048]{1,0:T(8,128)}, f32[64,640]{1,0:T(8,128)}, bf16[4,8,64,512]{3,2,1,0:T(8,128)(2,1)}, bf16[4,8,64,512]{3...) custom-call(bf16[128,2048]{1,0:T(8,128)(2,1)} %get-tuple-element.213, ...), custom_call_target="tpu_custom_call" | custom-call | tf_op jit(solution)/shard_map/pallas_call | solution.py:1660
  928.9 2.1 convert_reduce_fusion.1
  931.5 1.0 copy.241
  932.5 1.0 fusion.57
  937.6 1.2 reshape.694
  939.4 1.4 reshape.713
  941.3 1.4 reshape.715
  943.3 1.4 reshape.717
  955.7 2.3 concatenate.35
  966.5 3.0 convert.47
  969.8 2.9 convert.46
  972.8 2.9 convert.48
  975.8 1.0 copy.291
  (203 shorter events, 47.2 us)
Async XLA Ops:
  0.6 13.9 %copy-start.18 = (bf16[64,2816]{1,0:T(8,128)(2,1)S(1)}, bf16[64,2816]{1,0:T(8,128)(2,1)}, u32[]{:S(2)}) copy-start(bf16[64,2816]{1,0:T(8,128)(2,1)} %param.35) | copy-start | bytes 1081348
  0.7 12.6 %copy-start.17 = (bf16[64,2816]{1,0:T(8,128)(2,1)S(1)}, bf16[64,2816]{1,0:T(8,128)(2,1)}, u32[]{:S(2)}) copy-start(bf16[64,2816]{1,0:T(8,128)(2,1)} %param.34) | copy-start | bytes 1081348
  9.7 5.3 copy-start.19
  13.7 2.7 copy-start.12
  15.4 2.3 copy-start.13
  19.1 1.5 copy-start.20
  19.7 2.8 copy-start.1
  571.3 7.4 copy-start.21
  690.3 9.4 copy-start
  697.5 4.6 copy-start.2
  931.1 5.6 copy-start.7
  937.6 1.2 copy-start.16
  938.8 2.0 copy-start.15
  940.8 2.0 copy-start.14
  942.7 2.0 copy-start.6
  945.1 7.3 copy-start.9
  945.1 8.6 copy-start.10
  945.1 9.9 %copy-start.11 = (f32[64,512]{1,0:T(8,128)}, f32[64,512]{1,0:T(8,128)S(1)}, u32[]{:S(2)}) copy-start(f32[64,512]{1,0:T(8,128)S(1)} %get-tuple-element.222) | copy-start | bytes 393220
  946.5 20.0 %copy-start.5 = (bf16[1,2,8,64,1408]{4,3,2,1,0:T(8,128)(2,1)S(1)}, bf16[1,2,8,64,1408]{4,3,2,1,0:T(8,128)(2,1)}, u32[]{:S(2)}) copy-start(bf16[1,2,8,64,1408]{4,3,2,1,0:T(8,128)(2,1)} %get-tuple-element.118) | copy-start | bytes 8650756
  966.5 3.0 copy-start.23
  966.5 3.3 copy-start.4
  969.8 3.0 copy-start.3
  972.8 2.9 copy-start.8
  975.8 1.1 copy-start.22

commit v12 on v11

--- a/solution.py
+++ b/solution.py
@@ -488,104 +488,6 @@
     return [(start + lax.rem(z - start + i, inner), e) for i in range(inner)]
 
 
-def first_exchange(tok, heads_w, pack, n_dp, n_ex, collective_id):
-    chips = n_ex // 2
-
-    def kernel(
-        tok_ref, wa_ref, pk_ref, tok_out, wa_out, pk_out,
-        t_send, t_recv, ts_send, ts_recv, a_send, a_recv, az_send, az_recv,
-        p_send, p_recv, pf_send, pf_recv, ps_send, ps_recv, local,
-    ):
-        z, e, c, k, sibling, same_core, column = places(n_dp, n_ex)
-        plane = [(z, lax.rem(e + i, n_ex)) for i in range(1, n_ex)]
-        greet(plane + column)
-        wa_far, pk_col, tok_far, near = [], [], [], []
-        for i in range(1, n_ex):
-            copy = remote(
-                wa_ref.at[lax.rem(e + i, n_ex)], wa_out.at[z, e],
-                a_send.at[i], a_recv.at[i], plane[i - 1],
-            )
-            copy.start()
-            wa_far.append(copy)
-        for i in range(1, n_dp):
-            copy = remote(pk_ref, pk_out.at[z, e], p_send.at[i], p_recv.at[i], column[i - 1])
-            copy.start()
-            pk_col.append(copy)
-        for i in range(1, chips):
-            copy = remote(tok_ref, tok_out.at[e], t_send.at[i], t_recv.at[i], same_core[i - 1])
-            copy.start()
-            tok_far.append(copy)
-        copy = remote(tok_ref, tok_out.at[e], ts_send.at[0], ts_recv.at[0], sibling)
-        copy.start()
-        near.append(copy)
-        own = [
-            pltpu.make_async_copy(wa_ref.at[e], wa_out.at[z, e], local.at[0]),
-            pltpu.make_async_copy(pk_ref, pk_out.at[z, e], local.at[1]),
-            pltpu.make_async_copy(tok_ref, tok_out.at[e], local.at[2]),
-        ]
-        for copy in own:
-            copy.start()
-        for copy in own:
-            copy.wait()
-        for copy in wa_far:
-            copy.wait_recv()
-        wa_col = []
-        for i in range(1, n_dp):
-            copy = remote(
-                wa_out.at[z], wa_out.at[z], az_send.at[i], az_recv.at[i], column[i - 1]
-            )
-            copy.start()
-            wa_col.append(copy)
-        for copy in pk_col:
-            copy.wait_recv()
-        pk_far = []
-        for i in range(1, chips):
-            copy = remote(
-                pk_out.at[:, e], pk_out.at[:, e], pf_send.at[i], pf_recv.at[i], same_core[i - 1]
-            )
-            copy.start()
-            pk_far.append(copy)
-        copy = remote(pk_out.at[:, e], pk_out.at[:, e], ps_send.at[0], ps_recv.at[0], sibling)
-        copy.start()
-        near.append(copy)
-        for i in range(1, chips):
-            source = lax.rem(c + chips - i, chips) * 2 + k
-            tok_far[i - 1].wait_recv()
-            copy = remote(
-                tok_out.at[source], tok_out.at[source], ts_send.at[i], ts_recv.at[i], sibling
-            )
-            copy.start()
-            near.append(copy)
-            pk_far[i - 1].wait_recv()
-            copy = remote(
-                pk_out.at[:, source], pk_out.at[:, source], ps_send.at[i], ps_recv.at[i], sibling
-            )
-            copy.start()
-            near.append(copy)
-        for copy in near + wa_col:
-            copy.wait()
-        for copy in wa_far + pk_col + tok_far + pk_far:
-            copy.wait_send()
-
-    dma = pltpu.SemaphoreType.DMA
-    return pl.pallas_call(
-        kernel,
-        out_shape=[
-            jax.ShapeDtypeStruct((n_ex,) + tok.shape, tok.dtype),
-            jax.ShapeDtypeStruct((n_dp,) + heads_w.shape, heads_w.dtype),
-            jax.ShapeDtypeStruct((n_dp, n_ex) + pack.shape, pack.dtype),
-        ],
-        in_specs=[ANY] * 3,
-        out_specs=[ANY] * 3,
-        scratch_shapes=[dma((chips,))] * 4
-        + [dma((n_ex,))] * 2
-        + [dma((n_dp,))] * 4
-        + [dma((chips,))] * 4
-        + [dma((3,))],
-        compiler_params=params(collective_id),
-    )(tok, heads_w, pack)
-
-
 class ExpertsIn:
     @staticmethod
     def scratch(n_dp):
@@ -673,7 +575,23 @@
             wait_recv(region, self.sib_recv.at[i], self.sibling)
 
 
-def forward_exchange(attend, w_out, tok, gain, cot, experts, shared, n_dp, n_ex, inner, collective_id):
+def gain_rows(gains, target, width, order):
+    per = 128 // width
+    for t in range(len(order) // per):
+        tile = jnp.zeros((8, 128), F32)
+        for q in range(per):
+            d, e = order[t * per + q]
+            piece = gains[d, e, 0:8].astype(F32)
+            lane = lax.broadcasted_iota(jnp.int32, piece.shape, 1)
+            if q:
+                piece = pltpu.roll(piece, q * width, 1)
+            tile = jnp.where(lane // width == q, piece, tile)
+        target[:, t * 128 : (t + 1) * 128] = tile
+
+
+def forward_exchange(
+    first, tables, w_out, tok, cot, experts, shared, n_dp, n_ex, inner, collective_id
+):
     chips = n_ex // 2
     rows, width = tok.shape
     count = len(experts)
@@ -685,24 +603,25 @@
     we_cols = rl * hp * (DH + DV) // r
     wq_cols = hp * (DH + DR)
 
+    natural = [(d, j) for d in range(n_dp) for j in range(n_ex)]
+    by_owner = [(d, j) for j in range(n_ex) for d in range(n_dp)]
+
     def kernel(*refs):
-        att_hbm, refs = refs[:8], refs[8:]
-        wo_in, tok_ref, gain_ref, cot_in = refs[:4]
-        e_in, s_in = refs[4 : 4 + count], refs[4 + count : 7 + count]
-        refs = refs[7 + count :]
-        kept_hbm, refs = refs[:11], refs[11:]
-        res_ref, xcol_ref, cot_out = refs[:3]
-        refs = refs[3:]
+        first_in, tables_hbm, keep, refs = refs[:4], refs[4:6], refs[6], refs[7:]
+        wo_in, tok_ref, cot_in = refs[:3]
+        e_in, s_in = refs[3 : 3 + count], refs[3 + count : 6 + count]
+        refs = refs[6 + count :]
+        kept_hbm, refs = refs[:12], refs[12:]
+        gain_one, gain_ref, gain_lat, res_ref, xcol_ref, cot_out = refs[:6]
+        refs = refs[6:]
         w_out, s_out = refs[:count], refs[count : 3 + count]
         refs = refs[3 + count :]
-        staged, kept, refs = refs[:5], refs[5:16], refs[16:]
+        (cos, sin), (tok_all, wa_ref, gr_ref), refs = refs[:2], refs[2:5], refs[5:]
+        kept, refs = refs[:12], refs[12:]
         stage_sem, kept_sem, refs = refs[0], refs[1], refs[2:]
-        att_out, (wq_ref, we_ref, wo_out) = kept[:8], kept[8:]
-        big = (0, 2, 3, 5, 6)
-        moves = stage([att_hbm[j] for j in big], staged, stage_sem)
-        att_in = list(att_hbm)
-        for j, ref in zip(big, staged):
-            att_in[j] = ref
+        first_sems, own_sem, refs = refs[:14], refs[14], refs[15:]
+        att_out, (wq_ref, we_ref, wo_out, pk_ref) = kept[:8], kept[8:]
+        moves = stage(tables_hbm, (cos, sin), stage_sem)
         x_ref, from_sib, out_buf, from_far, xbuf = refs[:5]
         (
             near_s, near_r, far_s, far_r,
@@ -716,7 +635,8 @@
             for i in range(n_dp)
             for j in range(parts)
         ]
-        greet(same_core + column + [(device[0], sibling[1]) for device in column] + members[1:])
+        plane = [(z, lax.rem(e + i, n_ex)) for i in range(1, n_ex)]
+        greet(plane + column + [(device[0], sibling[1]) for device in column] + members[1:])
 
         def wo_sends(start):
             for i in range(n_dp):
@@ -758,6 +678,51 @@
             ExpertsIn(e_in[m], w_out[m], refs[4 * m : 4 * m + 4], n_dp, n_ex, inner)
             for m in range(count)
         ]
+        tok_in, wa_in, *packs_in = first_in
+        packs = (pk_ref, gr_ref)
+        (
+            t_send, t_recv, ts_send, ts_recv, a_send, a_recv, az_send, az_recv,
+            p_send, p_recv, pf_send, pf_recv, ps_send, ps_recv,
+        ) = first_sems
+        wa_far, pk_col, tok_far, first_near = [], [], [], []
+        for i in range(1, n_ex):
+            copy = remote(
+                wa_in.at[lax.rem(e + i, n_ex)], wa_ref.at[z, e],
+                a_send.at[i], a_recv.at[i], plane[i - 1],
+            )
+            copy.start()
+            wa_far.append(copy)
+        for i in range(1, n_dp):
+            for m in range(2):
+                copy = remote(
+                    packs_in[m], packs[m].at[z, e], p_send.at[m, i], p_recv.at[m, i],
+                    column[i - 1],
+                )
+                copy.start()
+                pk_col.append(copy)
+        for i in range(1, chips):
+            copy = remote(tok_in, tok_all.at[e], t_send.at[i], t_recv.at[i], same_core[i - 1])
+            copy.start()
+            tok_far.append(copy)
+        copy = remote(tok_in, tok_all.at[e], ts_send.at[0], ts_recv.at[0], sibling)
+        copy.start()
+        first_near.append(copy)
+        first_own = stage(
+            [wa_in.at[e], packs_in[0], packs_in[1], tok_in],
+            [wa_ref.at[z, e], pk_ref.at[z, e], gr_ref.at[z, e], tok_all.at[e]],
+            own_sem,
+        )
+        for copy in first_own:
+            copy.wait()
+        for copy in wa_far:
+            copy.wait_recv()
+        wa_col = []
+        for i in range(1, n_dp):
+            copy = remote(
+                wa_ref.at[z], wa_ref.at[z], az_send.at[i], az_recv.at[i], column[i - 1]
+            )
+            copy.start()
+            wa_col.append(copy)
         wo_sends(True)
         shared_copies = []
         for i in range(1, n_dp):
@@ -775,15 +740,49 @@
         for copy in own:
             copy.start()
         matrices[0].begin()
-        tok_all, gain_one, wa_ref, wl_ref, gain_lat, cos, sin, keep = att_in
+        for copy in pk_col:
+            copy.wait_recv()
+        pk_far = []
+        for m in range(2):
+            block = packs[m].at[:, e]
+            for i in range(1, chips):
+                copy = remote(block, block, pf_send.at[m, i], pf_recv.at[m, i], same_core[i - 1])
+                copy.start()
+                pk_far.append((i, m, copy))
+            copy = remote(block, block, ps_send.at[m, 0], ps_recv.at[m, 0], sibling)
+            copy.start()
+            first_near.append(copy)
+        for i in range(1, chips):
+            source = lax.rem(c + chips - i, chips) * 2 + k
+            tok_far[i - 1].wait_recv()
+            copy = remote(
+                tok_all.at[source], tok_all.at[source], ts_send.at[i], ts_recv.at[i], sibling
+            )
+            copy.start()
+            first_near.append(copy)
+        for i, m, copy in pk_far:
+            copy.wait_recv()
+            block = packs[m].at[:, lax.rem(c + chips - i, chips) * 2 + k]
+            copy = remote(block, block, ps_send.at[m, i], ps_recv.at[m, i], sibling)
+            copy.start()
+            first_near.append(copy)
+        for copy in first_near + wa_col:
+            copy.wait()
+        for copy in wa_far + pk_col + tok_far + [copy for _, _, copy in pk_far]:
+            copy.wait_send()
         for move in moves:
             move.wait()
+        gain_rows(gr_ref, gain_one, r, natural)
+        gain_rows(gr_ref, gain_ref, r, by_owner)
+        gain_rows(gr_ref, gain_lat, rl, natural)
+        wl_ref = pk_ref.reshape(width, pk_ref.shape[3])
         wq_ref[...] = wa_ref[:, :, :, :wq_cols].reshape(width, wq_cols)
         for j in range(r // rl):
             block = wa_ref[:, :, j * rl : (j + 1) * rl, wq_cols:].reshape(KVR, we_cols)
             we_ref[:, j * we_cols : (j + 1) * we_cols] = block
         attend_forward(
-            tok_all, gain_one, wq_ref, wl_ref, gain_lat, we_ref, cos, sin, keep, *att_out
+            tok_all, gain_one.at[0:1], wq_ref, wl_ref, gain_lat.at[2:3], we_ref, cos, sin, keep,
+            *att_out,
         )
         wo_arrivals()
         kept_moves = stage(kept, kept_hbm, kept_sem)
@@ -821,7 +820,7 @@
             res_ref[...] += from_far[i].astype(F32)
         residual = res_ref[...]
         scale = lax.rsqrt(jnp.mean(residual * residual, axis=-1, keepdims=True) + norm_eps)
-        xbuf[...] = (residual * scale * gain_ref[...]).astype(BF)
+        xbuf[...] = (residual * scale * gain_ref[1:2, :]).astype(BF)
         relays = [
             Relay(xbuf, xcol_ref, x_sems, n_dp, n_ex, inner),
             Relay(cot_in, cot_out, co_sems, n_dp, n_ex, inner),
@@ -875,7 +874,7 @@
     sds = jax.ShapeDtypeStruct
     kept = [
         sds((seq, width), BF),
-        sds((seq, attend[3].shape[1]), F32),
+        sds((seq, first[2].shape[1]), F32),
         sds((seq, KVR), BF),
         sds((2, seq, 2 * DH), BF),
         sds((2, seq, 2 * DH), BF),
@@ -885,26 +884,37 @@
         sds((width, wq_cols), BF),
         sds((KVR, hp * (DH + DV)), BF),
         sds((hp, parts, r, width), BF),
+        sds((n_dp, n_ex) + first[2].shape, BF),
     ]
-    big = (0, 2, 3, 5, 6)
     outs = pl.pallas_call(
         kernel,
         out_shape=kept
         + [
+            sds((8, width), F32),
+            sds((8, width), F32),
+            sds((8, KVR), F32),
             sds((rows, width), F32),
             sds((inner, rows, width), BF),
             sds((inner, rows, width), BF),
         ]
         + [ExpertsIn.out(w, n_dp, n_ex) for w in experts]
         + [sds((n_ex, n_dp, r, ff_s), BF)] * 3,
-        in_specs=[ANY if j in big else VMEM for j in range(8)]
-        + [ANY]
-        + [VMEM] * 2
-        + [ANY] * (4 + count),
-        out_specs=[ANY] * 11 + [VMEM] + [ANY] * (5 + count),
-        scratch_shapes=like([attend[j] for j in big])
+        in_specs=[ANY] * 6 + [VMEM, ANY, VMEM] + [ANY] * (4 + count),
+        out_specs=[ANY] * 12 + [VMEM] * 4 + [ANY] * (5 + count),
+        scratch_shapes=like(tables[:2])
+        + [
+            pltpu.VMEM((n_ex, rows, width), BF),
+            pltpu.VMEM((n_dp,) + first[1].shape, BF),
+            pltpu.VMEM((n_dp, n_ex) + first[3].shape, BF),
+        ]
         + like(kept)
-        + [dma((5,)), dma((11,))]
+        + [dma((2,)), dma((12,))]
+        + [dma((chips,))] * 4
+        + [dma((n_ex,))] * 2
+        + [dma((n_dp,))] * 2
+        + [dma((2, n_dp))] * 2
+        + [dma((2, chips))] * 4
+        + [dma((4,))]
         + [pltpu.VMEM((n_ex, rows, width), BF)]
         + [pltpu.VMEM((chips, rows, width), BF)] * 3
         + [pltpu.VMEM((rows, width), BF)]
@@ -915,8 +925,8 @@
         + Relay.scratch(inner) * 2
         + scratch,
         compiler_params=params(collective_id),
-    )(*attend, w_out, tok, gain, cot, *experts, *shared)
-    return outs[:8], outs[8:11], outs[11], outs[12], outs[13], outs[14 : 14 + count], outs[14 + count :]
+    )(*first, *tables, w_out, tok, cot, *experts, *shared)
+    return outs[:8], outs[8:12], outs[12:15], outs[15:18], outs[18 : 18 + count], outs[18 + count :]
 
 
 def silu_parts(a):
@@ -1760,15 +1770,12 @@
     slot_place = jnp.where(slot_own >= 0, slot_own - routes * capacity, -1)
     slot_cols = 2 * rows * top_k // r
     slot_pack = jnp.stack([routes, slot_place]).astype(BF).reshape(2, r, slot_cols // 2)
-    small_cols = lat + n_experts + 3
+    small_cols = lat + n_experts
     pack_cols = (small_cols + slot_cols + 127) // 128 * 128
     pack = jnp.concatenate(
         [
             w_latent,
             w_router,
-            attn_gain[:, None],
-            ffn_gain[:, None],
-            jnp.pad(latent_gain, (0, r - rl))[:, None],
             slot_pack[0],
             slot_pack[1],
             jnp.zeros((r, pack_cols - small_cols - slot_cols), BF),
@@ -1776,15 +1783,45 @@
         axis=1,
     )
     cot_owner = to_owner_order(cotangent)
-    tok_all, wa_all, pk_all = first_exchange(tokens, wa_send, pack, n_dp, n_ex, 1)
+    gains = jnp.stack(
+        [jnp.pad(gain, (0, 128 - gain.shape[0])) for gain in (attn_gain, ffn_gain, latent_gain)]
+    )
+    gains = jnp.pad(gains, ((0, 13), (0, 0)))
+
+    positions = jnp.arange(seq)
+    lane = jnp.arange(2 * DR) % (DR // 2)
+    angles = positions.astype(F32)[:, None] * (10000.0 ** (-(lane.astype(F32) * 2.0) / DR))[None, :]
+    cos_wide, sine_wide = jnp.cos(angles), jnp.sin(angles)
+    keep = (positions < lengths[0]).astype(F32)[None]
+    attend_out, (wq, wexp, wo_rows, pk_all), gain_outs, rows_outs, (wg,), shared_w = (
+        forward_exchange(
+            [tokens, wa_send, pack, gains],
+            [cos_wide, sine_wide, keep],
+            to_owner_order(w_out),
+            to_owner_order(tokens),
+            cot_owner,
+            [expert_gate.reshape(-1, n_ex, r, ff_e)],
+            [
+                w.reshape(r, inner, ff_s).transpose(1, 0, 2)
+                for w in (shared_gate, shared_up, shared_down)
+            ],
+            n_dp,
+            n_ex,
+            inner,
+            2,
+        )
+    )
+    residual, x_col, cot_col = rows_outs
+    gain_one, gain_two, gain_lat = (out[j] for j, out in enumerate(gain_outs))
+    hidden_one, latent_raw, latent_low, qcat, kcat, value, lse, attended = attend_out
+    wo_rows = wo_rows.reshape(hp * DV, width)
+    cot_col = cot_col.reshape(inner * rows, width)
+    hidden_two = pick(x_col, my_local)
+    x_col = x_col.reshape(inner * rows, width)
+
+    router = pk_all[..., lat : lat + n_experts].transpose(1, 0, 2, 3).reshape(width, n_experts)
     pk_flat = pk_all.reshape(width, pack_cols)
-    w_lat = pk_flat[:, :lat]
-    gain_one = pk_flat[:, lat + n_experts].astype(F32)
-    gain_two = pk_all[..., lat + n_experts + 1].transpose(1, 0, 2).reshape(width).astype(F32)
-    router = pk_all[..., lat : lat + n_experts].transpose(1, 0, 2, 3).reshape(width, n_experts)
-    gain_lat = (
-        pk_all[..., lat + n_experts + 2].reshape(n_dp * n_ex, r)[:, :rl].reshape(KVR).astype(F32)
-    )
+
     slots_all = n_experts * capacity
     slot_col = pick(pk_all[..., small_cols : small_cols + slot_cols], e, 1)
     slot_col = lax.dynamic_slice_in_dim(slot_col, z - my_local, inner, 0).astype(jnp.int32)
@@ -1807,30 +1844,6 @@
     per_far = n_slots // chips
     hot = sum((wanted[:, None] == slot_ids[None, :, j]).astype(BF) for j in range(top_k))
     hot_t = sum((slot_ids[:, j][:, None] == wanted[None, :]).astype(BF) for j in range(top_k))
-
-    positions = jnp.arange(seq)
-    lane = jnp.arange(2 * DR) % (DR // 2)
-    angles = positions.astype(F32)[:, None] * (10000.0 ** (-(lane.astype(F32) * 2.0) / DR))[None, :]
-    cos_wide, sine_wide = jnp.cos(angles), jnp.sin(angles)
-    keep = (positions < lengths[0]).astype(F32)[None]
-    attend_out, (wq, wexp, wo_rows), residual, x_col, cot_col, (wg,), shared_w = forward_exchange(
-        [tok_all, gain_one[None], wa_all, pk_flat, gain_lat[None], cos_wide, sine_wide, keep],
-        to_owner_order(w_out),
-        to_owner_order(tokens),
-        gain_two[None],
-        cot_owner,
-        [expert_gate.reshape(-1, n_ex, r, ff_e)],
-        [w.reshape(r, inner, ff_s).transpose(1, 0, 2) for w in (shared_gate, shared_up, shared_down)],
-        n_dp,
-        n_ex,
-        inner,
-        2,
-    )
-    hidden_one, latent_raw, latent_low, qcat, kcat, value, lse, attended = attend_out
-    wo_rows = wo_rows.reshape(hp * DV, width)
-    cot_col = cot_col.reshape(inner * rows, width)
-    hidden_two = pick(x_col, my_local)
-    x_col = x_col.reshape(inner * rows, width)
 
     (x_in, grad_in), (wu, wd), shared_out, shared_dx, shared_grads = dispatch(
         hot,

time: 987 us -> 969 us (0.982)
  Pallas kernels: 848 us -> 831 us
    pallas_call x2 -> x1, Pallas kernels: 273 us -> 256 us  [forward_exchange(): pl.pallas_call(kernel, out_shape=kept + [sds((8, width), F32), sds((8, wi...]
where the time goes in v12:
time: 969 us; the launch traced here: 959 us
  Pallas kernels  831 us (86%)
  local copies, waits for them, and re-layouts  75.7 us (8%)
  other arithmetic  32.4 us (3%)
  matrix products  17.8 us (2%)
    pallas_call x1, Pallas kernels, forward_exchange(): pl.pallas_call(kernel, out_shape=kept + [sds((8, width), F32), sds((8, wi...  256 us
    pallas_call x1, Pallas kernels, backward_exchange(): pl.pallas_call(kernel, out_shape=[sds((rows, width), F32), sds((8, width)...  222 us
    pallas_call x1, Pallas kernels, dispatch(): pl.pallas_call(kernel, out_shape=[sds((chips, per_far, width), BF)] * 2 +...  137 us
    pallas_call x1, Pallas kernels, experts_run(): pl.pallas_call(kernel, out_shape=[blocks, dots, blocks, ExpertsBack.out(t...  111 us
    pallas_call x1, Pallas kernels, column_sum(): pl.pallas_call(kernel, out_shape=[jax.ShapeDtypeStruct(shape, F32)] + [ja...  105 us

profile of v12, /device:TPU:11, one launch (start us, length us, event | category | flops | bytes accessed | tf_op | source)
XLA Modules:
  0.0 959.2 jit_solution(7588798963979964182)
XLA Ops:
  9.7 1.6 concatenate.31.refs_2_
  11.3 0.9 copy.232
  15.1 1.0 copy_bitcast_fusion.1
  16.4 1.0 copy.197.refs_9_
  21.0 1.2 reshape.612.refs_7_
  22.5 1.0 copy.196.refs_8_
  23.5 3.0 multiply_sine_fusion
  26.5 255.8 %shard_map.324 = (bf16[1024,2048]{1,0:T(8,128)(2,1)}, f32[1024,640]{1,0:T(8,128)}, bf16[1024,512]{1,0:T(8,128)(2,1)}, bf16[2,1024,256]{2,1,0:T(8,128)(2,1)}, bf1...) custom-call(bf16[128,2048]{1,0:T(8,128)(2,1)} %refs_16_.1, ...), custom_call_target="tpu_custom_call" | custom-call | tf_op jit(solution)/shard_map/pallas_call | solution.py:889
  282.3 1.4 multiply_reduce_fusion.3
  284.2 1.3 slice.351.refs_18_
  286.4 1.4 slice.350.refs_17_
  287.8 1.7 constant_dynamic-slice_fusion.2.refs_15_
  289.5 1.2 dynamic-slice_bitcast_fusion
  291.0 1.3 slice_bitcast_fusion
  294.8 1.2 slice.332
  297.7 2.3 fusion.10.hot_ref
  300.0 1.4 fusion.5
  301.4 1.3 slice_multiply_fusion.3
  302.7 136.8 %shard_map.325 = (bf16[4,256,2048]{2,1,0:T(8,128)(2,1)}, bf16[4,256,2048]{2,1,0:T(8,128)(2,1)}, bf16[8,4,64,1408]{3,2,1,0:T(8,128)(2,1)}, bf16[8,4,64,1408]{3,2,...) custom-call(bf16[1024,512]{1,0:T(8,128)(2,1)} %fusion.10.hot_ref, ...), custom_call_target="tpu_custom_call" | custom-call | tf_op jit(solution)/shard_map/pallas_call | solution.py:1033
  439.5 110.6 %shard_map.326 = (bf16[4,256,2048]{2,1,0:T(8,128)(2,1)}, bf16[4,256,128]{2,1,0:T(8,128)(2,1)}, bf16[4,256,2048]{2,1,0:T(8,128)(2,1)}, bf16[1,2,8,64,1408]{4,3,2,...) custom-call(bf16[1024,2048]{1,0:T(8,128)(2,1)} %bitcast.160, ...), custom_call_target="tpu_custom_call" | custom-call | tf_op jit(solution)/shard_map/pallas_call | solution.py:1180
  550.1 6.4 add_convert_fusion.1
  556.5 1.1 copy.221
  557.6 1.6 multiply_reduce_fusion
  559.2 1.0 add_convert_fusion.3
  560.9 3.6 concatenate.33.x_hbm
  564.6 105.0 %shard_map.327 = (f32[128,2176]{1,0:T(8,128)}, bf16[4,64,704]{2,1,0:T(8,128)(2,1)}, bf16[4,64,704]{2,1,0:T(8,128)(2,1)}, bf16[4,64,704]{2,1,0:T(8,128)(2,1)}, bf...) custom-call(bf16[4,128,2176]{2,1,0:T(8,128)(2,1)} %concatenate.33.x_hbm, ...), custom_call_target="tpu_custom_call" | custom-call | tf_op jit(solution)/shard_map/pallas_call | solution.py:309
  669.6 7.2 add_convert_fusion
  676.8 1.0 multiply_reduce_fusion.4
  677.8 1.2 convolution_convert_fusion
  679.0 2.4 multiply_reduce_fusion.1
  681.5 1.2 fusion.44
  682.9 1.0 pad.29.refs_20_
  683.9 1.3 copy.205
  685.2 1.3 copy.206
  686.5 1.3 copy.210.refs_19_
  687.8 222.4 %shard_map.328 = (f32[128,2048]{1,0:T(8,128)}, f32[8,2048]{1,0:T(8,128)}, f32[64,640]{1,0:T(8,128)}, bf16[4,8,64,512]{3,2,1,0:T(8,128)(2,1)}, bf16[4,8,64,512]{3...) custom-call(bf16[128,2048]{1,0:T(8,128)(2,1)} %get-tuple-element.215, ...), custom_call_target="tpu_custom_call" | custom-call | tf_op jit(solution)/shard_map/pallas_call | solution.py:1670
  910.3 2.1 convert_reduce_fusion.1
  912.9 1.0 copy.217
  913.9 1.0 fusion.62
  919.1 1.2 reshape.649
  920.8 1.4 reshape.664
  922.8 1.4 reshape.666
  924.7 1.4 reshape.668
  937.2 2.3 concatenate.35
  948.1 3.0 convert.39
  951.4 2.9 convert.38
  954.4 2.9 convert.40
  957.3 1.0 copy.267
  (214 shorter events, 48.8 us)
Async XLA Ops:
  0.6 13.5 %copy-start.19 = (bf16[64,2816]{1,0:T(8,128)(2,1)S(1)}, bf16[64,2816]{1,0:T(8,128)(2,1)}, u32[]{:S(2)}) copy-start(bf16[64,2816]{1,0:T(8,128)(2,1)} %param.35) | copy-start | bytes 1081348
  0.7 12.2 %copy-start.18 = (bf16[64,2816]{1,0:T(8,128)(2,1)S(1)}, bf16[64,2816]{1,0:T(8,128)(2,1)}, u32[]{:S(2)}) copy-start(bf16[64,2816]{1,0:T(8,128)(2,1)} %param.34) | copy-start | bytes 1081348
  3.0 290.4 %copy-start.27 = (pred[16]{0:T(512)(128)(4,1)}, pred[16]{0:T(512)(128)(4,1)S(1)}, u32[]{:S(2)}) copy-start(pred[16]{0:T(512)(128)(4,1)S(1)} %get-tuple-element.283) | copy-start | bytes 52
  3.0 290.4 %copy-start.28 = (pred[16]{0:T(512)(128)(4,1)}, pred[16]{0:T(512)(128)(4,1)S(1)}, u32[]{:S(2)}) copy-start(pred[16]{0:T(512)(128)(4,1)S(1)} %get-tuple-element.284) | copy-start | bytes 52
  8.8 5.8 copy-start.20
  13.4 2.7 copy-start.13
  15.1 2.3 copy-start.14
  18.8 1.5 copy-start.21
  19.3 2.8 copy-start.2
  283.7 8.6 copy-start.30
  289.5 2.8 copy-start.1
  564.5 105.0 %copy-start.22 = (bf16[512,256]{1,0:T(8,128)(2,1)S(1)}, bf16[512,256]{1,0:T(8,128)(2,1)}, u32[]{:S(2)}) copy-start(bf16[512,256]{1,0:T(8,128)(2,1)} %get-tuple-element.225) | copy-start | bytes 786436
  564.5 105.0 %copy-start.23 = (bf16[512,256]{1,0:T(8,128)(2,1)S(1)}, bf16[512,256]{1,0:T(8,128)(2,1)}, u32[]{:S(2)}) copy-start(bf16[512,256]{1,0:T(8,128)(2,1)} %get-tuple-element.226) | copy-start | bytes 786436
  564.6 105.0 %copy-start.24 = (bf16[512,256]{1,0:T(8,128)(2,1)S(1)}, bf16[512,256]{1,0:T(8,128)(2,1)}, u32[]{:S(2)}) copy-start(bf16[512,256]{1,0:T(8,128)(2,1)} %get-tuple-element.227) | copy-start | bytes 786436
  564.6 105.0 %copy-start.25 = (bf16[512,256]{1,0:T(8,128)(2,1)S(1)}, bf16[512,256]{1,0:T(8,128)(2,1)}, u32[]{:S(2)}) copy-start(bf16[512,256]{1,0:T(8,128)(2,1)} %get-tuple-element.228) | copy-start | bytes 786436
  669.6 9.4 copy-start
  669.6 9.4 copy-start.29
  676.8 4.6 copy-start.31
  676.8 4.6 copy-start.3
  912.6 5.6 copy-start.8
  919.0 1.2 copy-start.17
  920.2 2.0 copy-start.16
  922.2 2.0 copy-start.15
  924.2 2.0 copy-start.7
  926.5 7.4 copy-start.10
  926.5 8.7 copy-start.11
  926.6 10.0 %copy-start.12 = (f32[64,512]{1,0:T(8,128)}, f32[64,512]{1,0:T(8,128)S(1)}, u32[]{:S(2)}) copy-start(f32[64,512]{1,0:T(8,128)S(1)} %get-tuple-element.224) | copy-start | bytes 393220
  927.9 20.1 %copy-start.6 = (bf16[1,2,8,64,1408]{4,3,2,1,0:T(8,128)(2,1)S(1)}, bf16[1,2,8,64,1408]{4,3,2,1,0:T(8,128)(2,1)}, u32[]{:S(2)}) copy-start(bf16[1,2,8,64,1408]{4,3,2,1,0:T(8,128)(2,1)} %get-tuple-element.120) | copy-start | bytes 8650756
  948.0 3.0 copy-start.32
  948.1 3.3 copy-start.5
  951.4 3.0 copy-start.4
  954.4 2.9 copy-start.9
  957.3 1.1 copy-start.26

commit v13 on v12

--- a/solution.py
+++ b/solution.py
@@ -1,5 +1,6 @@
 import jax
 import jax.numpy as jnp
+import numpy as np
 from jax import lax
 from jax.experimental import pallas as pl
 from jax.experimental.pallas import tpu as pltpu
@@ -240,6 +241,11 @@
                 near[i, m].start()
         for back in backs:
             back.begin()
+        moves[0].wait()
+        relay.begin()
+        for back in backs:
+            back.pass_on()
+        relay.run()
         for i in range(1, chips):
             copy = remote(
                 r_ref.at[i], r_out.at[i], r_s.at[i], r_r.at[i], same_core[chips - i - 1]
@@ -249,8 +255,6 @@
         copy = pltpu.make_async_copy(r_ref.at[0], r_out.at[0], local)
         copy.start()
         rows_back.append(copy)
-        moves[0].wait()
-        relay.run()
 
         def pair(i, m):
             chip = lax.rem(c + i, chips)
@@ -264,8 +268,6 @@
 
             lax.fori_loop(0, n_dp, row, 0)
 
-        for back in backs:
-            back.pass_on()
         for move in moves[1:]:
             move.wait()
         for i in range(1, chips):
@@ -405,16 +407,18 @@
             (mine - 1 == t, last, inner),
         ]
 
-    def hop(self, t, step, start):
+    def hop(self, t, step, start, edge):
         for active, first, slot in self.routes(t, step):
+            if edge:
+                pl.when(jnp.logical_and(active, first))(
+                    lambda slot=slot: self.copy(t, self.blocks.at[t], slot, step).start()
+                )
+                continue
 
             @pl.when(jnp.logical_and(active, first))
             def _(slot=slot):
-                copy = self.copy(t, self.blocks.at[t], slot, step)
-                if start:
-                    copy.start()
-                else:
-                    copy.wait_send()
+                if not start:
+                    self.copy(t, self.blocks.at[t], slot, step).wait_send()
 
             @pl.when(jnp.logical_and(active, jnp.logical_not(first)))
             def _(slot=slot):
@@ -427,16 +431,22 @@
                 else:
                     copy.wait_send()
 
+    def begin(self):
+        for t in range(self.inner - 1, 0, -1):
+            self.hop(t, 1, True, True)
+        for t in range(self.inner - 1):
+            self.hop(t, -1, True, True)
+
     def run(self):
         inner = self.inner
 
         def up():
             for t in range(inner - 1, 0, -1):
-                self.hop(t, 1, True)
+                self.hop(t, 1, True, False)
 
         def down():
             for t in range(inner - 1):
-                self.hop(t, -1, True)
+                self.hop(t, -1, True, False)
 
         @pl.when(self.mine < inner // 2)
         def _():
@@ -464,9 +474,9 @@
     def end(self):
         for t in range(self.inner):
             if t:
-                self.hop(t, 1, False)
+                self.hop(t, 1, False, False)
             if t < self.inner - 1:
-                self.hop(t, -1, False)
+                self.hop(t, -1, False, False)
 
 
 def stage(sources, targets, sems):
@@ -1064,8 +1074,8 @@
     def kernel(*refs):
         in_hbm, refs = refs[:6], refs[6:]
         dx_out, dots_out, rows_out, back_out, g_out, refs = *refs[:4], refs[4:6], refs[6:]
-        x_v, s_v, wg, wu, wd, route, a_v, b_v, h_v, dx_v, total, stage, dots_v = refs[:13]
-        loads, send, recv, d_send, d_recv, local, rows_sem, out_sem = refs[13:21]
+        x_v, s_v, wg, wu, wd, route, a_v, b_v, h_v, dx_v, total, stage, dots_v, g_v = refs[:14]
+        loads, send, recv, d_send, d_recv, local, rows_sem, out_sem = refs[14:22]
         z, e, c, k, sibling, same_core, column = places(n_dp, n_ex)
         moves = [
             pltpu.make_async_copy(src, dst, loads.at[j])
@@ -1074,7 +1084,7 @@
         for j in (5, 0, 2, 3, 4, 1):
             moves[j].start()
         greet(same_core + [sibling] + column + [(device[0], sibling[1]) for device in column])
-        back = ExpertsBack(total, back_out, refs[21:], n_dp, n_ex, inner)
+        back = ExpertsBack(total, back_out, refs[22:], n_dp, n_ex, inner, True)
         expert = c * inner + lax.rem(z, inner)
         for j in (5, 0, 2, 3, 4, 1):
             moves[j].wait()
@@ -1094,16 +1104,35 @@
             b_v[at, :] = second.astype(BF)
             hid = (silu_parts(first)[0] * second).astype(BF)
             h_v[at, :] = hid
-            rows = mm_cols(hid, wd[...]).astype(BF)
+            g_v[at, :] = s_v[at, :]
+            s_v[at, :] = (gate * s_v[at, :].astype(F32)).astype(BF)
+            return carry
+
+        lax.fori_loop(0, chips, forward, 0)
+
+        for j in range(n_ex // 2):
+            at = pl.ds(pl.multiple_of(((1 - k) * (n_ex // 2) + j) * span, span), span)
+            block = mm_rows(s_v[:, at], h_v[...]).astype(BF)
+            total[j] = block.reshape(n_dp, r, ff)
+            back.near(j).start()
+        for j in range(n_ex // 2):
+            at = pl.ds(pl.multiple_of((k * (n_ex // 2) + j) * span, span), span)
+            block = mm_rows(s_v[:, at], h_v[...]).astype(BF)
+            back.own[j] = block.reshape(n_dp, r, ff)
+        back.pass_on()
+
+        def rows_of(i, carry):
+            at = pl.ds(pl.multiple_of(i * tile, tile), tile)
+            rows = mm_cols(h_v[at, :], wd[...]).astype(BF)
             dx_v[i] = rows
-            grad = s_v[at, :].astype(F32)
-            dots = jnp.sum(grad * rows.astype(F32), axis=-1, keepdims=True)
+            dots = jnp.sum(
+                g_v[at, :].astype(F32) * rows.astype(F32), axis=-1, keepdims=True
+            )
             dots_v[i] = jnp.broadcast_to(dots, (tile, 128)).astype(BF)
-            s_v[at, :] = (gate * grad).astype(BF)
             pltpu.make_async_copy(dx_v.at[i], rows_out.at[i], rows_sem.at[i]).start()
             return carry
 
-        lax.fori_loop(0, chips, forward, 0)
+        lax.fori_loop(0, chips, rows_of, 0)
         dot_copies = []
         for i in range(1, chips):
             copy = remote(
@@ -1114,16 +1143,6 @@
         copy = pltpu.make_async_copy(dots_v.at[0], dots_out.at[0], local.at[0])
         copy.start()
         dot_copies.append(copy)
-
-        def down_rows(t, carry):
-            j = lax.rem(t + (1 - k) * (n_ex // 2), n_ex)
-            at = pl.ds(pl.multiple_of(j * span, span), span)
-            block = mm_rows(s_v[:, at], h_v[...]).astype(BF)
-            total[j] = block.reshape(n_dp, r, ff)
-            return carry
-
-        lax.fori_loop(0, n_ex, down_rows, 0)
-        back.begin()
 
         def hidden_rows(i, carry):
             at = pl.ds(pl.multiple_of(i * tile, tile), tile)
@@ -1135,7 +1154,6 @@
             return carry
 
         lax.fori_loop(0, chips, hidden_rows, 0)
-        back.pass_on()
         copies = []
         for i in list(range(1, chips)) + [0]:
             at = slice(i * per_far, (i + 1) * per_far)
@@ -1188,9 +1206,10 @@
         + [vmem((n_slots, ff), BF)] * 3
         + [
             vmem(blocks.shape, BF),
-            vmem(total.shape, BF),
+            vmem((n_ex // 2,) + total.shape[1:], BF),
             vmem((2, n_dp, r, ff), BF),
             vmem(dots.shape, BF),
+            vmem((n_slots, width), BF),
             dma((6,)),
         ]
         + [dma((chips,))] * 4
@@ -1222,15 +1241,15 @@
         n_ex, _, r, ff = total.shape
         return jax.ShapeDtypeStruct((n_dp // inner, 2, n_ex, r, ff), BF)
 
-    def __init__(self, total, out, scratch, n_dp, n_ex, inner):
-        self.total, self.out, self.n_dp, self.inner = total, out, n_dp, inner
+    def __init__(self, total, out, scratch, n_dp, n_ex, inner, halved=False):
+        self.total, self.out, self.n_dp, self.inner, self.halved = total, out, n_dp, inner, halved
         self.own, self.sib, self.near_s, self.near_r, self.load, self.send, self.recv = scratch
         self.z, self.e, self.c, self.k, self.sibling, _, _ = places(n_dp, n_ex)
         self.hh = n_ex // 2
 
     def near(self, j):
         return remote(
-            self.total.at[(1 - self.k) * self.hh + j], self.sib.at[j],
+            self.total.at[j if self.halved else (1 - self.k) * self.hh + j], self.sib.at[j],
             self.near_s.at[j], self.near_r.at[j], self.sibling,
         )
 
@@ -1266,7 +1285,8 @@
     def pass_on(self):
         for j in range(self.hh):
             self.near(j).wait_recv()
-            self.loads(j).wait()
+            if not self.halved:
+                self.loads(j).wait()
             for d in range(self.n_dp):
                 self.own[j, d] = (
                     self.own[j, d].astype(F32) + self.sib[j, d].astype(F32)
@@ -1325,7 +1345,7 @@
     we_cols = rl * we.shape[1] // r
     head_cols = wq_cols + we_cols
     given_arrays = [*attend, hidden, latent_low, *own]
-    big = [j for j, array in enumerate(given_arrays) if array.shape[0] > 1]
+    big = [j for j, array in enumerate(given_arrays) if array.shape[0] > 8 or array.ndim > 2]
 
     def kernel(*refs):
         grad_ref, given, refs = refs[0], list(refs[1:22]), refs[22:]
@@ -1349,6 +1369,7 @@
             given[j] = ref
         att_in, hidden_ref, low_ref = given[:11], given[11], given[12]
         wl_ref, lat_ref, tok_ref, gain_ref, glat_ref, gnat_ref, router_ref, gtwo_ref = given[13:]
+        gain_ref, glat_ref = gain_ref.at[0:1], glat_ref.at[2:3]
         x_refs = (gbuf, part_l)
         group = column_group(lax.axis_index("dp"), lax.axis_index("expert"), inner)
         z, e, c, k, sibling, same_core, column = places(n_dp, n_ex)
@@ -1690,6 +1711,49 @@
     return outs[:3], outs[4], outs[5], outs[6], outs[7:10], outs[10:]
 
 
+def heads_together(got, order, hp, rl, wq_cols):
+    n_dp, n_ex, r, cols = got.shape
+    we_cols = cols - wq_cols
+    count = len(order)
+    per = (DH + DV) // we_cols
+
+    def kernel(x_ref, q_ref, e_ref):
+        for pair in range(count // 2):
+            pieces = []
+            for h in (2 * pair, 2 * pair + 1):
+                device, i = order[h] // hp, order[h] % hp
+                total = x_ref[0, device].astype(F32)
+                for d in range(1, n_dp):
+                    total = total + x_ref[d, device].astype(F32)
+                rope = total[:, hp * DH : hp * DH + 2 * DR]
+                pieces.append((total[:, i * DH : (i + 1) * DH], rope, i))
+                for j in range(per):
+                    at = (h * per + j) * we_cols
+                    e_ref[:, at : at + we_cols] = total[
+                        (i * per + j) * rl : (i * per + j + 1) * rl, wq_cols:
+                    ]
+            (plain, rope, i), (plain_b, rope_b, i_b) = pieces
+            lane = lax.broadcasted_iota(jnp.int32, plain.shape, 1)
+            rope = pltpu.roll(rope, DR, 1) if i else rope
+            rope_b = rope_b if i_b else pltpu.roll(rope_b, DR, 1)
+            turned = pltpu.roll(plain_b, DR, 1)
+            at = pair * 2 * (DH + DR)
+            q_ref[:, at : at + DH] = plain
+            q_ref[:, at + DH : at + 2 * DH] = jnp.where(lane < DR, rope, turned)
+            q_ref[:, at + 2 * DH : at + 3 * DH] = jnp.where(lane < DR, turned, rope_b)
+
+    return pl.pallas_call(
+        kernel,
+        out_shape=[
+            jax.ShapeDtypeStruct((r, count * (DH + DR)), F32),
+            jax.ShapeDtypeStruct((rl, count * (DH + DV)), F32),
+        ],
+        in_specs=[VMEM],
+        out_specs=[VMEM] * 2,
+        compiler_params=pltpu.CompilerParams(vmem_limit_bytes=40 << 20),
+    )(got)
+
+
 def shards(
     tokens,
     cotangent,
@@ -1789,9 +1853,9 @@
     gains = jnp.pad(gains, ((0, 13), (0, 0)))
 
     positions = jnp.arange(seq)
-    lane = jnp.arange(2 * DR) % (DR // 2)
-    angles = positions.astype(F32)[:, None] * (10000.0 ** (-(lane.astype(F32) * 2.0) / DR))[None, :]
-    cos_wide, sine_wide = jnp.cos(angles), jnp.sin(angles)
+    lane = np.arange(2 * DR) % (DR // 2)
+    angles = np.arange(seq)[:, None] * (10000.0 ** (-2.0 * lane / DR))[None, :]
+    cos_wide, sine_wide = (jnp.asarray(f(angles), F32) for f in (np.cos, np.sin))
     keep = (positions < lengths[0]).astype(F32)[None]
     attend_out, (wq, wexp, wo_rows, pk_all), gain_outs, rows_outs, (wg,), shared_w = (
         forward_exchange(
@@ -1812,7 +1876,7 @@
         )
     )
     residual, x_col, cot_col = rows_outs
-    gain_one, gain_two, gain_lat = (out[j] for j, out in enumerate(gain_outs))
+    gain_two = gain_outs[1][1]
     hidden_one, latent_raw, latent_low, qcat, kcat, value, lse, attended = attend_out
     wo_rows = wo_rows.reshape(hp * DV, width)
     cot_col = cot_col.reshape(inner * rows, width)
@@ -1933,8 +1997,8 @@
                 pk_flat,
                 latent_own,
                 tokens,
-                gain_one[None],
-                gain_lat[None],
+                gain_outs[0],
+                gain_outs[2],
                 from_owner_order(grad_residual),
                 router_back,
                 grad_gain_two[None],
@@ -1953,17 +2017,7 @@
         return jnp.sum(values.astype(F32), axis=0)
 
     out_tokens = from_owner_order((residual + added(out_got)).astype(BF))
-    heads_all = added(heads_got)
-    wq_parts, we_parts = [], []
-    for h in heads_back:
-        block, i = heads_all[h // hp], h % hp
-        wq_parts.append(block[:, i * DH : (i + 1) * DH])
-        wq_parts.append(block[:, hp * DH + i * DR : hp * DH + (i + 1) * DR])
-        per = (DH + DV) // we_cols
-        for j in range(i * per, (i + 1) * per):
-            we_parts.append(block[j * rl : (j + 1) * rl, head_cols:])
-    sum_wq = jnp.concatenate(wq_parts, axis=1)
-    sum_we = jnp.concatenate(we_parts, axis=1)
+    sum_wq, sum_we = heads_together(heads_got, heads_back, hp, rl, head_cols)
     sum_wout = from_owner_order(added(wout_got))
     device = z * n_ex + e
     sum_gain_one = lax.dynamic_slice_in_dim(vec_sum[0], device * r, r, 0)

time: 969 us -> 1010 us (1.042)
  Pallas kernels: 831 us -> 904 us
  local copies, waits for them, and re-layouts: 75.7 us -> 50.4 us
    pallas_call x1, Pallas kernels: 105 us -> 189 us  [column_sum(): pl.pallas_call(kernel, out_shape=[jax.ShapeDtypeStruct(shape, F32)] + [ja...]
    slice x19 -> x1, local copies, waits for them, and re-layouts: 14.2 us -> 0.85 us  [shards(): gain_two = gain_outs[1][1]]
where the time goes in v13:
time: 1010 us
  Pallas kernels  904 us (90%)
  local copies, waits for them, and re-layouts  50.4 us (5%)
  other arithmetic  30.9 us (3%)
  matrix products  18.2 us (2%)
    pallas_call x1, Pallas kernels, forward_exchange(): pl.pallas_call(kernel, out_shape=kept + [sds((8, width), F32), sds((8, wi...  256 us
    pallas_call x1, Pallas kernels, backward_exchange(): pl.pallas_call(kernel, out_shape=[sds((rows, width), F32), sds((8, width)...  220 us
    pallas_call x1, Pallas kernels, column_sum(): pl.pallas_call(kernel, out_shape=[jax.ShapeDtypeStruct(shape, F32)] + [ja...  189 us
    pallas_call x1, Pallas kernels, dispatch(): pl.pallas_call(kernel, out_shape=[sds((chips, per_far, width), BF)] * 2 +...  137 us
    pallas_call x1, Pallas kernels, experts_run(): pl.pallas_call(kernel, out_shape=[blocks, dots, blocks, ExpertsBack.out(t...  101 us

profile of v13, /device:TPU:11, one launch (start us, length us, event | category | flops | bytes accessed | tf_op | source)
XLA Modules:
  0.0 1006.0 jit_solution(9012860490191333833)
XLA Ops:
  9.6 1.6 concatenate.25.refs_2_
  11.2 0.9 copy.234
  15.1 1.0 copy_bitcast_fusion.1
  16.4 1.0 copy.199.refs_9_
  19.3 0.9 pad_maximum_fusion.refs_1_
  20.9 1.2 reshape.594.refs_7_
  22.4 1.0 copy.198.refs_8_
  23.4 255.8 %shard_map.342 = (bf16[1024,2048]{1,0:T(8,128)(2,1)}, f32[1024,640]{1,0:T(8,128)}, bf16[1024,512]{1,0:T(8,128)(2,1)}, bf16[2,1024,256]{2,1,0:T(8,128)(2,1)}, bf1...) custom-call(bf16[128,2048]{1,0:T(8,128)(2,1)} %refs_16_.1, ...), custom_call_target="tpu_custom_call" | custom-call | tf_op jit(solution)/shard_map/pallas_call | solution.py:899
  279.3 1.4 multiply_reduce_fusion.3
  282.0 1.7 constant_dynamic-slice_fusion.2.refs_15_
  283.8 1.2 dynamic-slice_bitcast_fusion
  285.3 1.3 slice_bitcast_fusion
  288.2 0.9 pad.28.refs_5_
  289.1 1.2 slice.102
  291.1 0.8 slice_reduce_fusion.5
  292.0 2.3 fusion.10.hot_ref
  294.2 1.4 fusion.5
  295.6 1.3 slice_multiply_fusion.3
  296.9 136.8 %shard_map.343 = (bf16[4,256,2048]{2,1,0:T(8,128)(2,1)}, bf16[4,256,2048]{2,1,0:T(8,128)(2,1)}, bf16[8,4,64,1408]{3,2,1,0:T(8,128)(2,1)}, bf16[8,4,64,1408]{3,2,...) custom-call(bf16[1024,512]{1,0:T(8,128)(2,1)} %fusion.10.hot_ref, ...), custom_call_target="tpu_custom_call" | custom-call | tf_op jit(solution)/shard_map/pallas_call | solution.py:1043
  433.8 101.0 %shard_map.344 = (bf16[4,256,2048]{2,1,0:T(8,128)(2,1)}, bf16[4,256,128]{2,1,0:T(8,128)(2,1)}, bf16[4,256,2048]{2,1,0:T(8,128)(2,1)}, bf16[1,2,8,64,1408]{4,3,2,...) custom-call(bf16[1024,2048]{1,0:T(8,128)(2,1)} %bitcast.144, ...), custom_call_target="tpu_custom_call" | custom-call | tf_op jit(solution)/shard_map/pallas_call | solution.py:1198
  534.7 6.8 add_convert_fusion.1
  541.5 1.1 copy.223
  542.6 1.6 multiply_reduce_fusion
  544.3 1.0 add_convert_fusion.3
  546.0 3.6 concatenate.27.x_hbm
  549.6 188.9 %shard_map.345 = (f32[128,2176]{1,0:T(8,128)}, bf16[4,64,704]{2,1,0:T(8,128)(2,1)}, bf16[4,64,704]{2,1,0:T(8,128)(2,1)}, bf16[4,64,704]{2,1,0:T(8,128)(2,1)}, bf...) custom-call(bf16[4,128,2176]{2,1,0:T(8,128)(2,1)} %concatenate.27.x_hbm, ...), custom_call_target="tpu_custom_call" | custom-call | tf_op jit(solution)/shard_map/pallas_call | solution.py:311
  738.6 7.2 add_convert_fusion
  745.8 1.0 multiply_reduce_fusion.4
  746.8 1.2 convolution_convert_fusion
  748.0 2.4 multiply_reduce_fusion.1
  750.4 1.2 fusion.39
  751.9 1.0 pad.29.refs_20_
  752.9 1.3 copy.207
  754.2 1.3 copy.208
  755.5 1.3 copy.212.refs_19_
  756.8 220.2 %shard_map.346 = (f32[128,2048]{1,0:T(8,128)}, f32[8,2048]{1,0:T(8,128)}, f32[64,640]{1,0:T(8,128)}, bf16[4,8,64,512]{3,2,1,0:T(8,128)(2,1)}, bf16[4,8,64,512]{3...) custom-call(bf16[128,2048]{1,0:T(8,128)(2,1)} %get-tuple-element.219, ...), custom_call_target="tpu_custom_call" | custom-call | tf_op jit(solution)/shard_map/pallas_call | solution.py:1691
  977.0 2.1 convert_reduce_fusion
  979.6 1.0 copy.219
  980.7 1.0 fusion.41
  985.1 1.2 reshape.631
  986.8 1.4 reshape.646
  988.8 1.4 reshape.648
  990.7 1.4 reshape.650
  992.1 1.2 shard_map.347
  993.3 4.9 convert.39
  998.2 2.9 convert.38
  1001.2 2.9 convert.40
  1004.1 1.0 copy.238
  (149 shorter events, 25.5 us)
Async XLA Ops:
  0.6 13.5 %copy-start.15 = (bf16[64,2816]{1,0:T(8,128)(2,1)S(1)}, bf16[64,2816]{1,0:T(8,128)(2,1)}, u32[]{:S(2)}) copy-start(bf16[64,2816]{1,0:T(8,128)(2,1)} %param.37) | copy-start | bytes 1081348
  0.7 12.2 %copy-start.14 = (bf16[64,2816]{1,0:T(8,128)(2,1)S(1)}, bf16[64,2816]{1,0:T(8,128)(2,1)}, u32[]{:S(2)}) copy-start(bf16[64,2816]{1,0:T(8,128)(2,1)} %param.36) | copy-start | bytes 1081348
  3.0 284.6 %copy-start.23 = (pred[16]{0:T(512)(128)(4,1)}, pred[16]{0:T(512)(128)(4,1)S(1)}, u32[]{:S(2)}) copy-start(pred[16]{0:T(512)(128)(4,1)S(1)} %get-tuple-element.245) | copy-start | bytes 52
  3.0 284.6 %copy-start.24 = (pred[16]{0:T(512)(128)(4,1)}, pred[16]{0:T(512)(128)(4,1)S(1)}, u32[]{:S(2)}) copy-start(pred[16]{0:T(512)(128)(4,1)S(1)} %get-tuple-element.246) | copy-start | bytes 52
  8.8 5.8 copy-start.16
  13.3 2.7 copy-start.9
  15.1 2.3 copy-start.10
  18.7 1.5 copy-start.17
  19.3 2.8 copy-start.4
  280.7 5.9 copy-start.26
  283.8 2.8 copy-start.2
  549.6 188.9 %copy-start.18 = (bf16[512,256]{1,0:T(8,128)(2,1)S(1)}, bf16[512,256]{1,0:T(8,128)(2,1)}, u32[]{:S(2)}) copy-start(bf16[512,256]{1,0:T(8,128)(2,1)} %get-tuple-element.221) | copy-start | bytes 786436
  549.6 189.0 %copy-start.19 = (bf16[512,256]{1,0:T(8,128)(2,1)S(1)}, bf16[512,256]{1,0:T(8,128)(2,1)}, u32[]{:S(2)}) copy-start(bf16[512,256]{1,0:T(8,128)(2,1)} %get-tuple-element.222) | copy-start | bytes 786436
  549.6 189.0 %copy-start.20 = (bf16[512,256]{1,0:T(8,128)(2,1)S(1)}, bf16[512,256]{1,0:T(8,128)(2,1)}, u32[]{:S(2)}) copy-start(bf16[512,256]{1,0:T(8,128)(2,1)} %get-tuple-element.223) | copy-start | bytes 786436
  549.6 189.0 %copy-start.21 = (bf16[512,256]{1,0:T(8,128)(2,1)S(1)}, bf16[512,256]{1,0:T(8,128)(2,1)}, u32[]{:S(2)}) copy-start(bf16[512,256]{1,0:T(8,128)(2,1)} %get-tuple-element.224) | copy-start | bytes 786436
  738.6 9.4 copy-start.1
  738.6 9.4 copy-start.25
  745.8 4.6 copy-start.27
  745.8 4.6 copy-start.3
  979.3 4.1 copy-start.22
  979.3 4.8 copy-start.7
  985.0 1.2 copy-start.13
  986.2 2.0 copy-start.12
  988.2 2.0 copy-start.11
  990.2 2.0 copy-start
  993.3 4.9 copy-start.6
  998.2 3.0 copy-start.5
  1001.2 2.9 copy-start.8

commit v14 on v13

--- a/solution.py
+++ b/solution.py
@@ -243,9 +243,9 @@
             back.begin()
         moves[0].wait()
         relay.begin()
+        relay.run()
         for back in backs:
             back.pass_on()
-        relay.run()
         for i in range(1, chips):
             copy = remote(
                 r_ref.at[i], r_out.at[i], r_s.at[i], r_r.at[i], same_core[chips - i - 1]
@@ -1711,13 +1711,27 @@
     return outs[:3], outs[4], outs[5], outs[6], outs[7:10], outs[10:]
 
 
-def heads_together(got, order, hp, rl, wq_cols):
-    n_dp, n_ex, r, cols = got.shape
+def finish(heads, wout, out, residual, shared, order, hp, rl, wq_cols):
+    n_dp, n_ex, r, cols = heads.shape
     we_cols = cols - wq_cols
     count = len(order)
     per = (DH + DV) // we_cols
-
-    def kernel(x_ref, q_ref, e_ref):
+    width = wout.shape[2]
+    inner, _, ff = shared[0].shape
+
+    def natural(values, t):
+        tile = values[:, :128]
+        lane = lax.broadcasted_iota(jnp.int32, tile.shape, 1)
+        for p in range(128 // r):
+            at = t * (128 // r) + p
+            start = (at % n_ex * n_dp + at // n_ex) * r
+            piece = values[:, start // 128 * 128 : start // 128 * 128 + 128]
+            turn_by = (p * r - start) % 128
+            piece = pltpu.roll(piece, turn_by, 1) if turn_by else piece
+            tile = jnp.where(lane // r == p, piece, tile) if p else piece
+        return tile
+
+    def kernel(x_ref, w_ref, y_ref, res_ref, s_a, s_b, s_c, q_ref, e_ref, wo_ref, out_ref, *s_out):
         for pair in range(count // 2):
             pieces = []
             for h in (2 * pair, 2 * pair + 1):
@@ -1741,17 +1755,35 @@
             q_ref[:, at : at + DH] = plain
             q_ref[:, at + DH : at + 2 * DH] = jnp.where(lane < DR, rope, turned)
             q_ref[:, at + 2 * DH : at + 3 * DH] = jnp.where(lane < DR, turned, rope_b)
-
+        total = w_ref[0].astype(F32)
+        for d in range(1, n_dp):
+            total = total + w_ref[d].astype(F32)
+        for t in range(width // 128):
+            wo_ref[:, t * 128 : (t + 1) * 128] = natural(total, t)
+        total = res_ref[...]
+        for d in range(inner):
+            total = total + y_ref[d].astype(F32)
+        for t in range(width // 128):
+            out_ref[:, t * 128 : (t + 1) * 128] = natural(total, t).astype(BF)
+        for source, target in zip((s_a, s_b, s_c), s_out):
+            for j in range(inner):
+                total = source[j].astype(F32)
+                target[:, j * ff : (j + 1) * ff] = total
+
+    sds = jax.ShapeDtypeStruct
     return pl.pallas_call(
         kernel,
         out_shape=[
-            jax.ShapeDtypeStruct((r, count * (DH + DR)), F32),
-            jax.ShapeDtypeStruct((rl, count * (DH + DV)), F32),
-        ],
-        in_specs=[VMEM],
-        out_specs=[VMEM] * 2,
+            sds((r, count * (DH + DR)), F32),
+            sds((rl, count * (DH + DV)), F32),
+            sds((r, width), F32),
+            sds(residual.shape, BF),
+        ]
+        + [sds((r, inner * ff), F32)] * 3,
+        in_specs=[VMEM] * 7,
+        out_specs=[VMEM] * 7,
         compiler_params=pltpu.CompilerParams(vmem_limit_bytes=40 << 20),
-    )(got)
+    )(heads, wout, out, residual, *shared)
 
 
 def shards(
@@ -2016,17 +2048,18 @@
     def added(values):
         return jnp.sum(values.astype(F32), axis=0)
 
-    out_tokens = from_owner_order((residual + added(out_got)).astype(BF))
-    sum_wq, sum_we = heads_together(heads_got, heads_back, hp, rl, head_cols)
-    sum_wout = from_owner_order(added(wout_got))
+    outer = n_dp // inner
+    if outer > 1:
+        shared_got = [
+            added(got.reshape(outer, inner, r, ff_s)).astype(BF) for got in shared_got
+        ]
+    sum_wq, sum_we, sum_wout, out_tokens, sum_sgate, sum_sup, sum_sdown = finish(
+        heads_got, wout_got, out_got, residual, shared_got, heads_back, hp, rl, head_cols
+    )
     device = z * n_ex + e
     sum_gain_one = lax.dynamic_slice_in_dim(vec_sum[0], device * r, r, 0)
     sum_gain_two = lax.dynamic_slice_in_dim(vec_sum[1], (e * n_dp + z) * r, r, 0)
     sum_gain_lat = lax.dynamic_slice_in_dim(vec_sum[2], device * rl, rl, 0)
-    sum_sgate, sum_sup, sum_sdown = (
-        added(got.reshape(n_dp // inner, inner, r, ff_s)).transpose(1, 0, 2).reshape(r, -1)
-        for got in shared_got
-    )
     sum_egate, sum_eup, sum_edown = (
         added(back).reshape(-1, n_ex * r, ff_e) for back in (gate_back, up_back, down_back)
     )

time: 1010 us -> 956 us (0.947)
  Pallas kernels: 904 us -> 848 us
    pallas_call x1, Pallas kernels: 189 us -> 131 us  [column_sum(): pl.pallas_call(kernel, out_shape=[jax.ShapeDtypeStruct(shape, F32)] + [ja...]
where the time goes in v14:
time: 956 us; the launch traced here: 946 us
  Pallas kernels  848 us (89%)
  local copies, waits for them, and re-layouts  48.9 us (5%)
  other arithmetic  28.3 us (3%)
  matrix products  18 us (2%)
    pallas_call x1, Pallas kernels, forward_exchange(): pl.pallas_call(kernel, out_shape=kept + [sds((8, width), F32), sds((8, wi...  256 us
    pallas_call x1, Pallas kernels, backward_exchange(): pl.pallas_call(kernel, out_shape=[sds((rows, width), F32), sds((8, width)...  220 us
    pallas_call x1, Pallas kernels, dispatch(): pl.pallas_call(kernel, out_shape=[sds((chips, per_far, width), BF)] * 2 +...  137 us
    pallas_call x1, Pallas kernels, column_sum(): pl.pallas_call(kernel, out_shape=[jax.ShapeDtypeStruct(shape, F32)] + [ja...  131 us
    pallas_call x1, Pallas kernels, experts_run(): pl.pallas_call(kernel, out_shape=[blocks, dots, blocks, ExpertsBack.out(t...  101 us

profile of v14, /device:TPU:11, one launch (start us, length us, event | category | flops | bytes accessed | tf_op | source)
XLA Modules:
  0.0 945.9 jit_solution(16084062231224906303)
XLA Ops:
  9.6 1.6 concatenate.25.refs_2_
  11.2 0.9 copy.206
  15.1 1.0 copy_bitcast_fusion.1
  16.4 1.0 copy.159.refs_9_
  19.3 0.9 pad_maximum_fusion.refs_1_
  20.9 1.2 reshape.554.refs_7_
  22.4 1.0 copy.178.refs_8_
  23.4 255.8 %shard_map.342 = (bf16[1024,2048]{1,0:T(8,128)(2,1)}, f32[1024,640]{1,0:T(8,128)}, bf16[1024,512]{1,0:T(8,128)(2,1)}, bf16[2,1024,256]{2,1,0:T(8,128)(2,1)}, bf1...) custom-call(bf16[128,2048]{1,0:T(8,128)(2,1)} %refs_16_.1, ...), custom_call_target="tpu_custom_call" | custom-call | tf_op jit(solution)/shard_map/pallas_call | solution.py:899
  279.3 1.4 multiply_reduce_fusion.3
  282.0 1.7 constant_dynamic-slice_fusion.2.refs_15_
  283.8 1.2 dynamic-slice_bitcast_fusion
  285.3 1.3 slice_bitcast_fusion
  288.2 0.9 pad.28.refs_5_
  289.1 1.2 slice.102
  291.1 0.8 slice_reduce_fusion.5
  292.0 2.3 fusion.10.hot_ref
  294.2 1.4 fusion.5
  295.6 1.3 slice_multiply_fusion.3
  296.9 136.8 %shard_map.343 = (bf16[4,256,2048]{2,1,0:T(8,128)(2,1)}, bf16[4,256,2048]{2,1,0:T(8,128)(2,1)}, bf16[8,4,64,1408]{3,2,1,0:T(8,128)(2,1)}, bf16[8,4,64,1408]{3,2,...) custom-call(bf16[1024,512]{1,0:T(8,128)(2,1)} %fusion.10.hot_ref, ...), custom_call_target="tpu_custom_call" | custom-call | tf_op jit(solution)/shard_map/pallas_call | solution.py:1043
  433.8 101.2 %shard_map.344 = (bf16[4,256,2048]{2,1,0:T(8,128)(2,1)}, bf16[4,256,128]{2,1,0:T(8,128)(2,1)}, bf16[4,256,2048]{2,1,0:T(8,128)(2,1)}, bf16[1,2,8,64,1408]{4,3,2,...) custom-call(bf16[1024,2048]{1,0:T(8,128)(2,1)} %bitcast.131, ...), custom_call_target="tpu_custom_call" | custom-call | tf_op jit(solution)/shard_map/pallas_call | solution.py:1198
  535.0 6.5 add_convert_fusion.1
  541.5 1.1 copy.195
  542.6 1.6 multiply_reduce_fusion
  544.3 1.0 add_convert_fusion.2
  546.0 3.6 concatenate.27.x_hbm
  549.6 130.9 %shard_map.345 = (f32[128,2176]{1,0:T(8,128)}, bf16[4,64,704]{2,1,0:T(8,128)(2,1)}, bf16[4,64,704]{2,1,0:T(8,128)(2,1)}, bf16[4,64,704]{2,1,0:T(8,128)(2,1)}, bf...) custom-call(bf16[4,128,2176]{2,1,0:T(8,128)(2,1)} %concatenate.27.x_hbm, ...), custom_call_target="tpu_custom_call" | custom-call | tf_op jit(solution)/shard_map/pallas_call | solution.py:311
  680.6 7.2 add_convert_fusion
  687.8 1.0 multiply_reduce_fusion.4
  688.8 1.2 convolution_convert_fusion
  690.0 2.4 multiply_reduce_fusion.1
  692.5 1.2 fusion.39
  693.9 1.0 pad.29.refs_20_
  694.9 1.3 copy.186
  696.3 1.3 copy.187
  697.6 1.3 copy.191.refs_19_
  698.9 220.5 %shard_map.346 = (f32[128,2048]{1,0:T(8,128)}, f32[8,2048]{1,0:T(8,128)}, f32[64,640]{1,0:T(8,128)}, bf16[4,8,64,512]{3,2,1,0:T(8,128)(2,1)}, bf16[4,8,64,512]{3...) custom-call(bf16[128,2048]{1,0:T(8,128)(2,1)} %get-tuple-element.229, ...), custom_call_target="tpu_custom_call" | custom-call | tf_op jit(solution)/shard_map/pallas_call | solution.py:1691
  919.4 1.6 copy-done.1
  920.9 1.6 copy-done.2
  922.5 1.2 copy-done.3
  923.8 1.0 copy-done.4
  924.8 1.0 copy-done.5
  925.8 1.0 copy-done.6
  926.8 3.0 shard_map.347
  929.8 1.0 fusion.41
  933.2 4.9 convert.33
  938.1 2.9 convert.32
  941.1 2.9 convert.34
  944.0 1.0 copy.210
  (133 shorter events, 22.5 us)
Async XLA Ops:
  0.6 13.5 %copy-start.16 = (bf16[64,2816]{1,0:T(8,128)(2,1)S(1)}, bf16[64,2816]{1,0:T(8,128)(2,1)}, u32[]{:S(2)}) copy-start(bf16[64,2816]{1,0:T(8,128)(2,1)} %param.37) | copy-start | bytes 1081348
  0.7 12.2 %copy-start.15 = (bf16[64,2816]{1,0:T(8,128)(2,1)S(1)}, bf16[64,2816]{1,0:T(8,128)(2,1)}, u32[]{:S(2)}) copy-start(bf16[64,2816]{1,0:T(8,128)(2,1)} %param.36) | copy-start | bytes 1081348
  3.0 284.6 %copy-start.24 = (pred[16]{0:T(512)(128)(4,1)}, pred[16]{0:T(512)(128)(4,1)S(1)}, u32[]{:S(2)}) copy-start(pred[16]{0:T(512)(128)(4,1)S(1)} %get-tuple-element.255) | copy-start | bytes 52
  3.0 284.6 %copy-start.25 = (pred[16]{0:T(512)(128)(4,1)}, pred[16]{0:T(512)(128)(4,1)S(1)}, u32[]{:S(2)}) copy-start(pred[16]{0:T(512)(128)(4,1)S(1)} %get-tuple-element.256) | copy-start | bytes 52
  8.8 5.8 copy-start.17
  13.3 2.7 copy-start.13
  15.1 2.3 copy-start.14
  18.7 1.5 copy-start.18
  19.3 2.8 copy-start.9
  280.7 5.9 copy-start.27
  283.8 2.8 copy-start.7
  549.6 131.0 %copy-start.19 = (bf16[512,256]{1,0:T(8,128)(2,1)S(1)}, bf16[512,256]{1,0:T(8,128)(2,1)}, u32[]{:S(2)}) copy-start(bf16[512,256]{1,0:T(8,128)(2,1)} %get-tuple-element.231) | copy-start | bytes 786436
  549.6 131.0 %copy-start.20 = (bf16[512,256]{1,0:T(8,128)(2,1)S(1)}, bf16[512,256]{1,0:T(8,128)(2,1)}, u32[]{:S(2)}) copy-start(bf16[512,256]{1,0:T(8,128)(2,1)} %get-tuple-element.232) | copy-start | bytes 786436
  549.6 131.0 %copy-start.21 = (bf16[512,256]{1,0:T(8,128)(2,1)S(1)}, bf16[512,256]{1,0:T(8,128)(2,1)}, u32[]{:S(2)}) copy-start(bf16[512,256]{1,0:T(8,128)(2,1)} %get-tuple-element.233) | copy-start | bytes 786436
  549.6 131.0 %copy-start.22 = (bf16[512,256]{1,0:T(8,128)(2,1)S(1)}, bf16[512,256]{1,0:T(8,128)(2,1)}, u32[]{:S(2)}) copy-start(bf16[512,256]{1,0:T(8,128)(2,1)} %get-tuple-element.234) | copy-start | bytes 786436
  680.6 9.4 copy-start
  680.6 9.4 copy-start.26
  687.8 4.6 copy-start.28
  687.8 4.6 copy-start.8
  919.4 1.6 copy-start.1
  920.9 1.6 copy-start.2
  922.5 1.2 copy-start.3
  923.8 1.0 copy-start.4
  924.8 1.0 copy-start.5
  925.8 1.0 copy-start.6
  926.8 5.7 copy-start.23
  933.2 4.9 copy-start.11
  938.1 3.0 copy-start.10
  941.1 2.9 copy-start.12

commit v15 on v14

--- a/solution.py
+++ b/solution.py
@@ -241,20 +241,20 @@
                 near[i, m].start()
         for back in backs:
             back.begin()
+        for i in range(1, chips):
+            copy = remote(
+                r_ref.at[i], r_out.at[i], r_s.at[i], r_r.at[i], same_core[chips - i - 1]
+            )
+            copy.start()
+            rows_back.append(copy)
+        copy = pltpu.make_async_copy(r_ref.at[0], r_out.at[0], local)
+        copy.start()
+        rows_back.append(copy)
         moves[0].wait()
         relay.begin()
         relay.run()
         for back in backs:
             back.pass_on()
-        for i in range(1, chips):
-            copy = remote(
-                r_ref.at[i], r_out.at[i], r_s.at[i], r_r.at[i], same_core[chips - i - 1]
-            )
-            copy.start()
-            rows_back.append(copy)
-        copy = pltpu.make_async_copy(r_ref.at[0], r_out.at[0], local)
-        copy.start()
-        rows_back.append(copy)
 
         def pair(i, m):
             chip = lax.rem(c + i, chips)

time: 956 us -> 933 us (0.976)
  Pallas kernels: 848 us -> 823 us
    pallas_call x1, Pallas kernels: 131 us -> 107 us  [column_sum(): pl.pallas_call(kernel, out_shape=[jax.ShapeDtypeStruct(shape, F32)] + [ja...]
where the time goes in v15:
time: 933 us; the launch traced here: 921 us
  Pallas kernels  823 us (88%)
  local copies, waits for them, and re-layouts  48.9 us (5%)
  other arithmetic  28.3 us (3%)
  matrix products  18 us (2%)
    pallas_call x1, Pallas kernels, forward_exchange(): pl.pallas_call(kernel, out_shape=kept + [sds((8, width), F32), sds((8, wi...  256 us
    pallas_call x1, Pallas kernels, backward_exchange(): pl.pallas_call(kernel, out_shape=[sds((rows, width), F32), sds((8, width)...  220 us
    pallas_call x1, Pallas kernels, dispatch(): pl.pallas_call(kernel, out_shape=[sds((chips, per_far, width), BF)] * 2 +...  137 us
    pallas_call x1, Pallas kernels, column_sum(): pl.pallas_call(kernel, out_shape=[jax.ShapeDtypeStruct(shape, F32)] + [ja...  107 us
    pallas_call x1, Pallas kernels, experts_run(): pl.pallas_call(kernel, out_shape=[blocks, dots, blocks, ExpertsBack.out(t...  101 us

profile of v15, /device:TPU:11, one launch (start us, length us, event | category | flops | bytes accessed | tf_op | source)
XLA Modules:
  0.0 921.1 jit_solution(8738223695592403363)
XLA Ops:
  9.6 1.6 concatenate.25.refs_2_
  11.2 0.9 copy.206
  15.1 1.0 copy_bitcast_fusion.1
  16.4 1.0 copy.159.refs_9_
  19.3 0.9 pad_maximum_fusion.refs_1_
  20.9 1.2 reshape.554.refs_7_
  22.4 1.0 copy.178.refs_8_
  23.4 255.8 %shard_map.342 = (bf16[1024,2048]{1,0:T(8,128)(2,1)}, f32[1024,640]{1,0:T(8,128)}, bf16[1024,512]{1,0:T(8,128)(2,1)}, bf16[2,1024,256]{2,1,0:T(8,128)(2,1)}, bf1...) custom-call(bf16[128,2048]{1,0:T(8,128)(2,1)} %refs_16_.1, ...), custom_call_target="tpu_custom_call" | custom-call | tf_op jit(solution)/shard_map/pallas_call | solution.py:899
  279.3 1.4 multiply_reduce_fusion.3
  282.0 1.7 constant_dynamic-slice_fusion.2.refs_15_
  283.8 1.2 dynamic-slice_bitcast_fusion
  285.3 1.3 slice_bitcast_fusion
  288.2 0.9 pad.28.refs_5_
  289.1 1.2 slice.102
  291.1 0.8 slice_reduce_fusion.5
  292.0 2.3 fusion.10.hot_ref
  294.2 1.4 fusion.5
  295.6 1.3 slice_multiply_fusion.3
  296.9 136.8 %shard_map.343 = (bf16[4,256,2048]{2,1,0:T(8,128)(2,1)}, bf16[4,256,2048]{2,1,0:T(8,128)(2,1)}, bf16[8,4,64,1408]{3,2,1,0:T(8,128)(2,1)}, bf16[8,4,64,1408]{3,2,...) custom-call(bf16[1024,512]{1,0:T(8,128)(2,1)} %fusion.10.hot_ref, ...), custom_call_target="tpu_custom_call" | custom-call | tf_op jit(solution)/shard_map/pallas_call | solution.py:1043
  433.8 101.2 %shard_map.344 = (bf16[4,256,2048]{2,1,0:T(8,128)(2,1)}, bf16[4,256,128]{2,1,0:T(8,128)(2,1)}, bf16[4,256,2048]{2,1,0:T(8,128)(2,1)}, bf16[1,2,8,64,1408]{4,3,2,...) custom-call(bf16[1024,2048]{1,0:T(8,128)(2,1)} %bitcast.131, ...), custom_call_target="tpu_custom_call" | custom-call | tf_op jit(solution)/shard_map/pallas_call | solution.py:1198
  535.0 6.5 add_convert_fusion.1
  541.5 1.1 copy.195
  542.6 1.6 multiply_reduce_fusion
  544.3 1.0 add_convert_fusion.2
  546.0 3.6 concatenate.27.x_hbm
  549.6 106.6 %shard_map.345 = (f32[128,2176]{1,0:T(8,128)}, bf16[4,64,704]{2,1,0:T(8,128)(2,1)}, bf16[4,64,704]{2,1,0:T(8,128)(2,1)}, bf16[4,64,704]{2,1,0:T(8,128)(2,1)}, bf...) custom-call(bf16[4,128,2176]{2,1,0:T(8,128)(2,1)} %concatenate.27.x_hbm, ...), custom_call_target="tpu_custom_call" | custom-call | tf_op jit(solution)/shard_map/pallas_call | solution.py:311
  656.3 7.2 add_convert_fusion
  663.5 1.0 multiply_reduce_fusion.4
  664.5 1.2 convolution_convert_fusion
  665.7 2.4 multiply_reduce_fusion.1
  668.1 1.2 fusion.39
  669.6 1.0 pad.29.refs_20_
  670.6 1.3 copy.186
  671.9 1.3 copy.187
  673.2 1.3 copy.191.refs_19_
  674.5 220.0 %shard_map.346 = (f32[128,2048]{1,0:T(8,128)}, f32[8,2048]{1,0:T(8,128)}, f32[64,640]{1,0:T(8,128)}, bf16[4,8,64,512]{3,2,1,0:T(8,128)(2,1)}, bf16[4,8,64,512]{3...) custom-call(bf16[128,2048]{1,0:T(8,128)(2,1)} %get-tuple-element.229, ...), custom_call_target="tpu_custom_call" | custom-call | tf_op jit(solution)/shard_map/pallas_call | solution.py:1691
  894.5 1.6 copy-done.1
  896.1 1.6 copy-done.2
  897.7 1.2 copy-done.3
  898.9 1.0 copy-done.4
  899.9 1.0 copy-done.5
  900.9 1.0 copy-done.6
  901.9 3.0 shard_map.347
  904.9 1.0 fusion.41
  908.4 4.9 convert.33
  913.2 2.9 convert.32
  916.2 2.9 convert.34
  919.1 1.0 copy.210
  (133 shorter events, 22.5 us)
Async XLA Ops:
  0.6 13.5 %copy-start.16 = (bf16[64,2816]{1,0:T(8,128)(2,1)S(1)}, bf16[64,2816]{1,0:T(8,128)(2,1)}, u32[]{:S(2)}) copy-start(bf16[64,2816]{1,0:T(8,128)(2,1)} %param.37) | copy-start | bytes 1081348
  0.7 12.2 %copy-start.15 = (bf16[64,2816]{1,0:T(8,128)(2,1)S(1)}, bf16[64,2816]{1,0:T(8,128)(2,1)}, u32[]{:S(2)}) copy-start(bf16[64,2816]{1,0:T(8,128)(2,1)} %param.36) | copy-start | bytes 1081348
  3.0 284.6 %copy-start.24 = (pred[16]{0:T(512)(128)(4,1)}, pred[16]{0:T(512)(128)(4,1)S(1)}, u32[]{:S(2)}) copy-start(pred[16]{0:T(512)(128)(4,1)S(1)} %get-tuple-element.255) | copy-start | bytes 52
  3.0 284.6 %copy-start.25 = (pred[16]{0:T(512)(128)(4,1)}, pred[16]{0:T(512)(128)(4,1)S(1)}, u32[]{:S(2)}) copy-start(pred[16]{0:T(512)(128)(4,1)S(1)} %get-tuple-element.256) | copy-start | bytes 52
  8.8 5.8 copy-start.17
  13.3 2.7 copy-start.13
  15.1 2.3 copy-start.14
  18.7 1.5 copy-start.18
  19.3 2.8 copy-start.9
  280.7 5.9 copy-start.27
  283.8 2.8 copy-start.7
  549.6 106.6 %copy-start.19 = (bf16[512,256]{1,0:T(8,128)(2,1)S(1)}, bf16[512,256]{1,0:T(8,128)(2,1)}, u32[]{:S(2)}) copy-start(bf16[512,256]{1,0:T(8,128)(2,1)} %get-tuple-element.231) | copy-start | bytes 786436
  549.6 106.7 %copy-start.20 = (bf16[512,256]{1,0:T(8,128)(2,1)S(1)}, bf16[512,256]{1,0:T(8,128)(2,1)}, u32[]{:S(2)}) copy-start(bf16[512,256]{1,0:T(8,128)(2,1)} %get-tuple-element.232) | copy-start | bytes 786436
  549.6 106.7 %copy-start.21 = (bf16[512,256]{1,0:T(8,128)(2,1)S(1)}, bf16[512,256]{1,0:T(8,128)(2,1)}, u32[]{:S(2)}) copy-start(bf16[512,256]{1,0:T(8,128)(2,1)} %get-tuple-element.233) | copy-start | bytes 786436
  549.6 106.7 %copy-start.22 = (bf16[512,256]{1,0:T(8,128)(2,1)S(1)}, bf16[512,256]{1,0:T(8,128)(2,1)}, u32[]{:S(2)}) copy-start(bf16[512,256]{1,0:T(8,128)(2,1)} %get-tuple-element.234) | copy-start | bytes 786436
  656.3 9.4 %copy-start = (f32[128,2048]{1,0:T(8,128)S(1)}, f32[128,2048]{1,0:T(8,128)}, u32[]{:S(2)}) copy-start(f32[128,2048]{1,0:T(8,128)} %get-tuple-element.97.res_ref) | copy-start | bytes 3145732
  656.3 9.4 %copy-start.26 = (f32[128]{0:T(128)S(1)}, f32[128]{0:T(128)}, u32[]{:S(2)}) copy-start(f32[128]{0:T(128)} %fusion.35) | copy-start | bytes 1540
  663.5 4.6 copy-start.28
  663.5 4.6 copy-start.8
  894.5 1.6 copy-start.1
  896.1 1.6 copy-start.2
  897.7 1.2 copy-start.3
  898.9 1.0 copy-start.4
  899.9 1.0 copy-start.5
  900.9 1.0 copy-start.6
  901.9 5.7 copy-start.23
  908.4 4.9 copy-start.11
  913.2 3.0 copy-start.10
  916.2 2.9 copy-start.12
